TPU v7x, 32 devices: a whole 2x2x4 slice. The times are simulated.
32 devices in a mesh: dom: 16 (over z, x, core), sub: 2 (over y).
Axes of the slice: x: 2, y: 2, z: 4, core: 2. Of those that a mesh axis runs over, the one named last changes fastest.
Arguments:
- entity_table: float32 [16384, 256], P(('dom', 'sub')), may hold values from -3 to 3
- entity_state: float32 [16384], P(('dom', 'sub')), may hold values from 0.1 to 1
- relations: float32 [400, 256], replicated, may hold values from -4 to 4
- relation_state: float32 [400], replicated, may hold values from 0.1 to 1
- head_rows: int32 [16, 2, 8192], P('dom', 'sub'), may hold values from 0 to 1023
- tail_rows: int32 [16, 2, 8192], P('dom', 'sub'), may hold values from 0 to 1023
- relation_ids: int32 [16, 2, 8192], P('dom', 'sub'), may hold values from 0 to 399
- negative_rows: int32 [16, 2, 512], P('dom', 'sub'), may hold values from 0 to 1023
- edge_counts: int32 [16, 2], P('dom', 'sub'), may hold values from 1 to 8192, as said below
Outputs:
- new_table: float32 [16384, 256], P(('dom', 'sub'))
- new_state: float32 [16384], P(('dom', 'sub'))
- new_relations: float32 [400, 256], replicated
Inputs may be any that keep to these rules, and one draw needn't show every extreme that they name: `edge_counts`: at least one device has all 8192 slots live.
All inputs are finite; a program needn't handle non-finite values.
Results may differ from a plain program's by a relative error of at most 0.0003.
The roundings to bfloat16 on the way count: a program that leaves them out, or rounds other values in their place, can miss the bound.
Values may be sent and summed in bfloat16 or wider, within the bound.
No kernel may reach another device: no remote copies, remote signals or barrier semaphores. Data moves between devices by JAX's collectives and lax.ppermute only.
A program may use at most 128 MiB of HBM per device.

v0:
```python
import functools
import math

import jax
import jax.numpy as jnp
from jax import lax
from jax.experimental import pallas as pl
from jax.experimental.pallas import tpu as pltpu
from jax.sharding import PartitionSpec as P

learn_rate = 0.1
bf16 = jnp.bfloat16
f32 = jnp.float32
i32 = jnp.int32
params = pltpu.CompilerParams(vmem_limit_bytes=10 * 2**20)


def dot(a, b):
    return jnp.dot(a, b, preferred_element_type=f32)


def dot_nt(a, b):
    return lax.dot_general(a, b, (((1,), (1,)), ((), ())), preferred_element_type=f32)


def one_hot(ids, rows):
    places = lax.broadcasted_iota(jnp.int16, (rows, ids.shape[1]), 0)
    return jnp.where(places == ids.astype(jnp.int16), jnp.ones((), bf16), jnp.zeros((), bf16))


def split(x):
    high = x.astype(bf16)
    return jnp.concatenate([high, (x - high.astype(f32)).astype(bf16)], axis=0)


def gather(pieces, ids):
    rows = pieces[0].shape[1]
    hot = one_hot(ids, len(pieces) * rows)
    total = dot(pieces[0][...], hot[:rows])
    for k in range(1, len(pieces)):
        total = total + dot(pieces[k][...], hot[k * rows : (k + 1) * rows])
    return total


def scatter_add(pieces, ids, pair):
    dims = pair.shape[0] // 2
    hot = one_hot(ids, sum(piece.shape[0] for piece in pieces))
    start = 0
    for piece in pieces:
        part = hot[start : start + piece.shape[0]]
        piece[...] += dot_nt(part, pair[:dims]) + dot_nt(part, pair[dims:])
        start += piece.shape[0]


def add_negatives(pieces, ids, pair):
    count = pair.shape[0] // 2
    hot = one_hot(ids, sum(piece.shape[0] for piece in pieces))
    start = 0
    for piece in pieces:
        part = hot[start : start + piece.shape[0]]
        piece[...] += dot(part, pair[:count]) + dot(part, pair[count:])
        start += piece.shape[0]


def rows_kernel(table, out):
    out[...] = table[...].T.astype(bf16)


def ids_kernel(count, heads, tails, kinds, negatives, ids_out):
    blocks, _, width = ids_out.shape
    for j in range(blocks - 1):
        at = slice(j * width, (j + 1) * width)
        block = jnp.concatenate([heads[:, at], tails[:, at], kinds[:, at]], axis=0)
        ids_out[j] = block.astype(jnp.int16)
    last = jnp.concatenate([negatives[...], jnp.full((2, width), count[0, 0], i32)], axis=0)
    ids_out[blocks - 1] = last.astype(jnp.int16)


def plan_kernel(n, codes, *refs):
    sources, (plan, step_ids, negative_ids) = refs[:-3], refs[-3:]
    team = len(sources)
    most, _, width = step_ids.shape
    me = codes[0]
    counts, blocks = [], []
    for k, ids in enumerate(sources):
        last = ids[most].astype(i32)
        counts.append(jnp.max(last[1:2]))
        blocks.append(lax.div(counts[k] + (width - 1), i32(width)))
        negative_ids[k] = last[0:1] ^ codes[1]
    total = sum(blocks)
    low = lax.div(me * total, i32(team))
    high = lax.div((me + 1) * total, i32(team))
    plan[2 * most] = high - low
    before = []
    for k in range(team):
        ahead = [jnp.where((me ^ j) < (me ^ k), blocks[j], 0) for j in range(team) if j != k]
        before.append(sum(ahead))
        seen = (before[k] < high) & (before[k] + blocks[k] > low)
        plan[2 * most + 1 + k] = seen.astype(i32)

    def one_step(i, carry):
        line = jnp.minimum(low + i, high - 1)
        for k, ids in enumerate(sources):

            @pl.when((line >= before[k]) & (line < before[k] + blocks[k]))
            def _(k=k, ids=ids):
                nth = line - before[k]
                plan[i] = k
                plan[most + i] = jnp.clip(counts[k] - nth * width, 0, width)
                entries = ids[nth].astype(i32)
                near, away = (0, 1) if k < n else (1, 0)
                step_ids[i, 0:1] = entries[near : near + 1] ^ codes[1]
                step_ids[i, 1:2] = entries[away : away + 1] ^ codes[1]
                step_ids[i, 2:3] = entries[2:3]
                step_ids[i, 3:4] = entries[2:3] ^ codes[2]

        return carry

    lax.fori_loop(0, high - low, one_step, 0)


def near_kernel(plan, ids, relations, *refs):
    slab, (rows_out, operator_out, rel_full, rel_split) = refs[:-4], refs[-4:]
    dims = relations.shape[1]
    rel_full[...] = jnp.zeros_like(rel_full)
    rel_full[: relations.shape[0], :] = relations[...]
    rel_split[...] = split(rel_full[...].T)

    def one_block(i, carry):
        entries = ids[i]
        rows_out[i] = gather(slab, entries[0:1]).astype(bf16)
        both = dot(rel_split[...], one_hot(entries[2:3], rel_full.shape[0]))
        operator_out[i] = both[:dims] + both[dims:]
        return carry

    lax.fori_loop(0, plan[2 * ids.shape[0]], one_block, 0)


def edge_kernel(n, plan, ids, negative_ids, near_in, operator_in, *refs):
    near, away = refs[:n], refs[n : 2 * n]
    near_grad, away_grad, negative_out = refs[2 * n : 2 * n + 3]
    away_other = refs[2 * n + 3 : 3 * n + 2]
    relation_out, (table, table_t, negative_grad, relation_sum) = refs[3 * n + 2 : -4], refs[-4:]
    most, _, width = ids.shape
    steps = plan[2 * most]
    count = table.shape[0]
    for piece in (*away_other, relation_sum):
        piece[...] = jnp.zeros_like(piece)
    rows = away[0].shape[1]

    def one_block(i, carry):
        here = plan[i]
        swapped = here >= n

        def take_table(slab):
            found = gather(slab, negative_ids[here])
            table_t[...] = found.astype(bf16)
            table[...] = found.T.astype(bf16)
            negative_grad[...] = jnp.zeros_like(negative_grad)

        fresh = (i == 0) | (plan[jnp.maximum(i - 1, 0)] != here)
        pl.when(fresh & ~swapped)(lambda: take_table(away))
        pl.when(fresh & swapped)(lambda: take_table(near))

        entries = ids[i]

        def score(swapped):
            alive = (lax.broadcasted_iota(i32, (1, width), 1) < plan[most + i]).astype(f32)
            near_rows = near_in[i].astype(f32)
            away_rows = gather(away, entries[1:2])
            head, tail = (away_rows, near_rows) if swapped else (near_rows, away_rows)
            operator = operator_in[i]
            query = head * operator
            query_b = query.astype(bf16)
            positive = jnp.sum(query * tail, axis=0, keepdims=True)
            scores = dot(table[...], query_b)
            pos_coef = -jax.nn.sigmoid(-positive) * alive
            neg_coef = (jax.nn.sigmoid(scores) * (alive * (1.0 / count))).astype(bf16)
            query_grad = pos_coef * tail + dot(table_t[...], neg_coef)
            negative_grad[...] += dot_nt(neg_coef, query_b)
            head_pair, tail_pair = split(query_grad * operator), split(pos_coef * query)
            near_pair, away_pair = (tail_pair, head_pair) if swapped else (head_pair, tail_pair)
            near_grad[i] = near_pair
            away_grad[i] = away_pair
            scatter_add(away_other, entries[1:2] - rows, away_pair)
            scatter_add([relation_sum], entries[3:4], split(query_grad * head))

        pl.when(~swapped)(lambda: score(False))
        pl.when(swapped)(lambda: score(True))

        ends = (i == steps - 1) | (plan[jnp.minimum(i + 1, steps - 1)] != here)

        @pl.when(ends)
        def _():
            negative_out[here] = split(negative_grad[...])

        @pl.when(ends & ~swapped)
        def _():
            add_negatives(away_other, negative_ids[here] - rows, negative_out[here])

        return carry

    lax.fori_loop(0, steps, one_block, 0)
    start = 0
    for piece in relation_out:
        piece[...] = relation_sum[start : start + piece.shape[0], :]
        start += piece.shape[0]


def scatter_kernel(row, start, first, plan, ids, negative_ids, grads, negative_grads, *sums):
    most = ids.shape[0]
    for piece in sums:
        piece[...] = jnp.zeros_like(piece)

    def one_block(i, carry):
        scatter_add(sums, ids[i][row : row + 1] - start, grads[i])
        return carry

    lax.fori_loop(0, plan[2 * most], one_block, 0)
    for k in range(first, first + negative_ids.shape[0] // 2):

        @pl.when(plan[2 * most + 1 + k] != 0)
        def _(k=k):
            add_negatives(sums, negative_ids[k] - start, negative_grads[k])


def entity_kernel(table, state, returned, own, new_table, new_state):
    grad = returned[...] + own[...]
    lanes = 128
    before = jnp.broadcast_to(state[...], (lanes, table.shape[0])).T[:, :1]
    after = before + jnp.mean(grad * grad, axis=-1, keepdims=True)
    new_table[...] = table[...] - learn_rate * grad / jnp.sqrt(after)
    new_state[...] = jnp.broadcast_to(after, (table.shape[0], lanes)).T[:1]


def relation_kernel(chunk, codes, relations, state, mine, theirs, out, grad, column):
    chunks = mine.shape[0] // chunk
    for k in range(2 * chunks):
        part = (mine, theirs)[k // chunks]
        start = (k % chunks) * chunk
        grad[pl.ds(pl.multiple_of(codes[2] ^ (k * chunk), chunk), chunk), :] = part[start : start + chunk, :]
    count = relations.shape[0]
    column[...] = jnp.ones_like(column)
    column[:, :count] = jnp.broadcast_to(state[...], (column.shape[0], count))
    g = grad[:count, :]
    total = column[...].T[:count, :1] + jnp.mean(g * g, axis=-1, keepdims=True)
    out[...] = relations[...] - learn_rate * g / jnp.sqrt(total)


def exchange(x, axis, mask):
    return lax.ppermute(x, axis, [(i, i ^ mask) for i in range(lax.axis_size(axis))])


def on_device(
    entity_table,
    entity_state,
    relations,
    relation_state,
    head_rows,
    tail_rows,
    relation_ids,
    negative_rows,
    edge_counts,
):
    n = lax.axis_size("sub")
    n_dom = lax.axis_size("dom")
    me_sub = lax.axis_index("sub")
    me_dom = lax.axis_index("dom")
    pair = n_dom // 2
    team = 2 * n
    rows, dims = entity_table.shape
    slots = head_rows.shape[2]
    count = negative_rows.shape[2]
    width = count
    most = slots // width
    rel_rows = -(-relations.shape[0] // 256) * 256
    chips = 2 * n
    chunk = rel_rows // (2 * chips)
    me = lax.shift_right_logical(me_dom, pair.bit_length() - 1) * n + me_sub
    chunk_code = (me_dom & 1) * chips + ((me_dom >> 1) & 1) * n + me_sub
    codes = jnp.stack([me, me_sub * rows, chunk_code * chunk]).astype(i32)

    in_vmem = pl.BlockSpec(memory_space=pltpu.VMEM)
    in_smem = pl.BlockSpec(memory_space=pltpu.SMEM)

    def call(kernel, name, outs, scratch, unit, scalars, arrays, held=True, fetch=False):
        place = (lambda x, t: pltpu.VMEM(x, t)) if held else jax.ShapeDtypeStruct
        return pl.pallas_call(
            kernel,
            in_specs=[in_smem] * len(scalars) + [in_vmem] * len(arrays),
            out_specs=[in_vmem] * len(outs),
            out_shape=[place(x, t) for x, t in outs],
            scratch_shapes=scratch,
            compiler_params=params,
            cost_estimate=pl.CostEstimate(flops=int(slots * dims * unit), bytes_accessed=rows * dims, transcendentals=0),
            name=name,
        )(*scalars, *(pltpu.with_memory_space_constraint(x, pltpu.HBM if fetch else pltpu.VMEM) for x in arrays))

    (ids,) = call(
        ids_kernel,
        "ids_kernel",
        [((most + 1, 3, width), jnp.int16)],
        [],
        1,
        (edge_counts,),
        (
            head_rows.reshape(1, slots),
            tail_rows.reshape(1, slots),
            relation_ids.reshape(1, slots),
            negative_rows.reshape(1, count),
        ),
        fetch=True,
    )
    ids, table = lax.optimization_barrier((ids, entity_table))
    (local,) = call(rows_kernel, "rows_kernel", [((dims, rows), bf16)], [], 1, (), (table,), fetch=True)

    def to_peer(x, across, aside):
        pairs = [(d * n + s, (d ^ across) * n + (s ^ aside)) for d in range(n_dom) for s in range(n)]
        return lax.ppermute(x, ("dom", "sub"), pairs)

    def along_sub(x):
        return [x] + [exchange(x, "sub", k) for k in range(1, n)]

    all_ids = along_sub(ids) + along_sub(exchange(ids, "dom", pair))
    near_slab = along_sub(local)
    away_first = exchange(local, "dom", pair)

    plan, step_ids, negative_ids = pl.pallas_call(
        functools.partial(plan_kernel, n),
        in_specs=[in_smem] + [in_vmem] * team,
        out_specs=[in_smem, in_vmem, in_vmem],
        out_shape=[
            jax.ShapeDtypeStruct((2 * most + 1 + team,), i32),
            pltpu.VMEM((most, 4, width), i32),
            pltpu.VMEM((team, 1, width), i32),
        ],
        compiler_params=params,
        cost_estimate=pl.CostEstimate(flops=32 * slots * dims * rows, bytes_accessed=slots * dims, transcendentals=0),
        name="plan_kernel",
    )(codes, *(pltpu.with_memory_space_constraint(x, pltpu.VMEM) for x in all_ids))

    near_plan, away_first = lax.optimization_barrier((plan, away_first))
    away_slab = along_sub(away_first)
    near_rows, operator = call(
        near_kernel,
        "near_kernel",
        [((most, dims, width), bf16), ((most, dims, width), f32)],
        [pltpu.VMEM((rel_rows, dims), f32), pltpu.VMEM((2 * dims, rel_rows), bf16)],
        n * rows + 2 * rel_rows,
        (near_plan,),
        (step_ids, relations, *near_slab),
    )
    sums = ((rows, dims), f32)
    pair_out = ((most, 2 * dims, width), bf16)
    near_grad, away_grad, negative_grad, *found = call(
        functools.partial(edge_kernel, n),
        "edge_kernel",
        [pair_out, pair_out, ((team, 2 * count, dims), bf16)]
        + [sums] * (n - 1)
        + [((chunk, dims), f32)] * chips
        + [((chips * chunk, dims), f32)],
        [pltpu.VMEM((count, dims), bf16), pltpu.VMEM((dims, count), bf16), pltpu.VMEM((count, dims), f32), pltpu.VMEM((rel_rows, dims), f32)],
        (2 * n - 1) * rows + 3 * count + 2 * rel_rows,
        (plan,),
        (step_ids, negative_ids, near_rows, operator, *near_slab, *away_slab),
    )
    away_other, relation_part = found[: n - 1], found[n - 1 :]

    def scatter(name, row, start, parts, first, plan, grads):
        return call(
            functools.partial(scatter_kernel, row, start, first),
            name,
            [sums] * parts,
            [],
            0,
            (plan,),
            (step_ids, negative_ids, grads, negative_grad),
        )

    scale = 2.0 ** -(math.ceil(math.log2(team * slots * 24 / 65504.0)) + 1)

    def narrow(x):
        return (x * scale).astype(jnp.float16)

    def widen(x):
        return x.astype(f32) * (1.0 / scale)

    def to_chip(x, k):
        return to_peer(x, k // n * 2, k % n)

    other_core = exchange(relation_part[chips], "dom", 1)
    partial = [relation_part[k] + other_core[k * chunk : (k + 1) * chunk] for k in range(chips)]
    away_other = [narrow(x) for x in away_other]
    partial, plan, away_other = lax.optimization_barrier((partial, plan, away_other))
    chunk_total = partial[0]
    for k in range(1, chips):
        chunk_total = chunk_total + to_chip(partial[k], k)
    away_received = [widen(exchange(away_other[k - 1], "sub", k)) for k in range(1, n)]
    (away_total,) = scatter("away_kernel", 1, 0, 1, 0, plan, away_grad)
    chunk_total, away_total, plan = lax.optimization_barrier((chunk_total, away_total, plan))
    mask = 4
    while mask < n_dom:
        chunk_total = chunk_total + exchange(chunk_total, "dom", mask)
        mask *= 2
    for x in away_received:
        away_total = away_total + x
    away_total = narrow(away_total)
    plan, away_total, chunk_total = lax.optimization_barrier((plan, away_total, chunk_total))
    returned = exchange(away_total, "dom", pair)
    mine = jnp.concatenate([chunk_total] + [to_chip(chunk_total, k) for k in range(1, chips)], axis=0)
    near_other = scatter("own_other_kernel", 0, rows, n - 1, n, plan, near_grad)
    near_other = [narrow(x) for x in near_other]
    plan, near_other, mine = lax.optimization_barrier((plan, near_other, mine))
    near_received = [widen(exchange(near_other[k - 1], "sub", k)) for k in range(1, n)]
    (near_sum,) = scatter("own_kernel", 0, 0, 1, n, plan, near_grad)
    returned, mine, near_sum = lax.optimization_barrier((returned, mine, near_sum))
    theirs = exchange(mine, "dom", 1)
    (new_relations,) = call(
        functools.partial(relation_kernel, chunk),
        "relation_kernel",
        [(relations.shape, f32)],
        [pltpu.VMEM((rel_rows, dims), f32), pltpu.VMEM((128, rel_rows), f32)],
        0,
        (codes,),
        (relations, relation_state.reshape(1, -1), mine, theirs),
        held=False,
    )
    returned = widen(returned)
    for x in near_received:
        returned = returned + x
    new_table, new_state = call(
        entity_kernel,
        "entity_kernel",
        [((rows, dims), f32), ((1, rows), f32)],
        [],
        1,
        (),
        (entity_table, entity_state.reshape(1, rows), returned, near_sum),
        held=False,
    )
    return (new_table, new_state.reshape(rows), new_relations)


def solution(mesh):
    in_specs = (
        P(("dom", "sub"), None),
        P(("dom", "sub")),
        P(),
        P(),
        P("dom", "sub", None),
        P("dom", "sub", None),
        P("dom", "sub", None),
        P("dom", "sub", None),
        P("dom", "sub"),
    )
    out_specs = (P(("dom", "sub"), None), P(("dom", "sub")), P())
    return jax.shard_map(
        on_device, mesh=mesh, in_specs=in_specs, out_specs=out_specs, check_vma=False
    )
```

profile of v0, /device:TPU:0, one launch (start us, length us, event | category | flops | bytes accessed | tf_op | source)
XLA Modules:
  0.0 84.1 jit_solution(8035865715034572263)
XLA Ops:
  1.3 0.8 ids_kernel.1.refs_0_
  2.1 4.1 %collective-permute-start.1 = (s16[17,3,512]{2,1,0:T(4,128)(2,1)S(1)}, s16[17,3,512]{2,1,0:T(4,128)(2,1)S(1)}, u32[]{:S(2)}, u32[]{:S(2)}) collective-permute-start(s16[17,3,512]{2,1,0:T(4,128)(2,1)S(1)} %ids_kernel.1.refs_0_), channel_id=1, source_target_pairs={{0,16},{2,18},{4,20},{6,22},{8,24},{10,26},{12,28},{14,30},{16,0},... | collective-permute-start | bytes 156680 | tf_op jit(solution)/shard_map/ppermute | solution.py:251
  6.2 1.5 %collective-permute-start = (s16[17,3,512]{2,1,0:T(4,128)(2,1)S(1)}, s16[17,3,512]{2,1,0:T(4,128)(2,1)S(1)}, u32[]{:S(2)}, u32[]{:S(2)}) collective-permute-start(s16[17,3,512]{2,1,0:T(4,128)(2,1)S(1)} %ids_kernel.1.refs_0_), channel_id=1, source_target_pairs={{0,1},{1,0},{2,3},{3,2},{4,5},{5,4},{6,7},{7,6},{8,9},{9,8},{10,11... | collective-permute-start | bytes 156680 | tf_op jit(solution)/shard_map/ppermute | solution.py:251
  7.7 1.2 %rows_kernel.1.refs_0_ = bf16[256,512]{1,0:T(8,128)(2,1)S(1)} custom-call(f32[512,256]{1,0:T(8,128)} %table.2), custom_call_target="tpu_custom_call" | custom-call | flops 2097152 | bytes 131072 | tf_op jit(solution)/shard_map/rows_kernel/pallas_call | solution.py:288
  8.9 0.6 collective-permute-start.4
  9.5 0.1 collective-permute-start.3
  9.6 0.4 collective-permute-done.1.refs_2_
  10.0 1.7 %collective-permute-start.2 = (s16[17,3,512]{2,1,0:T(4,128)(2,1)S(1)}, s16[17,3,512]{2,1,0:T(4,128)(2,1)S(1)}, u32[]{:S(2)}, u32[]{:S(2)}) collective-permute-start(s16[17,3,512]{2,1,0:T(4,128)(2,1)S(1)} %collective-permute-done.1.refs_2_), channel_id=1, source_target_pairs={{0,1},{1,0},{2,3},{3,2},{4,5},{5,4},{6,7},{7,6},{8,9},{9,8},{10,11... | collective-permute-start | bytes 156680 | tf_op jit(solution)/shard_map/ppermute | solution.py:251
  11.7 0.1 pad_add_fusion.codes
  11.8 0.0 copy-start.1
  11.8 0.0 collective-permute-done.refs_1_
  11.8 6.2 %collective-permute-done.2.refs_3_ = s16[17,3,512]{2,1,0:T(4,128)(2,1)S(1)} collective-permute-done((s16[17,3,512]{2,1,0:T(4,128)(2,1)S(1)}, s16[17,3,512]{2,1,0:T(4,128)(2,1)S(1)}, u32[]{:S(2)}, u32[]{:S(2)}) %collective-permute-start.2) | collective-permute-done | bytes 52256 | tf_op jit(solution)/shard_map/ppermute | solution.py:251
  18.0 1.6 %plan_kernel.1 = (s32[37]{0:T(128)S(1)}, s32[16,4,512]{2,1,0:T(4,128)S(1)}, s32[4,1,512]{2,1,0:T(1,128)S(1)}) custom-call(s32[3]{0:T(128)S(1)} %pad_add_fusion.codes, s16[17,3,512]{2,1,0:T(4,128)(2,1)S(1)} %ids_kernel.1.refs_0_, s16[17,3,512]{2,1,0:T(4,128)(2,1)S(1)} %collective-permute-done.refs_1_, s16[17,3,512]{2,1,0:T(4,128)(2,1)S(1)} %collective-permute-done.1.refs_2_, ...), custom_call_target="tpu_custom_call" | custom-call | flops 34359738368 | bytes 2097152 | tf_op jit(solution)/shard_map/plan_kernel/pallas_call | solution.py:328
  19.5 3.7 %collective-permute-done.3.refs_2_ = bf16[256,512]{1,0:T(8,128)(2,1)S(1)} collective-permute-done((bf16[256,512]{1,0:T(8,128)(2,1)S(1)}, bf16[256,512]{1,0:T(8,128)(2,1)S(1)}, u32[]{:S(2)}, u32[]{:S(2)}) %collective-permute-start.3) | collective-permute-done | bytes 262176 | tf_op jit(solution)/shard_map/ppermute | solution.py:251
  23.2 1.5 %collective-permute-start.5 = (bf16[256,512]{1,0:T(8,128)(2,1)S(1)}, bf16[256,512]{1,0:T(8,128)(2,1)S(1)}, u32[]{:S(2)}, u32[]{:S(2)}) collective-permute-start(bf16[256,512]{1,0:T(8,128)(2,1)S(1)} %collective-permute-done.3.refs_2_), channel_id=1, source_target_pairs={{0,1},{1,0},{2,3},{3,2},{4,5},{5,4},{6,7},{7,6},{8,9},{9,8},{10,11... | collective-permute-start | bytes 786440 | tf_op jit(solution)/shard_map/ppermute | solution.py:251
  24.7 0.0 collective-permute-done.4.refs_1_
  24.7 0.0 copy-done.1
  24.7 4.3 %near_kernel.1 = (bf16[16,256,512]{2,1,0:T(8,128)(2,1)S(1)}, f32[16,256,512]{2,1,0:T(8,128)S(1)}) custom-call(s32[37]{0:T(128)S(1)} %get-tuple-element.72.plan, s32[16,4,512]{2,1,0:T(4,128)S(1)} %get-tuple-element.43.ids, f32[400,256]{1,0:T(8,128)S(1)} %copy-done.1, bf16[256,512]{1,0:T(8,128)(2,1)S(1)} %rows_kernel.1.refs_0_, ...), custom_call_target="tpu_custom_call" | custom-call | flops 4294967296 | bytes 131072 | tf_op jit(solution)/shard_map/near_kernel/pallas_call | solution.py:288
  29.1 1.3 %collective-permute-done.5.refs_3_ = bf16[256,512]{1,0:T(8,128)(2,1)S(1)} collective-permute-done((bf16[256,512]{1,0:T(8,128)(2,1)S(1)}, bf16[256,512]{1,0:T(8,128)(2,1)S(1)}, u32[]{:S(2)}, u32[]{:S(2)}) %collective-permute-start.5) | collective-permute-done | bytes 262176 | tf_op jit(solution)/shard_map/ppermute | solution.py:251
  30.4 11.2 %edge_kernel.1 = (bf16[16,512,512]{2,1,0:T(8,128)(2,1)S(1)}, bf16[16,512,512]{2,1,0:T(8,128)(2,1)S(1)}, bf16[4,1024,256]{2,1,0:T(8,128)(2,1)S(1)}, f32[512,256]{...) custom-call(s32[37]{0:T(128)S(1)} %get-tuple-element.72.plan, ...), custom_call_target="tpu_custom_call" | custom-call | flops 8589934592 | bytes 131072 | tf_op jit(solution)/shard_map/edge_kernel/pallas_call | solution.py:288
  41.5 0.1 collective-permute-start.6
  41.6 0.1 multiply_convert_fusion.2
  41.7 1.5 %collective-permute-done.6 = f32[256,256]{1,0:T(8,128)S(1)} collective-permute-done((f32[256,256]{1,0:T(8,128)S(1)}, f32[256,256]{1,0:T(8,128)S(1)}, u32[]{:S(2)}, u32[]{:S(2)}) %collective-permute-start.6) | collective-permute-done | bytes 262176 | tf_op jit(solution)/shard_map/ppermute | solution.py:251
  43.2 0.6 collective-permute-start.7
  43.7 4.9 %collective-permute-start.8 = (f32[64,256]{1,0:T(8,128)S(1)}, f32[64,256]{1,0:T(8,128)S(1)}, u32[]{:S(2)}, u32[]{:S(2)}) collective-permute-start(f32[64,256]{1,0:T(8,128)S(1)} %get-tuple-element.58), channel_id=1, source_target_pairs={{0,4},{1,5},{2,6},{3,7},{4,0},{5,1},{6,2},{7,3},{8,12},{9,13},{10,... | collective-permute-start | bytes 196616 | tf_op jit(solution)/shard_map/ppermute | solution.py:319
  48.6 0.1 collective-permute-start.9
  48.7 1.4 %collective-permute-start.10 = (f16[512,256]{1,0:T(8,128)(2,1)S(1)}, f16[512,256]{1,0:T(8,128)(2,1)S(1)}, u32[]{:S(2)}, u32[]{:S(2)}) collective-permute-start(f16[512,256]{1,0:T(8,128)(2,1)S(1)} %multiply_convert_fusion.2), channel_id=1, source_target_pairs={{0,1},{1,0},{2,3},{3,2},{4,5},{5,4},{6,7},{7,6},{8,9},{9,8},{10,11... | collective-permute-start | bytes 786440 | tf_op jit(solution)/shard_map/ppermute | solution.py:251
  50.1 3.8 %away_kernel.1 = f32[512,256]{1,0:T(8,128)S(1)} custom-call(s32[37]{0:T(128)S(1)} %get-tuple-element.72.plan, s32[16,4,512]{2,1,0:T(4,128)S(1)} %get-tuple-element.43.ids, s32[4,1,512]{2,1,0:T(1,128)S(1)} %get-tuple-element.44.negative_ids, bf16[16,512,512]{2,1,0:T(8,128)(2,1)S(1)} %get-tuple-element.61.grads, ...), custom_call_target="tpu_custom_call" | custom-call | bytes 131072 | tf_op jit(solution)/shard_map/away_kernel/pallas_call | solution.py:288
  53.9 0.0 collective-permute-done.7
  53.9 0.0 collective-permute-done.8
  53.9 0.0 collective-permute-done.9
  54.0 3.9 %collective-permute-start.11 = (f32[64,256]{1,0:T(8,128)S(1)}, f32[64,256]{1,0:T(8,128)S(1)}, u32[]{:S(2)}, u32[]{:S(2)}) collective-permute-start(f32[64,256]{1,0:T(8,128)S(1)} %add_add_fusion), channel_id=1, source_target_pairs={{0,8},{2,10},{4,12},{6,14},{8,0},{10,2},{12,4},{14,6},{16,24},{18,... | collective-permute-start | bytes 196616 | tf_op jit(solution)/shard_map/ppermute | solution.py:251
  57.8 2.2 %collective-permute-done.11 = f32[64,256]{1,0:T(8,128)S(1)} collective-permute-done((f32[64,256]{1,0:T(8,128)S(1)}, f32[64,256]{1,0:T(8,128)S(1)}, u32[]{:S(2)}, u32[]{:S(2)}) %collective-permute-start.11) | collective-permute-done | bytes 65568 | tf_op jit(solution)/shard_map/ppermute | solution.py:251
  60.1 2.6 %collective-permute-start.12 = (f32[64,256]{1,0:T(8,128)S(1)}, f32[64,256]{1,0:T(8,128)S(1)}, u32[]{:S(2)}, u32[]{:S(2)}) collective-permute-start(f32[64,256]{1,0:T(8,128)S(1)} %add.54), channel_id=1, source_target_pairs={{0,16},{2,18},{4,20},{6,22},{8,24},{10,26},{12,28},{14,30},{16,0},... | collective-permute-start | bytes 196616 | tf_op jit(solution)/shard_map/ppermute | solution.py:251
  62.7 2.6 %collective-permute-done.12 = f32[64,256]{1,0:T(8,128)S(1)} collective-permute-done((f32[64,256]{1,0:T(8,128)S(1)}, f32[64,256]{1,0:T(8,128)S(1)}, u32[]{:S(2)}, u32[]{:S(2)}) %collective-permute-start.12) | collective-permute-done | bytes 65568 | tf_op jit(solution)/shard_map/ppermute | solution.py:251
  65.3 0.0 collective-permute-done.10
  65.3 0.1 multiply_convert_fusion.1
  65.5 1.6 %collective-permute-start.16 = (f32[64,256]{1,0:T(8,128)S(1)}, f32[64,256]{1,0:T(8,128)S(1)}, u32[]{:S(2)}, u32[]{:S(2)}) collective-permute-start(f32[64,256]{1,0:T(8,128)S(1)} %add.55), channel_id=1, source_target_pairs={{0,5},{1,4},{2,7},{3,6},{4,1},{5,0},{6,3},{7,2},{8,13},{9,12},{10,... | collective-permute-start | bytes 196616 | tf_op jit(solution)/shard_map/ppermute | solution.py:319
  67.1 0.5 collective-permute-start.15
  67.5 1.5 %collective-permute-start.14 = (f32[64,256]{1,0:T(8,128)S(1)}, f32[64,256]{1,0:T(8,128)S(1)}, u32[]{:S(2)}, u32[]{:S(2)}) collective-permute-start(f32[64,256]{1,0:T(8,128)S(1)} %add.55), channel_id=1, source_target_pairs={{0,1},{1,0},{2,3},{3,2},{4,5},{5,4},{6,7},{7,6},{8,9},{9,8},{10,11... | collective-permute-start | bytes 196616 | tf_op jit(solution)/shard_map/ppermute | solution.py:319
  69.0 2.6 %collective-permute-start.13 = (f16[512,256]{1,0:T(8,128)(2,1)S(1)}, f16[512,256]{1,0:T(8,128)(2,1)S(1)}, u32[]{:S(2)}, u32[]{:S(2)}) collective-permute-start(f16[512,256]{1,0:T(8,128)(2,1)S(1)} %multiply_convert_fusion.1), channel_id=1, source_target_pairs={{0,16},{2,18},{4,20},{6,22},{8,24},{10,26},{12,28},{14,30},{16,0},... | collective-permute-start | bytes 786440 | tf_op jit(solution)/shard_map/ppermute | solution.py:251
  71.6 2.9 %own_other_kernel.1 = f32[512,256]{1,0:T(8,128)S(1)} custom-call(s32[37]{0:T(128)S(1)} %get-tuple-element.72.plan, s32[16,4,512]{2,1,0:T(4,128)S(1)} %get-tuple-element.43.ids, s32[4,1,512]{2,1,0:T(1,128)S(1)} %get-tuple-element.44.negative_ids, bf16[16,512,512]{2,1,0:T(8,128)(2,1)S(1)} %get-tuple-element.69.grads, ...), custom_call_target="tpu_custom_call" | custom-call | bytes 131072 | tf_op jit(solution)/shard_map/own_other_kernel/pallas_call | solution.py:288
  74.5 0.0 copy-start
  74.5 0.0 copy-start.2
  74.6 0.0 copy-start.3
  74.6 0.1 multiply_convert_fusion
  74.6 0.0 collective-permute-done.16
  74.6 0.0 collective-permute-done.15
  74.7 0.0 collective-permute-done.14
  74.7 0.8 collective-permute-start.17
  75.5 2.9 %own_kernel.1.own = f32[512,256]{1,0:T(8,128)S(1)} custom-call(s32[37]{0:T(128)S(1)} %get-tuple-element.72.plan, s32[16,4,512]{2,1,0:T(4,128)S(1)} %get-tuple-element.43.ids, s32[4,1,512]{2,1,0:T(1,128)S(1)} %get-tuple-element.44.negative_ids, bf16[16,512,512]{2,1,0:T(8,128)(2,1)S(1)} %get-tuple-element.69.grads, ...), custom_call_target="tpu_custom_call" | custom-call | bytes 131072 | tf_op jit(solution)/shard_map/own_kernel/pallas_call | solution.py:288
  78.4 1.4 %collective-permute-done.13 = f16[512,256]{1,0:T(8,128)(2,1)S(1)} collective-permute-done((f16[512,256]{1,0:T(8,128)(2,1)S(1)}, f16[512,256]{1,0:T(8,128)(2,1)S(1)}, u32[]{:S(2)}, u32[]{:S(2)}) %collective-permute-start.13) | collective-permute-done | bytes 262176 | tf_op jit(solution)/shard_map/ppermute | solution.py:251
  79.8 0.0 collective-permute-start.18
  79.8 1.3 %collective-permute-done.17 = f16[512,256]{1,0:T(8,128)(2,1)S(1)} collective-permute-done((f16[512,256]{1,0:T(8,128)(2,1)S(1)}, f16[512,256]{1,0:T(8,128)(2,1)S(1)}, u32[]{:S(2)}, u32[]{:S(2)}) %collective-permute-start.17) | collective-permute-done | bytes 262176 | tf_op jit(solution)/shard_map/ppermute | solution.py:251
  81.1 0.1 add_multiply_fusion.returned
  81.2 0.0 copy-done
  81.2 0.0 copy-done.2
  81.2 1.2 %entity_kernel.1 = (f32[512,256]{1,0:T(8,128)}, f32[1,512]{1,0:T(1,128)}) custom-call(f32[512,256]{1,0:T(8,128)S(1)} %copy-done, f32[1,512]{1,0:T(1,128)S(1)} %bitcast.10, f32[512,256]{1,0:T(8,128)S(1)} %add_multiply_fusion.returned, f32[512,256]{1,0:T(8,128)S(1)} %own_kernel.1.own), custom_call_target="tpu_custom_call" | custom-call | flops 2097152 | bytes 131072 | tf_op jit(solution)/shard_map/entity_kernel/pallas_call | solution.py:288
  82.4 0.0 collective-permute-done.18.theirs
  82.4 0.0 copy-done.3
  82.4 1.6 %relation_kernel.1 = f32[400,256]{1,0:T(8,128)} custom-call(s32[3]{0:T(128)S(1)} %pad_add_fusion.codes, f32[400,256]{1,0:T(8,128)S(1)} %copy-done.1, f32[1,400]{1,0:T(1,128)S(1)} %bitcast.11, f32[256,256]{1,0:T(8,128)S(1)} %pad_maximum_fusion.mine, f32[256,256]{1,0:T(8,128)S(1)} %collective-permute-done.18.theirs), custom_call_target="tpu_custom_call" | custom-call | bytes 131072 | tf_op jit(solution)/shard_map/relation_kernel/pallas_call | solution.py:288
  (5 shorter events, 0.1 us)
Async XLA Ops:
  2.1 7.9 %collective-permute-start.1 = (s16[17,3,512]{2,1,0:T(4,128)(2,1)S(1)}, s16[17,3,512]{2,1,0:T(4,128)(2,1)S(1)}, u32[]{:S(2)}, u32[]{:S(2)}) collective-permute-start(s16[17,3,512]{2,1,0:T(4,128)(2,1)S(1)} %ids_kernel.1.refs_0_), channel_id=1, source_target_pairs={{0,16},{2,18},{4,20},{6,22},{8,24},{10,26},{12,28},{14,30},{16,0},... | collective-permute-start | bytes 156680 | tf_op jit(solution)/shard_map/ppermute | solution.py:251
  6.2 5.6 %collective-permute-start = (s16[17,3,512]{2,1,0:T(4,128)(2,1)S(1)}, s16[17,3,512]{2,1,0:T(4,128)(2,1)S(1)}, u32[]{:S(2)}, u32[]{:S(2)}) collective-permute-start(s16[17,3,512]{2,1,0:T(4,128)(2,1)S(1)} %ids_kernel.1.refs_0_), channel_id=1, source_target_pairs={{0,1},{1,0},{2,3},{3,2},{4,5},{5,4},{6,7},{7,6},{8,9},{9,8},{10,11... | collective-permute-start | bytes 156680 | tf_op jit(solution)/shard_map/ppermute | solution.py:251
  8.9 15.8 %collective-permute-start.4 = (bf16[256,512]{1,0:T(8,128)(2,1)S(1)}, bf16[256,512]{1,0:T(8,128)(2,1)S(1)}, u32[]{:S(2)}, u32[]{:S(2)}) collective-permute-start(bf16[256,512]{1,0:T(8,128)(2,1)S(1)} %rows_kernel.1.refs_0_), channel_id=1, source_target_pairs={{0,1},{1,0},{2,3},{3,2},{4,5},{5,4},{6,7},{7,6},{8,9},{9,8},{10,11... | collective-permute-start | bytes 786440 | tf_op jit(solution)/shard_map/ppermute | solution.py:251
  9.5 13.7 %collective-permute-start.3 = (bf16[256,512]{1,0:T(8,128)(2,1)S(1)}, bf16[256,512]{1,0:T(8,128)(2,1)S(1)}, u32[]{:S(2)}, u32[]{:S(2)}) collective-permute-start(bf16[256,512]{1,0:T(8,128)(2,1)S(1)} %rows_kernel.1.refs_0_), channel_id=1, source_target_pairs={{0,16},{2,18},{4,20},{6,22},{8,24},{10,26},{12,28},{14,30},{16,0},... | collective-permute-start | bytes 786440 | tf_op jit(solution)/shard_map/ppermute | solution.py:251
  10.0 8.0 %collective-permute-start.2 = (s16[17,3,512]{2,1,0:T(4,128)(2,1)S(1)}, s16[17,3,512]{2,1,0:T(4,128)(2,1)S(1)}, u32[]{:S(2)}, u32[]{:S(2)}) collective-permute-start(s16[17,3,512]{2,1,0:T(4,128)(2,1)S(1)} %collective-permute-done.1.refs_2_), channel_id=1, source_target_pairs={{0,1},{1,0},{2,3},{3,2},{4,5},{5,4},{6,7},{7,6},{8,9},{9,8},{10,11... | collective-permute-start | bytes 156680 | tf_op jit(solution)/shard_map/ppermute | solution.py:251
  11.8 12.9 %copy-start.1 = (f32[400,256]{1,0:T(8,128)S(1)}, f32[400,256]{1,0:T(8,128)}, u32[]{:S(2)}) copy-start(f32[400,256]{1,0:T(8,128)} %relations.3) | copy-start | bytes 1228804
  23.2 7.1 %collective-permute-start.5 = (bf16[256,512]{1,0:T(8,128)(2,1)S(1)}, bf16[256,512]{1,0:T(8,128)(2,1)S(1)}, u32[]{:S(2)}, u32[]{:S(2)}) collective-permute-start(bf16[256,512]{1,0:T(8,128)(2,1)S(1)} %collective-permute-done.3.refs_2_), channel_id=1, source_target_pairs={{0,1},{1,0},{2,3},{3,2},{4,5},{5,4},{6,7},{7,6},{8,9},{9,8},{10,11... | collective-permute-start | bytes 786440 | tf_op jit(solution)/shard_map/ppermute | solution.py:251
  41.5 1.6 %collective-permute-start.6 = (f32[256,256]{1,0:T(8,128)S(1)}, f32[256,256]{1,0:T(8,128)S(1)}, u32[]{:S(2)}, u32[]{:S(2)}) collective-permute-start(f32[256,256]{1,0:T(8,128)S(1)} %get-tuple-element.51), channel_id=1, source_target_pairs={{0,2},{2,0},{4,6},{6,4},{8,10},{10,8},{12,14},{14,12},{16,18},{18,... | collective-permute-start | bytes 786440 | tf_op jit(solution)/shard_map/ppermute | solution.py:251
  43.2 10.7 %collective-permute-start.7 = (f32[64,256]{1,0:T(8,128)S(1)}, f32[64,256]{1,0:T(8,128)S(1)}, u32[]{:S(2)}, u32[]{:S(2)}) collective-permute-start(f32[64,256]{1,0:T(8,128)S(1)} %get-tuple-element.57), channel_id=1, source_target_pairs={{0,1},{1,0},{2,3},{3,2},{4,5},{5,4},{6,7},{7,6},{8,9},{9,8},{10,11... | collective-permute-start | bytes 196616 | tf_op jit(solution)/shard_map/ppermute | solution.py:319
  43.7 10.2 %collective-permute-start.8 = (f32[64,256]{1,0:T(8,128)S(1)}, f32[64,256]{1,0:T(8,128)S(1)}, u32[]{:S(2)}, u32[]{:S(2)}) collective-permute-start(f32[64,256]{1,0:T(8,128)S(1)} %get-tuple-element.58), channel_id=1, source_target_pairs={{0,4},{1,5},{2,6},{3,7},{4,0},{5,1},{6,2},{7,3},{8,12},{9,13},{10,... | collective-permute-start | bytes 196616 | tf_op jit(solution)/shard_map/ppermute | solution.py:319
  48.6 5.3 %collective-permute-start.9 = (f32[64,256]{1,0:T(8,128)S(1)}, f32[64,256]{1,0:T(8,128)S(1)}, u32[]{:S(2)}, u32[]{:S(2)}) collective-permute-start(f32[64,256]{1,0:T(8,128)S(1)} %get-tuple-element.59), channel_id=1, source_target_pairs={{0,5},{1,4},{2,7},{3,6},{4,1},{5,0},{6,3},{7,2},{8,13},{9,12},{10,... | collective-permute-start | bytes 196616 | tf_op jit(solution)/shard_map/ppermute | solution.py:319
  48.7 16.6 %collective-permute-start.10 = (f16[512,256]{1,0:T(8,128)(2,1)S(1)}, f16[512,256]{1,0:T(8,128)(2,1)S(1)}, u32[]{:S(2)}, u32[]{:S(2)}) collective-permute-start(f16[512,256]{1,0:T(8,128)(2,1)S(1)} %multiply_convert_fusion.2), channel_id=1, source_target_pairs={{0,1},{1,0},{2,3},{3,2},{4,5},{5,4},{6,7},{7,6},{8,9},{9,8},{10,11... | collective-permute-start | bytes 786440 | tf_op jit(solution)/shard_map/ppermute | solution.py:251
  54.0 6.1 %collective-permute-start.11 = (f32[64,256]{1,0:T(8,128)S(1)}, f32[64,256]{1,0:T(8,128)S(1)}, u32[]{:S(2)}, u32[]{:S(2)}) collective-permute-start(f32[64,256]{1,0:T(8,128)S(1)} %add_add_fusion), channel_id=1, source_target_pairs={{0,8},{2,10},{4,12},{6,14},{8,0},{10,2},{12,4},{14,6},{16,24},{18,... | collective-permute-start | bytes 196616 | tf_op jit(solution)/shard_map/ppermute | solution.py:251
  60.1 5.2 %collective-permute-start.12 = (f32[64,256]{1,0:T(8,128)S(1)}, f32[64,256]{1,0:T(8,128)S(1)}, u32[]{:S(2)}, u32[]{:S(2)}) collective-permute-start(f32[64,256]{1,0:T(8,128)S(1)} %add.54), channel_id=1, source_target_pairs={{0,16},{2,18},{4,20},{6,22},{8,24},{10,26},{12,28},{14,30},{16,0},... | collective-permute-start | bytes 196616 | tf_op jit(solution)/shard_map/ppermute | solution.py:251
  65.5 9.2 %collective-permute-start.16 = (f32[64,256]{1,0:T(8,128)S(1)}, f32[64,256]{1,0:T(8,128)S(1)}, u32[]{:S(2)}, u32[]{:S(2)}) collective-permute-start(f32[64,256]{1,0:T(8,128)S(1)} %add.55), channel_id=1, source_target_pairs={{0,5},{1,4},{2,7},{3,6},{4,1},{5,0},{6,3},{7,2},{8,13},{9,12},{10,... | collective-permute-start | bytes 196616 | tf_op jit(solution)/shard_map/ppermute | solution.py:319
  67.1 7.6 %collective-permute-start.15 = (f32[64,256]{1,0:T(8,128)S(1)}, f32[64,256]{1,0:T(8,128)S(1)}, u32[]{:S(2)}, u32[]{:S(2)}) collective-permute-start(f32[64,256]{1,0:T(8,128)S(1)} %add.55), channel_id=1, source_target_pairs={{0,4},{1,5},{2,6},{3,7},{4,0},{5,1},{6,2},{7,3},{8,12},{9,13},{10,... | collective-permute-start | bytes 196616 | tf_op jit(solution)/shard_map/ppermute | solution.py:319
  67.5 7.1 %collective-permute-start.14 = (f32[64,256]{1,0:T(8,128)S(1)}, f32[64,256]{1,0:T(8,128)S(1)}, u32[]{:S(2)}, u32[]{:S(2)}) collective-permute-start(f32[64,256]{1,0:T(8,128)S(1)} %add.55), channel_id=1, source_target_pairs={{0,1},{1,0},{2,3},{3,2},{4,5},{5,4},{6,7},{7,6},{8,9},{9,8},{10,11... | collective-permute-start | bytes 196616 | tf_op jit(solution)/shard_map/ppermute | solution.py:319
  69.0 10.8 %collective-permute-start.13 = (f16[512,256]{1,0:T(8,128)(2,1)S(1)}, f16[512,256]{1,0:T(8,128)(2,1)S(1)}, u32[]{:S(2)}, u32[]{:S(2)}) collective-permute-start(f16[512,256]{1,0:T(8,128)(2,1)S(1)} %multiply_convert_fusion.1), channel_id=1, source_target_pairs={{0,16},{2,18},{4,20},{6,22},{8,24},{10,26},{12,28},{14,30},{16,0},... | collective-permute-start | bytes 786440 | tf_op jit(solution)/shard_map/ppermute | solution.py:251
  74.5 6.7 %copy-start = (f32[512,256]{1,0:T(8,128)S(1)}, f32[512,256]{1,0:T(8,128)}, u32[]{:S(2)}) copy-start(f32[512,256]{1,0:T(8,128)} %table.2) | copy-start | bytes 1572868
  74.5 6.7 %copy-start.2 = (f32[512]{0:T(512)S(1)}, f32[512]{0:T(512)}, u32[]{:S(2)}) copy-start(f32[512]{0:T(512)} %param.10) | copy-start | bytes 6148
  74.6 7.8 %copy-start.3 = (f32[400]{0:T(512)S(1)}, f32[400]{0:T(512)}, u32[]{:S(2)}) copy-start(f32[400]{0:T(512)} %param.12) | copy-start | bytes 4804
  74.7 6.4 %collective-permute-start.17 = (f16[512,256]{1,0:T(8,128)(2,1)S(1)}, f16[512,256]{1,0:T(8,128)(2,1)S(1)}, u32[]{:S(2)}, u32[]{:S(2)}) collective-permute-start(f16[512,256]{1,0:T(8,128)(2,1)S(1)} %multiply_convert_fusion), channel_id=1, source_target_pairs={{0,1},{1,0},{2,3},{3,2},{4,5},{5,4},{6,7},{7,6},{8,9},{9,8},{10,11... | collective-permute-start | bytes 786440 | tf_op jit(solution)/shard_map/ppermute | solution.py:251
  79.8 2.6 %collective-permute-start.18 = (f32[256,256]{1,0:T(8,128)S(1)}, f32[256,256]{1,0:T(8,128)S(1)}, u32[]{:S(2)}, u32[]{:S(2)}) collective-permute-start(f32[256,256]{1,0:T(8,128)S(1)} %pad_maximum_fusion.mine), channel_id=1, source_target_pairs={{0,2},{2,0},{4,6},{6,4},{8,10},{10,8},{12,14},{14,12},{16,18},{18,... | collective-permute-start | bytes 786440 | tf_op jit(solution)/shard_map/ppermute | solution.py:251
where the time goes:
time: 84.2 us; the launch traced here: 84.1 us
  Pallas kernels  31.6 us (38%)
  starting transfers between devices  29.9 us (36%)
  waiting for transfers between devices  20.6 us (24%)
  between operations  1.5 us (2%)
    pallas_call x9, Pallas kernels, call(): pl.pallas_call(kernel, in_specs=[in_smem] * len(scalars) + [in_vmem] * le...  30 us
    ppermute x13, starting transfers between devices, exchange(): lax.ppermute(x, axis, [(i, i ^ mask) for i in range(lax.axis_size(axis))])  20.8 us
    ppermute x13, waiting for transfers between devices, exchange(): lax.ppermute(x, axis, [(i, i ^ mask) for i in range(lax.axis_size(axis))])  20.6 us
    ppermute x6, starting transfers between devices, to_peer(): return lax.ppermute(x, ('dom', 'sub'), pairs)  9.07 us
  transfers between devices with their start and end apart: 19, of which 9 were waited for; matrix products, arithmetic and copies ran while one was open for 0% of the time, Pallas kernels for 21%

commit v1 on v0

--- a/solution.py
+++ b/solution.py
@@ -62,11 +62,8 @@
         start += piece.shape[0]
 
 
-def rows_kernel(table, out):
-    out[...] = table[...].T.astype(bf16)
-
-
-def ids_kernel(count, heads, tails, kinds, negatives, ids_out):
+def prep_kernel(count, table, heads, tails, kinds, negatives, rows_out, ids_out):
+    rows_out[...] = table[...].T.astype(bf16)
     blocks, _, width = ids_out.shape
     for j in range(blocks - 1):
         at = slice(j * width, (j + 1) * width)
@@ -296,14 +293,15 @@
             name=name,
         )(*scalars, *(pltpu.with_memory_space_constraint(x, pltpu.HBM if fetch else pltpu.VMEM) for x in arrays))
 
-    (ids,) = call(
-        ids_kernel,
-        "ids_kernel",
-        [((most + 1, 3, width), jnp.int16)],
+    local, ids = call(
+        prep_kernel,
+        "prep_kernel",
+        [((dims, rows), bf16), ((most + 1, 3, width), jnp.int16)],
         [],
         1,
         (edge_counts,),
         (
+            entity_table,
             head_rows.reshape(1, slots),
             tail_rows.reshape(1, slots),
             relation_ids.reshape(1, slots),
@@ -311,8 +309,6 @@
         ),
         fetch=True,
     )
-    ids, table = lax.optimization_barrier((ids, entity_table))
-    (local,) = call(rows_kernel, "rows_kernel", [((dims, rows), bf16)], [], 1, (), (table,), fetch=True)
 
     def to_peer(x, across, aside):
         pairs = [(d * n + s, (d ^ across) * n + (s ^ aside)) for d in range(n_dom) for s in range(n)]
@@ -321,9 +317,10 @@
     def along_sub(x):
         return [x] + [exchange(x, "sub", k) for k in range(1, n)]
 
-    all_ids = along_sub(ids) + along_sub(exchange(ids, "dom", pair))
+    away_first = exchange(local, "dom", pair)
+    across, local, ids = lax.optimization_barrier((exchange(ids, "dom", pair), local, ids))
+    all_ids = along_sub(ids) + along_sub(across)
     near_slab = along_sub(local)
-    away_first = exchange(local, "dom", pair)
 
     plan, step_ids, negative_ids = pl.pallas_call(
         functools.partial(plan_kernel, n),
@@ -396,21 +393,20 @@
     for k in range(1, chips):
         chunk_total = chunk_total + to_chip(partial[k], k)
     away_received = [widen(exchange(away_other[k - 1], "sub", k)) for k in range(1, n)]
+    chunk_total, plan = lax.optimization_barrier((chunk_total, plan))
+    terms = [chunk_total] + [exchange(chunk_total, "dom", mask) for mask in range(4, n_dom, 4)]
     (away_total,) = scatter("away_kernel", 1, 0, 1, 0, plan, away_grad)
-    chunk_total, away_total, plan = lax.optimization_barrier((chunk_total, away_total, plan))
-    mask = 4
-    while mask < n_dom:
-        chunk_total = chunk_total + exchange(chunk_total, "dom", mask)
-        mask *= 2
     for x in away_received:
         away_total = away_total + x
     away_total = narrow(away_total)
-    plan, away_total, chunk_total = lax.optimization_barrier((plan, away_total, chunk_total))
+    while len(terms) > 1:
+        terms = [terms[k] + terms[k + 1] for k in range(0, len(terms), 2)]
+    plan, away_total, chunk_total = lax.optimization_barrier((plan, away_total, terms[0]))
     returned = exchange(away_total, "dom", pair)
-    mine = jnp.concatenate([chunk_total] + [to_chip(chunk_total, k) for k in range(1, chips)], axis=0)
     near_other = scatter("own_other_kernel", 0, rows, n - 1, n, plan, near_grad)
     near_other = [narrow(x) for x in near_other]
-    plan, near_other, mine = lax.optimization_barrier((plan, near_other, mine))
+    plan, near_other, chunk_total = lax.optimization_barrier((plan, near_other, chunk_total))
+    mine = jnp.concatenate([chunk_total] + [to_chip(chunk_total, k) for k in range(1, chips)], axis=0)
     near_received = [widen(exchange(near_other[k - 1], "sub", k)) for k in range(1, n)]
     (near_sum,) = scatter("own_kernel", 0, 0, 1, n, plan, near_grad)
     returned, mine, near_sum = lax.optimization_barrier((returned, mine, near_sum))

time: 84.2 us -> 90.3 us (1.072)
  starting transfers between devices: 29.9 us -> 37.7 us
  waiting for transfers between devices: 20.6 us -> 16.6 us
  Pallas kernels: 31.6 us -> 34.7 us
    ppermute x13 -> x14, starting transfers between devices: 20.8 us -> 30.6 us  [exchange(): lax.ppermute(x, axis, [(i, i ^ mask) for i in range(lax.axis_size(axis))])]
    ppermute x13 -> x14, waiting for transfers between devices: 20.6 us -> 11.1 us  [exchange(): lax.ppermute(x, axis, [(i, i ^ mask) for i in range(lax.axis_size(axis))])]
    ppermute x6, waiting for transfers between devices: 0.02 us -> 5.51 us  [to_peer(): return lax.ppermute(x, ('dom', 'sub'), pairs)]
    pallas_call x9 -> x8, Pallas kernels: 30 us -> 33.1 us  [call(): pl.pallas_call(kernel, in_specs=[in_smem] * len(scalars) + [in_vmem] * le...]
    ppermute x6, starting transfers between devices: 9.07 us -> 7.04 us  [to_peer(): return lax.ppermute(x, ('dom', 'sub'), pairs)]
  transfers between devices with their start and end apart: 19 -> 20, of which waited for: 9 -> 12; matrix products, arithmetic and copies ran while one was open for 0% -> 0% of each run, Pallas kernels for 21% -> 21%
where the time goes in v1:
time: 90.3 us; the launch traced here: 90.9 us
  starting transfers between devices  37.7 us (42%)
  Pallas kernels  34.7 us (38%)
  waiting for transfers between devices  16.6 us (18%)
  between operations  1.49 us (2%)
    pallas_call x8, Pallas kernels, call(): pl.pallas_call(kernel, in_specs=[in_smem] * len(scalars) + [in_vmem] * le...  33.1 us
    ppermute x14, starting transfers between devices, exchange(): lax.ppermute(x, axis, [(i, i ^ mask) for i in range(lax.axis_size(axis))])  30.6 us
    ppermute x14, waiting for transfers between devices, exchange(): lax.ppermute(x, axis, [(i, i ^ mask) for i in range(lax.axis_size(axis))])  11.1 us
    ppermute x6, starting transfers between devices, to_peer(): return lax.ppermute(x, ('dom', 'sub'), pairs)  7.04 us
    ppermute x6, waiting for transfers between devices, to_peer(): return lax.ppermute(x, ('dom', 'sub'), pairs)  5.51 us
  transfers between devices with their start and end apart: 20, of which 12 were waited for; matrix products, arithmetic and copies ran while one was open for 0% of the time, Pallas kernels for 21%

profile of v1, /device:TPU:0, one launch (start us, length us, event | category | flops | bytes accessed | tf_op | source)
XLA Modules:
  0.0 90.9 jit_solution(3908251710602731358)
XLA Ops:
  1.3 1.3 %prep_kernel.1 = (bf16[256,512]{1,0:T(8,128)(2,1)S(1)}, s16[17,3,512]{2,1,0:T(4,128)(2,1)S(1)}) custom-call(s32[1,1]{1,0:T(1,128)S(6)} %copy.12.count, f32[512,256]{1,0:T(8,128)} %table.3, s32[1,8192]{1,0:T(1,128)} %bitcast.12, s32[1,8192]{1,0:T(1,128)} %bitcast.13, s32[1,8192]{1,0:T(1,128)} %bitcast.14, s32[1,512]{1,0:T(1,128)} %bitcast.15), custom_call_target="tpu_custom_call" | custom-call | flops 2097152 | bytes 131072 | tf_op jit(solution)/shard_map/prep_kernel/pallas_call | solution.py:285
  2.5 4.1 %collective-permute-start = (s16[17,3,512]{2,1,0:T(4,128)(2,1)S(1)}, s16[17,3,512]{2,1,0:T(4,128)(2,1)S(1)}, u32[]{:S(2)}, u32[]{:S(2)}) collective-permute-start(s16[17,3,512]{2,1,0:T(4,128)(2,1)S(1)} %get-tuple-element.45.refs_0_), channel_id=1, source_target_pairs={{0,16},{2,18},{4,20},{6,22},{8,24},{10,26},{12,28},{14,30},{16,0},... | collective-permute-start | bytes 156680 | tf_op jit(solution)/shard_map/ppermute | solution.py:248
  6.6 0.1 collective-permute-start.3
  6.7 3.8 %collective-permute-done.refs_2_ = s16[17,3,512]{2,1,0:T(4,128)(2,1)S(1)} collective-permute-done((s16[17,3,512]{2,1,0:T(4,128)(2,1)S(1)}, s16[17,3,512]{2,1,0:T(4,128)(2,1)S(1)}, u32[]{:S(2)}, u32[]{:S(2)}) %collective-permute-start) | collective-permute-done | bytes 52256 | tf_op jit(solution)/shard_map/ppermute | solution.py:248
  10.5 7.6 %collective-permute-start.1 = (s16[17,3,512]{2,1,0:T(4,128)(2,1)S(1)}, s16[17,3,512]{2,1,0:T(4,128)(2,1)S(1)}, u32[]{:S(2)}, u32[]{:S(2)}) collective-permute-start(s16[17,3,512]{2,1,0:T(4,128)(2,1)S(1)} %get-tuple-element.45.refs_0_), channel_id=1, source_target_pairs={{0,1},{1,0},{2,3},{3,2},{4,5},{5,4},{6,7},{7,6},{8,9},{9,8},{10,11... | collective-permute-start | bytes 156680 | tf_op jit(solution)/shard_map/ppermute | solution.py:248
  18.1 0.0 collective-permute-start.2
  18.1 0.1 pad_add_fusion.codes
  18.2 0.0 copy-start.1
  18.2 2.0 %collective-permute-start.4 = (bf16[256,512]{1,0:T(8,128)(2,1)S(1)}, bf16[256,512]{1,0:T(8,128)(2,1)S(1)}, u32[]{:S(2)}, u32[]{:S(2)}) collective-permute-start(bf16[256,512]{1,0:T(8,128)(2,1)S(1)} %get-tuple-element.51.refs_0_), channel_id=1, source_target_pairs={{0,1},{1,0},{2,3},{3,2},{4,5},{5,4},{6,7},{7,6},{8,9},{9,8},{10,11... | collective-permute-start | bytes 786440 | tf_op jit(solution)/shard_map/ppermute | solution.py:248
  20.2 0.2 collective-permute-done.1.refs_1_
  20.4 2.0 %collective-permute-done.2.refs_3_ = s16[17,3,512]{2,1,0:T(4,128)(2,1)S(1)} collective-permute-done((s16[17,3,512]{2,1,0:T(4,128)(2,1)S(1)}, s16[17,3,512]{2,1,0:T(4,128)(2,1)S(1)}, u32[]{:S(2)}, u32[]{:S(2)}) %collective-permute-start.2) | collective-permute-done | bytes 52256 | tf_op jit(solution)/shard_map/ppermute | solution.py:248
  22.4 1.6 %plan_kernel.1 = (s32[37]{0:T(128)S(1)}, s32[16,4,512]{2,1,0:T(4,128)S(1)}, s32[4,1,512]{2,1,0:T(1,128)S(1)}) custom-call(s32[3]{0:T(128)S(1)} %pad_add_fusion.codes, s16[17,3,512]{2,1,0:T(4,128)(2,1)S(1)} %get-tuple-element.45.refs_0_, s16[17,3,512]{2,1,0:T(4,128)(2,1)S(1)} %collective-permute-done.1.refs_1_, ...), custom_call_target="tpu_custom_call" | custom-call | flops 34359738368 | bytes 2097152 | tf_op jit(solution)/shard_map/plan_kernel/pallas_call | solution.py:325
  24.0 0.0 collective-permute-done.3.refs_2_
  24.0 0.8 collective-permute-start.5
  24.8 1.4 %collective-permute-done.4.refs_1_ = bf16[256,512]{1,0:T(8,128)(2,1)S(1)} collective-permute-done((bf16[256,512]{1,0:T(8,128)(2,1)S(1)}, bf16[256,512]{1,0:T(8,128)(2,1)S(1)}, u32[]{:S(2)}, u32[]{:S(2)}) %collective-permute-start.4) | collective-permute-done | bytes 262176 | tf_op jit(solution)/shard_map/ppermute | solution.py:248
  26.3 0.0 copy-done.1
  26.3 5.0 %near_kernel.1 = (bf16[16,256,512]{2,1,0:T(8,128)(2,1)S(1)}, f32[16,256,512]{2,1,0:T(8,128)S(1)}) custom-call(s32[37]{0:T(128)S(1)} %get-tuple-element.76.plan, s32[16,4,512]{2,1,0:T(4,128)S(1)} %get-tuple-element.48.ids, f32[400,256]{1,0:T(8,128)S(1)} %copy-done.1, bf16[256,512]{1,0:T(8,128)(2,1)S(1)} %get-tuple-element.51.refs_0_, ...), custom_call_target="tpu_custom_call" | custom-call | flops 4294967296 | bytes 131072 | tf_op jit(solution)/shard_map/near_kernel/pallas_call | solution.py:285
  31.3 0.0 collective-permute-done.5.refs_3_
  31.3 12.9 %edge_kernel.1 = (bf16[16,512,512]{2,1,0:T(8,128)(2,1)S(1)}, bf16[16,512,512]{2,1,0:T(8,128)(2,1)S(1)}, bf16[4,1024,256]{2,1,0:T(8,128)(2,1)S(1)}, f32[512,256]{...) custom-call(s32[37]{0:T(128)S(1)} %get-tuple-element.76.plan, ...), custom_call_target="tpu_custom_call" | custom-call | flops 8589934592 | bytes 131072 | tf_op jit(solution)/shard_map/edge_kernel/pallas_call | solution.py:285
  44.2 0.1 collective-permute-start.6
  44.3 0.1 multiply_convert_fusion.2
  44.3 1.5 %collective-permute-done.6 = f32[256,256]{1,0:T(8,128)S(1)} collective-permute-done((f32[256,256]{1,0:T(8,128)S(1)}, f32[256,256]{1,0:T(8,128)S(1)}, u32[]{:S(2)}, u32[]{:S(2)}) %collective-permute-start.6) | collective-permute-done | bytes 262176 | tf_op jit(solution)/shard_map/ppermute | solution.py:248
  45.8 0.1 collective-permute-start.7
  46.0 3.3 %collective-permute-start.8 = (f32[64,256]{1,0:T(8,128)S(1)}, f32[64,256]{1,0:T(8,128)S(1)}, u32[]{:S(2)}, u32[]{:S(2)}) collective-permute-start(f32[64,256]{1,0:T(8,128)S(1)} %get-tuple-element.63), channel_id=1, source_target_pairs={{0,4},{1,5},{2,6},{3,7},{4,0},{5,1},{6,2},{7,3},{8,12},{9,13},{10,... | collective-permute-start | bytes 196616 | tf_op jit(solution)/shard_map/ppermute | solution.py:315
  49.2 0.2 collective-permute-start.9
  49.4 0.8 collective-permute-done.7
  50.2 1.7 %collective-permute-done.8 = f32[64,256]{1,0:T(8,128)S(1)} collective-permute-done((f32[64,256]{1,0:T(8,128)S(1)}, f32[64,256]{1,0:T(8,128)S(1)}, u32[]{:S(2)}, u32[]{:S(2)}) %collective-permute-start.8) | collective-permute-done | bytes 65568 | tf_op jit(solution)/shard_map/ppermute | solution.py:315
  51.8 2.6 %collective-permute-done.9 = f32[64,256]{1,0:T(8,128)S(1)} collective-permute-done((f32[64,256]{1,0:T(8,128)S(1)}, f32[64,256]{1,0:T(8,128)S(1)}, u32[]{:S(2)}, u32[]{:S(2)}) %collective-permute-start.9) | collective-permute-done | bytes 65568 | tf_op jit(solution)/shard_map/ppermute | solution.py:315
  54.4 12.4 %collective-permute-start.13 = (f32[64,256]{1,0:T(8,128)S(1)}, f32[64,256]{1,0:T(8,128)S(1)}, u32[]{:S(2)}, u32[]{:S(2)}) collective-permute-start(f32[64,256]{1,0:T(8,128)S(1)} %add_add_fusion.1), channel_id=1, source_target_pairs={{0,24},{2,26},{4,28},{6,30},{8,16},{10,18},{12,20},{14,22},{16,8},... | collective-permute-start | bytes 196616 | tf_op jit(solution)/shard_map/ppermute | solution.py:248
  66.8 0.0 collective-permute-start.12
  66.8 0.6 collective-permute-start.11
  67.5 0.1 collective-permute-start.10
  67.6 4.3 %away_kernel.1 = f32[512,256]{1,0:T(8,128)S(1)} custom-call(s32[37]{0:T(128)S(1)} %get-tuple-element.76.plan, s32[16,4,512]{2,1,0:T(4,128)S(1)} %get-tuple-element.48.ids, s32[4,1,512]{2,1,0:T(1,128)S(1)} %get-tuple-element.49.negative_ids, bf16[16,512,512]{2,1,0:T(8,128)(2,1)S(1)} %get-tuple-element.67.grads, ...), custom_call_target="tpu_custom_call" | custom-call | bytes 131072 | tf_op jit(solution)/shard_map/away_kernel/pallas_call | solution.py:285
  71.8 0.0 collective-permute-done.13
  71.9 0.1 collective-permute-done.12
  72.0 0.0 collective-permute-done.11
  72.0 1.8 %collective-permute-done.10 = f16[512,256]{1,0:T(8,128)(2,1)S(1)} collective-permute-done((f16[512,256]{1,0:T(8,128)(2,1)S(1)}, f16[512,256]{1,0:T(8,128)(2,1)S(1)}, u32[]{:S(2)}, u32[]{:S(2)}) %collective-permute-start.10) | collective-permute-done | bytes 262176 | tf_op jit(solution)/shard_map/ppermute | solution.py:248
  73.8 0.1 multiply_convert_fusion.1
  73.9 2.4 %collective-permute-start.14 = (f16[512,256]{1,0:T(8,128)(2,1)S(1)}, f16[512,256]{1,0:T(8,128)(2,1)S(1)}, u32[]{:S(2)}, u32[]{:S(2)}) collective-permute-start(f16[512,256]{1,0:T(8,128)(2,1)S(1)} %multiply_convert_fusion.1), channel_id=1, source_target_pairs={{0,16},{2,18},{4,20},{6,22},{8,24},{10,26},{12,28},{14,30},{16,0},... | collective-permute-start | bytes 786440 | tf_op jit(solution)/shard_map/ppermute | solution.py:248
  76.3 3.4 %own_other_kernel.1 = f32[512,256]{1,0:T(8,128)S(1)} custom-call(s32[37]{0:T(128)S(1)} %get-tuple-element.76.plan, s32[16,4,512]{2,1,0:T(4,128)S(1)} %get-tuple-element.48.ids, s32[4,1,512]{2,1,0:T(1,128)S(1)} %get-tuple-element.49.negative_ids, bf16[16,512,512]{2,1,0:T(8,128)(2,1)S(1)} %get-tuple-element.73.grads, ...), custom_call_target="tpu_custom_call" | custom-call | bytes 131072 | tf_op jit(solution)/shard_map/own_other_kernel/pallas_call | solution.py:285
  79.7 0.0 copy-start
  79.7 0.0 copy-start.2
  79.7 0.0 copy-start.3
  79.8 0.1 multiply_convert_fusion
  79.8 0.4 collective-permute-start.18
  80.2 1.4 %collective-permute-start.17 = (f32[64,256]{1,0:T(8,128)S(1)}, f32[64,256]{1,0:T(8,128)S(1)}, u32[]{:S(2)}, u32[]{:S(2)}) collective-permute-start(f32[64,256]{1,0:T(8,128)S(1)} %add_add_fusion), channel_id=1, source_target_pairs={{0,5},{1,4},{2,7},{3,6},{4,1},{5,0},{6,3},{7,2},{8,13},{9,12},{10,... | collective-permute-start | bytes 196616 | tf_op jit(solution)/shard_map/ppermute | solution.py:315
  81.6 1.8 %collective-permute-start.16 = (f32[64,256]{1,0:T(8,128)S(1)}, f32[64,256]{1,0:T(8,128)S(1)}, u32[]{:S(2)}, u32[]{:S(2)}) collective-permute-start(f32[64,256]{1,0:T(8,128)S(1)} %add_add_fusion), channel_id=1, source_target_pairs={{0,4},{1,5},{2,6},{3,7},{4,0},{5,1},{6,2},{7,3},{8,12},{9,13},{10,... | collective-permute-start | bytes 196616 | tf_op jit(solution)/shard_map/ppermute | solution.py:315
  83.4 0.3 collective-permute-start.15
  83.7 3.4 %own_kernel.1.own = f32[512,256]{1,0:T(8,128)S(1)} custom-call(s32[37]{0:T(128)S(1)} %get-tuple-element.76.plan, s32[16,4,512]{2,1,0:T(4,128)S(1)} %get-tuple-element.48.ids, s32[4,1,512]{2,1,0:T(1,128)S(1)} %get-tuple-element.49.negative_ids, bf16[16,512,512]{2,1,0:T(8,128)(2,1)S(1)} %get-tuple-element.73.grads, ...), custom_call_target="tpu_custom_call" | custom-call | bytes 131072 | tf_op jit(solution)/shard_map/own_kernel/pallas_call | solution.py:285
  87.1 0.0 collective-permute-done.17
  87.2 0.0 collective-permute-done.16
  87.2 0.5 collective-permute-done.15
  87.7 0.0 collective-permute-done.14
  87.7 0.1 collective-permute-start.19
  87.8 0.0 collective-permute-done.18
  87.8 0.1 add_multiply_fusion.returned
  87.9 0.0 copy-done
  87.9 0.0 copy-done.2
  87.9 1.2 %entity_kernel.1 = (f32[512,256]{1,0:T(8,128)}, f32[1,512]{1,0:T(1,128)}) custom-call(f32[512,256]{1,0:T(8,128)S(1)} %copy-done, f32[1,512]{1,0:T(1,128)S(1)} %bitcast.10, f32[512,256]{1,0:T(8,128)S(1)} %add_multiply_fusion.returned, f32[512,256]{1,0:T(8,128)S(1)} %own_kernel.1.own), custom_call_target="tpu_custom_call" | custom-call | flops 2097152 | bytes 131072 | tf_op jit(solution)/shard_map/entity_kernel/pallas_call | solution.py:285
  89.1 0.2 collective-permute-done.19.theirs
  89.3 0.0 copy-done.3
  89.3 1.6 %relation_kernel.1 = f32[400,256]{1,0:T(8,128)} custom-call(s32[3]{0:T(128)S(1)} %pad_add_fusion.codes, f32[400,256]{1,0:T(8,128)S(1)} %copy-done.1, f32[1,400]{1,0:T(1,128)S(1)} %bitcast.11, f32[256,256]{1,0:T(8,128)S(1)} %pad_maximum_fusion.mine, f32[256,256]{1,0:T(8,128)S(1)} %collective-permute-done.19.theirs), custom_call_target="tpu_custom_call" | custom-call | bytes 131072 | tf_op jit(solution)/shard_map/relation_kernel/pallas_call | solution.py:285
  (4 shorter events, 0.1 us)
Async XLA Ops:
  2.5 8.0 %collective-permute-start = (s16[17,3,512]{2,1,0:T(4,128)(2,1)S(1)}, s16[17,3,512]{2,1,0:T(4,128)(2,1)S(1)}, u32[]{:S(2)}, u32[]{:S(2)}) collective-permute-start(s16[17,3,512]{2,1,0:T(4,128)(2,1)S(1)} %get-tuple-element.45.refs_0_), channel_id=1, source_target_pairs={{0,16},{2,18},{4,20},{6,22},{8,24},{10,26},{12,28},{14,30},{16,0},... | collective-permute-start | bytes 156680 | tf_op jit(solution)/shard_map/ppermute | solution.py:248
  6.6 17.4 %collective-permute-start.3 = (bf16[256,512]{1,0:T(8,128)(2,1)S(1)}, bf16[256,512]{1,0:T(8,128)(2,1)S(1)}, u32[]{:S(2)}, u32[]{:S(2)}) collective-permute-start(bf16[256,512]{1,0:T(8,128)(2,1)S(1)} %get-tuple-element.51.refs_0_), channel_id=1, source_target_pairs={{0,16},{2,18},{4,20},{6,22},{8,24},{10,26},{12,28},{14,30},{16,0},... | collective-permute-start | bytes 786440 | tf_op jit(solution)/shard_map/ppermute | solution.py:248
  10.5 9.9 %collective-permute-start.1 = (s16[17,3,512]{2,1,0:T(4,128)(2,1)S(1)}, s16[17,3,512]{2,1,0:T(4,128)(2,1)S(1)}, u32[]{:S(2)}, u32[]{:S(2)}) collective-permute-start(s16[17,3,512]{2,1,0:T(4,128)(2,1)S(1)} %get-tuple-element.45.refs_0_), channel_id=1, source_target_pairs={{0,1},{1,0},{2,3},{3,2},{4,5},{5,4},{6,7},{7,6},{8,9},{9,8},{10,11... | collective-permute-start | bytes 156680 | tf_op jit(solution)/shard_map/ppermute | solution.py:248
  18.1 4.3 %collective-permute-start.2 = (s16[17,3,512]{2,1,0:T(4,128)(2,1)S(1)}, s16[17,3,512]{2,1,0:T(4,128)(2,1)S(1)}, u32[]{:S(2)}, u32[]{:S(2)}) collective-permute-start(s16[17,3,512]{2,1,0:T(4,128)(2,1)S(1)} %collective-permute-done.refs_2_), channel_id=1, source_target_pairs={{0,1},{1,0},{2,3},{3,2},{4,5},{5,4},{6,7},{7,6},{8,9},{9,8},{10,11... | collective-permute-start | bytes 156680 | tf_op jit(solution)/shard_map/ppermute | solution.py:248
  18.2 8.1 %copy-start.1 = (f32[400,256]{1,0:T(8,128)S(1)}, f32[400,256]{1,0:T(8,128)}, u32[]{:S(2)}) copy-start(f32[400,256]{1,0:T(8,128)} %relations.3) | copy-start | bytes 1228804
  18.2 8.1 %collective-permute-start.4 = (bf16[256,512]{1,0:T(8,128)(2,1)S(1)}, bf16[256,512]{1,0:T(8,128)(2,1)S(1)}, u32[]{:S(2)}, u32[]{:S(2)}) collective-permute-start(bf16[256,512]{1,0:T(8,128)(2,1)S(1)} %get-tuple-element.51.refs_0_), channel_id=1, source_target_pairs={{0,1},{1,0},{2,3},{3,2},{4,5},{5,4},{6,7},{7,6},{8,9},{9,8},{10,11... | collective-permute-start | bytes 786440 | tf_op jit(solution)/shard_map/ppermute | solution.py:248
  24.0 7.3 %collective-permute-start.5 = (bf16[256,512]{1,0:T(8,128)(2,1)S(1)}, bf16[256,512]{1,0:T(8,128)(2,1)S(1)}, u32[]{:S(2)}, u32[]{:S(2)}) collective-permute-start(bf16[256,512]{1,0:T(8,128)(2,1)S(1)} %collective-permute-done.3.refs_2_), channel_id=1, source_target_pairs={{0,1},{1,0},{2,3},{3,2},{4,5},{5,4},{6,7},{7,6},{8,9},{9,8},{10,11... | collective-permute-start | bytes 786440 | tf_op jit(solution)/shard_map/ppermute | solution.py:248
  44.2 1.6 %collective-permute-start.6 = (f32[256,256]{1,0:T(8,128)S(1)}, f32[256,256]{1,0:T(8,128)S(1)}, u32[]{:S(2)}, u32[]{:S(2)}) collective-permute-start(f32[256,256]{1,0:T(8,128)S(1)} %get-tuple-element.56), channel_id=1, source_target_pairs={{0,2},{2,0},{4,6},{6,4},{8,10},{10,8},{12,14},{14,12},{16,18},{18,... | collective-permute-start | bytes 786440 | tf_op jit(solution)/shard_map/ppermute | solution.py:248
  45.8 4.3 %collective-permute-start.7 = (f32[64,256]{1,0:T(8,128)S(1)}, f32[64,256]{1,0:T(8,128)S(1)}, u32[]{:S(2)}, u32[]{:S(2)}) collective-permute-start(f32[64,256]{1,0:T(8,128)S(1)} %get-tuple-element.62), channel_id=1, source_target_pairs={{0,1},{1,0},{2,3},{3,2},{4,5},{5,4},{6,7},{7,6},{8,9},{9,8},{10,11... | collective-permute-start | bytes 196616 | tf_op jit(solution)/shard_map/ppermute | solution.py:315
  46.0 5.9 %collective-permute-start.8 = (f32[64,256]{1,0:T(8,128)S(1)}, f32[64,256]{1,0:T(8,128)S(1)}, u32[]{:S(2)}, u32[]{:S(2)}) collective-permute-start(f32[64,256]{1,0:T(8,128)S(1)} %get-tuple-element.63), channel_id=1, source_target_pairs={{0,4},{1,5},{2,6},{3,7},{4,0},{5,1},{6,2},{7,3},{8,12},{9,13},{10,... | collective-permute-start | bytes 196616 | tf_op jit(solution)/shard_map/ppermute | solution.py:315
  49.2 5.2 %collective-permute-start.9 = (f32[64,256]{1,0:T(8,128)S(1)}, f32[64,256]{1,0:T(8,128)S(1)}, u32[]{:S(2)}, u32[]{:S(2)}) collective-permute-start(f32[64,256]{1,0:T(8,128)S(1)} %get-tuple-element.64), channel_id=1, source_target_pairs={{0,5},{1,4},{2,7},{3,6},{4,1},{5,0},{6,3},{7,2},{8,13},{9,12},{10,... | collective-permute-start | bytes 196616 | tf_op jit(solution)/shard_map/ppermute | solution.py:315
  54.4 17.4 %collective-permute-start.13 = (f32[64,256]{1,0:T(8,128)S(1)}, f32[64,256]{1,0:T(8,128)S(1)}, u32[]{:S(2)}, u32[]{:S(2)}) collective-permute-start(f32[64,256]{1,0:T(8,128)S(1)} %add_add_fusion.1), channel_id=1, source_target_pairs={{0,24},{2,26},{4,28},{6,30},{8,16},{10,18},{12,20},{14,22},{16,8},... | collective-permute-start | bytes 196616 | tf_op jit(solution)/shard_map/ppermute | solution.py:248
  66.8 5.2 %collective-permute-start.12 = (f32[64,256]{1,0:T(8,128)S(1)}, f32[64,256]{1,0:T(8,128)S(1)}, u32[]{:S(2)}, u32[]{:S(2)}) collective-permute-start(f32[64,256]{1,0:T(8,128)S(1)} %add_add_fusion.1), channel_id=1, source_target_pairs={{0,16},{2,18},{4,20},{6,22},{8,24},{10,26},{12,28},{14,30},{16,0},... | collective-permute-start | bytes 196616 | tf_op jit(solution)/shard_map/ppermute | solution.py:248
  66.8 5.2 %collective-permute-start.11 = (f32[64,256]{1,0:T(8,128)S(1)}, f32[64,256]{1,0:T(8,128)S(1)}, u32[]{:S(2)}, u32[]{:S(2)}) collective-permute-start(f32[64,256]{1,0:T(8,128)S(1)} %add_add_fusion.1), channel_id=1, source_target_pairs={{0,8},{2,10},{4,12},{6,14},{8,0},{10,2},{12,4},{14,6},{16,24},{18,... | collective-permute-start | bytes 196616 | tf_op jit(solution)/shard_map/ppermute | solution.py:248
  67.5 6.4 %collective-permute-start.10 = (f16[512,256]{1,0:T(8,128)(2,1)S(1)}, f16[512,256]{1,0:T(8,128)(2,1)S(1)}, u32[]{:S(2)}, u32[]{:S(2)}) collective-permute-start(f16[512,256]{1,0:T(8,128)(2,1)S(1)} %multiply_convert_fusion.2), channel_id=1, source_target_pairs={{0,1},{1,0},{2,3},{3,2},{4,5},{5,4},{6,7},{7,6},{8,9},{9,8},{10,11... | collective-permute-start | bytes 786440 | tf_op jit(solution)/shard_map/ppermute | solution.py:248
  73.9 13.7 %collective-permute-start.14 = (f16[512,256]{1,0:T(8,128)(2,1)S(1)}, f16[512,256]{1,0:T(8,128)(2,1)S(1)}, u32[]{:S(2)}, u32[]{:S(2)}) collective-permute-start(f16[512,256]{1,0:T(8,128)(2,1)S(1)} %multiply_convert_fusion.1), channel_id=1, source_target_pairs={{0,16},{2,18},{4,20},{6,22},{8,24},{10,26},{12,28},{14,30},{16,0},... | collective-permute-start | bytes 786440 | tf_op jit(solution)/shard_map/ppermute | solution.py:248
  79.7 8.1 %copy-start = (f32[512,256]{1,0:T(8,128)S(1)}, f32[512,256]{1,0:T(8,128)}, u32[]{:S(2)}) copy-start(f32[512,256]{1,0:T(8,128)} %table.3) | copy-start | bytes 1572868
  79.7 8.1 %copy-start.2 = (f32[512]{0:T(512)S(1)}, f32[512]{0:T(512)}, u32[]{:S(2)}) copy-start(f32[512]{0:T(512)} %param.10) | copy-start | bytes 6148
  79.7 9.6 %copy-start.3 = (f32[400]{0:T(512)S(1)}, f32[400]{0:T(512)}, u32[]{:S(2)}) copy-start(f32[400]{0:T(512)} %param.12) | copy-start | bytes 4804
  79.8 8.0 %collective-permute-start.18 = (f16[512,256]{1,0:T(8,128)(2,1)S(1)}, f16[512,256]{1,0:T(8,128)(2,1)S(1)}, u32[]{:S(2)}, u32[]{:S(2)}) collective-permute-start(f16[512,256]{1,0:T(8,128)(2,1)S(1)} %multiply_convert_fusion), channel_id=1, source_target_pairs={{0,1},{1,0},{2,3},{3,2},{4,5},{5,4},{6,7},{7,6},{8,9},{9,8},{10,11... | collective-permute-start | bytes 786440 | tf_op jit(solution)/shard_map/ppermute | solution.py:248
  80.2 6.9 %collective-permute-start.17 = (f32[64,256]{1,0:T(8,128)S(1)}, f32[64,256]{1,0:T(8,128)S(1)}, u32[]{:S(2)}, u32[]{:S(2)}) collective-permute-start(f32[64,256]{1,0:T(8,128)S(1)} %add_add_fusion), channel_id=1, source_target_pairs={{0,5},{1,4},{2,7},{3,6},{4,1},{5,0},{6,3},{7,2},{8,13},{9,12},{10,... | collective-permute-start | bytes 196616 | tf_op jit(solution)/shard_map/ppermute | solution.py:315
  81.6 5.6 %collective-permute-start.16 = (f32[64,256]{1,0:T(8,128)S(1)}, f32[64,256]{1,0:T(8,128)S(1)}, u32[]{:S(2)}, u32[]{:S(2)}) collective-permute-start(f32[64,256]{1,0:T(8,128)S(1)} %add_add_fusion), channel_id=1, source_target_pairs={{0,4},{1,5},{2,6},{3,7},{4,0},{5,1},{6,2},{7,3},{8,12},{9,13},{10,... | collective-permute-start | bytes 196616 | tf_op jit(solution)/shard_map/ppermute | solution.py:315
  83.4 4.3 %collective-permute-start.15 = (f32[64,256]{1,0:T(8,128)S(1)}, f32[64,256]{1,0:T(8,128)S(1)}, u32[]{:S(2)}, u32[]{:S(2)}) collective-permute-start(f32[64,256]{1,0:T(8,128)S(1)} %add_add_fusion), channel_id=1, source_target_pairs={{0,1},{1,0},{2,3},{3,2},{4,5},{5,4},{6,7},{7,6},{8,9},{9,8},{10,11... | collective-permute-start | bytes 196616 | tf_op jit(solution)/shard_map/ppermute | solution.py:315
  87.7 1.6 %collective-permute-start.19 = (f32[256,256]{1,0:T(8,128)S(1)}, f32[256,256]{1,0:T(8,128)S(1)}, u32[]{:S(2)}, u32[]{:S(2)}) collective-permute-start(f32[256,256]{1,0:T(8,128)S(1)} %pad_maximum_fusion.mine), channel_id=1, source_target_pairs={{0,2},{2,0},{4,6},{6,4},{8,10},{10,8},{12,14},{14,12},{16,18},{18,... | collective-permute-start | bytes 786440 | tf_op jit(solution)/shard_map/ppermute | solution.py:248

commit v2 on v0

--- a/solution.py
+++ b/solution.py
@@ -398,22 +398,24 @@
     away_received = [widen(exchange(away_other[k - 1], "sub", k)) for k in range(1, n)]
     (away_total,) = scatter("away_kernel", 1, 0, 1, 0, plan, away_grad)
     chunk_total, away_total, plan = lax.optimization_barrier((chunk_total, away_total, plan))
-    mask = 4
-    while mask < n_dom:
+    masks = [4 << k for k in range((n_dom // 4).bit_length() - 1)]
+    for mask in masks[:-1]:
         chunk_total = chunk_total + exchange(chunk_total, "dom", mask)
-        mask *= 2
+    near_other = scatter("own_other_kernel", 0, rows, n - 1, n, plan, near_grad)
+    near_other = [narrow(x) for x in near_other]
+    chunk_total, near_other, plan = lax.optimization_barrier((chunk_total, near_other, plan))
+    near_received = [widen(exchange(near_other[k - 1], "sub", k)) for k in range(1, n)]
+    for mask in masks[-1:]:
+        chunk_total = chunk_total + exchange(chunk_total, "dom", mask)
+    (near_sum,) = scatter("own_kernel", 0, 0, 1, n, plan, near_grad)
     for x in away_received:
         away_total = away_total + x
     away_total = narrow(away_total)
-    plan, away_total, chunk_total = lax.optimization_barrier((plan, away_total, chunk_total))
+    chunk_total, away_total, near_sum = lax.optimization_barrier((chunk_total, away_total, near_sum))
     returned = exchange(away_total, "dom", pair)
+    chunk_total, near_received = lax.optimization_barrier((chunk_total, near_received))
     mine = jnp.concatenate([chunk_total] + [to_chip(chunk_total, k) for k in range(1, chips)], axis=0)
-    near_other = scatter("own_other_kernel", 0, rows, n - 1, n, plan, near_grad)
-    near_other = [narrow(x) for x in near_other]
-    plan, near_other, mine = lax.optimization_barrier((plan, near_other, mine))
-    near_received = [widen(exchange(near_other[k - 1], "sub", k)) for k in range(1, n)]
-    (near_sum,) = scatter("own_kernel", 0, 0, 1, n, plan, near_grad)
-    returned, mine, near_sum = lax.optimization_barrier((returned, mine, near_sum))
+    returned, mine = lax.optimization_barrier((returned, mine))
     theirs = exchange(mine, "dom", 1)
     (new_relations,) = call(
         functools.partial(relation_kernel, chunk),

time: 84.2 us -> 85 us (level)
  waiting for transfers between devices: 20.6 us -> 22.2 us
  starting transfers between devices: 29.9 us -> 29 us
    ppermute x13, starting transfers between devices: 20.8 us -> 14.1 us  [exchange(): lax.ppermute(x, axis, [(i, i ^ mask) for i in range(lax.axis_size(axis))])]
    ppermute x6, starting transfers between devices: 9.07 us -> 14.8 us  [to_peer(): return lax.ppermute(x, ('dom', 'sub'), pairs)]
    ppermute x6, waiting for transfers between devices: 0.02 us -> 3.3 us  [to_peer(): return lax.ppermute(x, ('dom', 'sub'), pairs)]
    ppermute x13, waiting for transfers between devices: 20.6 us -> 18.9 us  [exchange(): lax.ppermute(x, axis, [(i, i ^ mask) for i in range(lax.axis_size(axis))])]
  transfers between devices with their start and end apart: 19 -> 19, of which waited for: 9 -> 12; matrix products, arithmetic and copies ran while one was open for 0% -> 1% of each run, Pallas kernels for 21% -> 21%
where the time goes in v2:
time: 85 us; the launch traced here: 84.7 us
  Pallas kernels  31.5 us (37%)
  starting transfers between devices  29 us (34%)
  waiting for transfers between devices  22.2 us (26%)
  between operations  1.49 us (2%)
    pallas_call x9, Pallas kernels, call(): pl.pallas_call(kernel, in_specs=[in_smem] * len(scalars) + [in_vmem] * le...  30 us
    ppermute x13, waiting for transfers between devices, exchange(): lax.ppermute(x, axis, [(i, i ^ mask) for i in range(lax.axis_size(axis))])  18.9 us
    ppermute x6, starting transfers between devices, to_peer(): return lax.ppermute(x, ('dom', 'sub'), pairs)  14.8 us
    ppermute x13, starting transfers between devices, exchange(): lax.ppermute(x, axis, [(i, i ^ mask) for i in range(lax.axis_size(axis))])  14.1 us
    ppermute x6, waiting for transfers between devices, to_peer(): return lax.ppermute(x, ('dom', 'sub'), pairs)  3.3 us
  transfers between devices with their start and end apart: 19, of which 12 were waited for; matrix products, arithmetic and copies ran while one was open for 1% of the time, Pallas kernels for 21%

profile of v2, /device:TPU:0, one launch (start us, length us, event | category | flops | bytes accessed | tf_op | source)
XLA Modules:
  0.0 84.7 jit_solution(7472307432390481337)
XLA Ops:
  1.3 0.8 ids_kernel.1.refs_0_
  2.1 4.1 %collective-permute-start.1 = (s16[17,3,512]{2,1,0:T(4,128)(2,1)S(1)}, s16[17,3,512]{2,1,0:T(4,128)(2,1)S(1)}, u32[]{:S(2)}, u32[]{:S(2)}) collective-permute-start(s16[17,3,512]{2,1,0:T(4,128)(2,1)S(1)} %ids_kernel.1.refs_0_), channel_id=1, source_target_pairs={{0,16},{2,18},{4,20},{6,22},{8,24},{10,26},{12,28},{14,30},{16,0},... | collective-permute-start | bytes 156680 | tf_op jit(solution)/shard_map/ppermute | solution.py:251
  6.2 1.5 %collective-permute-start = (s16[17,3,512]{2,1,0:T(4,128)(2,1)S(1)}, s16[17,3,512]{2,1,0:T(4,128)(2,1)S(1)}, u32[]{:S(2)}, u32[]{:S(2)}) collective-permute-start(s16[17,3,512]{2,1,0:T(4,128)(2,1)S(1)} %ids_kernel.1.refs_0_), channel_id=1, source_target_pairs={{0,1},{1,0},{2,3},{3,2},{4,5},{5,4},{6,7},{7,6},{8,9},{9,8},{10,11... | collective-permute-start | bytes 156680 | tf_op jit(solution)/shard_map/ppermute | solution.py:251
  7.7 1.2 %rows_kernel.1.refs_0_ = bf16[256,512]{1,0:T(8,128)(2,1)S(1)} custom-call(f32[512,256]{1,0:T(8,128)} %table.2), custom_call_target="tpu_custom_call" | custom-call | flops 2097152 | bytes 131072 | tf_op jit(solution)/shard_map/rows_kernel/pallas_call | solution.py:288
  8.9 0.6 collective-permute-start.4
  9.5 0.1 collective-permute-start.3
  9.6 0.4 collective-permute-done.1.refs_2_
  10.0 1.7 %collective-permute-start.2 = (s16[17,3,512]{2,1,0:T(4,128)(2,1)S(1)}, s16[17,3,512]{2,1,0:T(4,128)(2,1)S(1)}, u32[]{:S(2)}, u32[]{:S(2)}) collective-permute-start(s16[17,3,512]{2,1,0:T(4,128)(2,1)S(1)} %collective-permute-done.1.refs_2_), channel_id=1, source_target_pairs={{0,1},{1,0},{2,3},{3,2},{4,5},{5,4},{6,7},{7,6},{8,9},{9,8},{10,11... | collective-permute-start | bytes 156680 | tf_op jit(solution)/shard_map/ppermute | solution.py:251
  11.7 0.1 pad_add_fusion.codes
  11.8 0.0 copy-start.1
  11.8 0.0 collective-permute-done.refs_1_
  11.8 6.2 %collective-permute-done.2.refs_3_ = s16[17,3,512]{2,1,0:T(4,128)(2,1)S(1)} collective-permute-done((s16[17,3,512]{2,1,0:T(4,128)(2,1)S(1)}, s16[17,3,512]{2,1,0:T(4,128)(2,1)S(1)}, u32[]{:S(2)}, u32[]{:S(2)}) %collective-permute-start.2) | collective-permute-done | bytes 52256 | tf_op jit(solution)/shard_map/ppermute | solution.py:251
  18.0 1.6 %plan_kernel.1 = (s32[37]{0:T(128)S(1)}, s32[16,4,512]{2,1,0:T(4,128)S(1)}, s32[4,1,512]{2,1,0:T(1,128)S(1)}) custom-call(s32[3]{0:T(128)S(1)} %pad_add_fusion.codes, s16[17,3,512]{2,1,0:T(4,128)(2,1)S(1)} %ids_kernel.1.refs_0_, s16[17,3,512]{2,1,0:T(4,128)(2,1)S(1)} %collective-permute-done.refs_1_, s16[17,3,512]{2,1,0:T(4,128)(2,1)S(1)} %collective-permute-done.1.refs_2_, ...), custom_call_target="tpu_custom_call" | custom-call | flops 34359738368 | bytes 2097152 | tf_op jit(solution)/shard_map/plan_kernel/pallas_call | solution.py:328
  19.5 3.7 %collective-permute-done.3.refs_2_ = bf16[256,512]{1,0:T(8,128)(2,1)S(1)} collective-permute-done((bf16[256,512]{1,0:T(8,128)(2,1)S(1)}, bf16[256,512]{1,0:T(8,128)(2,1)S(1)}, u32[]{:S(2)}, u32[]{:S(2)}) %collective-permute-start.3) | collective-permute-done | bytes 262176 | tf_op jit(solution)/shard_map/ppermute | solution.py:251
  23.2 1.5 %collective-permute-start.5 = (bf16[256,512]{1,0:T(8,128)(2,1)S(1)}, bf16[256,512]{1,0:T(8,128)(2,1)S(1)}, u32[]{:S(2)}, u32[]{:S(2)}) collective-permute-start(bf16[256,512]{1,0:T(8,128)(2,1)S(1)} %collective-permute-done.3.refs_2_), channel_id=1, source_target_pairs={{0,1},{1,0},{2,3},{3,2},{4,5},{5,4},{6,7},{7,6},{8,9},{9,8},{10,11... | collective-permute-start | bytes 786440 | tf_op jit(solution)/shard_map/ppermute | solution.py:251
  24.7 0.0 collective-permute-done.4.refs_1_
  24.7 0.0 copy-done.1
  24.7 4.3 %near_kernel.1 = (bf16[16,256,512]{2,1,0:T(8,128)(2,1)S(1)}, f32[16,256,512]{2,1,0:T(8,128)S(1)}) custom-call(s32[37]{0:T(128)S(1)} %get-tuple-element.70.plan, s32[16,4,512]{2,1,0:T(4,128)S(1)} %get-tuple-element.44.ids, f32[400,256]{1,0:T(8,128)S(1)} %copy-done.1, bf16[256,512]{1,0:T(8,128)(2,1)S(1)} %rows_kernel.1.refs_0_, ...), custom_call_target="tpu_custom_call" | custom-call | flops 4294967296 | bytes 131072 | tf_op jit(solution)/shard_map/near_kernel/pallas_call | solution.py:288
  29.1 1.3 %collective-permute-done.5.refs_3_ = bf16[256,512]{1,0:T(8,128)(2,1)S(1)} collective-permute-done((bf16[256,512]{1,0:T(8,128)(2,1)S(1)}, bf16[256,512]{1,0:T(8,128)(2,1)S(1)}, u32[]{:S(2)}, u32[]{:S(2)}) %collective-permute-start.5) | collective-permute-done | bytes 262176 | tf_op jit(solution)/shard_map/ppermute | solution.py:251
  30.4 11.2 %edge_kernel.1 = (bf16[16,512,512]{2,1,0:T(8,128)(2,1)S(1)}, bf16[16,512,512]{2,1,0:T(8,128)(2,1)S(1)}, bf16[4,1024,256]{2,1,0:T(8,128)(2,1)S(1)}, f32[512,256]{...) custom-call(s32[37]{0:T(128)S(1)} %get-tuple-element.70.plan, ...), custom_call_target="tpu_custom_call" | custom-call | flops 8589934592 | bytes 131072 | tf_op jit(solution)/shard_map/edge_kernel/pallas_call | solution.py:288
  41.5 0.1 collective-permute-start.6
  41.6 0.1 multiply_convert_fusion.2
  41.7 1.5 %collective-permute-done.6 = f32[256,256]{1,0:T(8,128)S(1)} collective-permute-done((f32[256,256]{1,0:T(8,128)S(1)}, f32[256,256]{1,0:T(8,128)S(1)}, u32[]{:S(2)}, u32[]{:S(2)}) %collective-permute-start.6) | collective-permute-done | bytes 262176 | tf_op jit(solution)/shard_map/ppermute | solution.py:251
  43.2 2.6 %collective-permute-start.7 = (f32[64,256]{1,0:T(8,128)S(1)}, f32[64,256]{1,0:T(8,128)S(1)}, u32[]{:S(2)}, u32[]{:S(2)}) collective-permute-start(f32[64,256]{1,0:T(8,128)S(1)} %get-tuple-element.58), channel_id=1, source_target_pairs={{0,1},{1,0},{2,3},{3,2},{4,5},{5,4},{6,7},{7,6},{8,9},{9,8},{10,11... | collective-permute-start | bytes 196616 | tf_op jit(solution)/shard_map/ppermute | solution.py:319
  45.8 4.9 %collective-permute-start.8 = (f32[64,256]{1,0:T(8,128)S(1)}, f32[64,256]{1,0:T(8,128)S(1)}, u32[]{:S(2)}, u32[]{:S(2)}) collective-permute-start(f32[64,256]{1,0:T(8,128)S(1)} %get-tuple-element.59), channel_id=1, source_target_pairs={{0,4},{1,5},{2,6},{3,7},{4,0},{5,1},{6,2},{7,3},{8,12},{9,13},{10,... | collective-permute-start | bytes 196616 | tf_op jit(solution)/shard_map/ppermute | solution.py:319
  50.7 1.4 %collective-permute-start.9 = (f32[64,256]{1,0:T(8,128)S(1)}, f32[64,256]{1,0:T(8,128)S(1)}, u32[]{:S(2)}, u32[]{:S(2)}) collective-permute-start(f32[64,256]{1,0:T(8,128)S(1)} %get-tuple-element.60), channel_id=1, source_target_pairs={{0,5},{1,4},{2,7},{3,6},{4,1},{5,0},{6,3},{7,2},{8,13},{9,12},{10,... | collective-permute-start | bytes 196616 | tf_op jit(solution)/shard_map/ppermute | solution.py:319
  52.1 0.6 collective-permute-start.12
  52.7 3.8 %away_kernel.1 = f32[512,256]{1,0:T(8,128)S(1)} custom-call(s32[37]{0:T(128)S(1)} %get-tuple-element.70.plan, s32[16,4,512]{2,1,0:T(4,128)S(1)} %get-tuple-element.44.ids, s32[4,1,512]{2,1,0:T(1,128)S(1)} %get-tuple-element.45.negative_ids, bf16[16,512,512]{2,1,0:T(8,128)(2,1)S(1)} %get-tuple-element.62.grads, ...), custom_call_target="tpu_custom_call" | custom-call | bytes 131072 | tf_op jit(solution)/shard_map/away_kernel/pallas_call | solution.py:288
  56.5 0.0 collective-permute-done.7
  56.5 0.0 collective-permute-done.8
  56.5 0.0 collective-permute-done.9
  56.6 0.1 collective-permute-start.10
  56.6 2.9 %own_other_kernel.1 = f32[512,256]{1,0:T(8,128)S(1)} custom-call(s32[37]{0:T(128)S(1)} %get-tuple-element.70.plan, s32[16,4,512]{2,1,0:T(4,128)S(1)} %get-tuple-element.44.ids, s32[4,1,512]{2,1,0:T(1,128)S(1)} %get-tuple-element.45.negative_ids, bf16[16,512,512]{2,1,0:T(8,128)(2,1)S(1)} %get-tuple-element.66.grads, ...), custom_call_target="tpu_custom_call" | custom-call | bytes 131072 | tf_op jit(solution)/shard_map/own_other_kernel/pallas_call | solution.py:288
  59.6 0.0 copy-start
  59.6 0.0 copy-start.2
  59.6 0.1 multiply_convert_fusion.1
  59.7 0.0 copy-start.3
  59.7 1.2 %collective-permute-done.10 = f32[64,256]{1,0:T(8,128)S(1)} collective-permute-done((f32[64,256]{1,0:T(8,128)S(1)}, f32[64,256]{1,0:T(8,128)S(1)}, u32[]{:S(2)}, u32[]{:S(2)}) %collective-permute-start.10) | collective-permute-done | bytes 65568 | tf_op jit(solution)/shard_map/ppermute | solution.py:251
  60.9 1.1 %collective-permute-start.11 = (f32[64,256]{1,0:T(8,128)S(1)}, f32[64,256]{1,0:T(8,128)S(1)}, u32[]{:S(2)}, u32[]{:S(2)}) collective-permute-start(f32[64,256]{1,0:T(8,128)S(1)} %add.52), channel_id=1, source_target_pairs={{0,16},{2,18},{4,20},{6,22},{8,24},{10,26},{12,28},{14,30},{16,0},... | collective-permute-start | bytes 196616 | tf_op jit(solution)/shard_map/ppermute | solution.py:251
  62.0 0.5 collective-permute-start.14
  62.6 2.9 %own_kernel.1.own = f32[512,256]{1,0:T(8,128)S(1)} custom-call(s32[37]{0:T(128)S(1)} %get-tuple-element.70.plan, s32[16,4,512]{2,1,0:T(4,128)S(1)} %get-tuple-element.44.ids, s32[4,1,512]{2,1,0:T(1,128)S(1)} %get-tuple-element.45.negative_ids, bf16[16,512,512]{2,1,0:T(8,128)(2,1)S(1)} %get-tuple-element.66.grads, ...), custom_call_target="tpu_custom_call" | custom-call | bytes 131072 | tf_op jit(solution)/shard_map/own_kernel/pallas_call | solution.py:288
  65.6 0.6 collective-permute-done.11
  66.2 0.0 collective-permute-done.12
  66.2 0.1 multiply_convert_fusion
  66.3 2.2 %collective-permute-start.13 = (f16[512,256]{1,0:T(8,128)(2,1)S(1)}, f16[512,256]{1,0:T(8,128)(2,1)S(1)}, u32[]{:S(2)}, u32[]{:S(2)}) collective-permute-start(f16[512,256]{1,0:T(8,128)(2,1)S(1)} %multiply_convert_fusion), channel_id=1, source_target_pairs={{0,16},{2,18},{4,20},{6,22},{8,24},{10,26},{12,28},{14,30},{16,0},... | collective-permute-start | bytes 786440 | tf_op jit(solution)/shard_map/ppermute | solution.py:251
  68.5 1.4 %collective-permute-done.14 = f16[512,256]{1,0:T(8,128)(2,1)S(1)} collective-permute-done((f16[512,256]{1,0:T(8,128)(2,1)S(1)}, f16[512,256]{1,0:T(8,128)(2,1)S(1)}, u32[]{:S(2)}, u32[]{:S(2)}) %collective-permute-start.14) | collective-permute-done | bytes 262176 | tf_op jit(solution)/shard_map/ppermute | solution.py:251
  69.9 4.9 %collective-permute-start.17 = (f32[64,256]{1,0:T(8,128)S(1)}, f32[64,256]{1,0:T(8,128)S(1)}, u32[]{:S(2)}, u32[]{:S(2)}) collective-permute-start(f32[64,256]{1,0:T(8,128)S(1)} %add.53), channel_id=1, source_target_pairs={{0,5},{1,4},{2,7},{3,6},{4,1},{5,0},{6,3},{7,2},{8,13},{9,12},{10,... | collective-permute-start | bytes 196616 | tf_op jit(solution)/shard_map/ppermute | solution.py:319
  74.8 0.0 collective-permute-start.16
  74.8 1.0 %collective-permute-start.15 = (f32[64,256]{1,0:T(8,128)S(1)}, f32[64,256]{1,0:T(8,128)S(1)}, u32[]{:S(2)}, u32[]{:S(2)}) collective-permute-start(f32[64,256]{1,0:T(8,128)S(1)} %add.53), channel_id=1, source_target_pairs={{0,1},{1,0},{2,3},{3,2},{4,5},{5,4},{6,7},{7,6},{8,9},{9,8},{10,11... | collective-permute-start | bytes 196616 | tf_op jit(solution)/shard_map/ppermute | solution.py:319
  75.8 1.3 %collective-permute-done.17 = f32[64,256]{1,0:T(8,128)S(1)} collective-permute-done((f32[64,256]{1,0:T(8,128)S(1)}, f32[64,256]{1,0:T(8,128)S(1)}, u32[]{:S(2)}, u32[]{:S(2)}) %collective-permute-start.17) | collective-permute-done | bytes 65568 | tf_op jit(solution)/shard_map/ppermute | solution.py:319
  77.1 2.0 %collective-permute-done.16 = f32[64,256]{1,0:T(8,128)S(1)} collective-permute-done((f32[64,256]{1,0:T(8,128)S(1)}, f32[64,256]{1,0:T(8,128)S(1)}, u32[]{:S(2)}, u32[]{:S(2)}) %collective-permute-start.16) | collective-permute-done | bytes 65568 | tf_op jit(solution)/shard_map/ppermute | solution.py:319
  79.1 0.0 collective-permute-done.15
  79.1 2.4 %collective-permute-done.13 = f16[512,256]{1,0:T(8,128)(2,1)S(1)} collective-permute-done((f16[512,256]{1,0:T(8,128)(2,1)S(1)}, f16[512,256]{1,0:T(8,128)(2,1)S(1)}, u32[]{:S(2)}, u32[]{:S(2)}) %collective-permute-start.13) | collective-permute-done | bytes 262176 | tf_op jit(solution)/shard_map/ppermute | solution.py:251
  81.5 0.0 collective-permute-start.18
  81.5 0.1 multiply_add_fusion.returned
  81.6 0.0 copy-done
  81.6 0.0 copy-done.2
  81.6 1.2 %entity_kernel.1 = (f32[512,256]{1,0:T(8,128)}, f32[1,512]{1,0:T(1,128)}) custom-call(f32[512,256]{1,0:T(8,128)S(1)} %copy-done, f32[1,512]{1,0:T(1,128)S(1)} %bitcast.10, f32[512,256]{1,0:T(8,128)S(1)} %multiply_add_fusion.returned, f32[512,256]{1,0:T(8,128)S(1)} %own_kernel.1.own), custom_call_target="tpu_custom_call" | custom-call | flops 2097152 | bytes 131072 | tf_op jit(solution)/shard_map/entity_kernel/pallas_call | solution.py:288
  82.8 0.3 collective-permute-done.18.theirs
  83.0 0.0 copy-done.3
  83.0 1.6 %relation_kernel.1 = f32[400,256]{1,0:T(8,128)} custom-call(s32[3]{0:T(128)S(1)} %pad_add_fusion.codes, f32[400,256]{1,0:T(8,128)S(1)} %copy-done.1, f32[1,400]{1,0:T(1,128)S(1)} %bitcast.11, f32[256,256]{1,0:T(8,128)S(1)} %pad_maximum_fusion.mine, f32[256,256]{1,0:T(8,128)S(1)} %collective-permute-done.18.theirs), custom_call_target="tpu_custom_call" | custom-call | bytes 131072 | tf_op jit(solution)/shard_map/relation_kernel/pallas_call | solution.py:288
  (6 shorter events, 0.1 us)
Async XLA Ops:
  2.1 7.9 %collective-permute-start.1 = (s16[17,3,512]{2,1,0:T(4,128)(2,1)S(1)}, s16[17,3,512]{2,1,0:T(4,128)(2,1)S(1)}, u32[]{:S(2)}, u32[]{:S(2)}) collective-permute-start(s16[17,3,512]{2,1,0:T(4,128)(2,1)S(1)} %ids_kernel.1.refs_0_), channel_id=1, source_target_pairs={{0,16},{2,18},{4,20},{6,22},{8,24},{10,26},{12,28},{14,30},{16,0},... | collective-permute-start | bytes 156680 | tf_op jit(solution)/shard_map/ppermute | solution.py:251
  6.2 5.6 %collective-permute-start = (s16[17,3,512]{2,1,0:T(4,128)(2,1)S(1)}, s16[17,3,512]{2,1,0:T(4,128)(2,1)S(1)}, u32[]{:S(2)}, u32[]{:S(2)}) collective-permute-start(s16[17,3,512]{2,1,0:T(4,128)(2,1)S(1)} %ids_kernel.1.refs_0_), channel_id=1, source_target_pairs={{0,1},{1,0},{2,3},{3,2},{4,5},{5,4},{6,7},{7,6},{8,9},{9,8},{10,11... | collective-permute-start | bytes 156680 | tf_op jit(solution)/shard_map/ppermute | solution.py:251
  8.9 15.8 %collective-permute-start.4 = (bf16[256,512]{1,0:T(8,128)(2,1)S(1)}, bf16[256,512]{1,0:T(8,128)(2,1)S(1)}, u32[]{:S(2)}, u32[]{:S(2)}) collective-permute-start(bf16[256,512]{1,0:T(8,128)(2,1)S(1)} %rows_kernel.1.refs_0_), channel_id=1, source_target_pairs={{0,1},{1,0},{2,3},{3,2},{4,5},{5,4},{6,7},{7,6},{8,9},{9,8},{10,11... | collective-permute-start | bytes 786440 | tf_op jit(solution)/shard_map/ppermute | solution.py:251
  9.5 13.7 %collective-permute-start.3 = (bf16[256,512]{1,0:T(8,128)(2,1)S(1)}, bf16[256,512]{1,0:T(8,128)(2,1)S(1)}, u32[]{:S(2)}, u32[]{:S(2)}) collective-permute-start(bf16[256,512]{1,0:T(8,128)(2,1)S(1)} %rows_kernel.1.refs_0_), channel_id=1, source_target_pairs={{0,16},{2,18},{4,20},{6,22},{8,24},{10,26},{12,28},{14,30},{16,0},... | collective-permute-start | bytes 786440 | tf_op jit(solution)/shard_map/ppermute | solution.py:251
  10.0 8.0 %collective-permute-start.2 = (s16[17,3,512]{2,1,0:T(4,128)(2,1)S(1)}, s16[17,3,512]{2,1,0:T(4,128)(2,1)S(1)}, u32[]{:S(2)}, u32[]{:S(2)}) collective-permute-start(s16[17,3,512]{2,1,0:T(4,128)(2,1)S(1)} %collective-permute-done.1.refs_2_), channel_id=1, source_target_pairs={{0,1},{1,0},{2,3},{3,2},{4,5},{5,4},{6,7},{7,6},{8,9},{9,8},{10,11... | collective-permute-start | bytes 156680 | tf_op jit(solution)/shard_map/ppermute | solution.py:251
  11.8 12.9 %copy-start.1 = (f32[400,256]{1,0:T(8,128)S(1)}, f32[400,256]{1,0:T(8,128)}, u32[]{:S(2)}) copy-start(f32[400,256]{1,0:T(8,128)} %relations.3) | copy-start | bytes 1228804
  23.2 7.1 %collective-permute-start.5 = (bf16[256,512]{1,0:T(8,128)(2,1)S(1)}, bf16[256,512]{1,0:T(8,128)(2,1)S(1)}, u32[]{:S(2)}, u32[]{:S(2)}) collective-permute-start(bf16[256,512]{1,0:T(8,128)(2,1)S(1)} %collective-permute-done.3.refs_2_), channel_id=1, source_target_pairs={{0,1},{1,0},{2,3},{3,2},{4,5},{5,4},{6,7},{7,6},{8,9},{9,8},{10,11... | collective-permute-start | bytes 786440 | tf_op jit(solution)/shard_map/ppermute | solution.py:251
  41.5 1.6 %collective-permute-start.6 = (f32[256,256]{1,0:T(8,128)S(1)}, f32[256,256]{1,0:T(8,128)S(1)}, u32[]{:S(2)}, u32[]{:S(2)}) collective-permute-start(f32[256,256]{1,0:T(8,128)S(1)} %get-tuple-element.52), channel_id=1, source_target_pairs={{0,2},{2,0},{4,6},{6,4},{8,10},{10,8},{12,14},{14,12},{16,18},{18,... | collective-permute-start | bytes 786440 | tf_op jit(solution)/shard_map/ppermute | solution.py:251
  43.2 13.3 %collective-permute-start.7 = (f32[64,256]{1,0:T(8,128)S(1)}, f32[64,256]{1,0:T(8,128)S(1)}, u32[]{:S(2)}, u32[]{:S(2)}) collective-permute-start(f32[64,256]{1,0:T(8,128)S(1)} %get-tuple-element.58), channel_id=1, source_target_pairs={{0,1},{1,0},{2,3},{3,2},{4,5},{5,4},{6,7},{7,6},{8,9},{9,8},{10,11... | collective-permute-start | bytes 196616 | tf_op jit(solution)/shard_map/ppermute | solution.py:319
  45.8 10.7 %collective-permute-start.8 = (f32[64,256]{1,0:T(8,128)S(1)}, f32[64,256]{1,0:T(8,128)S(1)}, u32[]{:S(2)}, u32[]{:S(2)}) collective-permute-start(f32[64,256]{1,0:T(8,128)S(1)} %get-tuple-element.59), channel_id=1, source_target_pairs={{0,4},{1,5},{2,6},{3,7},{4,0},{5,1},{6,2},{7,3},{8,12},{9,13},{10,... | collective-permute-start | bytes 196616 | tf_op jit(solution)/shard_map/ppermute | solution.py:319
  50.7 5.8 %collective-permute-start.9 = (f32[64,256]{1,0:T(8,128)S(1)}, f32[64,256]{1,0:T(8,128)S(1)}, u32[]{:S(2)}, u32[]{:S(2)}) collective-permute-start(f32[64,256]{1,0:T(8,128)S(1)} %get-tuple-element.60), channel_id=1, source_target_pairs={{0,5},{1,4},{2,7},{3,6},{4,1},{5,0},{6,3},{7,2},{8,13},{9,12},{10,... | collective-permute-start | bytes 196616 | tf_op jit(solution)/shard_map/ppermute | solution.py:319
  52.1 14.0 %collective-permute-start.12 = (f16[512,256]{1,0:T(8,128)(2,1)S(1)}, f16[512,256]{1,0:T(8,128)(2,1)S(1)}, u32[]{:S(2)}, u32[]{:S(2)}) collective-permute-start(f16[512,256]{1,0:T(8,128)(2,1)S(1)} %multiply_convert_fusion.2), channel_id=1, source_target_pairs={{0,1},{1,0},{2,3},{3,2},{4,5},{5,4},{6,7},{7,6},{8,9},{9,8},{10,11... | collective-permute-start | bytes 786440 | tf_op jit(solution)/shard_map/ppermute | solution.py:251
  56.6 4.3 %collective-permute-start.10 = (f32[64,256]{1,0:T(8,128)S(1)}, f32[64,256]{1,0:T(8,128)S(1)}, u32[]{:S(2)}, u32[]{:S(2)}) collective-permute-start(f32[64,256]{1,0:T(8,128)S(1)} %add_add_fusion), channel_id=1, source_target_pairs={{0,8},{2,10},{4,12},{6,14},{8,0},{10,2},{12,4},{14,6},{16,24},{18,... | collective-permute-start | bytes 196616 | tf_op jit(solution)/shard_map/ppermute | solution.py:251
  59.6 22.0 %copy-start = (f32[512,256]{1,0:T(8,128)S(1)}, f32[512,256]{1,0:T(8,128)}, u32[]{:S(2)}) copy-start(f32[512,256]{1,0:T(8,128)} %table.2) | copy-start | bytes 1572868
  59.6 22.0 %copy-start.2 = (f32[512]{0:T(512)S(1)}, f32[512]{0:T(512)}, u32[]{:S(2)}) copy-start(f32[512]{0:T(512)} %param.10) | copy-start | bytes 6148
  59.7 23.4 %copy-start.3 = (f32[400]{0:T(512)S(1)}, f32[400]{0:T(512)}, u32[]{:S(2)}) copy-start(f32[400]{0:T(512)} %param.12) | copy-start | bytes 4804
  60.9 5.2 %collective-permute-start.11 = (f32[64,256]{1,0:T(8,128)S(1)}, f32[64,256]{1,0:T(8,128)S(1)}, u32[]{:S(2)}, u32[]{:S(2)}) collective-permute-start(f32[64,256]{1,0:T(8,128)S(1)} %add.52), channel_id=1, source_target_pairs={{0,16},{2,18},{4,20},{6,22},{8,24},{10,26},{12,28},{14,30},{16,0},... | collective-permute-start | bytes 196616 | tf_op jit(solution)/shard_map/ppermute | solution.py:251
  62.0 7.8 %collective-permute-start.14 = (f16[512,256]{1,0:T(8,128)(2,1)S(1)}, f16[512,256]{1,0:T(8,128)(2,1)S(1)}, u32[]{:S(2)}, u32[]{:S(2)}) collective-permute-start(f16[512,256]{1,0:T(8,128)(2,1)S(1)} %multiply_convert_fusion.1), channel_id=1, source_target_pairs={{0,1},{1,0},{2,3},{3,2},{4,5},{5,4},{6,7},{7,6},{8,9},{9,8},{10,11... | collective-permute-start | bytes 786440 | tf_op jit(solution)/shard_map/ppermute | solution.py:251
  66.3 15.2 %collective-permute-start.13 = (f16[512,256]{1,0:T(8,128)(2,1)S(1)}, f16[512,256]{1,0:T(8,128)(2,1)S(1)}, u32[]{:S(2)}, u32[]{:S(2)}) collective-permute-start(f16[512,256]{1,0:T(8,128)(2,1)S(1)} %multiply_convert_fusion), channel_id=1, source_target_pairs={{0,16},{2,18},{4,20},{6,22},{8,24},{10,26},{12,28},{14,30},{16,0},... | collective-permute-start | bytes 786440 | tf_op jit(solution)/shard_map/ppermute | solution.py:251
  69.9 7.1 %collective-permute-start.17 = (f32[64,256]{1,0:T(8,128)S(1)}, f32[64,256]{1,0:T(8,128)S(1)}, u32[]{:S(2)}, u32[]{:S(2)}) collective-permute-start(f32[64,256]{1,0:T(8,128)S(1)} %add.53), channel_id=1, source_target_pairs={{0,5},{1,4},{2,7},{3,6},{4,1},{5,0},{6,3},{7,2},{8,13},{9,12},{10,... | collective-permute-start | bytes 196616 | tf_op jit(solution)/shard_map/ppermute | solution.py:319
  74.8 4.3 %collective-permute-start.16 = (f32[64,256]{1,0:T(8,128)S(1)}, f32[64,256]{1,0:T(8,128)S(1)}, u32[]{:S(2)}, u32[]{:S(2)}) collective-permute-start(f32[64,256]{1,0:T(8,128)S(1)} %add.53), channel_id=1, source_target_pairs={{0,4},{1,5},{2,6},{3,7},{4,0},{5,1},{6,2},{7,3},{8,12},{9,13},{10,... | collective-permute-start | bytes 196616 | tf_op jit(solution)/shard_map/ppermute | solution.py:319
  74.8 4.3 %collective-permute-start.15 = (f32[64,256]{1,0:T(8,128)S(1)}, f32[64,256]{1,0:T(8,128)S(1)}, u32[]{:S(2)}, u32[]{:S(2)}) collective-permute-start(f32[64,256]{1,0:T(8,128)S(1)} %add.53), channel_id=1, source_target_pairs={{0,1},{1,0},{2,3},{3,2},{4,5},{5,4},{6,7},{7,6},{8,9},{9,8},{10,11... | collective-permute-start | bytes 196616 | tf_op jit(solution)/shard_map/ppermute | solution.py:319
  81.5 1.5 %collective-permute-start.18 = (f32[256,256]{1,0:T(8,128)S(1)}, f32[256,256]{1,0:T(8,128)S(1)}, u32[]{:S(2)}, u32[]{:S(2)}) collective-permute-start(f32[256,256]{1,0:T(8,128)S(1)} %pad_maximum_fusion.mine), channel_id=1, source_target_pairs={{0,2},{2,0},{4,6},{6,4},{8,10},{10,8},{12,14},{14,12},{16,18},{18,... | collective-permute-start | bytes 786440 | tf_op jit(solution)/shard_map/ppermute | solution.py:251

commit v3 on v2

--- a/solution.py
+++ b/solution.py
@@ -33,18 +33,16 @@
     return jnp.concatenate([high, (x - high.astype(f32)).astype(bf16)], axis=0)
 
 
-def gather(pieces, ids):
+def gather(pieces, hot):
     rows = pieces[0].shape[1]
-    hot = one_hot(ids, len(pieces) * rows)
     total = dot(pieces[0][...], hot[:rows])
     for k in range(1, len(pieces)):
         total = total + dot(pieces[k][...], hot[k * rows : (k + 1) * rows])
     return total
 
 
-def scatter_add(pieces, ids, pair):
+def scatter_add(pieces, hot, pair):
     dims = pair.shape[0] // 2
-    hot = one_hot(ids, sum(piece.shape[0] for piece in pieces))
     start = 0
     for piece in pieces:
         part = hot[start : start + piece.shape[0]]
@@ -52,9 +50,8 @@
         start += piece.shape[0]
 
 
-def add_negatives(pieces, ids, pair):
+def add_negatives(pieces, hot, pair):
     count = pair.shape[0] // 2
-    hot = one_hot(ids, sum(piece.shape[0] for piece in pieces))
     start = 0
     for piece in pieces:
         part = hot[start : start + piece.shape[0]]
@@ -112,7 +109,6 @@
                 step_ids[i, 0:1] = entries[near : near + 1] ^ codes[1]
                 step_ids[i, 1:2] = entries[away : away + 1] ^ codes[1]
                 step_ids[i, 2:3] = entries[2:3]
-                step_ids[i, 3:4] = entries[2:3] ^ codes[2]
 
         return carry
 
@@ -122,25 +118,34 @@
 def near_kernel(plan, ids, relations, *refs):
     slab, (rows_out, operator_out, rel_full, rel_split) = refs[:-4], refs[-4:]
     dims = relations.shape[1]
+    n, rows = len(slab), slab[0].shape[1]
     rel_full[...] = jnp.zeros_like(rel_full)
     rel_full[: relations.shape[0], :] = relations[...]
     rel_split[...] = split(rel_full[...].T)
 
-    def one_block(i, carry):
+    def one_block(i):
         entries = ids[i]
-        rows_out[i] = gather(slab, entries[0:1]).astype(bf16)
+        rows_out[i] = gather(slab, one_hot(entries[0:1], n * rows)).astype(bf16)
         both = dot(rel_split[...], one_hot(entries[2:3], rel_full.shape[0]))
         operator_out[i] = both[:dims] + both[dims:]
+
+    steps = plan[2 * ids.shape[0]]
+
+    def two_blocks(i, carry):
+        one_block(2 * i)
+        one_block(2 * i + 1)
         return carry
 
-    lax.fori_loop(0, plan[2 * ids.shape[0]], one_block, 0)
-
-
-def edge_kernel(n, plan, ids, negative_ids, near_in, operator_in, *refs):
+    lax.fori_loop(0, steps >> 1, two_blocks, 0)
+    pl.when((steps & 1) == 1)(lambda: one_block(steps - 1))
+
+
+def edge_kernel(n, codes, plan, ids, negative_ids, near_in, operator_in, *refs):
     near, away = refs[:n], refs[n : 2 * n]
     near_grad, away_grad, negative_out = refs[2 * n : 2 * n + 3]
     away_other = refs[2 * n + 3 : 3 * n + 2]
-    relation_out, (table, table_t, negative_grad, relation_sum) = refs[3 * n + 2 : -4], refs[-4:]
+    relation_out = refs[3 * n + 2 : -5]
+    table, table_t, negative_grad, relation_sum, ordered = refs[-5:]
     most, _, width = ids.shape
     steps = plan[2 * most]
     count = table.shape[0]
@@ -153,7 +158,7 @@
         swapped = here >= n
 
         def take_table(slab):
-            found = gather(slab, negative_ids[here])
+            found = gather(slab, one_hot(negative_ids[here], n * rows))
             table_t[...] = found.astype(bf16)
             table[...] = found.T.astype(bf16)
             negative_grad[...] = jnp.zeros_like(negative_grad)
@@ -167,7 +172,8 @@
         def score(swapped):
             alive = (lax.broadcasted_iota(i32, (1, width), 1) < plan[most + i]).astype(f32)
             near_rows = near_in[i].astype(f32)
-            away_rows = gather(away, entries[1:2])
+            away_hot = one_hot(entries[1:2], n * rows)
+            away_rows = gather(away, away_hot)
             head, tail = (away_rows, near_rows) if swapped else (near_rows, away_rows)
             operator = operator_in[i]
             query = head * operator
@@ -182,8 +188,8 @@
             near_pair, away_pair = (tail_pair, head_pair) if swapped else (head_pair, tail_pair)
             near_grad[i] = near_pair
             away_grad[i] = away_pair
-            scatter_add(away_other, entries[1:2] - rows, away_pair)
-            scatter_add([relation_sum], entries[3:4], split(query_grad * head))
+            scatter_add(away_other, away_hot[rows:], away_pair)
+            scatter_add([relation_sum], one_hot(entries[2:3], relation_sum.shape[0]), split(query_grad * head))
 
         pl.when(~swapped)(lambda: score(False))
         pl.when(swapped)(lambda: score(True))
@@ -196,32 +202,49 @@
 
         @pl.when(ends & ~swapped)
         def _():
-            add_negatives(away_other, negative_ids[here] - rows, negative_out[here])
+            add_negatives(away_other, one_hot(negative_ids[here] - rows, (n - 1) * rows), negative_out[here])
 
         return carry
 
     lax.fori_loop(0, steps, one_block, 0)
+    chunk = relation_out[0].shape[0]
+    ordered[...] = jnp.zeros_like(ordered)
+    ordered[: relation_sum.shape[0], :] = relation_sum[...]
     start = 0
     for piece in relation_out:
-        piece[...] = relation_sum[start : start + piece.shape[0], :]
+        for k in range(0, piece.shape[0], chunk):
+            at = pl.multiple_of(codes[2] ^ (start + k), chunk)
+            piece[k : k + chunk, :] = ordered[pl.ds(at, chunk), :]
         start += piece.shape[0]
 
 
 def scatter_kernel(row, start, first, plan, ids, negative_ids, grads, negative_grads, *sums):
     most = ids.shape[0]
+    height = sum(piece.shape[0] for piece in sums)
     for piece in sums:
         piece[...] = jnp.zeros_like(piece)
 
-    def one_block(i, carry):
-        scatter_add(sums, ids[i][row : row + 1] - start, grads[i])
+    steps = plan[2 * most]
+
+    def hot_of(i):
+        return one_hot(ids[i][row : row + 1] - start, height)
+
+    def two_blocks(i, carry):
+        hot = jnp.concatenate([hot_of(2 * i), hot_of(2 * i + 1)], axis=1)
+        scatter_add(sums, hot, jnp.concatenate([grads[2 * i], grads[2 * i + 1]], axis=1))
         return carry
 
-    lax.fori_loop(0, plan[2 * most], one_block, 0)
+    lax.fori_loop(0, steps >> 1, two_blocks, 0)
+
+    @pl.when((steps & 1) == 1)
+    def _():
+        scatter_add(sums, hot_of(steps - 1), grads[steps - 1])
+
     for k in range(first, first + negative_ids.shape[0] // 2):
 
         @pl.when(plan[2 * most + 1 + k] != 0)
         def _(k=k):
-            add_negatives(sums, negative_ids[k] - start, negative_grads[k])
+            add_negatives(sums, one_hot(negative_ids[k] - start, height), negative_grads[k])
 
 
 def entity_kernel(table, state, returned, own, new_table, new_state):
@@ -331,7 +354,7 @@
         out_specs=[in_smem, in_vmem, in_vmem],
         out_shape=[
             jax.ShapeDtypeStruct((2 * most + 1 + team,), i32),
-            pltpu.VMEM((most, 4, width), i32),
+            pltpu.VMEM((most, 3, width), i32),
             pltpu.VMEM((team, 1, width), i32),
         ],
         compiler_params=params,
@@ -359,9 +382,10 @@
         + [sums] * (n - 1)
         + [((chunk, dims), f32)] * chips
         + [((chips * chunk, dims), f32)],
-        [pltpu.VMEM((count, dims), bf16), pltpu.VMEM((dims, count), bf16), pltpu.VMEM((count, dims), f32), pltpu.VMEM((rel_rows, dims), f32)],
-        (2 * n - 1) * rows + 3 * count + 2 * rel_rows,
-        (plan,),
+        [pltpu.VMEM((count, dims), bf16), pltpu.VMEM((dims, count), bf16), pltpu.VMEM((count, dims), f32)]
+        + [pltpu.VMEM((-(-relations.shape[0] // 16) * 16, dims), f32), pltpu.VMEM((rel_rows, dims), f32)],
+        3 * n * rows + 3 * count + 2 * rel_rows,
+        (codes, plan),
         (step_ids, negative_ids, near_rows, operator, *near_slab, *away_slab),
     )
     away_other, relation_part = found[: n - 1], found[n - 1 :]
@@ -403,19 +427,18 @@
         chunk_total = chunk_total + exchange(chunk_total, "dom", mask)
     near_other = scatter("own_other_kernel", 0, rows, n - 1, n, plan, near_grad)
     near_other = [narrow(x) for x in near_other]
-    chunk_total, near_other, plan = lax.optimization_barrier((chunk_total, near_other, plan))
+    for x in away_received:
+        away_total = away_total + x
+    away_total = narrow(away_total)
+    chunk_total, away_total, near_other, plan = lax.optimization_barrier((chunk_total, away_total, near_other, plan))
     near_received = [widen(exchange(near_other[k - 1], "sub", k)) for k in range(1, n)]
     for mask in masks[-1:]:
         chunk_total = chunk_total + exchange(chunk_total, "dom", mask)
+    chunk_total, away_total, plan = lax.optimization_barrier((chunk_total, away_total, plan))
+    returned = exchange(away_total, "dom", pair)
+    mine = jnp.concatenate([chunk_total] + [to_chip(chunk_total, k) for k in range(1, chips)], axis=0)
     (near_sum,) = scatter("own_kernel", 0, 0, 1, n, plan, near_grad)
-    for x in away_received:
-        away_total = away_total + x
-    away_total = narrow(away_total)
-    chunk_total, away_total, near_sum = lax.optimization_barrier((chunk_total, away_total, near_sum))
-    returned = exchange(away_total, "dom", pair)
-    chunk_total, near_received = lax.optimization_barrier((chunk_total, near_received))
-    mine = jnp.concatenate([chunk_total] + [to_chip(chunk_total, k) for k in range(1, chips)], axis=0)
-    returned, mine = lax.optimization_barrier((returned, mine))
+    returned, mine, near_sum = lax.optimization_barrier((returned, mine, near_sum))
     theirs = exchange(mine, "dom", 1)
     (new_relations,) = call(
         functools.partial(relation_kernel, chunk),

time: 85 us -> 80.8 us (0.951)
  Pallas kernels: 31.5 us -> 28.2 us
  starting transfers between devices: 29 us -> 27.3 us
    pallas_call x9, Pallas kernels: 30 us -> 26.6 us  [call(): pl.pallas_call(kernel, in_specs=[in_smem] * len(scalars) + [in_vmem] * le...]
    ppermute x13, waiting for transfers between devices: 18.9 us -> 20.6 us  [exchange(): lax.ppermute(x, axis, [(i, i ^ mask) for i in range(lax.axis_size(axis))])]
    ppermute x6, waiting for transfers between devices: 3.3 us -> 1.95 us  [to_peer(): return lax.ppermute(x, ('dom', 'sub'), pairs)]
    ppermute x13, starting transfers between devices: 14.1 us -> 12.8 us  [exchange(): lax.ppermute(x, axis, [(i, i ^ mask) for i in range(lax.axis_size(axis))])]
  transfers between devices with their start and end apart: 19 -> 19, of which waited for: 12 -> 11; matrix products, arithmetic and copies ran while one was open for 1% -> 0% of each run, Pallas kernels for 21% -> 20%
where the time goes in v3:
time: 80.8 us; the launch traced here: 79.9 us
  Pallas kernels  28.2 us (35%)
  starting transfers between devices  27.3 us (34%)
  waiting for transfers between devices  22.5 us (28%)
  between operations  1.49 us (2%)
    pallas_call x9, Pallas kernels, call(): pl.pallas_call(kernel, in_specs=[in_smem] * len(scalars) + [in_vmem] * le...  26.6 us
    ppermute x13, waiting for transfers between devices, exchange(): lax.ppermute(x, axis, [(i, i ^ mask) for i in range(lax.axis_size(axis))])  20.6 us
    ppermute x6, starting transfers between devices, to_peer(): return lax.ppermute(x, ('dom', 'sub'), pairs)  14.4 us
    ppermute x13, starting transfers between devices, exchange(): lax.ppermute(x, axis, [(i, i ^ mask) for i in range(lax.axis_size(axis))])  12.8 us
    ppermute x6, waiting for transfers between devices, to_peer(): return lax.ppermute(x, ('dom', 'sub'), pairs)  1.95 us
  transfers between devices with their start and end apart: 19, of which 11 were waited for; matrix products, arithmetic and copies ran while one was open for 0% of the time, Pallas kernels for 20%

profile of v3, /device:TPU:0, one launch (start us, length us, event | category | flops | bytes accessed | tf_op | source)
XLA Modules:
  0.0 79.9 jit_solution(5051581381926316096)
XLA Ops:
  1.3 0.8 %ids_kernel.1.refs_0_ = s16[17,3,512]{2,1,0:T(4,128)(2,1)S(1)} custom-call(s32[1,1]{1,0:T(1,128)S(6)} %copy.12.count, s32[1,8192]{1,0:T(1,128)} %bitcast.12, s32[1,8192]{1,0:T(1,128)} %bitcast.13, s32[1,8192]{1,0:T(1,128)} %bitcast.14, s32[1,512]{1,0:T(1,128)} %bitcast.15), custom_call_target="tpu_custom_call" | custom-call | flops 2097152 | bytes 131072 | tf_op jit(solution)/shard_map/ids_kernel/pallas_call | solution.py:311
  2.1 4.1 %collective-permute-start.1 = (s16[17,3,512]{2,1,0:T(4,128)(2,1)S(1)}, s16[17,3,512]{2,1,0:T(4,128)(2,1)S(1)}, u32[]{:S(2)}, u32[]{:S(2)}) collective-permute-start(s16[17,3,512]{2,1,0:T(4,128)(2,1)S(1)} %ids_kernel.1.refs_0_), channel_id=1, source_target_pairs={{0,16},{2,18},{4,20},{6,22},{8,24},{10,26},{12,28},{14,30},{16,0},... | collective-permute-start | bytes 156680 | tf_op jit(solution)/shard_map/ppermute | solution.py:274
  6.2 1.5 %collective-permute-start = (s16[17,3,512]{2,1,0:T(4,128)(2,1)S(1)}, s16[17,3,512]{2,1,0:T(4,128)(2,1)S(1)}, u32[]{:S(2)}, u32[]{:S(2)}) collective-permute-start(s16[17,3,512]{2,1,0:T(4,128)(2,1)S(1)} %ids_kernel.1.refs_0_), channel_id=1, source_target_pairs={{0,1},{1,0},{2,3},{3,2},{4,5},{5,4},{6,7},{7,6},{8,9},{9,8},{10,11... | collective-permute-start | bytes 156680 | tf_op jit(solution)/shard_map/ppermute | solution.py:274
  7.7 1.2 %rows_kernel.1.refs_0_ = bf16[256,512]{1,0:T(8,128)(2,1)S(1)} custom-call(f32[512,256]{1,0:T(8,128)} %table.2), custom_call_target="tpu_custom_call" | custom-call | flops 2097152 | bytes 131072 | tf_op jit(solution)/shard_map/rows_kernel/pallas_call | solution.py:311
  8.9 0.6 collective-permute-start.4
  9.5 0.1 collective-permute-start.3
  9.6 0.4 collective-permute-done.1.refs_2_
  10.0 1.7 %collective-permute-start.2 = (s16[17,3,512]{2,1,0:T(4,128)(2,1)S(1)}, s16[17,3,512]{2,1,0:T(4,128)(2,1)S(1)}, u32[]{:S(2)}, u32[]{:S(2)}) collective-permute-start(s16[17,3,512]{2,1,0:T(4,128)(2,1)S(1)} %collective-permute-done.1.refs_2_), channel_id=1, source_target_pairs={{0,1},{1,0},{2,3},{3,2},{4,5},{5,4},{6,7},{7,6},{8,9},{9,8},{10,11... | collective-permute-start | bytes 156680 | tf_op jit(solution)/shard_map/ppermute | solution.py:274
  11.7 0.1 pad_add_fusion.codes
  11.8 0.0 copy-start.1
  11.8 0.0 collective-permute-done.refs_1_
  11.8 6.2 %collective-permute-done.2.refs_3_ = s16[17,3,512]{2,1,0:T(4,128)(2,1)S(1)} collective-permute-done((s16[17,3,512]{2,1,0:T(4,128)(2,1)S(1)}, s16[17,3,512]{2,1,0:T(4,128)(2,1)S(1)}, u32[]{:S(2)}, u32[]{:S(2)}) %collective-permute-start.2) | collective-permute-done | bytes 52256 | tf_op jit(solution)/shard_map/ppermute | solution.py:274
  18.0 1.5 %plan_kernel.1 = (s32[37]{0:T(128)S(1)}, s32[16,3,512]{2,1,0:T(4,128)S(1)}, s32[4,1,512]{2,1,0:T(1,128)S(1)}) custom-call(s32[3]{0:T(128)S(1)} %pad_add_fusion.codes, s16[17,3,512]{2,1,0:T(4,128)(2,1)S(1)} %ids_kernel.1.refs_0_, s16[17,3,512]{2,1,0:T(4,128)(2,1)S(1)} %collective-permute-done.refs_1_, s16[17,3,512]{2,1,0:T(4,128)(2,1)S(1)} %collective-permute-done.1.refs_2_, ...), custom_call_target="tpu_custom_call" | custom-call | flops 34359738368 | bytes 2097152 | tf_op jit(solution)/shard_map/plan_kernel/pallas_call | solution.py:351
  19.5 3.7 %collective-permute-done.3.refs_2_ = bf16[256,512]{1,0:T(8,128)(2,1)S(1)} collective-permute-done((bf16[256,512]{1,0:T(8,128)(2,1)S(1)}, bf16[256,512]{1,0:T(8,128)(2,1)S(1)}, u32[]{:S(2)}, u32[]{:S(2)}) %collective-permute-start.3) | collective-permute-done | bytes 262176 | tf_op jit(solution)/shard_map/ppermute | solution.py:274
  23.2 1.5 %collective-permute-start.5 = (bf16[256,512]{1,0:T(8,128)(2,1)S(1)}, bf16[256,512]{1,0:T(8,128)(2,1)S(1)}, u32[]{:S(2)}, u32[]{:S(2)}) collective-permute-start(bf16[256,512]{1,0:T(8,128)(2,1)S(1)} %collective-permute-done.3.refs_2_), channel_id=1, source_target_pairs={{0,1},{1,0},{2,3},{3,2},{4,5},{5,4},{6,7},{7,6},{8,9},{9,8},{10,11... | collective-permute-start | bytes 786440 | tf_op jit(solution)/shard_map/ppermute | solution.py:274
  24.7 0.0 collective-permute-done.4.refs_1_
  24.7 0.0 copy-done.1
  24.7 4.0 %near_kernel.1 = (bf16[16,256,512]{2,1,0:T(8,128)(2,1)S(1)}, f32[16,256,512]{2,1,0:T(8,128)S(1)}) custom-call(s32[37]{0:T(128)S(1)} %get-tuple-element.74.plan, s32[16,3,512]{2,1,0:T(4,128)S(1)} %get-tuple-element.44.ids, f32[400,256]{1,0:T(8,128)S(1)} %copy-done.1, bf16[256,512]{1,0:T(8,128)(2,1)S(1)} %rows_kernel.1.refs_0_, ...), custom_call_target="tpu_custom_call" | custom-call | flops 4294967296 | bytes 131072 | tf_op jit(solution)/shard_map/near_kernel/pallas_call | solution.py:311
  28.7 1.6 %collective-permute-done.5.refs_3_ = bf16[256,512]{1,0:T(8,128)(2,1)S(1)} collective-permute-done((bf16[256,512]{1,0:T(8,128)(2,1)S(1)}, bf16[256,512]{1,0:T(8,128)(2,1)S(1)}, u32[]{:S(2)}, u32[]{:S(2)}) %collective-permute-start.5) | collective-permute-done | bytes 262176 | tf_op jit(solution)/shard_map/ppermute | solution.py:274
  30.4 9.8 %edge_kernel.1 = (bf16[16,512,512]{2,1,0:T(8,128)(2,1)S(1)}, bf16[16,512,512]{2,1,0:T(8,128)(2,1)S(1)}, bf16[4,1024,256]{2,1,0:T(8,128)(2,1)S(1)}, f32[512,256]{...) custom-call(s32[3]{0:T(128)S(1)} %pad_add_fusion.codes, ...), custom_call_target="tpu_custom_call" | custom-call | flops 11811160064 | bytes 131072 | tf_op jit(solution)/shard_map/edge_kernel/pallas_call | solution.py:311
  40.2 0.1 collective-permute-start.6
  40.2 0.1 multiply_convert_fusion.2
  40.3 1.5 %collective-permute-done.6 = f32[256,256]{1,0:T(8,128)S(1)} collective-permute-done((f32[256,256]{1,0:T(8,128)S(1)}, f32[256,256]{1,0:T(8,128)S(1)}, u32[]{:S(2)}, u32[]{:S(2)}) %collective-permute-start.6) | collective-permute-done | bytes 262176 | tf_op jit(solution)/shard_map/ppermute | solution.py:274
  41.8 4.2 %collective-permute-start.7 = (f32[64,256]{1,0:T(8,128)S(1)}, f32[64,256]{1,0:T(8,128)S(1)}, u32[]{:S(2)}, u32[]{:S(2)}) collective-permute-start(f32[64,256]{1,0:T(8,128)S(1)} %get-tuple-element.58), channel_id=1, source_target_pairs={{0,1},{1,0},{2,3},{3,2},{4,5},{5,4},{6,7},{7,6},{8,9},{9,8},{10,11... | collective-permute-start | bytes 196616 | tf_op jit(solution)/shard_map/ppermute | solution.py:342
  46.0 3.7 %collective-permute-start.8 = (f32[64,256]{1,0:T(8,128)S(1)}, f32[64,256]{1,0:T(8,128)S(1)}, u32[]{:S(2)}, u32[]{:S(2)}) collective-permute-start(f32[64,256]{1,0:T(8,128)S(1)} %get-tuple-element.59), channel_id=1, source_target_pairs={{0,4},{1,5},{2,6},{3,7},{4,0},{5,1},{6,2},{7,3},{8,12},{9,13},{10,... | collective-permute-start | bytes 196616 | tf_op jit(solution)/shard_map/ppermute | solution.py:342
  49.7 0.0 collective-permute-start.9
  49.7 1.5 %collective-permute-start.11 = (f16[512,256]{1,0:T(8,128)(2,1)S(1)}, f16[512,256]{1,0:T(8,128)(2,1)S(1)}, u32[]{:S(2)}, u32[]{:S(2)}) collective-permute-start(f16[512,256]{1,0:T(8,128)(2,1)S(1)} %multiply_convert_fusion.2), channel_id=1, source_target_pairs={{0,1},{1,0},{2,3},{3,2},{4,5},{5,4},{6,7},{7,6},{8,9},{9,8},{10,11... | collective-permute-start | bytes 786440 | tf_op jit(solution)/shard_map/ppermute | solution.py:274
  51.2 3.0 %away_kernel.1 = f32[512,256]{1,0:T(8,128)S(1)} custom-call(s32[37]{0:T(128)S(1)} %get-tuple-element.74.plan, s32[16,3,512]{2,1,0:T(4,128)S(1)} %get-tuple-element.44.ids, s32[4,1,512]{2,1,0:T(1,128)S(1)} %get-tuple-element.45.negative_ids, bf16[16,512,512]{2,1,0:T(8,128)(2,1)S(1)} %get-tuple-element.62.grads, ...), custom_call_target="tpu_custom_call" | custom-call | bytes 131072 | tf_op jit(solution)/shard_map/away_kernel/pallas_call | solution.py:311
  54.2 0.0 collective-permute-done.7
  54.2 0.0 collective-permute-done.8
  54.2 0.8 %collective-permute-done.9 = f32[64,256]{1,0:T(8,128)S(1)} collective-permute-done((f32[64,256]{1,0:T(8,128)S(1)}, f32[64,256]{1,0:T(8,128)S(1)}, u32[]{:S(2)}, u32[]{:S(2)}) %collective-permute-start.9) | collective-permute-done | bytes 65568 | tf_op jit(solution)/shard_map/ppermute | solution.py:342
  55.0 0.1 collective-permute-start.10
  55.1 2.5 %own_other_kernel.1 = f32[512,256]{1,0:T(8,128)S(1)} custom-call(s32[37]{0:T(128)S(1)} %get-tuple-element.74.plan, s32[16,3,512]{2,1,0:T(4,128)S(1)} %get-tuple-element.44.ids, s32[4,1,512]{2,1,0:T(1,128)S(1)} %get-tuple-element.45.negative_ids, bf16[16,512,512]{2,1,0:T(8,128)(2,1)S(1)} %get-tuple-element.68.grads, ...), custom_call_target="tpu_custom_call" | custom-call | bytes 131072 | tf_op jit(solution)/shard_map/own_other_kernel/pallas_call | solution.py:311
  57.7 0.0 copy-start
  57.7 0.0 copy-start.2
  57.7 0.0 copy-start.3
  57.7 0.1 multiply_convert_fusion
  57.8 1.6 %collective-permute-done.10 = f32[64,256]{1,0:T(8,128)S(1)} collective-permute-done((f32[64,256]{1,0:T(8,128)S(1)}, f32[64,256]{1,0:T(8,128)S(1)}, u32[]{:S(2)}, u32[]{:S(2)}) %collective-permute-start.10) | collective-permute-done | bytes 65568 | tf_op jit(solution)/shard_map/ppermute | solution.py:274
  59.4 0.0 collective-permute-done.11
  59.4 0.1 multiply_convert_fusion.1
  59.5 0.6 collective-permute-start.12
  60.1 5.2 %collective-permute-done.12 = f32[64,256]{1,0:T(8,128)S(1)} collective-permute-done((f32[64,256]{1,0:T(8,128)S(1)}, f32[64,256]{1,0:T(8,128)S(1)}, u32[]{:S(2)}, u32[]{:S(2)}) %collective-permute-start.12) | collective-permute-done | bytes 65568 | tf_op jit(solution)/shard_map/ppermute | solution.py:274
  65.3 0.1 collective-permute-start.13
  65.4 1.0 %collective-permute-start.17 = (f16[512,256]{1,0:T(8,128)(2,1)S(1)}, f16[512,256]{1,0:T(8,128)(2,1)S(1)}, u32[]{:S(2)}, u32[]{:S(2)}) collective-permute-start(f16[512,256]{1,0:T(8,128)(2,1)S(1)} %multiply_convert_fusion), channel_id=1, source_target_pairs={{0,1},{1,0},{2,3},{3,2},{4,5},{5,4},{6,7},{7,6},{8,9},{9,8},{10,11... | collective-permute-start | bytes 786440 | tf_op jit(solution)/shard_map/ppermute | solution.py:274
  66.4 5.9 %collective-permute-start.16 = (f32[64,256]{1,0:T(8,128)S(1)}, f32[64,256]{1,0:T(8,128)S(1)}, u32[]{:S(2)}, u32[]{:S(2)}) collective-permute-start(f32[64,256]{1,0:T(8,128)S(1)} %add.55), channel_id=1, source_target_pairs={{0,5},{1,4},{2,7},{3,6},{4,1},{5,0},{6,3},{7,2},{8,13},{9,12},{10,... | collective-permute-start | bytes 196616 | tf_op jit(solution)/shard_map/ppermute | solution.py:342
  72.3 0.0 collective-permute-start.15
  72.3 0.6 collective-permute-start.14
  72.9 2.5 %own_kernel.1.own = f32[512,256]{1,0:T(8,128)S(1)} custom-call(s32[37]{0:T(128)S(1)} %get-tuple-element.74.plan, s32[16,3,512]{2,1,0:T(4,128)S(1)} %get-tuple-element.44.ids, s32[4,1,512]{2,1,0:T(1,128)S(1)} %get-tuple-element.45.negative_ids, bf16[16,512,512]{2,1,0:T(8,128)(2,1)S(1)} %get-tuple-element.68.grads, ...), custom_call_target="tpu_custom_call" | custom-call | bytes 131072 | tf_op jit(solution)/shard_map/own_kernel/pallas_call | solution.py:311
  75.4 0.0 collective-permute-done.16
  75.4 1.1 %collective-permute-done.15 = f32[64,256]{1,0:T(8,128)S(1)} collective-permute-done((f32[64,256]{1,0:T(8,128)S(1)}, f32[64,256]{1,0:T(8,128)S(1)}, u32[]{:S(2)}, u32[]{:S(2)}) %collective-permute-start.15) | collective-permute-done | bytes 65568 | tf_op jit(solution)/shard_map/ppermute | solution.py:342
  76.6 0.0 collective-permute-done.14
  76.6 0.2 collective-permute-done.13
  76.8 0.0 collective-permute-start.18
  76.8 0.0 collective-permute-done.17
  76.8 0.1 add_multiply_fusion.returned
  76.9 0.0 copy-done
  76.9 0.0 copy-done.2
  76.9 1.2 %entity_kernel.1 = (f32[512,256]{1,0:T(8,128)}, f32[1,512]{1,0:T(1,128)}) custom-call(f32[512,256]{1,0:T(8,128)S(1)} %copy-done, f32[1,512]{1,0:T(1,128)S(1)} %bitcast.10, f32[512,256]{1,0:T(8,128)S(1)} %add_multiply_fusion.returned, f32[512,256]{1,0:T(8,128)S(1)} %own_kernel.1.own), custom_call_target="tpu_custom_call" | custom-call | flops 2097152 | bytes 131072 | tf_op jit(solution)/shard_map/entity_kernel/pallas_call | solution.py:311
  78.0 0.3 collective-permute-done.18.theirs
  78.3 0.0 copy-done.3
  78.3 1.6 %relation_kernel.1 = f32[400,256]{1,0:T(8,128)} custom-call(s32[3]{0:T(128)S(1)} %pad_add_fusion.codes, f32[400,256]{1,0:T(8,128)S(1)} %copy-done.1, f32[1,400]{1,0:T(1,128)S(1)} %bitcast.11, f32[256,256]{1,0:T(8,128)S(1)} %pad_maximum_fusion.mine, f32[256,256]{1,0:T(8,128)S(1)} %collective-permute-done.18.theirs), custom_call_target="tpu_custom_call" | custom-call | bytes 131072 | tf_op jit(solution)/shard_map/relation_kernel/pallas_call | solution.py:311
  (5 shorter events, 0.1 us)
Async XLA Ops:
  2.1 7.9 %collective-permute-start.1 = (s16[17,3,512]{2,1,0:T(4,128)(2,1)S(1)}, s16[17,3,512]{2,1,0:T(4,128)(2,1)S(1)}, u32[]{:S(2)}, u32[]{:S(2)}) collective-permute-start(s16[17,3,512]{2,1,0:T(4,128)(2,1)S(1)} %ids_kernel.1.refs_0_), channel_id=1, source_target_pairs={{0,16},{2,18},{4,20},{6,22},{8,24},{10,26},{12,28},{14,30},{16,0},... | collective-permute-start | bytes 156680 | tf_op jit(solution)/shard_map/ppermute | solution.py:274
  6.2 5.6 %collective-permute-start = (s16[17,3,512]{2,1,0:T(4,128)(2,1)S(1)}, s16[17,3,512]{2,1,0:T(4,128)(2,1)S(1)}, u32[]{:S(2)}, u32[]{:S(2)}) collective-permute-start(s16[17,3,512]{2,1,0:T(4,128)(2,1)S(1)} %ids_kernel.1.refs_0_), channel_id=1, source_target_pairs={{0,1},{1,0},{2,3},{3,2},{4,5},{5,4},{6,7},{7,6},{8,9},{9,8},{10,11... | collective-permute-start | bytes 156680 | tf_op jit(solution)/shard_map/ppermute | solution.py:274
  8.9 15.8 %collective-permute-start.4 = (bf16[256,512]{1,0:T(8,128)(2,1)S(1)}, bf16[256,512]{1,0:T(8,128)(2,1)S(1)}, u32[]{:S(2)}, u32[]{:S(2)}) collective-permute-start(bf16[256,512]{1,0:T(8,128)(2,1)S(1)} %rows_kernel.1.refs_0_), channel_id=1, source_target_pairs={{0,1},{1,0},{2,3},{3,2},{4,5},{5,4},{6,7},{7,6},{8,9},{9,8},{10,11... | collective-permute-start | bytes 786440 | tf_op jit(solution)/shard_map/ppermute | solution.py:274
  9.5 13.7 %collective-permute-start.3 = (bf16[256,512]{1,0:T(8,128)(2,1)S(1)}, bf16[256,512]{1,0:T(8,128)(2,1)S(1)}, u32[]{:S(2)}, u32[]{:S(2)}) collective-permute-start(bf16[256,512]{1,0:T(8,128)(2,1)S(1)} %rows_kernel.1.refs_0_), channel_id=1, source_target_pairs={{0,16},{2,18},{4,20},{6,22},{8,24},{10,26},{12,28},{14,30},{16,0},... | collective-permute-start | bytes 786440 | tf_op jit(solution)/shard_map/ppermute | solution.py:274
  10.0 8.0 %collective-permute-start.2 = (s16[17,3,512]{2,1,0:T(4,128)(2,1)S(1)}, s16[17,3,512]{2,1,0:T(4,128)(2,1)S(1)}, u32[]{:S(2)}, u32[]{:S(2)}) collective-permute-start(s16[17,3,512]{2,1,0:T(4,128)(2,1)S(1)} %collective-permute-done.1.refs_2_), channel_id=1, source_target_pairs={{0,1},{1,0},{2,3},{3,2},{4,5},{5,4},{6,7},{7,6},{8,9},{9,8},{10,11... | collective-permute-start | bytes 156680 | tf_op jit(solution)/shard_map/ppermute | solution.py:274
  11.8 12.9 %copy-start.1 = (f32[400,256]{1,0:T(8,128)S(1)}, f32[400,256]{1,0:T(8,128)}, u32[]{:S(2)}) copy-start(f32[400,256]{1,0:T(8,128)} %relations.3) | copy-start | bytes 1228804
  23.2 7.1 %collective-permute-start.5 = (bf16[256,512]{1,0:T(8,128)(2,1)S(1)}, bf16[256,512]{1,0:T(8,128)(2,1)S(1)}, u32[]{:S(2)}, u32[]{:S(2)}) collective-permute-start(bf16[256,512]{1,0:T(8,128)(2,1)S(1)} %collective-permute-done.3.refs_2_), channel_id=1, source_target_pairs={{0,1},{1,0},{2,3},{3,2},{4,5},{5,4},{6,7},{7,6},{8,9},{9,8},{10,11... | collective-permute-start | bytes 786440 | tf_op jit(solution)/shard_map/ppermute | solution.py:274
  40.2 1.6 %collective-permute-start.6 = (f32[256,256]{1,0:T(8,128)S(1)}, f32[256,256]{1,0:T(8,128)S(1)}, u32[]{:S(2)}, u32[]{:S(2)}) collective-permute-start(f32[256,256]{1,0:T(8,128)S(1)} %get-tuple-element.52), channel_id=1, source_target_pairs={{0,2},{2,0},{4,6},{6,4},{8,10},{10,8},{12,14},{14,12},{16,18},{18,... | collective-permute-start | bytes 786440 | tf_op jit(solution)/shard_map/ppermute | solution.py:274
  41.8 12.4 %collective-permute-start.7 = (f32[64,256]{1,0:T(8,128)S(1)}, f32[64,256]{1,0:T(8,128)S(1)}, u32[]{:S(2)}, u32[]{:S(2)}) collective-permute-start(f32[64,256]{1,0:T(8,128)S(1)} %get-tuple-element.58), channel_id=1, source_target_pairs={{0,1},{1,0},{2,3},{3,2},{4,5},{5,4},{6,7},{7,6},{8,9},{9,8},{10,11... | collective-permute-start | bytes 196616 | tf_op jit(solution)/shard_map/ppermute | solution.py:342
  46.0 8.2 %collective-permute-start.8 = (f32[64,256]{1,0:T(8,128)S(1)}, f32[64,256]{1,0:T(8,128)S(1)}, u32[]{:S(2)}, u32[]{:S(2)}) collective-permute-start(f32[64,256]{1,0:T(8,128)S(1)} %get-tuple-element.59), channel_id=1, source_target_pairs={{0,4},{1,5},{2,6},{3,7},{4,0},{5,1},{6,2},{7,3},{8,12},{9,13},{10,... | collective-permute-start | bytes 196616 | tf_op jit(solution)/shard_map/ppermute | solution.py:342
  49.7 5.3 %collective-permute-start.9 = (f32[64,256]{1,0:T(8,128)S(1)}, f32[64,256]{1,0:T(8,128)S(1)}, u32[]{:S(2)}, u32[]{:S(2)}) collective-permute-start(f32[64,256]{1,0:T(8,128)S(1)} %get-tuple-element.60), channel_id=1, source_target_pairs={{0,5},{1,4},{2,7},{3,6},{4,1},{5,0},{6,3},{7,2},{8,13},{9,12},{10,... | collective-permute-start | bytes 196616 | tf_op jit(solution)/shard_map/ppermute | solution.py:342
  49.7 9.6 %collective-permute-start.11 = (f16[512,256]{1,0:T(8,128)(2,1)S(1)}, f16[512,256]{1,0:T(8,128)(2,1)S(1)}, u32[]{:S(2)}, u32[]{:S(2)}) collective-permute-start(f16[512,256]{1,0:T(8,128)(2,1)S(1)} %multiply_convert_fusion.2), channel_id=1, source_target_pairs={{0,1},{1,0},{2,3},{3,2},{4,5},{5,4},{6,7},{7,6},{8,9},{9,8},{10,11... | collective-permute-start | bytes 786440 | tf_op jit(solution)/shard_map/ppermute | solution.py:274
  55.0 4.3 %collective-permute-start.10 = (f32[64,256]{1,0:T(8,128)S(1)}, f32[64,256]{1,0:T(8,128)S(1)}, u32[]{:S(2)}, u32[]{:S(2)}) collective-permute-start(f32[64,256]{1,0:T(8,128)S(1)} %add_add_fusion), channel_id=1, source_target_pairs={{0,8},{2,10},{4,12},{6,14},{8,0},{10,2},{12,4},{14,6},{16,24},{18,... | collective-permute-start | bytes 196616 | tf_op jit(solution)/shard_map/ppermute | solution.py:274
  57.7 19.2 %copy-start = (f32[512,256]{1,0:T(8,128)S(1)}, f32[512,256]{1,0:T(8,128)}, u32[]{:S(2)}) copy-start(f32[512,256]{1,0:T(8,128)} %table.2) | copy-start | bytes 1572868
  57.7 19.2 %copy-start.2 = (f32[512]{0:T(512)S(1)}, f32[512]{0:T(512)}, u32[]{:S(2)}) copy-start(f32[512]{0:T(512)} %param.10) | copy-start | bytes 6148
  57.7 20.6 %copy-start.3 = (f32[400]{0:T(512)S(1)}, f32[400]{0:T(512)}, u32[]{:S(2)}) copy-start(f32[400]{0:T(512)} %param.12) | copy-start | bytes 4804
  59.5 5.8 %collective-permute-start.12 = (f32[64,256]{1,0:T(8,128)S(1)}, f32[64,256]{1,0:T(8,128)S(1)}, u32[]{:S(2)}, u32[]{:S(2)}) collective-permute-start(f32[64,256]{1,0:T(8,128)S(1)} %add.53), channel_id=1, source_target_pairs={{0,16},{2,18},{4,20},{6,22},{8,24},{10,26},{12,28},{14,30},{16,0},... | collective-permute-start | bytes 196616 | tf_op jit(solution)/shard_map/ppermute | solution.py:274
  65.3 11.5 %collective-permute-start.13 = (f16[512,256]{1,0:T(8,128)(2,1)S(1)}, f16[512,256]{1,0:T(8,128)(2,1)S(1)}, u32[]{:S(2)}, u32[]{:S(2)}) collective-permute-start(f16[512,256]{1,0:T(8,128)(2,1)S(1)} %multiply_convert_fusion.1), channel_id=1, source_target_pairs={{0,16},{2,18},{4,20},{6,22},{8,24},{10,26},{12,28},{14,30},{16,0},... | collective-permute-start | bytes 786440 | tf_op jit(solution)/shard_map/ppermute | solution.py:274
  65.4 11.4 %collective-permute-start.17 = (f16[512,256]{1,0:T(8,128)(2,1)S(1)}, f16[512,256]{1,0:T(8,128)(2,1)S(1)}, u32[]{:S(2)}, u32[]{:S(2)}) collective-permute-start(f16[512,256]{1,0:T(8,128)(2,1)S(1)} %multiply_convert_fusion), channel_id=1, source_target_pairs={{0,1},{1,0},{2,3},{3,2},{4,5},{5,4},{6,7},{7,6},{8,9},{9,8},{10,11... | collective-permute-start | bytes 786440 | tf_op jit(solution)/shard_map/ppermute | solution.py:274
  66.4 9.0 %collective-permute-start.16 = (f32[64,256]{1,0:T(8,128)S(1)}, f32[64,256]{1,0:T(8,128)S(1)}, u32[]{:S(2)}, u32[]{:S(2)}) collective-permute-start(f32[64,256]{1,0:T(8,128)S(1)} %add.55), channel_id=1, source_target_pairs={{0,5},{1,4},{2,7},{3,6},{4,1},{5,0},{6,3},{7,2},{8,13},{9,12},{10,... | collective-permute-start | bytes 196616 | tf_op jit(solution)/shard_map/ppermute | solution.py:342
  72.3 4.3 %collective-permute-start.15 = (f32[64,256]{1,0:T(8,128)S(1)}, f32[64,256]{1,0:T(8,128)S(1)}, u32[]{:S(2)}, u32[]{:S(2)}) collective-permute-start(f32[64,256]{1,0:T(8,128)S(1)} %add.55), channel_id=1, source_target_pairs={{0,4},{1,5},{2,6},{3,7},{4,0},{5,1},{6,2},{7,3},{8,12},{9,13},{10,... | collective-permute-start | bytes 196616 | tf_op jit(solution)/shard_map/ppermute | solution.py:342
  72.3 4.3 %collective-permute-start.14 = (f32[64,256]{1,0:T(8,128)S(1)}, f32[64,256]{1,0:T(8,128)S(1)}, u32[]{:S(2)}, u32[]{:S(2)}) collective-permute-start(f32[64,256]{1,0:T(8,128)S(1)} %add.55), channel_id=1, source_target_pairs={{0,1},{1,0},{2,3},{3,2},{4,5},{5,4},{6,7},{7,6},{8,9},{9,8},{10,11... | collective-permute-start | bytes 196616 | tf_op jit(solution)/shard_map/ppermute | solution.py:342
  76.8 1.5 %collective-permute-start.18 = (f32[256,256]{1,0:T(8,128)S(1)}, f32[256,256]{1,0:T(8,128)S(1)}, u32[]{:S(2)}, u32[]{:S(2)}) collective-permute-start(f32[256,256]{1,0:T(8,128)S(1)} %pad_maximum_fusion.mine), channel_id=1, source_target_pairs={{0,2},{2,0},{4,6},{6,4},{8,10},{10,8},{12,14},{14,12},{16,18},{18,... | collective-permute-start | bytes 786440 | tf_op jit(solution)/shard_map/ppermute | solution.py:274

commit v4 on v3

--- a/solution.py
+++ b/solution.py
@@ -59,8 +59,11 @@
         start += piece.shape[0]
 
 
-def rows_kernel(table, out):
+def rows_kernel(table, out, *parts):
     out[...] = table[...].T.astype(bf16)
+    each = parts[0].shape[1]
+    for k, part in enumerate(parts):
+        part[...] = out[:, k * each : (k + 1) * each]
 
 
 def ids_kernel(count, heads, tails, kinds, negatives, ids_out):
@@ -140,18 +143,22 @@
     pl.when((steps & 1) == 1)(lambda: one_block(steps - 1))
 
 
-def edge_kernel(n, codes, plan, ids, negative_ids, near_in, operator_in, *refs):
-    near, away = refs[:n], refs[n : 2 * n]
-    near_grad, away_grad, negative_out = refs[2 * n : 2 * n + 3]
-    away_other = refs[2 * n + 3 : 3 * n + 2]
-    relation_out = refs[3 * n + 2 : -5]
-    table, table_t, negative_grad, relation_sum, ordered = refs[-5:]
+def edge_kernel(n, cuts, codes, plan, ids, negative_ids, near_in, operator_in, *refs):
+    near, refs = refs[:n], refs[n:]
+    pieces, refs = refs[:cuts], refs[cuts:]
+    near_grad, away_grad, negative_out = refs[:3]
+    away_other = refs[3 : n + 2]
+    relation_out = refs[n + 2 : -6]
+    table, table_t, negative_grad, relation_sum, ordered, away = refs[-6:]
+    each = pieces[0].shape[1]
+    for k, piece in enumerate(pieces):
+        away[:, k * each : (k + 1) * each] = piece[...]
     most, _, width = ids.shape
     steps = plan[2 * most]
     count = table.shape[0]
     for piece in (*away_other, relation_sum):
         piece[...] = jnp.zeros_like(piece)
-    rows = away[0].shape[1]
+    rows = near[0].shape[1]
 
     def one_block(i, carry):
         here = plan[i]
@@ -164,7 +171,7 @@
             negative_grad[...] = jnp.zeros_like(negative_grad)
 
         fresh = (i == 0) | (plan[jnp.maximum(i - 1, 0)] != here)
-        pl.when(fresh & ~swapped)(lambda: take_table(away))
+        pl.when(fresh & ~swapped)(lambda: take_table([away]))
         pl.when(fresh & swapped)(lambda: take_table(near))
 
         entries = ids[i]
@@ -173,7 +180,7 @@
             alive = (lax.broadcasted_iota(i32, (1, width), 1) < plan[most + i]).astype(f32)
             near_rows = near_in[i].astype(f32)
             away_hot = one_hot(entries[1:2], n * rows)
-            away_rows = gather(away, away_hot)
+            away_rows = gather([away], away_hot)
             head, tail = (away_rows, near_rows) if swapped else (near_rows, away_rows)
             operator = operator_in[i]
             query = head * operator
@@ -335,7 +342,17 @@
         fetch=True,
     )
     ids, table = lax.optimization_barrier((ids, entity_table))
-    (local,) = call(rows_kernel, "rows_kernel", [((dims, rows), bf16)], [], 1, (), (table,), fetch=True)
+    cuts = 2
+    local, *cut = call(
+        rows_kernel,
+        "rows_kernel",
+        [((dims, rows), bf16)] + [((dims, rows // cuts), bf16)] * cuts,
+        [],
+        1,
+        (),
+        (table,),
+        fetch=True,
+    )
 
     def to_peer(x, across, aside):
         pairs = [(d * n + s, (d ^ across) * n + (s ^ aside)) for d in range(n_dom) for s in range(n)]
@@ -346,7 +363,8 @@
 
     all_ids = along_sub(ids) + along_sub(exchange(ids, "dom", pair))
     near_slab = along_sub(local)
-    away_first = exchange(local, "dom", pair)
+    away_cut = [exchange(x, "dom", pair) for x in cut]
+    forwarded = [along_sub(x) for x in away_cut[:-1]]
 
     plan, step_ids, negative_ids = pl.pallas_call(
         functools.partial(plan_kernel, n),
@@ -362,8 +380,9 @@
         name="plan_kernel",
     )(codes, *(pltpu.with_memory_space_constraint(x, pltpu.VMEM) for x in all_ids))
 
-    near_plan, away_first = lax.optimization_barrier((plan, away_first))
-    away_slab = along_sub(away_first)
+    near_plan, away_cut, forwarded = lax.optimization_barrier((plan, away_cut, forwarded))
+    forwarded.append(along_sub(away_cut[-1]))
+    away_slab = [forwarded[c][k] for k in range(n) for c in range(cuts)]
     near_rows, operator = call(
         near_kernel,
         "near_kernel",
@@ -376,14 +395,15 @@
     sums = ((rows, dims), f32)
     pair_out = ((most, 2 * dims, width), bf16)
     near_grad, away_grad, negative_grad, *found = call(
-        functools.partial(edge_kernel, n),
+        functools.partial(edge_kernel, n, n * cuts),
         "edge_kernel",
         [pair_out, pair_out, ((team, 2 * count, dims), bf16)]
         + [sums] * (n - 1)
         + [((chunk, dims), f32)] * chips
         + [((chips * chunk, dims), f32)],
         [pltpu.VMEM((count, dims), bf16), pltpu.VMEM((dims, count), bf16), pltpu.VMEM((count, dims), f32)]
-        + [pltpu.VMEM((-(-relations.shape[0] // 16) * 16, dims), f32), pltpu.VMEM((rel_rows, dims), f32)],
+        + [pltpu.VMEM((-(-relations.shape[0] // 16) * 16, dims), f32), pltpu.VMEM((rel_rows, dims), f32)]
+        + [pltpu.VMEM((dims, n * rows), bf16)],
         3 * n * rows + 3 * count + 2 * rel_rows,
         (codes, plan),
         (step_ids, negative_ids, near_rows, operator, *near_slab, *away_slab),
@@ -422,19 +442,16 @@
     away_received = [widen(exchange(away_other[k - 1], "sub", k)) for k in range(1, n)]
     (away_total,) = scatter("away_kernel", 1, 0, 1, 0, plan, away_grad)
     chunk_total, away_total, plan = lax.optimization_barrier((chunk_total, away_total, plan))
-    masks = [4 << k for k in range((n_dom // 4).bit_length() - 1)]
-    for mask in masks[:-1]:
-        chunk_total = chunk_total + exchange(chunk_total, "dom", mask)
+    terms = [chunk_total] + [exchange(chunk_total, "dom", mask) for mask in range(4, n_dom, 4)]
     near_other = scatter("own_other_kernel", 0, rows, n - 1, n, plan, near_grad)
     near_other = [narrow(x) for x in near_other]
     for x in away_received:
         away_total = away_total + x
     away_total = narrow(away_total)
-    chunk_total, away_total, near_other, plan = lax.optimization_barrier((chunk_total, away_total, near_other, plan))
+    while len(terms) > 1:
+        terms = [terms[k] + terms[k + 1] for k in range(0, len(terms), 2)]
+    chunk_total, away_total, near_other, plan = lax.optimization_barrier((terms[0], away_total, near_other, plan))
     near_received = [widen(exchange(near_other[k - 1], "sub", k)) for k in range(1, n)]
-    for mask in masks[-1:]:
-        chunk_total = chunk_total + exchange(chunk_total, "dom", mask)
-    chunk_total, away_total, plan = lax.optimization_barrier((chunk_total, away_total, plan))
     returned = exchange(away_total, "dom", pair)
     mine = jnp.concatenate([chunk_total] + [to_chip(chunk_total, k) for k in range(1, chips)], axis=0)
     (near_sum,) = scatter("own_kernel", 0, 0, 1, n, plan, near_grad)

time: 80.8 us -> 82.2 us (1.017)
  starting transfers between devices: 27.3 us -> 33.5 us
  waiting for transfers between devices: 22.5 us -> 16.5 us
  Pallas kernels: 28.2 us -> 29.7 us
    ppermute x13 -> x16, starting transfers between devices: 12.8 us -> 25.8 us  [exchange(): lax.ppermute(x, axis, [(i, i ^ mask) for i in range(lax.axis_size(axis))])]
    ppermute x6, starting transfers between devices: 14.4 us -> 7.7 us  [to_peer(): return lax.ppermute(x, ('dom', 'sub'), pairs)]
    ppermute x13 -> x16, waiting for transfers between devices: 20.6 us -> 15.3 us  [exchange(): lax.ppermute(x, axis, [(i, i ^ mask) for i in range(lax.axis_size(axis))])]
    pallas_call x9, Pallas kernels: 26.6 us -> 28.1 us  [call(): pl.pallas_call(kernel, in_specs=[in_smem] * len(scalars) + [in_vmem] * le...]
  transfers between devices with their start and end apart: 19 -> 22, of which waited for: 11 -> 8; matrix products, arithmetic and copies ran while one was open for 0% -> 0% of each run, Pallas kernels for 20% -> 20%
where the time goes in v4:
time: 82.2 us; the launch traced here: 81.6 us
  starting transfers between devices  33.5 us (41%)
  Pallas kernels  29.7 us (36%)
  waiting for transfers between devices  16.5 us (20%)
  between operations  1.51 us (2%)
    pallas_call x9, Pallas kernels, call(): pl.pallas_call(kernel, in_specs=[in_smem] * len(scalars) + [in_vmem] * le...  28.1 us
    ppermute x16, starting transfers between devices, exchange(): lax.ppermute(x, axis, [(i, i ^ mask) for i in range(lax.axis_size(axis))])  25.8 us
    ppermute x16, waiting for transfers between devices, exchange(): lax.ppermute(x, axis, [(i, i ^ mask) for i in range(lax.axis_size(axis))])  15.3 us
    ppermute x6, starting transfers between devices, to_peer(): return lax.ppermute(x, ('dom', 'sub'), pairs)  7.7 us
  transfers between devices with their start and end apart: 22, of which 8 were waited for; matrix products, arithmetic and copies ran while one was open for 0% of the time, Pallas kernels for 20%

profile of v4, /device:TPU:0, one launch (start us, length us, event | category | flops | bytes accessed | tf_op | source)
XLA Modules:
  0.0 81.6 jit_solution(17638747939219697980)
XLA Ops:
  1.3 0.8 %ids_kernel.1.refs_0_ = s16[17,3,512]{2,1,0:T(4,128)(2,1)S(1)} custom-call(s32[1,1]{1,0:T(1,128)S(6)} %copy.12.count, s32[1,8192]{1,0:T(1,128)} %bitcast.12, s32[1,8192]{1,0:T(1,128)} %bitcast.13, s32[1,8192]{1,0:T(1,128)} %bitcast.14, s32[1,512]{1,0:T(1,128)} %bitcast.15), custom_call_target="tpu_custom_call" | custom-call | flops 2097152 | bytes 131072 | tf_op jit(solution)/shard_map/ids_kernel/pallas_call | solution.py:318
  2.1 4.1 %collective-permute-start.1 = (s16[17,3,512]{2,1,0:T(4,128)(2,1)S(1)}, s16[17,3,512]{2,1,0:T(4,128)(2,1)S(1)}, u32[]{:S(2)}, u32[]{:S(2)}) collective-permute-start(s16[17,3,512]{2,1,0:T(4,128)(2,1)S(1)} %ids_kernel.1.refs_0_), channel_id=1, source_target_pairs={{0,16},{2,18},{4,20},{6,22},{8,24},{10,26},{12,28},{14,30},{16,0},... | collective-permute-start | bytes 156680 | tf_op jit(solution)/shard_map/ppermute | solution.py:281
  6.2 1.2 %rows_kernel.1 = (bf16[256,512]{1,0:T(8,128)(2,1)S(1)}, bf16[256,256]{1,0:T(8,128)(2,1)S(1)}, bf16[256,256]{1,0:T(8,128)(2,1)S(1)}) custom-call(f32[512,256]{1,0:T(8,128)} %table.2), custom_call_target="tpu_custom_call" | custom-call | flops 2097152 | bytes 131072 | tf_op jit(solution)/shard_map/rows_kernel/pallas_call | solution.py:318
  7.4 0.1 collective-permute-start.3
  7.5 1.8 %collective-permute-start = (s16[17,3,512]{2,1,0:T(4,128)(2,1)S(1)}, s16[17,3,512]{2,1,0:T(4,128)(2,1)S(1)}, u32[]{:S(2)}, u32[]{:S(2)}) collective-permute-start(s16[17,3,512]{2,1,0:T(4,128)(2,1)S(1)} %ids_kernel.1.refs_0_), channel_id=1, source_target_pairs={{0,1},{1,0},{2,3},{3,2},{4,5},{5,4},{6,7},{7,6},{8,9},{9,8},{10,11... | collective-permute-start | bytes 156680 | tf_op jit(solution)/shard_map/ppermute | solution.py:281
  9.3 2.6 %collective-permute-start.4 = (bf16[256,256]{1,0:T(8,128)(2,1)S(1)}, bf16[256,256]{1,0:T(8,128)(2,1)S(1)}, u32[]{:S(2)}, u32[]{:S(2)}) collective-permute-start(bf16[256,256]{1,0:T(8,128)(2,1)S(1)} %get-tuple-element.50), channel_id=1, source_target_pairs={{0,16},{2,18},{4,20},{6,22},{8,24},{10,26},{12,28},{14,30},{16,0},... | collective-permute-start | bytes 393224 | tf_op jit(solution)/shard_map/ppermute | solution.py:281
  11.9 0.5 collective-permute-start.6
  12.4 0.0 collective-permute-done.1.refs_2_
  12.4 1.5 %collective-permute-start.2 = (s16[17,3,512]{2,1,0:T(4,128)(2,1)S(1)}, s16[17,3,512]{2,1,0:T(4,128)(2,1)S(1)}, u32[]{:S(2)}, u32[]{:S(2)}) collective-permute-start(s16[17,3,512]{2,1,0:T(4,128)(2,1)S(1)} %collective-permute-done.1.refs_2_), channel_id=1, source_target_pairs={{0,1},{1,0},{2,3},{3,2},{4,5},{5,4},{6,7},{7,6},{8,9},{9,8},{10,11... | collective-permute-start | bytes 156680 | tf_op jit(solution)/shard_map/ppermute | solution.py:281
  13.9 0.1 pad_add_fusion.codes
  14.0 6.1 %collective-permute-done.3.refs_2_ = bf16[256,256]{1,0:T(8,128)(2,1)S(1)} collective-permute-done((bf16[256,256]{1,0:T(8,128)(2,1)S(1)}, bf16[256,256]{1,0:T(8,128)(2,1)S(1)}, u32[]{:S(2)}, u32[]{:S(2)}) %collective-permute-start.3) | collective-permute-done | bytes 131104 | tf_op jit(solution)/shard_map/ppermute | solution.py:281
  20.1 1.5 %collective-permute-start.5 = (bf16[256,256]{1,0:T(8,128)(2,1)S(1)}, bf16[256,256]{1,0:T(8,128)(2,1)S(1)}, u32[]{:S(2)}, u32[]{:S(2)}) collective-permute-start(bf16[256,256]{1,0:T(8,128)(2,1)S(1)} %collective-permute-done.3.refs_2_), channel_id=1, source_target_pairs={{0,1},{1,0},{2,3},{3,2},{4,5},{5,4},{6,7},{7,6},{8,9},{9,8},{10,11... | collective-permute-start | bytes 393224 | tf_op jit(solution)/shard_map/ppermute | solution.py:281
  21.6 0.0 collective-permute-done.refs_1_
  21.6 0.0 collective-permute-done.2.refs_3_
  21.6 1.5 %plan_kernel.1 = (s32[37]{0:T(128)S(1)}, s32[16,3,512]{2,1,0:T(4,128)S(1)}, s32[4,1,512]{2,1,0:T(1,128)S(1)}) custom-call(s32[3]{0:T(128)S(1)} %pad_add_fusion.codes, s16[17,3,512]{2,1,0:T(4,128)(2,1)S(1)} %ids_kernel.1.refs_0_, s16[17,3,512]{2,1,0:T(4,128)(2,1)S(1)} %collective-permute-done.refs_1_, s16[17,3,512]{2,1,0:T(4,128)(2,1)S(1)} %collective-permute-done.1.refs_2_, ...), custom_call_target="tpu_custom_call" | custom-call | flops 34359738368 | bytes 2097152 | tf_op jit(solution)/shard_map/plan_kernel/pallas_call | solution.py:369
  23.2 0.0 collective-permute-done.4.refs_3_
  23.2 2.5 %collective-permute-done.5.refs_4_ = bf16[256,256]{1,0:T(8,128)(2,1)S(1)} collective-permute-done((bf16[256,256]{1,0:T(8,128)(2,1)S(1)}, bf16[256,256]{1,0:T(8,128)(2,1)S(1)}, u32[]{:S(2)}, u32[]{:S(2)}) %collective-permute-start.5) | collective-permute-done | bytes 131104 | tf_op jit(solution)/shard_map/ppermute | solution.py:281
  25.7 1.5 %collective-permute-start.7 = (bf16[256,256]{1,0:T(8,128)(2,1)S(1)}, bf16[256,256]{1,0:T(8,128)(2,1)S(1)}, u32[]{:S(2)}, u32[]{:S(2)}) collective-permute-start(bf16[256,256]{1,0:T(8,128)(2,1)S(1)} %collective-permute-done.4.refs_3_), channel_id=1, source_target_pairs={{0,1},{1,0},{2,3},{3,2},{4,5},{5,4},{6,7},{7,6},{8,9},{9,8},{10,11... | collective-permute-start | bytes 393224 | tf_op jit(solution)/shard_map/ppermute | solution.py:281
  27.2 0.0 collective-permute-done.6.refs_1_
  27.2 0.0 copy-done.1
  27.2 4.0 %near_kernel.1 = (bf16[16,256,512]{2,1,0:T(8,128)(2,1)S(1)}, f32[16,256,512]{2,1,0:T(8,128)S(1)}) custom-call(s32[37]{0:T(128)S(1)} %get-tuple-element.78.plan, s32[16,3,512]{2,1,0:T(4,128)S(1)} %get-tuple-element.46.ids, f32[400,256]{1,0:T(8,128)S(1)} %copy-done.1, bf16[256,512]{1,0:T(8,128)(2,1)S(1)} %get-tuple-element.52.refs_0_, ...), custom_call_target="tpu_custom_call" | custom-call | flops 4294967296 | bytes 131072 | tf_op jit(solution)/shard_map/near_kernel/pallas_call | solution.py:318
  31.2 0.0 collective-permute-done.7.refs_5_
  31.2 10.8 %edge_kernel.1 = (bf16[16,512,512]{2,1,0:T(8,128)(2,1)S(1)}, bf16[16,512,512]{2,1,0:T(8,128)(2,1)S(1)}, bf16[4,1024,256]{2,1,0:T(8,128)(2,1)S(1)}, f32[512,256]{...) custom-call(s32[3]{0:T(128)S(1)} %pad_add_fusion.codes, ...), custom_call_target="tpu_custom_call" | custom-call | flops 11811160064 | bytes 131072 | tf_op jit(solution)/shard_map/edge_kernel/pallas_call | solution.py:318
  42.1 0.1 collective-permute-start.8
  42.1 0.1 multiply_convert_fusion.2
  42.2 1.5 %collective-permute-done.8 = f32[256,256]{1,0:T(8,128)S(1)} collective-permute-done((f32[256,256]{1,0:T(8,128)S(1)}, f32[256,256]{1,0:T(8,128)S(1)}, u32[]{:S(2)}, u32[]{:S(2)}) %collective-permute-start.8) | collective-permute-done | bytes 262176 | tf_op jit(solution)/shard_map/ppermute | solution.py:281
  43.7 2.6 %collective-permute-start.9 = (f32[64,256]{1,0:T(8,128)S(1)}, f32[64,256]{1,0:T(8,128)S(1)}, u32[]{:S(2)}, u32[]{:S(2)}) collective-permute-start(f32[64,256]{1,0:T(8,128)S(1)} %get-tuple-element.65), channel_id=1, source_target_pairs={{0,1},{1,0},{2,3},{3,2},{4,5},{5,4},{6,7},{7,6},{8,9},{9,8},{10,11... | collective-permute-start | bytes 196616 | tf_op jit(solution)/shard_map/ppermute | solution.py:359
  46.3 1.6 %collective-permute-start.10 = (f32[64,256]{1,0:T(8,128)S(1)}, f32[64,256]{1,0:T(8,128)S(1)}, u32[]{:S(2)}, u32[]{:S(2)}) collective-permute-start(f32[64,256]{1,0:T(8,128)S(1)} %get-tuple-element.66), channel_id=1, source_target_pairs={{0,4},{1,5},{2,6},{3,7},{4,0},{5,1},{6,2},{7,3},{8,12},{9,13},{10,... | collective-permute-start | bytes 196616 | tf_op jit(solution)/shard_map/ppermute | solution.py:359
  47.9 0.0 collective-permute-start.11
  47.9 1.9 %collective-permute-start.15 = (f16[512,256]{1,0:T(8,128)(2,1)S(1)}, f16[512,256]{1,0:T(8,128)(2,1)S(1)}, u32[]{:S(2)}, u32[]{:S(2)}) collective-permute-start(f16[512,256]{1,0:T(8,128)(2,1)S(1)} %multiply_convert_fusion.2), channel_id=1, source_target_pairs={{0,1},{1,0},{2,3},{3,2},{4,5},{5,4},{6,7},{7,6},{8,9},{9,8},{10,11... | collective-permute-start | bytes 786440 | tf_op jit(solution)/shard_map/ppermute | solution.py:281
  49.8 3.4 %away_kernel.1 = f32[512,256]{1,0:T(8,128)S(1)} custom-call(s32[37]{0:T(128)S(1)} %get-tuple-element.78.plan, s32[16,3,512]{2,1,0:T(4,128)S(1)} %get-tuple-element.46.ids, s32[4,1,512]{2,1,0:T(1,128)S(1)} %get-tuple-element.47.negative_ids, bf16[16,512,512]{2,1,0:T(8,128)(2,1)S(1)} %get-tuple-element.69.grads, ...), custom_call_target="tpu_custom_call" | custom-call | bytes 131072 | tf_op jit(solution)/shard_map/away_kernel/pallas_call | solution.py:318
  53.2 0.0 collective-permute-done.9
  53.2 0.0 collective-permute-done.10
  53.2 0.0 collective-permute-done.11
  53.3 5.8 %collective-permute-start.14 = (f32[64,256]{1,0:T(8,128)S(1)}, f32[64,256]{1,0:T(8,128)S(1)}, u32[]{:S(2)}, u32[]{:S(2)}) collective-permute-start(f32[64,256]{1,0:T(8,128)S(1)} %add_add_fusion.1), channel_id=1, source_target_pairs={{0,24},{2,26},{4,28},{6,30},{8,16},{10,18},{12,20},{14,22},{16,8},... | collective-permute-start | bytes 196616 | tf_op jit(solution)/shard_map/ppermute | solution.py:281
  59.1 0.0 collective-permute-start.13
  59.1 0.6 collective-permute-start.12
  59.8 2.5 %own_other_kernel.1 = f32[512,256]{1,0:T(8,128)S(1)} custom-call(s32[37]{0:T(128)S(1)} %get-tuple-element.78.plan, s32[16,3,512]{2,1,0:T(4,128)S(1)} %get-tuple-element.46.ids, s32[4,1,512]{2,1,0:T(1,128)S(1)} %get-tuple-element.47.negative_ids, bf16[16,512,512]{2,1,0:T(8,128)(2,1)S(1)} %get-tuple-element.75.grads, ...), custom_call_target="tpu_custom_call" | custom-call | bytes 131072 | tf_op jit(solution)/shard_map/own_other_kernel/pallas_call | solution.py:318
  62.3 0.0 copy-start
  62.3 0.0 copy-start.2
  62.3 0.0 copy-start.3
  62.3 0.1 multiply_convert_fusion
  62.4 0.0 collective-permute-done.14
  62.4 2.1 %collective-permute-done.13 = f32[64,256]{1,0:T(8,128)S(1)} collective-permute-done((f32[64,256]{1,0:T(8,128)S(1)}, f32[64,256]{1,0:T(8,128)S(1)}, u32[]{:S(2)}, u32[]{:S(2)}) %collective-permute-start.13) | collective-permute-done | bytes 65568 | tf_op jit(solution)/shard_map/ppermute | solution.py:281
  64.5 0.1 collective-permute-done.12
  64.7 0.0 collective-permute-done.15
  64.7 0.1 multiply_convert_fusion.1
  64.8 1.7 %collective-permute-start.16 = (f16[512,256]{1,0:T(8,128)(2,1)S(1)}, f16[512,256]{1,0:T(8,128)(2,1)S(1)}, u32[]{:S(2)}, u32[]{:S(2)}) collective-permute-start(f16[512,256]{1,0:T(8,128)(2,1)S(1)} %multiply_convert_fusion.1), channel_id=1, source_target_pairs={{0,16},{2,18},{4,20},{6,22},{8,24},{10,26},{12,28},{14,30},{16,0},... | collective-permute-start | bytes 786440 | tf_op jit(solution)/shard_map/ppermute | solution.py:281
  66.5 1.9 %collective-permute-start.20 = (f16[512,256]{1,0:T(8,128)(2,1)S(1)}, f16[512,256]{1,0:T(8,128)(2,1)S(1)}, u32[]{:S(2)}, u32[]{:S(2)}) collective-permute-start(f16[512,256]{1,0:T(8,128)(2,1)S(1)} %multiply_convert_fusion), channel_id=1, source_target_pairs={{0,1},{1,0},{2,3},{3,2},{4,5},{5,4},{6,7},{7,6},{8,9},{9,8},{10,11... | collective-permute-start | bytes 786440 | tf_op jit(solution)/shard_map/ppermute | solution.py:281
  68.4 1.6 %collective-permute-start.19 = (f32[64,256]{1,0:T(8,128)S(1)}, f32[64,256]{1,0:T(8,128)S(1)}, u32[]{:S(2)}, u32[]{:S(2)}) collective-permute-start(f32[64,256]{1,0:T(8,128)S(1)} %add_add_fusion), channel_id=1, source_target_pairs={{0,5},{1,4},{2,7},{3,6},{4,1},{5,0},{6,3},{7,2},{8,13},{9,12},{10,... | collective-permute-start | bytes 196616 | tf_op jit(solution)/shard_map/ppermute | solution.py:359
  70.0 0.1 collective-permute-start.18
  70.1 1.8 %collective-permute-start.17 = (f32[64,256]{1,0:T(8,128)S(1)}, f32[64,256]{1,0:T(8,128)S(1)}, u32[]{:S(2)}, u32[]{:S(2)}) collective-permute-start(f32[64,256]{1,0:T(8,128)S(1)} %add_add_fusion), channel_id=1, source_target_pairs={{0,1},{1,0},{2,3},{3,2},{4,5},{5,4},{6,7},{7,6},{8,9},{9,8},{10,11... | collective-permute-start | bytes 196616 | tf_op jit(solution)/shard_map/ppermute | solution.py:359
  71.9 2.5 %own_kernel.1.own = f32[512,256]{1,0:T(8,128)S(1)} custom-call(s32[37]{0:T(128)S(1)} %get-tuple-element.78.plan, s32[16,3,512]{2,1,0:T(4,128)S(1)} %get-tuple-element.46.ids, s32[4,1,512]{2,1,0:T(1,128)S(1)} %get-tuple-element.47.negative_ids, bf16[16,512,512]{2,1,0:T(8,128)(2,1)S(1)} %get-tuple-element.75.grads, ...), custom_call_target="tpu_custom_call" | custom-call | bytes 131072 | tf_op jit(solution)/shard_map/own_kernel/pallas_call | solution.py:318
  74.5 0.0 collective-permute-done.19
  74.5 0.0 collective-permute-done.18
  74.5 1.2 %collective-permute-done.17 = f32[64,256]{1,0:T(8,128)S(1)} collective-permute-done((f32[64,256]{1,0:T(8,128)S(1)}, f32[64,256]{1,0:T(8,128)S(1)}, u32[]{:S(2)}, u32[]{:S(2)}) %collective-permute-start.17) | collective-permute-done | bytes 65568 | tf_op jit(solution)/shard_map/ppermute | solution.py:359
  75.7 2.7 %collective-permute-done.16 = f16[512,256]{1,0:T(8,128)(2,1)S(1)} collective-permute-done((f16[512,256]{1,0:T(8,128)(2,1)S(1)}, f16[512,256]{1,0:T(8,128)(2,1)S(1)}, u32[]{:S(2)}, u32[]{:S(2)}) %collective-permute-start.16) | collective-permute-done | bytes 262176 | tf_op jit(solution)/shard_map/ppermute | solution.py:281
  78.4 0.0 collective-permute-start.21
  78.5 0.0 collective-permute-done.20
  78.5 0.1 add_multiply_fusion.returned
  78.6 1.2 %entity_kernel.1 = (f32[512,256]{1,0:T(8,128)}, f32[1,512]{1,0:T(1,128)}) custom-call(f32[512,256]{1,0:T(8,128)S(1)} %copy-done, f32[1,512]{1,0:T(1,128)S(1)} %bitcast.10, f32[512,256]{1,0:T(8,128)S(1)} %add_multiply_fusion.returned, f32[512,256]{1,0:T(8,128)S(1)} %own_kernel.1.own), custom_call_target="tpu_custom_call" | custom-call | flops 2097152 | bytes 131072 | tf_op jit(solution)/shard_map/entity_kernel/pallas_call | solution.py:318
  79.7 0.2 collective-permute-done.21.theirs
  80.0 0.0 copy-done.3
  80.0 1.6 %relation_kernel.1 = f32[400,256]{1,0:T(8,128)} custom-call(s32[3]{0:T(128)S(1)} %pad_add_fusion.codes, f32[400,256]{1,0:T(8,128)S(1)} %copy-done.1, f32[1,400]{1,0:T(1,128)S(1)} %bitcast.11, f32[256,256]{1,0:T(8,128)S(1)} %pad_maximum_fusion.mine, f32[256,256]{1,0:T(8,128)S(1)} %collective-permute-done.21.theirs), custom_call_target="tpu_custom_call" | custom-call | bytes 131072 | tf_op jit(solution)/shard_map/relation_kernel/pallas_call | solution.py:318
  (7 shorter events, 0.1 us)
Async XLA Ops:
  2.1 10.3 %collective-permute-start.1 = (s16[17,3,512]{2,1,0:T(4,128)(2,1)S(1)}, s16[17,3,512]{2,1,0:T(4,128)(2,1)S(1)}, u32[]{:S(2)}, u32[]{:S(2)}) collective-permute-start(s16[17,3,512]{2,1,0:T(4,128)(2,1)S(1)} %ids_kernel.1.refs_0_), channel_id=1, source_target_pairs={{0,16},{2,18},{4,20},{6,22},{8,24},{10,26},{12,28},{14,30},{16,0},... | collective-permute-start | bytes 156680 | tf_op jit(solution)/shard_map/ppermute | solution.py:281
  7.4 12.7 %collective-permute-start.3 = (bf16[256,256]{1,0:T(8,128)(2,1)S(1)}, bf16[256,256]{1,0:T(8,128)(2,1)S(1)}, u32[]{:S(2)}, u32[]{:S(2)}) collective-permute-start(bf16[256,256]{1,0:T(8,128)(2,1)S(1)} %get-tuple-element.49), channel_id=1, source_target_pairs={{0,16},{2,18},{4,20},{6,22},{8,24},{10,26},{12,28},{14,30},{16,0},... | collective-permute-start | bytes 393224 | tf_op jit(solution)/shard_map/ppermute | solution.py:281
  7.5 14.1 %collective-permute-start = (s16[17,3,512]{2,1,0:T(4,128)(2,1)S(1)}, s16[17,3,512]{2,1,0:T(4,128)(2,1)S(1)}, u32[]{:S(2)}, u32[]{:S(2)}) collective-permute-start(s16[17,3,512]{2,1,0:T(4,128)(2,1)S(1)} %ids_kernel.1.refs_0_), channel_id=1, source_target_pairs={{0,1},{1,0},{2,3},{3,2},{4,5},{5,4},{6,7},{7,6},{8,9},{9,8},{10,11... | collective-permute-start | bytes 156680 | tf_op jit(solution)/shard_map/ppermute | solution.py:281
  9.3 13.9 %collective-permute-start.4 = (bf16[256,256]{1,0:T(8,128)(2,1)S(1)}, bf16[256,256]{1,0:T(8,128)(2,1)S(1)}, u32[]{:S(2)}, u32[]{:S(2)}) collective-permute-start(bf16[256,256]{1,0:T(8,128)(2,1)S(1)} %get-tuple-element.50), channel_id=1, source_target_pairs={{0,16},{2,18},{4,20},{6,22},{8,24},{10,26},{12,28},{14,30},{16,0},... | collective-permute-start | bytes 393224 | tf_op jit(solution)/shard_map/ppermute | solution.py:281
  11.9 15.3 %collective-permute-start.6 = (bf16[256,512]{1,0:T(8,128)(2,1)S(1)}, bf16[256,512]{1,0:T(8,128)(2,1)S(1)}, u32[]{:S(2)}, u32[]{:S(2)}) collective-permute-start(bf16[256,512]{1,0:T(8,128)(2,1)S(1)} %get-tuple-element.52.refs_0_), channel_id=1, source_target_pairs={{0,1},{1,0},{2,3},{3,2},{4,5},{5,4},{6,7},{7,6},{8,9},{9,8},{10,11... | collective-permute-start | bytes 786440 | tf_op jit(solution)/shard_map/ppermute | solution.py:281
  12.4 9.2 %collective-permute-start.2 = (s16[17,3,512]{2,1,0:T(4,128)(2,1)S(1)}, s16[17,3,512]{2,1,0:T(4,128)(2,1)S(1)}, u32[]{:S(2)}, u32[]{:S(2)}) collective-permute-start(s16[17,3,512]{2,1,0:T(4,128)(2,1)S(1)} %collective-permute-done.1.refs_2_), channel_id=1, source_target_pairs={{0,1},{1,0},{2,3},{3,2},{4,5},{5,4},{6,7},{7,6},{8,9},{9,8},{10,11... | collective-permute-start | bytes 156680 | tf_op jit(solution)/shard_map/ppermute | solution.py:281
  14.0 13.2 %copy-start.1 = (f32[400,256]{1,0:T(8,128)S(1)}, f32[400,256]{1,0:T(8,128)}, u32[]{:S(2)}) copy-start(f32[400,256]{1,0:T(8,128)} %relations.3) | copy-start | bytes 1228804
  20.1 5.6 %collective-permute-start.5 = (bf16[256,256]{1,0:T(8,128)(2,1)S(1)}, bf16[256,256]{1,0:T(8,128)(2,1)S(1)}, u32[]{:S(2)}, u32[]{:S(2)}) collective-permute-start(bf16[256,256]{1,0:T(8,128)(2,1)S(1)} %collective-permute-done.3.refs_2_), channel_id=1, source_target_pairs={{0,1},{1,0},{2,3},{3,2},{4,5},{5,4},{6,7},{7,6},{8,9},{9,8},{10,11... | collective-permute-start | bytes 393224 | tf_op jit(solution)/shard_map/ppermute | solution.py:281
  25.7 5.5 %collective-permute-start.7 = (bf16[256,256]{1,0:T(8,128)(2,1)S(1)}, bf16[256,256]{1,0:T(8,128)(2,1)S(1)}, u32[]{:S(2)}, u32[]{:S(2)}) collective-permute-start(bf16[256,256]{1,0:T(8,128)(2,1)S(1)} %collective-permute-done.4.refs_3_), channel_id=1, source_target_pairs={{0,1},{1,0},{2,3},{3,2},{4,5},{5,4},{6,7},{7,6},{8,9},{9,8},{10,11... | collective-permute-start | bytes 393224 | tf_op jit(solution)/shard_map/ppermute | solution.py:281
  42.1 1.6 %collective-permute-start.8 = (f32[256,256]{1,0:T(8,128)S(1)}, f32[256,256]{1,0:T(8,128)S(1)}, u32[]{:S(2)}, u32[]{:S(2)}) collective-permute-start(f32[256,256]{1,0:T(8,128)S(1)} %get-tuple-element.59), channel_id=1, source_target_pairs={{0,2},{2,0},{4,6},{6,4},{8,10},{10,8},{12,14},{14,12},{16,18},{18,... | collective-permute-start | bytes 786440 | tf_op jit(solution)/shard_map/ppermute | solution.py:281
  43.7 9.5 %collective-permute-start.9 = (f32[64,256]{1,0:T(8,128)S(1)}, f32[64,256]{1,0:T(8,128)S(1)}, u32[]{:S(2)}, u32[]{:S(2)}) collective-permute-start(f32[64,256]{1,0:T(8,128)S(1)} %get-tuple-element.65), channel_id=1, source_target_pairs={{0,1},{1,0},{2,3},{3,2},{4,5},{5,4},{6,7},{7,6},{8,9},{9,8},{10,11... | collective-permute-start | bytes 196616 | tf_op jit(solution)/shard_map/ppermute | solution.py:359
  46.3 6.9 %collective-permute-start.10 = (f32[64,256]{1,0:T(8,128)S(1)}, f32[64,256]{1,0:T(8,128)S(1)}, u32[]{:S(2)}, u32[]{:S(2)}) collective-permute-start(f32[64,256]{1,0:T(8,128)S(1)} %get-tuple-element.66), channel_id=1, source_target_pairs={{0,4},{1,5},{2,6},{3,7},{4,0},{5,1},{6,2},{7,3},{8,12},{9,13},{10,... | collective-permute-start | bytes 196616 | tf_op jit(solution)/shard_map/ppermute | solution.py:359
  47.9 5.3 %collective-permute-start.11 = (f32[64,256]{1,0:T(8,128)S(1)}, f32[64,256]{1,0:T(8,128)S(1)}, u32[]{:S(2)}, u32[]{:S(2)}) collective-permute-start(f32[64,256]{1,0:T(8,128)S(1)} %get-tuple-element.67), channel_id=1, source_target_pairs={{0,5},{1,4},{2,7},{3,6},{4,1},{5,0},{6,3},{7,2},{8,13},{9,12},{10,... | collective-permute-start | bytes 196616 | tf_op jit(solution)/shard_map/ppermute | solution.py:359
  47.9 16.7 %collective-permute-start.15 = (f16[512,256]{1,0:T(8,128)(2,1)S(1)}, f16[512,256]{1,0:T(8,128)(2,1)S(1)}, u32[]{:S(2)}, u32[]{:S(2)}) collective-permute-start(f16[512,256]{1,0:T(8,128)(2,1)S(1)} %multiply_convert_fusion.2), channel_id=1, source_target_pairs={{0,1},{1,0},{2,3},{3,2},{4,5},{5,4},{6,7},{7,6},{8,9},{9,8},{10,11... | collective-permute-start | bytes 786440 | tf_op jit(solution)/shard_map/ppermute | solution.py:281
  53.3 9.1 %collective-permute-start.14 = (f32[64,256]{1,0:T(8,128)S(1)}, f32[64,256]{1,0:T(8,128)S(1)}, u32[]{:S(2)}, u32[]{:S(2)}) collective-permute-start(f32[64,256]{1,0:T(8,128)S(1)} %add_add_fusion.1), channel_id=1, source_target_pairs={{0,24},{2,26},{4,28},{6,30},{8,16},{10,18},{12,20},{14,22},{16,8},... | collective-permute-start | bytes 196616 | tf_op jit(solution)/shard_map/ppermute | solution.py:281
  59.1 5.4 %collective-permute-start.13 = (f32[64,256]{1,0:T(8,128)S(1)}, f32[64,256]{1,0:T(8,128)S(1)}, u32[]{:S(2)}, u32[]{:S(2)}) collective-permute-start(f32[64,256]{1,0:T(8,128)S(1)} %add_add_fusion.1), channel_id=1, source_target_pairs={{0,16},{2,18},{4,20},{6,22},{8,24},{10,26},{12,28},{14,30},{16,0},... | collective-permute-start | bytes 196616 | tf_op jit(solution)/shard_map/ppermute | solution.py:281
  59.1 5.5 %collective-permute-start.12 = (f32[64,256]{1,0:T(8,128)S(1)}, f32[64,256]{1,0:T(8,128)S(1)}, u32[]{:S(2)}, u32[]{:S(2)}) collective-permute-start(f32[64,256]{1,0:T(8,128)S(1)} %add_add_fusion.1), channel_id=1, source_target_pairs={{0,8},{2,10},{4,12},{6,14},{8,0},{10,2},{12,4},{14,6},{16,24},{18,... | collective-permute-start | bytes 196616 | tf_op jit(solution)/shard_map/ppermute | solution.py:281
  62.3 16.2 %copy-start = (f32[512,256]{1,0:T(8,128)S(1)}, f32[512,256]{1,0:T(8,128)}, u32[]{:S(2)}) copy-start(f32[512,256]{1,0:T(8,128)} %table.2) | copy-start | bytes 1572868
  62.3 16.2 %copy-start.2 = (f32[512]{0:T(512)S(1)}, f32[512]{0:T(512)}, u32[]{:S(2)}) copy-start(f32[512]{0:T(512)} %param.10) | copy-start | bytes 6148
  62.3 17.7 %copy-start.3 = (f32[400]{0:T(512)S(1)}, f32[400]{0:T(512)}, u32[]{:S(2)}) copy-start(f32[400]{0:T(512)} %param.12) | copy-start | bytes 4804
  64.8 13.7 %collective-permute-start.16 = (f16[512,256]{1,0:T(8,128)(2,1)S(1)}, f16[512,256]{1,0:T(8,128)(2,1)S(1)}, u32[]{:S(2)}, u32[]{:S(2)}) collective-permute-start(f16[512,256]{1,0:T(8,128)(2,1)S(1)} %multiply_convert_fusion.1), channel_id=1, source_target_pairs={{0,16},{2,18},{4,20},{6,22},{8,24},{10,26},{12,28},{14,30},{16,0},... | collective-permute-start | bytes 786440 | tf_op jit(solution)/shard_map/ppermute | solution.py:281
  66.5 12.0 %collective-permute-start.20 = (f16[512,256]{1,0:T(8,128)(2,1)S(1)}, f16[512,256]{1,0:T(8,128)(2,1)S(1)}, u32[]{:S(2)}, u32[]{:S(2)}) collective-permute-start(f16[512,256]{1,0:T(8,128)(2,1)S(1)} %multiply_convert_fusion), channel_id=1, source_target_pairs={{0,1},{1,0},{2,3},{3,2},{4,5},{5,4},{6,7},{7,6},{8,9},{9,8},{10,11... | collective-permute-start | bytes 786440 | tf_op jit(solution)/shard_map/ppermute | solution.py:281
  68.4 6.0 %collective-permute-start.19 = (f32[64,256]{1,0:T(8,128)S(1)}, f32[64,256]{1,0:T(8,128)S(1)}, u32[]{:S(2)}, u32[]{:S(2)}) collective-permute-start(f32[64,256]{1,0:T(8,128)S(1)} %add_add_fusion), channel_id=1, source_target_pairs={{0,5},{1,4},{2,7},{3,6},{4,1},{5,0},{6,3},{7,2},{8,13},{9,12},{10,... | collective-permute-start | bytes 196616 | tf_op jit(solution)/shard_map/ppermute | solution.py:359
  70.0 4.5 %collective-permute-start.18 = (f32[64,256]{1,0:T(8,128)S(1)}, f32[64,256]{1,0:T(8,128)S(1)}, u32[]{:S(2)}, u32[]{:S(2)}) collective-permute-start(f32[64,256]{1,0:T(8,128)S(1)} %add_add_fusion), channel_id=1, source_target_pairs={{0,4},{1,5},{2,6},{3,7},{4,0},{5,1},{6,2},{7,3},{8,12},{9,13},{10,... | collective-permute-start | bytes 196616 | tf_op jit(solution)/shard_map/ppermute | solution.py:359
  70.1 5.5 %collective-permute-start.17 = (f32[64,256]{1,0:T(8,128)S(1)}, f32[64,256]{1,0:T(8,128)S(1)}, u32[]{:S(2)}, u32[]{:S(2)}) collective-permute-start(f32[64,256]{1,0:T(8,128)S(1)} %add_add_fusion), channel_id=1, source_target_pairs={{0,1},{1,0},{2,3},{3,2},{4,5},{5,4},{6,7},{7,6},{8,9},{9,8},{10,11... | collective-permute-start | bytes 196616 | tf_op jit(solution)/shard_map/ppermute | solution.py:359
  78.4 1.5 %collective-permute-start.21 = (f32[256,256]{1,0:T(8,128)S(1)}, f32[256,256]{1,0:T(8,128)S(1)}, u32[]{:S(2)}, u32[]{:S(2)}) collective-permute-start(f32[256,256]{1,0:T(8,128)S(1)} %pad_maximum_fusion.mine), channel_id=1, source_target_pairs={{0,2},{2,0},{4,6},{6,4},{8,10},{10,8},{12,14},{14,12},{16,18},{18,... | collective-permute-start | bytes 786440 | tf_op jit(solution)/shard_map/ppermute | solution.py:281

commit v5 on v3

--- a/solution.py
+++ b/solution.py
@@ -415,27 +415,24 @@
     other_core = exchange(relation_part[chips], "dom", 1)
     partial = [relation_part[k] + other_core[k * chunk : (k + 1) * chunk] for k in range(chips)]
     away_other = [narrow(x) for x in away_other]
-    partial, plan, away_other = lax.optimization_barrier((partial, plan, away_other))
+    away_received = [widen(exchange(away_other[k - 1], "sub", k)) for k in range(1, n)]
+    partial, plan = lax.optimization_barrier((partial, plan))
     chunk_total = partial[0]
     for k in range(1, chips):
         chunk_total = chunk_total + to_chip(partial[k], k)
-    away_received = [widen(exchange(away_other[k - 1], "sub", k)) for k in range(1, n)]
     (away_total,) = scatter("away_kernel", 1, 0, 1, 0, plan, away_grad)
-    chunk_total, away_total, plan = lax.optimization_barrier((chunk_total, away_total, plan))
-    masks = [4 << k for k in range((n_dom // 4).bit_length() - 1)]
-    for mask in masks[:-1]:
-        chunk_total = chunk_total + exchange(chunk_total, "dom", mask)
-    near_other = scatter("own_other_kernel", 0, rows, n - 1, n, plan, near_grad)
-    near_other = [narrow(x) for x in near_other]
     for x in away_received:
         away_total = away_total + x
     away_total = narrow(away_total)
-    chunk_total, away_total, near_other, plan = lax.optimization_barrier((chunk_total, away_total, near_other, plan))
+    chunk_total, away_total, plan = lax.optimization_barrier((chunk_total, away_total, plan))
+    terms = [chunk_total] + [exchange(chunk_total, "dom", mask) for mask in range(4, n_dom, 4)]
+    returned = exchange(away_total, "dom", pair)
+    near_other = scatter("own_other_kernel", 0, rows, n - 1, n, plan, near_grad)
+    near_other = [narrow(x) for x in near_other]
+    while len(terms) > 1:
+        terms = [terms[k] + terms[k + 1] for k in range(0, len(terms), 2)]
+    chunk_total, near_other, plan = lax.optimization_barrier((terms[0], near_other, plan))
     near_received = [widen(exchange(near_other[k - 1], "sub", k)) for k in range(1, n)]
-    for mask in masks[-1:]:
-        chunk_total = chunk_total + exchange(chunk_total, "dom", mask)
-    chunk_total, away_total, plan = lax.optimization_barrier((chunk_total, away_total, plan))
-    returned = exchange(away_total, "dom", pair)
     mine = jnp.concatenate([chunk_total] + [to_chip(chunk_total, k) for k in range(1, chips)], axis=0)
     (near_sum,) = scatter("own_kernel", 0, 0, 1, n, plan, near_grad)
     returned, mine, near_sum = lax.optimization_barrier((returned, mine, near_sum))

time: 80.8 us -> 81 us (level)
  waiting for transfers between devices: 22.5 us -> 17.9 us
  Pallas kernels: 28.2 us -> 32.6 us
    ppermute x13 -> x14, starting transfers between devices: 12.8 us -> 18.1 us  [exchange(): lax.ppermute(x, axis, [(i, i ^ mask) for i in range(lax.axis_size(axis))])]
    ppermute x6, starting transfers between devices: 14.4 us -> 9.93 us  [to_peer(): return lax.ppermute(x, ('dom', 'sub'), pairs)]
    pallas_call x9, Pallas kernels: 26.6 us -> 31.1 us  [call(): pl.pallas_call(kernel, in_specs=[in_smem] * len(scalars) + [in_vmem] * le...]
    ppermute x13 -> x14, waiting for transfers between devices: 20.6 us -> 17.4 us  [exchange(): lax.ppermute(x, axis, [(i, i ^ mask) for i in range(lax.axis_size(axis))])]
    ppermute x6, waiting for transfers between devices: 1.95 us -> 0.52 us  [to_peer(): return lax.ppermute(x, ('dom', 'sub'), pairs)]
  transfers between devices with their start and end apart: 19 -> 20, of which waited for: 11 -> 7; matrix products, arithmetic and copies ran while one was open for 0% -> 1% of each run, Pallas kernels for 20% -> 22%
where the time goes in v5:
time: 81 us; the launch traced here: 80.5 us
  Pallas kernels  32.6 us (40%)
  starting transfers between devices  28 us (35%)
  waiting for transfers between devices  17.9 us (22%)
  between operations  1.52 us (2%)
    pallas_call x9, Pallas kernels, call(): pl.pallas_call(kernel, in_specs=[in_smem] * len(scalars) + [in_vmem] * le...  31.1 us
    ppermute x14, starting transfers between devices, exchange(): lax.ppermute(x, axis, [(i, i ^ mask) for i in range(lax.axis_size(axis))])  18.1 us
    ppermute x14, waiting for transfers between devices, exchange(): lax.ppermute(x, axis, [(i, i ^ mask) for i in range(lax.axis_size(axis))])  17.4 us
    ppermute x6, starting transfers between devices, to_peer(): return lax.ppermute(x, ('dom', 'sub'), pairs)  9.93 us
  transfers between devices with their start and end apart: 20, of which 7 were waited for; matrix products, arithmetic and copies ran while one was open for 1% of the time, Pallas kernels for 22%

profile of v5, /device:TPU:0, one launch (start us, length us, event | category | flops | bytes accessed | tf_op | source)
XLA Modules:
  0.0 80.5 jit_solution(3105990957971671937)
XLA Ops:
  1.3 0.8 %ids_kernel.1.refs_0_ = s16[17,3,512]{2,1,0:T(4,128)(2,1)S(1)} custom-call(s32[1,1]{1,0:T(1,128)S(6)} %copy.12.count, s32[1,8192]{1,0:T(1,128)} %bitcast.12, s32[1,8192]{1,0:T(1,128)} %bitcast.13, s32[1,8192]{1,0:T(1,128)} %bitcast.14, s32[1,512]{1,0:T(1,128)} %bitcast.15), custom_call_target="tpu_custom_call" | custom-call | flops 2097152 | bytes 131072 | tf_op jit(solution)/shard_map/ids_kernel/pallas_call | solution.py:311
  2.1 4.1 %collective-permute-start.1 = (s16[17,3,512]{2,1,0:T(4,128)(2,1)S(1)}, s16[17,3,512]{2,1,0:T(4,128)(2,1)S(1)}, u32[]{:S(2)}, u32[]{:S(2)}) collective-permute-start(s16[17,3,512]{2,1,0:T(4,128)(2,1)S(1)} %ids_kernel.1.refs_0_), channel_id=1, source_target_pairs={{0,16},{2,18},{4,20},{6,22},{8,24},{10,26},{12,28},{14,30},{16,0},... | collective-permute-start | bytes 156680 | tf_op jit(solution)/shard_map/ppermute | solution.py:274
  6.2 1.5 %collective-permute-start = (s16[17,3,512]{2,1,0:T(4,128)(2,1)S(1)}, s16[17,3,512]{2,1,0:T(4,128)(2,1)S(1)}, u32[]{:S(2)}, u32[]{:S(2)}) collective-permute-start(s16[17,3,512]{2,1,0:T(4,128)(2,1)S(1)} %ids_kernel.1.refs_0_), channel_id=1, source_target_pairs={{0,1},{1,0},{2,3},{3,2},{4,5},{5,4},{6,7},{7,6},{8,9},{9,8},{10,11... | collective-permute-start | bytes 156680 | tf_op jit(solution)/shard_map/ppermute | solution.py:274
  7.7 1.2 %rows_kernel.1.refs_0_ = bf16[256,512]{1,0:T(8,128)(2,1)S(1)} custom-call(f32[512,256]{1,0:T(8,128)} %table.2), custom_call_target="tpu_custom_call" | custom-call | flops 2097152 | bytes 131072 | tf_op jit(solution)/shard_map/rows_kernel/pallas_call | solution.py:311
  8.9 0.6 collective-permute-start.4
  9.5 0.1 collective-permute-start.3
  9.6 0.4 collective-permute-done.1.refs_2_
  10.0 1.7 %collective-permute-start.2 = (s16[17,3,512]{2,1,0:T(4,128)(2,1)S(1)}, s16[17,3,512]{2,1,0:T(4,128)(2,1)S(1)}, u32[]{:S(2)}, u32[]{:S(2)}) collective-permute-start(s16[17,3,512]{2,1,0:T(4,128)(2,1)S(1)} %collective-permute-done.1.refs_2_), channel_id=1, source_target_pairs={{0,1},{1,0},{2,3},{3,2},{4,5},{5,4},{6,7},{7,6},{8,9},{9,8},{10,11... | collective-permute-start | bytes 156680 | tf_op jit(solution)/shard_map/ppermute | solution.py:274
  11.7 0.1 pad_add_fusion.codes
  11.8 0.0 copy-start.1
  11.8 0.0 collective-permute-done.refs_1_
  11.8 6.2 %collective-permute-done.2.refs_3_ = s16[17,3,512]{2,1,0:T(4,128)(2,1)S(1)} collective-permute-done((s16[17,3,512]{2,1,0:T(4,128)(2,1)S(1)}, s16[17,3,512]{2,1,0:T(4,128)(2,1)S(1)}, u32[]{:S(2)}, u32[]{:S(2)}) %collective-permute-start.2) | collective-permute-done | bytes 52256 | tf_op jit(solution)/shard_map/ppermute | solution.py:274
  18.0 1.6 %plan_kernel.1 = (s32[37]{0:T(128)S(1)}, s32[16,3,512]{2,1,0:T(4,128)S(1)}, s32[4,1,512]{2,1,0:T(1,128)S(1)}) custom-call(s32[3]{0:T(128)S(1)} %pad_add_fusion.codes, s16[17,3,512]{2,1,0:T(4,128)(2,1)S(1)} %ids_kernel.1.refs_0_, s16[17,3,512]{2,1,0:T(4,128)(2,1)S(1)} %collective-permute-done.refs_1_, s16[17,3,512]{2,1,0:T(4,128)(2,1)S(1)} %collective-permute-done.1.refs_2_, ...), custom_call_target="tpu_custom_call" | custom-call | flops 34359738368 | bytes 2097152 | tf_op jit(solution)/shard_map/plan_kernel/pallas_call | solution.py:351
  19.6 3.7 %collective-permute-done.3.refs_2_ = bf16[256,512]{1,0:T(8,128)(2,1)S(1)} collective-permute-done((bf16[256,512]{1,0:T(8,128)(2,1)S(1)}, bf16[256,512]{1,0:T(8,128)(2,1)S(1)}, u32[]{:S(2)}, u32[]{:S(2)}) %collective-permute-start.3) | collective-permute-done | bytes 262176 | tf_op jit(solution)/shard_map/ppermute | solution.py:274
  23.2 1.5 %collective-permute-start.5 = (bf16[256,512]{1,0:T(8,128)(2,1)S(1)}, bf16[256,512]{1,0:T(8,128)(2,1)S(1)}, u32[]{:S(2)}, u32[]{:S(2)}) collective-permute-start(bf16[256,512]{1,0:T(8,128)(2,1)S(1)} %collective-permute-done.3.refs_2_), channel_id=1, source_target_pairs={{0,1},{1,0},{2,3},{3,2},{4,5},{5,4},{6,7},{7,6},{8,9},{9,8},{10,11... | collective-permute-start | bytes 786440 | tf_op jit(solution)/shard_map/ppermute | solution.py:274
  24.7 0.0 collective-permute-done.4.refs_1_
  24.7 0.0 copy-done.1
  24.7 4.5 %near_kernel.1 = (bf16[16,256,512]{2,1,0:T(8,128)(2,1)S(1)}, f32[16,256,512]{2,1,0:T(8,128)S(1)}) custom-call(s32[37]{0:T(128)S(1)} %get-tuple-element.64.plan, s32[16,3,512]{2,1,0:T(4,128)S(1)} %get-tuple-element.39.ids, f32[400,256]{1,0:T(8,128)S(1)} %copy-done.1, bf16[256,512]{1,0:T(8,128)(2,1)S(1)} %rows_kernel.1.refs_0_, ...), custom_call_target="tpu_custom_call" | custom-call | flops 4294967296 | bytes 131072 | tf_op jit(solution)/shard_map/near_kernel/pallas_call | solution.py:311
  29.3 1.1 %collective-permute-done.5.refs_3_ = bf16[256,512]{1,0:T(8,128)(2,1)S(1)} collective-permute-done((bf16[256,512]{1,0:T(8,128)(2,1)S(1)}, bf16[256,512]{1,0:T(8,128)(2,1)S(1)}, u32[]{:S(2)}, u32[]{:S(2)}) %collective-permute-start.5) | collective-permute-done | bytes 262176 | tf_op jit(solution)/shard_map/ppermute | solution.py:274
  30.4 12.4 %edge_kernel.1 = (bf16[16,512,512]{2,1,0:T(8,128)(2,1)S(1)}, bf16[16,512,512]{2,1,0:T(8,128)(2,1)S(1)}, bf16[4,1024,256]{2,1,0:T(8,128)(2,1)S(1)}, f32[512,256]{...) custom-call(s32[3]{0:T(128)S(1)} %pad_add_fusion.codes, ...), custom_call_target="tpu_custom_call" | custom-call | flops 11811160064 | bytes 131072 | tf_op jit(solution)/shard_map/edge_kernel/pallas_call | solution.py:311
  42.8 0.1 collective-permute-start.6
  42.9 0.1 multiply_convert_fusion.2
  42.9 1.4 %collective-permute-start.10 = (f16[512,256]{1,0:T(8,128)(2,1)S(1)}, f16[512,256]{1,0:T(8,128)(2,1)S(1)}, u32[]{:S(2)}, u32[]{:S(2)}) collective-permute-start(f16[512,256]{1,0:T(8,128)(2,1)S(1)} %multiply_convert_fusion.2), channel_id=1, source_target_pairs={{0,1},{1,0},{2,3},{3,2},{4,5},{5,4},{6,7},{7,6},{8,9},{9,8},{10,11... | collective-permute-start | bytes 786440 | tf_op jit(solution)/shard_map/ppermute | solution.py:274
  44.4 0.0 collective-permute-done.6
  44.4 1.4 %collective-permute-start.7 = (f32[64,256]{1,0:T(8,128)S(1)}, f32[64,256]{1,0:T(8,128)S(1)}, u32[]{:S(2)}, u32[]{:S(2)}) collective-permute-start(f32[64,256]{1,0:T(8,128)S(1)} %get-tuple-element.52), channel_id=1, source_target_pairs={{0,1},{1,0},{2,3},{3,2},{4,5},{5,4},{6,7},{7,6},{8,9},{9,8},{10,11... | collective-permute-start | bytes 196616 | tf_op jit(solution)/shard_map/ppermute | solution.py:342
  45.9 4.2 %collective-permute-start.8 = (f32[64,256]{1,0:T(8,128)S(1)}, f32[64,256]{1,0:T(8,128)S(1)}, u32[]{:S(2)}, u32[]{:S(2)}) collective-permute-start(f32[64,256]{1,0:T(8,128)S(1)} %get-tuple-element.53), channel_id=1, source_target_pairs={{0,4},{1,5},{2,6},{3,7},{4,0},{5,1},{6,2},{7,3},{8,12},{9,13},{10,... | collective-permute-start | bytes 196616 | tf_op jit(solution)/shard_map/ppermute | solution.py:342
  50.0 0.8 %collective-permute-start.9 = (f32[64,256]{1,0:T(8,128)S(1)}, f32[64,256]{1,0:T(8,128)S(1)}, u32[]{:S(2)}, u32[]{:S(2)}) collective-permute-start(f32[64,256]{1,0:T(8,128)S(1)} %get-tuple-element.54), channel_id=1, source_target_pairs={{0,5},{1,4},{2,7},{3,6},{4,1},{5,0},{6,3},{7,2},{8,13},{9,12},{10,... | collective-permute-start | bytes 196616 | tf_op jit(solution)/shard_map/ppermute | solution.py:342
  50.9 3.7 %away_kernel.1 = f32[512,256]{1,0:T(8,128)S(1)} custom-call(s32[37]{0:T(128)S(1)} %get-tuple-element.64.plan, s32[16,3,512]{2,1,0:T(4,128)S(1)} %get-tuple-element.39.ids, s32[4,1,512]{2,1,0:T(1,128)S(1)} %get-tuple-element.40.negative_ids, bf16[16,512,512]{2,1,0:T(8,128)(2,1)S(1)} %get-tuple-element.56.grads, ...), custom_call_target="tpu_custom_call" | custom-call | bytes 131072 | tf_op jit(solution)/shard_map/away_kernel/pallas_call | solution.py:311
  54.6 0.0 collective-permute-done.10
  54.6 0.1 multiply_convert_fusion.1
  54.7 0.0 collective-permute-done.7
  54.7 0.0 collective-permute-done.8
  54.7 0.5 collective-permute-done.9
  55.2 2.3 %collective-permute-start.14 = (f32[64,256]{1,0:T(8,128)S(1)}, f32[64,256]{1,0:T(8,128)S(1)}, u32[]{:S(2)}, u32[]{:S(2)}) collective-permute-start(f32[64,256]{1,0:T(8,128)S(1)} %add_add_fusion.1), channel_id=1, source_target_pairs={{0,24},{2,26},{4,28},{6,30},{8,16},{10,18},{12,20},{14,22},{16,8},... | collective-permute-start | bytes 196616 | tf_op jit(solution)/shard_map/ppermute | solution.py:274
  57.6 0.0 collective-permute-start.13
  57.6 2.1 %collective-permute-start.12 = (f32[64,256]{1,0:T(8,128)S(1)}, f32[64,256]{1,0:T(8,128)S(1)}, u32[]{:S(2)}, u32[]{:S(2)}) collective-permute-start(f32[64,256]{1,0:T(8,128)S(1)} %add_add_fusion.1), channel_id=1, source_target_pairs={{0,8},{2,10},{4,12},{6,14},{8,0},{10,2},{12,4},{14,6},{16,24},{18,... | collective-permute-start | bytes 196616 | tf_op jit(solution)/shard_map/ppermute | solution.py:274
  59.7 0.8 %collective-permute-start.11 = (f16[512,256]{1,0:T(8,128)(2,1)S(1)}, f16[512,256]{1,0:T(8,128)(2,1)S(1)}, u32[]{:S(2)}, u32[]{:S(2)}) collective-permute-start(f16[512,256]{1,0:T(8,128)(2,1)S(1)} %multiply_convert_fusion.1), channel_id=1, source_target_pairs={{0,16},{2,18},{4,20},{6,22},{8,24},{10,26},{12,28},{14,30},{16,0},... | collective-permute-start | bytes 786440 | tf_op jit(solution)/shard_map/ppermute | solution.py:274
  60.5 2.8 %own_other_kernel.1 = f32[512,256]{1,0:T(8,128)S(1)} custom-call(s32[37]{0:T(128)S(1)} %get-tuple-element.64.plan, s32[16,3,512]{2,1,0:T(4,128)S(1)} %get-tuple-element.39.ids, s32[4,1,512]{2,1,0:T(1,128)S(1)} %get-tuple-element.40.negative_ids, bf16[16,512,512]{2,1,0:T(8,128)(2,1)S(1)} %get-tuple-element.62.grads, ...), custom_call_target="tpu_custom_call" | custom-call | bytes 131072 | tf_op jit(solution)/shard_map/own_other_kernel/pallas_call | solution.py:311
  63.3 0.0 copy-start
  63.3 0.0 copy-start.2
  63.4 0.0 copy-start.3
  63.4 0.1 multiply_convert_fusion
  63.4 0.0 collective-permute-done.14
  63.4 5.7 %collective-permute-done.13 = f32[64,256]{1,0:T(8,128)S(1)} collective-permute-done((f32[64,256]{1,0:T(8,128)S(1)}, f32[64,256]{1,0:T(8,128)S(1)}, u32[]{:S(2)}, u32[]{:S(2)}) %collective-permute-start.13) | collective-permute-done | bytes 65568 | tf_op jit(solution)/shard_map/ppermute | solution.py:274
  69.2 0.0 collective-permute-done.12
  69.2 1.7 %collective-permute-start.18 = (f16[512,256]{1,0:T(8,128)(2,1)S(1)}, f16[512,256]{1,0:T(8,128)(2,1)S(1)}, u32[]{:S(2)}, u32[]{:S(2)}) collective-permute-start(f16[512,256]{1,0:T(8,128)(2,1)S(1)} %multiply_convert_fusion), channel_id=1, source_target_pairs={{0,1},{1,0},{2,3},{3,2},{4,5},{5,4},{6,7},{7,6},{8,9},{9,8},{10,11... | collective-permute-start | bytes 786440 | tf_op jit(solution)/shard_map/ppermute | solution.py:274
  70.9 0.0 collective-permute-start.17
  70.9 1.9 %collective-permute-start.16 = (f32[64,256]{1,0:T(8,128)S(1)}, f32[64,256]{1,0:T(8,128)S(1)}, u32[]{:S(2)}, u32[]{:S(2)}) collective-permute-start(f32[64,256]{1,0:T(8,128)S(1)} %add_add_fusion), channel_id=1, source_target_pairs={{0,4},{1,5},{2,6},{3,7},{4,0},{5,1},{6,2},{7,3},{8,12},{9,13},{10,... | collective-permute-start | bytes 196616 | tf_op jit(solution)/shard_map/ppermute | solution.py:342
  72.8 1.6 %collective-permute-start.15 = (f32[64,256]{1,0:T(8,128)S(1)}, f32[64,256]{1,0:T(8,128)S(1)}, u32[]{:S(2)}, u32[]{:S(2)}) collective-permute-start(f32[64,256]{1,0:T(8,128)S(1)} %add_add_fusion), channel_id=1, source_target_pairs={{0,1},{1,0},{2,3},{3,2},{4,5},{5,4},{6,7},{7,6},{8,9},{9,8},{10,11... | collective-permute-start | bytes 196616 | tf_op jit(solution)/shard_map/ppermute | solution.py:342
  74.4 2.8 %own_kernel.1.own = f32[512,256]{1,0:T(8,128)S(1)} custom-call(s32[37]{0:T(128)S(1)} %get-tuple-element.64.plan, s32[16,3,512]{2,1,0:T(4,128)S(1)} %get-tuple-element.39.ids, s32[4,1,512]{2,1,0:T(1,128)S(1)} %get-tuple-element.40.negative_ids, bf16[16,512,512]{2,1,0:T(8,128)(2,1)S(1)} %get-tuple-element.62.grads, ...), custom_call_target="tpu_custom_call" | custom-call | bytes 131072 | tf_op jit(solution)/shard_map/own_kernel/pallas_call | solution.py:311
  77.2 0.0 collective-permute-done.17
  77.2 0.0 collective-permute-done.16
  77.2 0.0 collective-permute-done.15
  77.3 0.0 collective-permute-done.11
  77.3 0.1 collective-permute-start.19
  77.4 0.0 collective-permute-done.18
  77.4 0.1 add_multiply_fusion.returned
  77.4 0.0 copy-done
  77.5 0.0 copy-done.2
  77.5 1.2 %entity_kernel.1 = (f32[512,256]{1,0:T(8,128)}, f32[1,512]{1,0:T(1,128)}) custom-call(f32[512,256]{1,0:T(8,128)S(1)} %copy-done, f32[1,512]{1,0:T(1,128)S(1)} %bitcast.10, f32[512,256]{1,0:T(8,128)S(1)} %add_multiply_fusion.returned, f32[512,256]{1,0:T(8,128)S(1)} %own_kernel.1.own), custom_call_target="tpu_custom_call" | custom-call | flops 2097152 | bytes 131072 | tf_op jit(solution)/shard_map/entity_kernel/pallas_call | solution.py:311
  78.6 0.3 collective-permute-done.19.theirs
  78.9 0.0 copy-done.3
  78.9 1.6 %relation_kernel.1 = f32[400,256]{1,0:T(8,128)} custom-call(s32[3]{0:T(128)S(1)} %pad_add_fusion.codes, f32[400,256]{1,0:T(8,128)S(1)} %copy-done.1, f32[1,400]{1,0:T(1,128)S(1)} %bitcast.11, f32[256,256]{1,0:T(8,128)S(1)} %pad_maximum_fusion.mine, f32[256,256]{1,0:T(8,128)S(1)} %collective-permute-done.19.theirs), custom_call_target="tpu_custom_call" | custom-call | bytes 131072 | tf_op jit(solution)/shard_map/relation_kernel/pallas_call | solution.py:311
  (4 shorter events, 0.1 us)
Async XLA Ops:
  2.1 7.9 %collective-permute-start.1 = (s16[17,3,512]{2,1,0:T(4,128)(2,1)S(1)}, s16[17,3,512]{2,1,0:T(4,128)(2,1)S(1)}, u32[]{:S(2)}, u32[]{:S(2)}) collective-permute-start(s16[17,3,512]{2,1,0:T(4,128)(2,1)S(1)} %ids_kernel.1.refs_0_), channel_id=1, source_target_pairs={{0,16},{2,18},{4,20},{6,22},{8,24},{10,26},{12,28},{14,30},{16,0},... | collective-permute-start | bytes 156680 | tf_op jit(solution)/shard_map/ppermute | solution.py:274
  6.2 5.6 %collective-permute-start = (s16[17,3,512]{2,1,0:T(4,128)(2,1)S(1)}, s16[17,3,512]{2,1,0:T(4,128)(2,1)S(1)}, u32[]{:S(2)}, u32[]{:S(2)}) collective-permute-start(s16[17,3,512]{2,1,0:T(4,128)(2,1)S(1)} %ids_kernel.1.refs_0_), channel_id=1, source_target_pairs={{0,1},{1,0},{2,3},{3,2},{4,5},{5,4},{6,7},{7,6},{8,9},{9,8},{10,11... | collective-permute-start | bytes 156680 | tf_op jit(solution)/shard_map/ppermute | solution.py:274
  8.9 15.8 %collective-permute-start.4 = (bf16[256,512]{1,0:T(8,128)(2,1)S(1)}, bf16[256,512]{1,0:T(8,128)(2,1)S(1)}, u32[]{:S(2)}, u32[]{:S(2)}) collective-permute-start(bf16[256,512]{1,0:T(8,128)(2,1)S(1)} %rows_kernel.1.refs_0_), channel_id=1, source_target_pairs={{0,1},{1,0},{2,3},{3,2},{4,5},{5,4},{6,7},{7,6},{8,9},{9,8},{10,11... | collective-permute-start | bytes 786440 | tf_op jit(solution)/shard_map/ppermute | solution.py:274
  9.5 13.7 %collective-permute-start.3 = (bf16[256,512]{1,0:T(8,128)(2,1)S(1)}, bf16[256,512]{1,0:T(8,128)(2,1)S(1)}, u32[]{:S(2)}, u32[]{:S(2)}) collective-permute-start(bf16[256,512]{1,0:T(8,128)(2,1)S(1)} %rows_kernel.1.refs_0_), channel_id=1, source_target_pairs={{0,16},{2,18},{4,20},{6,22},{8,24},{10,26},{12,28},{14,30},{16,0},... | collective-permute-start | bytes 786440 | tf_op jit(solution)/shard_map/ppermute | solution.py:274
  10.0 8.0 %collective-permute-start.2 = (s16[17,3,512]{2,1,0:T(4,128)(2,1)S(1)}, s16[17,3,512]{2,1,0:T(4,128)(2,1)S(1)}, u32[]{:S(2)}, u32[]{:S(2)}) collective-permute-start(s16[17,3,512]{2,1,0:T(4,128)(2,1)S(1)} %collective-permute-done.1.refs_2_), channel_id=1, source_target_pairs={{0,1},{1,0},{2,3},{3,2},{4,5},{5,4},{6,7},{7,6},{8,9},{9,8},{10,11... | collective-permute-start | bytes 156680 | tf_op jit(solution)/shard_map/ppermute | solution.py:274
  11.8 12.9 %copy-start.1 = (f32[400,256]{1,0:T(8,128)S(1)}, f32[400,256]{1,0:T(8,128)}, u32[]{:S(2)}) copy-start(f32[400,256]{1,0:T(8,128)} %relations.3) | copy-start | bytes 1228804
  23.2 7.1 %collective-permute-start.5 = (bf16[256,512]{1,0:T(8,128)(2,1)S(1)}, bf16[256,512]{1,0:T(8,128)(2,1)S(1)}, u32[]{:S(2)}, u32[]{:S(2)}) collective-permute-start(bf16[256,512]{1,0:T(8,128)(2,1)S(1)} %collective-permute-done.3.refs_2_), channel_id=1, source_target_pairs={{0,1},{1,0},{2,3},{3,2},{4,5},{5,4},{6,7},{7,6},{8,9},{9,8},{10,11... | collective-permute-start | bytes 786440 | tf_op jit(solution)/shard_map/ppermute | solution.py:274
  42.8 1.6 %collective-permute-start.6 = (f32[256,256]{1,0:T(8,128)S(1)}, f32[256,256]{1,0:T(8,128)S(1)}, u32[]{:S(2)}, u32[]{:S(2)}) collective-permute-start(f32[256,256]{1,0:T(8,128)S(1)} %get-tuple-element.47), channel_id=1, source_target_pairs={{0,2},{2,0},{4,6},{6,4},{8,10},{10,8},{12,14},{14,12},{16,18},{18,... | collective-permute-start | bytes 786440 | tf_op jit(solution)/shard_map/ppermute | solution.py:274
  42.9 11.6 %collective-permute-start.10 = (f16[512,256]{1,0:T(8,128)(2,1)S(1)}, f16[512,256]{1,0:T(8,128)(2,1)S(1)}, u32[]{:S(2)}, u32[]{:S(2)}) collective-permute-start(f16[512,256]{1,0:T(8,128)(2,1)S(1)} %multiply_convert_fusion.2), channel_id=1, source_target_pairs={{0,1},{1,0},{2,3},{3,2},{4,5},{5,4},{6,7},{7,6},{8,9},{9,8},{10,11... | collective-permute-start | bytes 786440 | tf_op jit(solution)/shard_map/ppermute | solution.py:274
  44.4 10.2 %collective-permute-start.7 = (f32[64,256]{1,0:T(8,128)S(1)}, f32[64,256]{1,0:T(8,128)S(1)}, u32[]{:S(2)}, u32[]{:S(2)}) collective-permute-start(f32[64,256]{1,0:T(8,128)S(1)} %get-tuple-element.52), channel_id=1, source_target_pairs={{0,1},{1,0},{2,3},{3,2},{4,5},{5,4},{6,7},{7,6},{8,9},{9,8},{10,11... | collective-permute-start | bytes 196616 | tf_op jit(solution)/shard_map/ppermute | solution.py:342
  45.9 8.8 %collective-permute-start.8 = (f32[64,256]{1,0:T(8,128)S(1)}, f32[64,256]{1,0:T(8,128)S(1)}, u32[]{:S(2)}, u32[]{:S(2)}) collective-permute-start(f32[64,256]{1,0:T(8,128)S(1)} %get-tuple-element.53), channel_id=1, source_target_pairs={{0,4},{1,5},{2,6},{3,7},{4,0},{5,1},{6,2},{7,3},{8,12},{9,13},{10,... | collective-permute-start | bytes 196616 | tf_op jit(solution)/shard_map/ppermute | solution.py:342
  50.0 5.2 %collective-permute-start.9 = (f32[64,256]{1,0:T(8,128)S(1)}, f32[64,256]{1,0:T(8,128)S(1)}, u32[]{:S(2)}, u32[]{:S(2)}) collective-permute-start(f32[64,256]{1,0:T(8,128)S(1)} %get-tuple-element.54), channel_id=1, source_target_pairs={{0,5},{1,4},{2,7},{3,6},{4,1},{5,0},{6,3},{7,2},{8,13},{9,12},{10,... | collective-permute-start | bytes 196616 | tf_op jit(solution)/shard_map/ppermute | solution.py:342
  55.2 8.2 %collective-permute-start.14 = (f32[64,256]{1,0:T(8,128)S(1)}, f32[64,256]{1,0:T(8,128)S(1)}, u32[]{:S(2)}, u32[]{:S(2)}) collective-permute-start(f32[64,256]{1,0:T(8,128)S(1)} %add_add_fusion.1), channel_id=1, source_target_pairs={{0,24},{2,26},{4,28},{6,30},{8,16},{10,18},{12,20},{14,22},{16,8},... | collective-permute-start | bytes 196616 | tf_op jit(solution)/shard_map/ppermute | solution.py:274
  57.6 11.6 %collective-permute-start.13 = (f32[64,256]{1,0:T(8,128)S(1)}, f32[64,256]{1,0:T(8,128)S(1)}, u32[]{:S(2)}, u32[]{:S(2)}) collective-permute-start(f32[64,256]{1,0:T(8,128)S(1)} %add_add_fusion.1), channel_id=1, source_target_pairs={{0,16},{2,18},{4,20},{6,22},{8,24},{10,26},{12,28},{14,30},{16,0},... | collective-permute-start | bytes 196616 | tf_op jit(solution)/shard_map/ppermute | solution.py:274
  57.6 11.6 %collective-permute-start.12 = (f32[64,256]{1,0:T(8,128)S(1)}, f32[64,256]{1,0:T(8,128)S(1)}, u32[]{:S(2)}, u32[]{:S(2)}) collective-permute-start(f32[64,256]{1,0:T(8,128)S(1)} %add_add_fusion.1), channel_id=1, source_target_pairs={{0,8},{2,10},{4,12},{6,14},{8,0},{10,2},{12,4},{14,6},{16,24},{18,... | collective-permute-start | bytes 196616 | tf_op jit(solution)/shard_map/ppermute | solution.py:274
  59.7 17.6 %collective-permute-start.11 = (f16[512,256]{1,0:T(8,128)(2,1)S(1)}, f16[512,256]{1,0:T(8,128)(2,1)S(1)}, u32[]{:S(2)}, u32[]{:S(2)}) collective-permute-start(f16[512,256]{1,0:T(8,128)(2,1)S(1)} %multiply_convert_fusion.1), channel_id=1, source_target_pairs={{0,16},{2,18},{4,20},{6,22},{8,24},{10,26},{12,28},{14,30},{16,0},... | collective-permute-start | bytes 786440 | tf_op jit(solution)/shard_map/ppermute | solution.py:274
  63.3 14.1 %copy-start = (f32[512,256]{1,0:T(8,128)S(1)}, f32[512,256]{1,0:T(8,128)}, u32[]{:S(2)}) copy-start(f32[512,256]{1,0:T(8,128)} %table.2) | copy-start | bytes 1572868
  63.3 14.1 %copy-start.2 = (f32[512]{0:T(512)S(1)}, f32[512]{0:T(512)}, u32[]{:S(2)}) copy-start(f32[512]{0:T(512)} %param.10) | copy-start | bytes 6148
  63.4 15.5 %copy-start.3 = (f32[400]{0:T(512)S(1)}, f32[400]{0:T(512)}, u32[]{:S(2)}) copy-start(f32[400]{0:T(512)} %param.12) | copy-start | bytes 4804
  69.2 8.2 %collective-permute-start.18 = (f16[512,256]{1,0:T(8,128)(2,1)S(1)}, f16[512,256]{1,0:T(8,128)(2,1)S(1)}, u32[]{:S(2)}, u32[]{:S(2)}) collective-permute-start(f16[512,256]{1,0:T(8,128)(2,1)S(1)} %multiply_convert_fusion), channel_id=1, source_target_pairs={{0,1},{1,0},{2,3},{3,2},{4,5},{5,4},{6,7},{7,6},{8,9},{9,8},{10,11... | collective-permute-start | bytes 786440 | tf_op jit(solution)/shard_map/ppermute | solution.py:274
  70.9 6.3 %collective-permute-start.17 = (f32[64,256]{1,0:T(8,128)S(1)}, f32[64,256]{1,0:T(8,128)S(1)}, u32[]{:S(2)}, u32[]{:S(2)}) collective-permute-start(f32[64,256]{1,0:T(8,128)S(1)} %add_add_fusion), channel_id=1, source_target_pairs={{0,5},{1,4},{2,7},{3,6},{4,1},{5,0},{6,3},{7,2},{8,13},{9,12},{10,... | collective-permute-start | bytes 196616 | tf_op jit(solution)/shard_map/ppermute | solution.py:342
  70.9 6.3 %collective-permute-start.16 = (f32[64,256]{1,0:T(8,128)S(1)}, f32[64,256]{1,0:T(8,128)S(1)}, u32[]{:S(2)}, u32[]{:S(2)}) collective-permute-start(f32[64,256]{1,0:T(8,128)S(1)} %add_add_fusion), channel_id=1, source_target_pairs={{0,4},{1,5},{2,6},{3,7},{4,0},{5,1},{6,2},{7,3},{8,12},{9,13},{10,... | collective-permute-start | bytes 196616 | tf_op jit(solution)/shard_map/ppermute | solution.py:342
  72.8 4.5 %collective-permute-start.15 = (f32[64,256]{1,0:T(8,128)S(1)}, f32[64,256]{1,0:T(8,128)S(1)}, u32[]{:S(2)}, u32[]{:S(2)}) collective-permute-start(f32[64,256]{1,0:T(8,128)S(1)} %add_add_fusion), channel_id=1, source_target_pairs={{0,1},{1,0},{2,3},{3,2},{4,5},{5,4},{6,7},{7,6},{8,9},{9,8},{10,11... | collective-permute-start | bytes 196616 | tf_op jit(solution)/shard_map/ppermute | solution.py:342
  77.3 1.6 %collective-permute-start.19 = (f32[256,256]{1,0:T(8,128)S(1)}, f32[256,256]{1,0:T(8,128)S(1)}, u32[]{:S(2)}, u32[]{:S(2)}) collective-permute-start(f32[256,256]{1,0:T(8,128)S(1)} %pad_maximum_fusion.mine), channel_id=1, source_target_pairs={{0,2},{2,0},{4,6},{6,4},{8,10},{10,8},{12,14},{14,12},{16,18},{18,... | collective-permute-start | bytes 786440 | tf_op jit(solution)/shard_map/ppermute | solution.py:274

commit v6 on v5

--- a/solution.py
+++ b/solution.py
@@ -402,11 +402,12 @@
         )
 
     scale = 2.0 ** -(math.ceil(math.log2(team * slots * 24 / 65504.0)) + 1)
-
-    def narrow(x):
+    plane_scale = 2.0 ** -(math.ceil(math.log2(2 * chips * slots * 18 / 65504.0)) + 1)
+
+    def narrow(x, scale=scale):
         return (x * scale).astype(jnp.float16)
 
-    def widen(x):
+    def widen(x, scale=scale):
         return x.astype(f32) * (1.0 / scale)
 
     def to_chip(x, k):
@@ -424,8 +425,10 @@
     for x in away_received:
         away_total = away_total + x
     away_total = narrow(away_total)
+    chunk_total = narrow(chunk_total, plane_scale)
     chunk_total, away_total, plan = lax.optimization_barrier((chunk_total, away_total, plan))
     terms = [chunk_total] + [exchange(chunk_total, "dom", mask) for mask in range(4, n_dom, 4)]
+    terms = [widen(x, plane_scale) for x in terms]
     returned = exchange(away_total, "dom", pair)
     near_other = scatter("own_other_kernel", 0, rows, n - 1, n, plan, near_grad)
     near_other = [narrow(x) for x in near_other]

time: 81 us -> 82.5 us (1.019); the launches traced: 80.5 us -> 83.8 us
  Pallas kernels: 32.6 us -> 24.4 us
  starting transfers between devices: 28 us -> 34.8 us
  waiting for transfers between devices: 17.9 us -> 22.6 us
    ppermute x14, starting transfers between devices: 18.1 us -> 27.8 us  [exchange(): lax.ppermute(x, axis, [(i, i ^ mask) for i in range(lax.axis_size(axis))])]
    pallas_call x9, Pallas kernels: 31.1 us -> 22.9 us  [call(): pl.pallas_call(kernel, in_specs=[in_smem] * len(scalars) + [in_vmem] * le...]
    ppermute x14, waiting for transfers between devices: 17.4 us -> 21 us  [exchange(): lax.ppermute(x, axis, [(i, i ^ mask) for i in range(lax.axis_size(axis))])]
    ppermute x6, starting transfers between devices: 9.93 us -> 7.04 us  [to_peer(): return lax.ppermute(x, ('dom', 'sub'), pairs)]
    ppermute x6, waiting for transfers between devices: 0.52 us -> 1.54 us  [to_peer(): return lax.ppermute(x, ('dom', 'sub'), pairs)]
  transfers between devices with their start and end apart: 20 -> 20, of which waited for: 7 -> 9; matrix products, arithmetic and copies ran while one was open for 1% -> 1% of each run, Pallas kernels for 22% -> 16%
where the time goes in v6:
time: 82.5 us; the launch traced here: 83.8 us
  starting transfers between devices  34.8 us (42%)
  Pallas kernels  24.4 us (30%)
  waiting for transfers between devices  22.6 us (27%)
  between operations  1.49 us (2%)
    ppermute x14, starting transfers between devices, exchange(): lax.ppermute(x, axis, [(i, i ^ mask) for i in range(lax.axis_size(axis))])  27.8 us
    pallas_call x9, Pallas kernels, call(): pl.pallas_call(kernel, in_specs=[in_smem] * len(scalars) + [in_vmem] * le...  22.9 us
    ppermute x14, waiting for transfers between devices, exchange(): lax.ppermute(x, axis, [(i, i ^ mask) for i in range(lax.axis_size(axis))])  21 us
    ppermute x6, starting transfers between devices, to_peer(): return lax.ppermute(x, ('dom', 'sub'), pairs)  7.04 us
  transfers between devices with their start and end apart: 20, of which 9 were waited for; matrix products, arithmetic and copies ran while one was open for 1% of the time, Pallas kernels for 16%

profile of v6, /device:TPU:0, one launch (start us, length us, event | category | flops | bytes accessed | tf_op | source)
XLA Modules:
  0.0 83.8 jit_solution(15149881933296389996)
XLA Ops:
  1.3 0.8 %ids_kernel.1.refs_0_ = s16[17,3,512]{2,1,0:T(4,128)(2,1)S(1)} custom-call(s32[1,1]{1,0:T(1,128)S(6)} %copy.12.count, s32[1,8192]{1,0:T(1,128)} %bitcast.12, s32[1,8192]{1,0:T(1,128)} %bitcast.13, s32[1,8192]{1,0:T(1,128)} %bitcast.14, s32[1,512]{1,0:T(1,128)} %bitcast.15), custom_call_target="tpu_custom_call" | custom-call | flops 2097152 | bytes 131072 | tf_op jit(solution)/shard_map/ids_kernel/pallas_call | solution.py:311
  2.1 4.1 %collective-permute-start.1 = (s16[17,3,512]{2,1,0:T(4,128)(2,1)S(1)}, s16[17,3,512]{2,1,0:T(4,128)(2,1)S(1)}, u32[]{:S(2)}, u32[]{:S(2)}) collective-permute-start(s16[17,3,512]{2,1,0:T(4,128)(2,1)S(1)} %ids_kernel.1.refs_0_), channel_id=1, source_target_pairs={{0,16},{2,18},{4,20},{6,22},{8,24},{10,26},{12,28},{14,30},{16,0},... | collective-permute-start | bytes 156680 | tf_op jit(solution)/shard_map/ppermute | solution.py:274
  6.2 1.5 %collective-permute-start = (s16[17,3,512]{2,1,0:T(4,128)(2,1)S(1)}, s16[17,3,512]{2,1,0:T(4,128)(2,1)S(1)}, u32[]{:S(2)}, u32[]{:S(2)}) collective-permute-start(s16[17,3,512]{2,1,0:T(4,128)(2,1)S(1)} %ids_kernel.1.refs_0_), channel_id=1, source_target_pairs={{0,1},{1,0},{2,3},{3,2},{4,5},{5,4},{6,7},{7,6},{8,9},{9,8},{10,11... | collective-permute-start | bytes 156680 | tf_op jit(solution)/shard_map/ppermute | solution.py:274
  7.7 1.2 %rows_kernel.1.refs_0_ = bf16[256,512]{1,0:T(8,128)(2,1)S(1)} custom-call(f32[512,256]{1,0:T(8,128)} %table.2), custom_call_target="tpu_custom_call" | custom-call | flops 2097152 | bytes 131072 | tf_op jit(solution)/shard_map/rows_kernel/pallas_call | solution.py:311
  8.9 0.6 collective-permute-start.4
  9.5 0.1 collective-permute-start.3
  9.6 0.4 collective-permute-done.1.refs_2_
  10.0 1.7 %collective-permute-start.2 = (s16[17,3,512]{2,1,0:T(4,128)(2,1)S(1)}, s16[17,3,512]{2,1,0:T(4,128)(2,1)S(1)}, u32[]{:S(2)}, u32[]{:S(2)}) collective-permute-start(s16[17,3,512]{2,1,0:T(4,128)(2,1)S(1)} %collective-permute-done.1.refs_2_), channel_id=1, source_target_pairs={{0,1},{1,0},{2,3},{3,2},{4,5},{5,4},{6,7},{7,6},{8,9},{9,8},{10,11... | collective-permute-start | bytes 156680 | tf_op jit(solution)/shard_map/ppermute | solution.py:274
  11.7 0.1 pad_add_fusion.codes
  11.8 0.0 copy-start.1
  11.8 0.0 collective-permute-done.refs_1_
  11.8 6.2 %collective-permute-done.2.refs_3_ = s16[17,3,512]{2,1,0:T(4,128)(2,1)S(1)} collective-permute-done((s16[17,3,512]{2,1,0:T(4,128)(2,1)S(1)}, s16[17,3,512]{2,1,0:T(4,128)(2,1)S(1)}, u32[]{:S(2)}, u32[]{:S(2)}) %collective-permute-start.2) | collective-permute-done | bytes 52256 | tf_op jit(solution)/shard_map/ppermute | solution.py:274
  18.0 1.5 %plan_kernel.1 = (s32[37]{0:T(128)S(1)}, s32[16,3,512]{2,1,0:T(4,128)S(1)}, s32[4,1,512]{2,1,0:T(1,128)S(1)}) custom-call(s32[3]{0:T(128)S(1)} %pad_add_fusion.codes, s16[17,3,512]{2,1,0:T(4,128)(2,1)S(1)} %ids_kernel.1.refs_0_, s16[17,3,512]{2,1,0:T(4,128)(2,1)S(1)} %collective-permute-done.refs_1_, s16[17,3,512]{2,1,0:T(4,128)(2,1)S(1)} %collective-permute-done.1.refs_2_, ...), custom_call_target="tpu_custom_call" | custom-call | flops 34359738368 | bytes 2097152 | tf_op jit(solution)/shard_map/plan_kernel/pallas_call | solution.py:351
  19.5 3.7 %collective-permute-done.3.refs_2_ = bf16[256,512]{1,0:T(8,128)(2,1)S(1)} collective-permute-done((bf16[256,512]{1,0:T(8,128)(2,1)S(1)}, bf16[256,512]{1,0:T(8,128)(2,1)S(1)}, u32[]{:S(2)}, u32[]{:S(2)}) %collective-permute-start.3) | collective-permute-done | bytes 262176 | tf_op jit(solution)/shard_map/ppermute | solution.py:274
  23.2 1.5 %collective-permute-start.5 = (bf16[256,512]{1,0:T(8,128)(2,1)S(1)}, bf16[256,512]{1,0:T(8,128)(2,1)S(1)}, u32[]{:S(2)}, u32[]{:S(2)}) collective-permute-start(bf16[256,512]{1,0:T(8,128)(2,1)S(1)} %collective-permute-done.3.refs_2_), channel_id=1, source_target_pairs={{0,1},{1,0},{2,3},{3,2},{4,5},{5,4},{6,7},{7,6},{8,9},{9,8},{10,11... | collective-permute-start | bytes 786440 | tf_op jit(solution)/shard_map/ppermute | solution.py:274
  24.7 0.0 collective-permute-done.4.refs_1_
  24.7 0.0 copy-done.1
  24.7 3.3 %near_kernel.1 = (bf16[16,256,512]{2,1,0:T(8,128)(2,1)S(1)}, f32[16,256,512]{2,1,0:T(8,128)S(1)}) custom-call(s32[37]{0:T(128)S(1)} %get-tuple-element.64.plan, s32[16,3,512]{2,1,0:T(4,128)S(1)} %get-tuple-element.39.ids, f32[400,256]{1,0:T(8,128)S(1)} %copy-done.1, bf16[256,512]{1,0:T(8,128)(2,1)S(1)} %rows_kernel.1.refs_0_, ...), custom_call_target="tpu_custom_call" | custom-call | flops 4294967296 | bytes 131072 | tf_op jit(solution)/shard_map/near_kernel/pallas_call | solution.py:311
  28.0 2.4 %collective-permute-done.5.refs_3_ = bf16[256,512]{1,0:T(8,128)(2,1)S(1)} collective-permute-done((bf16[256,512]{1,0:T(8,128)(2,1)S(1)}, bf16[256,512]{1,0:T(8,128)(2,1)S(1)}, u32[]{:S(2)}, u32[]{:S(2)}) %collective-permute-start.5) | collective-permute-done | bytes 262176 | tf_op jit(solution)/shard_map/ppermute | solution.py:274
  30.4 8.2 %edge_kernel.1 = (bf16[16,512,512]{2,1,0:T(8,128)(2,1)S(1)}, bf16[16,512,512]{2,1,0:T(8,128)(2,1)S(1)}, bf16[4,1024,256]{2,1,0:T(8,128)(2,1)S(1)}, f32[512,256]{...) custom-call(s32[3]{0:T(128)S(1)} %pad_add_fusion.codes, ...), custom_call_target="tpu_custom_call" | custom-call | flops 11811160064 | bytes 131072 | tf_op jit(solution)/shard_map/edge_kernel/pallas_call | solution.py:311
  38.5 0.1 collective-permute-start.6
  38.6 0.1 multiply_convert_fusion.2
  38.7 4.1 %collective-permute-start.10 = (f16[512,256]{1,0:T(8,128)(2,1)S(1)}, f16[512,256]{1,0:T(8,128)(2,1)S(1)}, u32[]{:S(2)}, u32[]{:S(2)}) collective-permute-start(f16[512,256]{1,0:T(8,128)(2,1)S(1)} %multiply_convert_fusion.2), channel_id=1, source_target_pairs={{0,1},{1,0},{2,3},{3,2},{4,5},{5,4},{6,7},{7,6},{8,9},{9,8},{10,11... | collective-permute-start | bytes 786440 | tf_op jit(solution)/shard_map/ppermute | solution.py:274
  42.8 0.0 collective-permute-done.6
  42.8 1.5 %collective-permute-start.7 = (f32[64,256]{1,0:T(8,128)S(1)}, f32[64,256]{1,0:T(8,128)S(1)}, u32[]{:S(2)}, u32[]{:S(2)}) collective-permute-start(f32[64,256]{1,0:T(8,128)S(1)} %get-tuple-element.52), channel_id=1, source_target_pairs={{0,1},{1,0},{2,3},{3,2},{4,5},{5,4},{6,7},{7,6},{8,9},{9,8},{10,11... | collective-permute-start | bytes 196616 | tf_op jit(solution)/shard_map/ppermute | solution.py:342
  44.3 1.5 %collective-permute-start.8 = (f32[64,256]{1,0:T(8,128)S(1)}, f32[64,256]{1,0:T(8,128)S(1)}, u32[]{:S(2)}, u32[]{:S(2)}) collective-permute-start(f32[64,256]{1,0:T(8,128)S(1)} %get-tuple-element.53), channel_id=1, source_target_pairs={{0,4},{1,5},{2,6},{3,7},{4,0},{5,1},{6,2},{7,3},{8,12},{9,13},{10,... | collective-permute-start | bytes 196616 | tf_op jit(solution)/shard_map/ppermute | solution.py:342
  45.8 0.6 collective-permute-start.9
  46.4 2.5 %away_kernel.1 = f32[512,256]{1,0:T(8,128)S(1)} custom-call(s32[37]{0:T(128)S(1)} %get-tuple-element.64.plan, s32[16,3,512]{2,1,0:T(4,128)S(1)} %get-tuple-element.39.ids, s32[4,1,512]{2,1,0:T(1,128)S(1)} %get-tuple-element.40.negative_ids, bf16[16,512,512]{2,1,0:T(8,128)(2,1)S(1)} %get-tuple-element.56.grads, ...), custom_call_target="tpu_custom_call" | custom-call | bytes 131072 | tf_op jit(solution)/shard_map/away_kernel/pallas_call | solution.py:311
  48.9 2.4 %collective-permute-done.10 = f16[512,256]{1,0:T(8,128)(2,1)S(1)} collective-permute-done((f16[512,256]{1,0:T(8,128)(2,1)S(1)}, f16[512,256]{1,0:T(8,128)(2,1)S(1)}, u32[]{:S(2)}, u32[]{:S(2)}) %collective-permute-start.10) | collective-permute-done | bytes 262176 | tf_op jit(solution)/shard_map/ppermute | solution.py:274
  51.3 0.1 multiply_convert_fusion.1
  51.4 1.1 %collective-permute-done.7 = f32[64,256]{1,0:T(8,128)S(1)} collective-permute-done((f32[64,256]{1,0:T(8,128)S(1)}, f32[64,256]{1,0:T(8,128)S(1)}, u32[]{:S(2)}, u32[]{:S(2)}) %collective-permute-start.7) | collective-permute-done | bytes 65568 | tf_op jit(solution)/shard_map/ppermute | solution.py:342
  52.5 0.0 collective-permute-done.8
  52.5 0.0 collective-permute-done.9
  52.6 9.3 %collective-permute-start.14 = (f16[64,256]{1,0:T(8,128)(2,1)S(1)}, f16[64,256]{1,0:T(8,128)(2,1)S(1)}, u32[]{:S(2)}, u32[]{:S(2)}) collective-permute-start(f16[64,256]{1,0:T(8,128)(2,1)S(1)} %multiply_convert_fusion.3), channel_id=1, source_target_pairs={{0,24},{2,26},{4,28},{6,30},{8,16},{10,18},{12,20},{14,22},{16,8},... | collective-permute-start | bytes 98312 | tf_op jit(solution)/shard_map/ppermute | solution.py:274
  61.9 0.0 collective-permute-start.13
  61.9 0.6 collective-permute-start.12
  62.5 2.3 %collective-permute-start.11 = (f16[512,256]{1,0:T(8,128)(2,1)S(1)}, f16[512,256]{1,0:T(8,128)(2,1)S(1)}, u32[]{:S(2)}, u32[]{:S(2)}) collective-permute-start(f16[512,256]{1,0:T(8,128)(2,1)S(1)} %multiply_convert_fusion.1), channel_id=1, source_target_pairs={{0,16},{2,18},{4,20},{6,22},{8,24},{10,26},{12,28},{14,30},{16,0},... | collective-permute-start | bytes 786440 | tf_op jit(solution)/shard_map/ppermute | solution.py:274
  64.8 2.1 %own_other_kernel.1 = f32[512,256]{1,0:T(8,128)S(1)} custom-call(s32[37]{0:T(128)S(1)} %get-tuple-element.64.plan, s32[16,3,512]{2,1,0:T(4,128)S(1)} %get-tuple-element.39.ids, s32[4,1,512]{2,1,0:T(1,128)S(1)} %get-tuple-element.40.negative_ids, bf16[16,512,512]{2,1,0:T(8,128)(2,1)S(1)} %get-tuple-element.62.grads, ...), custom_call_target="tpu_custom_call" | custom-call | bytes 131072 | tf_op jit(solution)/shard_map/own_other_kernel/pallas_call | solution.py:311
  66.9 0.0 copy-start
  66.9 0.0 copy-start.2
  66.9 0.0 copy-start.3
  66.9 0.1 multiply_convert_fusion
  67.0 0.0 collective-permute-done.14
  67.0 5.7 %collective-permute-done.13 = f16[64,256]{1,0:T(8,128)(2,1)S(1)} collective-permute-done((f16[64,256]{1,0:T(8,128)(2,1)S(1)}, f16[64,256]{1,0:T(8,128)(2,1)S(1)}, u32[]{:S(2)}, u32[]{:S(2)}) %collective-permute-start.13) | collective-permute-done | bytes 32800 | tf_op jit(solution)/shard_map/ppermute | solution.py:274
  72.6 0.0 collective-permute-done.12
  72.7 1.8 %collective-permute-start.18 = (f16[512,256]{1,0:T(8,128)(2,1)S(1)}, f16[512,256]{1,0:T(8,128)(2,1)S(1)}, u32[]{:S(2)}, u32[]{:S(2)}) collective-permute-start(f16[512,256]{1,0:T(8,128)(2,1)S(1)} %multiply_convert_fusion), channel_id=1, source_target_pairs={{0,1},{1,0},{2,3},{3,2},{4,5},{5,4},{6,7},{7,6},{8,9},{9,8},{10,11... | collective-permute-start | bytes 786440 | tf_op jit(solution)/shard_map/ppermute | solution.py:274
  74.5 0.0 collective-permute-start.17
  74.5 1.7 %collective-permute-start.16 = (f32[64,256]{1,0:T(8,128)S(1)}, f32[64,256]{1,0:T(8,128)S(1)}, u32[]{:S(2)}, u32[]{:S(2)}) collective-permute-start(f32[64,256]{1,0:T(8,128)S(1)} %add_multiply_fusion.1), channel_id=1, source_target_pairs={{0,4},{1,5},{2,6},{3,7},{4,0},{5,1},{6,2},{7,3},{8,12},{9,13},{10,... | collective-permute-start | bytes 196616 | tf_op jit(solution)/shard_map/ppermute | solution.py:342
  76.2 1.8 %collective-permute-start.15 = (f32[64,256]{1,0:T(8,128)S(1)}, f32[64,256]{1,0:T(8,128)S(1)}, u32[]{:S(2)}, u32[]{:S(2)}) collective-permute-start(f32[64,256]{1,0:T(8,128)S(1)} %add_multiply_fusion.1), channel_id=1, source_target_pairs={{0,1},{1,0},{2,3},{3,2},{4,5},{5,4},{6,7},{7,6},{8,9},{9,8},{10,11... | collective-permute-start | bytes 196616 | tf_op jit(solution)/shard_map/ppermute | solution.py:342
  78.0 2.1 %own_kernel.1.own = f32[512,256]{1,0:T(8,128)S(1)} custom-call(s32[37]{0:T(128)S(1)} %get-tuple-element.64.plan, s32[16,3,512]{2,1,0:T(4,128)S(1)} %get-tuple-element.39.ids, s32[4,1,512]{2,1,0:T(1,128)S(1)} %get-tuple-element.40.negative_ids, bf16[16,512,512]{2,1,0:T(8,128)(2,1)S(1)} %get-tuple-element.62.grads, ...), custom_call_target="tpu_custom_call" | custom-call | bytes 131072 | tf_op jit(solution)/shard_map/own_kernel/pallas_call | solution.py:311
  80.1 0.0 collective-permute-done.17
  80.1 0.0 collective-permute-done.16
  80.1 0.4 collective-permute-done.15
  80.5 0.0 collective-permute-done.11
  80.5 0.1 collective-permute-start.19
  80.6 0.0 collective-permute-done.18
  80.6 0.1 add_multiply_fusion.returned
  80.7 0.0 copy-done
  80.7 0.0 copy-done.2
  80.7 1.2 %entity_kernel.1 = (f32[512,256]{1,0:T(8,128)}, f32[1,512]{1,0:T(1,128)}) custom-call(f32[512,256]{1,0:T(8,128)S(1)} %copy-done, f32[1,512]{1,0:T(1,128)S(1)} %bitcast.10, f32[512,256]{1,0:T(8,128)S(1)} %add_multiply_fusion.returned, f32[512,256]{1,0:T(8,128)S(1)} %own_kernel.1.own), custom_call_target="tpu_custom_call" | custom-call | flops 2097152 | bytes 131072 | tf_op jit(solution)/shard_map/entity_kernel/pallas_call | solution.py:311
  81.9 0.3 collective-permute-done.19.theirs
  82.1 0.0 copy-done.3
  82.1 1.6 %relation_kernel.1 = f32[400,256]{1,0:T(8,128)} custom-call(s32[3]{0:T(128)S(1)} %pad_add_fusion.codes, f32[400,256]{1,0:T(8,128)S(1)} %copy-done.1, f32[1,400]{1,0:T(1,128)S(1)} %bitcast.11, f32[256,256]{1,0:T(8,128)S(1)} %pad_maximum_fusion.mine, f32[256,256]{1,0:T(8,128)S(1)} %collective-permute-done.19.theirs), custom_call_target="tpu_custom_call" | custom-call | bytes 131072 | tf_op jit(solution)/shard_map/relation_kernel/pallas_call | solution.py:311
  (4 shorter events, 0.1 us)
Async XLA Ops:
  2.1 7.9 %collective-permute-start.1 = (s16[17,3,512]{2,1,0:T(4,128)(2,1)S(1)}, s16[17,3,512]{2,1,0:T(4,128)(2,1)S(1)}, u32[]{:S(2)}, u32[]{:S(2)}) collective-permute-start(s16[17,3,512]{2,1,0:T(4,128)(2,1)S(1)} %ids_kernel.1.refs_0_), channel_id=1, source_target_pairs={{0,16},{2,18},{4,20},{6,22},{8,24},{10,26},{12,28},{14,30},{16,0},... | collective-permute-start | bytes 156680 | tf_op jit(solution)/shard_map/ppermute | solution.py:274
  6.2 5.6 %collective-permute-start = (s16[17,3,512]{2,1,0:T(4,128)(2,1)S(1)}, s16[17,3,512]{2,1,0:T(4,128)(2,1)S(1)}, u32[]{:S(2)}, u32[]{:S(2)}) collective-permute-start(s16[17,3,512]{2,1,0:T(4,128)(2,1)S(1)} %ids_kernel.1.refs_0_), channel_id=1, source_target_pairs={{0,1},{1,0},{2,3},{3,2},{4,5},{5,4},{6,7},{7,6},{8,9},{9,8},{10,11... | collective-permute-start | bytes 156680 | tf_op jit(solution)/shard_map/ppermute | solution.py:274
  8.9 15.8 %collective-permute-start.4 = (bf16[256,512]{1,0:T(8,128)(2,1)S(1)}, bf16[256,512]{1,0:T(8,128)(2,1)S(1)}, u32[]{:S(2)}, u32[]{:S(2)}) collective-permute-start(bf16[256,512]{1,0:T(8,128)(2,1)S(1)} %rows_kernel.1.refs_0_), channel_id=1, source_target_pairs={{0,1},{1,0},{2,3},{3,2},{4,5},{5,4},{6,7},{7,6},{8,9},{9,8},{10,11... | collective-permute-start | bytes 786440 | tf_op jit(solution)/shard_map/ppermute | solution.py:274
  9.5 13.7 %collective-permute-start.3 = (bf16[256,512]{1,0:T(8,128)(2,1)S(1)}, bf16[256,512]{1,0:T(8,128)(2,1)S(1)}, u32[]{:S(2)}, u32[]{:S(2)}) collective-permute-start(bf16[256,512]{1,0:T(8,128)(2,1)S(1)} %rows_kernel.1.refs_0_), channel_id=1, source_target_pairs={{0,16},{2,18},{4,20},{6,22},{8,24},{10,26},{12,28},{14,30},{16,0},... | collective-permute-start | bytes 786440 | tf_op jit(solution)/shard_map/ppermute | solution.py:274
  10.0 8.0 %collective-permute-start.2 = (s16[17,3,512]{2,1,0:T(4,128)(2,1)S(1)}, s16[17,3,512]{2,1,0:T(4,128)(2,1)S(1)}, u32[]{:S(2)}, u32[]{:S(2)}) collective-permute-start(s16[17,3,512]{2,1,0:T(4,128)(2,1)S(1)} %collective-permute-done.1.refs_2_), channel_id=1, source_target_pairs={{0,1},{1,0},{2,3},{3,2},{4,5},{5,4},{6,7},{7,6},{8,9},{9,8},{10,11... | collective-permute-start | bytes 156680 | tf_op jit(solution)/shard_map/ppermute | solution.py:274
  11.8 12.9 %copy-start.1 = (f32[400,256]{1,0:T(8,128)S(1)}, f32[400,256]{1,0:T(8,128)}, u32[]{:S(2)}) copy-start(f32[400,256]{1,0:T(8,128)} %relations.3) | copy-start | bytes 1228804
  23.2 7.1 %collective-permute-start.5 = (bf16[256,512]{1,0:T(8,128)(2,1)S(1)}, bf16[256,512]{1,0:T(8,128)(2,1)S(1)}, u32[]{:S(2)}, u32[]{:S(2)}) collective-permute-start(bf16[256,512]{1,0:T(8,128)(2,1)S(1)} %collective-permute-done.3.refs_2_), channel_id=1, source_target_pairs={{0,1},{1,0},{2,3},{3,2},{4,5},{5,4},{6,7},{7,6},{8,9},{9,8},{10,11... | collective-permute-start | bytes 786440 | tf_op jit(solution)/shard_map/ppermute | solution.py:274
  38.5 4.2 %collective-permute-start.6 = (f32[256,256]{1,0:T(8,128)S(1)}, f32[256,256]{1,0:T(8,128)S(1)}, u32[]{:S(2)}, u32[]{:S(2)}) collective-permute-start(f32[256,256]{1,0:T(8,128)S(1)} %get-tuple-element.47), channel_id=1, source_target_pairs={{0,2},{2,0},{4,6},{6,4},{8,10},{10,8},{12,14},{14,12},{16,18},{18,... | collective-permute-start | bytes 786440 | tf_op jit(solution)/shard_map/ppermute | solution.py:274
  38.7 12.6 %collective-permute-start.10 = (f16[512,256]{1,0:T(8,128)(2,1)S(1)}, f16[512,256]{1,0:T(8,128)(2,1)S(1)}, u32[]{:S(2)}, u32[]{:S(2)}) collective-permute-start(f16[512,256]{1,0:T(8,128)(2,1)S(1)} %multiply_convert_fusion.2), channel_id=1, source_target_pairs={{0,1},{1,0},{2,3},{3,2},{4,5},{5,4},{6,7},{7,6},{8,9},{9,8},{10,11... | collective-permute-start | bytes 786440 | tf_op jit(solution)/shard_map/ppermute | solution.py:274
  42.8 9.7 %collective-permute-start.7 = (f32[64,256]{1,0:T(8,128)S(1)}, f32[64,256]{1,0:T(8,128)S(1)}, u32[]{:S(2)}, u32[]{:S(2)}) collective-permute-start(f32[64,256]{1,0:T(8,128)S(1)} %get-tuple-element.52), channel_id=1, source_target_pairs={{0,1},{1,0},{2,3},{3,2},{4,5},{5,4},{6,7},{7,6},{8,9},{9,8},{10,11... | collective-permute-start | bytes 196616 | tf_op jit(solution)/shard_map/ppermute | solution.py:342
  44.3 8.3 %collective-permute-start.8 = (f32[64,256]{1,0:T(8,128)S(1)}, f32[64,256]{1,0:T(8,128)S(1)}, u32[]{:S(2)}, u32[]{:S(2)}) collective-permute-start(f32[64,256]{1,0:T(8,128)S(1)} %get-tuple-element.53), channel_id=1, source_target_pairs={{0,4},{1,5},{2,6},{3,7},{4,0},{5,1},{6,2},{7,3},{8,12},{9,13},{10,... | collective-permute-start | bytes 196616 | tf_op jit(solution)/shard_map/ppermute | solution.py:342
  45.8 6.8 %collective-permute-start.9 = (f32[64,256]{1,0:T(8,128)S(1)}, f32[64,256]{1,0:T(8,128)S(1)}, u32[]{:S(2)}, u32[]{:S(2)}) collective-permute-start(f32[64,256]{1,0:T(8,128)S(1)} %get-tuple-element.54), channel_id=1, source_target_pairs={{0,5},{1,4},{2,7},{3,6},{4,1},{5,0},{6,3},{7,2},{8,13},{9,12},{10,... | collective-permute-start | bytes 196616 | tf_op jit(solution)/shard_map/ppermute | solution.py:342
  52.6 14.4 %collective-permute-start.14 = (f16[64,256]{1,0:T(8,128)(2,1)S(1)}, f16[64,256]{1,0:T(8,128)(2,1)S(1)}, u32[]{:S(2)}, u32[]{:S(2)}) collective-permute-start(f16[64,256]{1,0:T(8,128)(2,1)S(1)} %multiply_convert_fusion.3), channel_id=1, source_target_pairs={{0,24},{2,26},{4,28},{6,30},{8,16},{10,18},{12,20},{14,22},{16,8},... | collective-permute-start | bytes 98312 | tf_op jit(solution)/shard_map/ppermute | solution.py:274
  61.9 10.8 %collective-permute-start.13 = (f16[64,256]{1,0:T(8,128)(2,1)S(1)}, f16[64,256]{1,0:T(8,128)(2,1)S(1)}, u32[]{:S(2)}, u32[]{:S(2)}) collective-permute-start(f16[64,256]{1,0:T(8,128)(2,1)S(1)} %multiply_convert_fusion.3), channel_id=1, source_target_pairs={{0,16},{2,18},{4,20},{6,22},{8,24},{10,26},{12,28},{14,30},{16,0},... | collective-permute-start | bytes 98312 | tf_op jit(solution)/shard_map/ppermute | solution.py:274
  61.9 10.8 %collective-permute-start.12 = (f16[64,256]{1,0:T(8,128)(2,1)S(1)}, f16[64,256]{1,0:T(8,128)(2,1)S(1)}, u32[]{:S(2)}, u32[]{:S(2)}) collective-permute-start(f16[64,256]{1,0:T(8,128)(2,1)S(1)} %multiply_convert_fusion.3), channel_id=1, source_target_pairs={{0,8},{2,10},{4,12},{6,14},{8,0},{10,2},{12,4},{14,6},{16,24},{18,... | collective-permute-start | bytes 98312 | tf_op jit(solution)/shard_map/ppermute | solution.py:274
  62.5 18.0 %collective-permute-start.11 = (f16[512,256]{1,0:T(8,128)(2,1)S(1)}, f16[512,256]{1,0:T(8,128)(2,1)S(1)}, u32[]{:S(2)}, u32[]{:S(2)}) collective-permute-start(f16[512,256]{1,0:T(8,128)(2,1)S(1)} %multiply_convert_fusion.1), channel_id=1, source_target_pairs={{0,16},{2,18},{4,20},{6,22},{8,24},{10,26},{12,28},{14,30},{16,0},... | collective-permute-start | bytes 786440 | tf_op jit(solution)/shard_map/ppermute | solution.py:274
  66.9 13.8 %copy-start = (f32[512,256]{1,0:T(8,128)S(1)}, f32[512,256]{1,0:T(8,128)}, u32[]{:S(2)}) copy-start(f32[512,256]{1,0:T(8,128)} %table.2) | copy-start | bytes 1572868
  66.9 13.8 %copy-start.2 = (f32[512]{0:T(512)S(1)}, f32[512]{0:T(512)}, u32[]{:S(2)}) copy-start(f32[512]{0:T(512)} %param.10) | copy-start | bytes 6148
  66.9 15.2 %copy-start.3 = (f32[400]{0:T(512)S(1)}, f32[400]{0:T(512)}, u32[]{:S(2)}) copy-start(f32[400]{0:T(512)} %param.12) | copy-start | bytes 4804
  72.7 8.0 %collective-permute-start.18 = (f16[512,256]{1,0:T(8,128)(2,1)S(1)}, f16[512,256]{1,0:T(8,128)(2,1)S(1)}, u32[]{:S(2)}, u32[]{:S(2)}) collective-permute-start(f16[512,256]{1,0:T(8,128)(2,1)S(1)} %multiply_convert_fusion), channel_id=1, source_target_pairs={{0,1},{1,0},{2,3},{3,2},{4,5},{5,4},{6,7},{7,6},{8,9},{9,8},{10,11... | collective-permute-start | bytes 786440 | tf_op jit(solution)/shard_map/ppermute | solution.py:274
  74.5 5.6 %collective-permute-start.17 = (f32[64,256]{1,0:T(8,128)S(1)}, f32[64,256]{1,0:T(8,128)S(1)}, u32[]{:S(2)}, u32[]{:S(2)}) collective-permute-start(f32[64,256]{1,0:T(8,128)S(1)} %add_multiply_fusion.1), channel_id=1, source_target_pairs={{0,5},{1,4},{2,7},{3,6},{4,1},{5,0},{6,3},{7,2},{8,13},{9,12},{10,... | collective-permute-start | bytes 196616 | tf_op jit(solution)/shard_map/ppermute | solution.py:342
  74.5 5.6 %collective-permute-start.16 = (f32[64,256]{1,0:T(8,128)S(1)}, f32[64,256]{1,0:T(8,128)S(1)}, u32[]{:S(2)}, u32[]{:S(2)}) collective-permute-start(f32[64,256]{1,0:T(8,128)S(1)} %add_multiply_fusion.1), channel_id=1, source_target_pairs={{0,4},{1,5},{2,6},{3,7},{4,0},{5,1},{6,2},{7,3},{8,12},{9,13},{10,... | collective-permute-start | bytes 196616 | tf_op jit(solution)/shard_map/ppermute | solution.py:342
  76.2 4.3 %collective-permute-start.15 = (f32[64,256]{1,0:T(8,128)S(1)}, f32[64,256]{1,0:T(8,128)S(1)}, u32[]{:S(2)}, u32[]{:S(2)}) collective-permute-start(f32[64,256]{1,0:T(8,128)S(1)} %add_multiply_fusion.1), channel_id=1, source_target_pairs={{0,1},{1,0},{2,3},{3,2},{4,5},{5,4},{6,7},{7,6},{8,9},{9,8},{10,11... | collective-permute-start | bytes 196616 | tf_op jit(solution)/shard_map/ppermute | solution.py:342
  80.5 1.6 %collective-permute-start.19 = (f32[256,256]{1,0:T(8,128)S(1)}, f32[256,256]{1,0:T(8,128)S(1)}, u32[]{:S(2)}, u32[]{:S(2)}) collective-permute-start(f32[256,256]{1,0:T(8,128)S(1)} %pad_maximum_fusion.mine), channel_id=1, source_target_pairs={{0,2},{2,0},{4,6},{6,4},{8,10},{10,8},{12,14},{14,12},{16,18},{18,... | collective-permute-start | bytes 786440 | tf_op jit(solution)/shard_map/ppermute | solution.py:274

commit v7 on v6

--- a/solution.py
+++ b/solution.py
@@ -429,12 +429,12 @@
     chunk_total, away_total, plan = lax.optimization_barrier((chunk_total, away_total, plan))
     terms = [chunk_total] + [exchange(chunk_total, "dom", mask) for mask in range(4, n_dom, 4)]
     terms = [widen(x, plane_scale) for x in terms]
-    returned = exchange(away_total, "dom", pair)
     near_other = scatter("own_other_kernel", 0, rows, n - 1, n, plan, near_grad)
     near_other = [narrow(x) for x in near_other]
     while len(terms) > 1:
         terms = [terms[k] + terms[k + 1] for k in range(0, len(terms), 2)]
-    chunk_total, near_other, plan = lax.optimization_barrier((terms[0], near_other, plan))
+    chunk_total, away_total, near_other, plan = lax.optimization_barrier((terms[0], away_total, near_other, plan))
+    returned = exchange(away_total, "dom", pair)
     near_received = [widen(exchange(near_other[k - 1], "sub", k)) for k in range(1, n)]
     mine = jnp.concatenate([chunk_total] + [to_chip(chunk_total, k) for k in range(1, chips)], axis=0)
     (near_sum,) = scatter("own_kernel", 0, 0, 1, n, plan, near_grad)

time: 82.5 us -> 78.7 us (0.954); the launches traced: 83.8 us -> 78.6 us
  starting transfers between devices: 34.8 us -> 29.5 us
  Pallas kernels: 24.4 us -> 28.2 us
  waiting for transfers between devices: 22.6 us -> 19 us
    ppermute x14, starting transfers between devices: 27.8 us -> 21.4 us  [exchange(): lax.ppermute(x, axis, [(i, i ^ mask) for i in range(lax.axis_size(axis))])]
    ppermute x14, waiting for transfers between devices: 21 us -> 15.4 us  [exchange(): lax.ppermute(x, axis, [(i, i ^ mask) for i in range(lax.axis_size(axis))])]
    pallas_call x9, Pallas kernels: 22.9 us -> 26.6 us  [call(): pl.pallas_call(kernel, in_specs=[in_smem] * len(scalars) + [in_vmem] * le...]
    ppermute x6, waiting for transfers between devices: 1.54 us -> 3.65 us  [to_peer(): return lax.ppermute(x, ('dom', 'sub'), pairs)]
    ppermute x6, starting transfers between devices: 7.04 us -> 8.09 us  [to_peer(): return lax.ppermute(x, ('dom', 'sub'), pairs)]
  transfers between devices with their start and end apart: 20 -> 20, of which waited for: 9 -> 8; matrix products, arithmetic and copies ran while one was open for 1% -> 1% of each run, Pallas kernels for 16% -> 20%
where the time goes in v7:
time: 78.7 us; the launch traced here: 78.6 us
  starting transfers between devices  29.5 us (37%)
  Pallas kernels  28.2 us (36%)
  waiting for transfers between devices  19 us (24%)
  between operations  1.49 us (2%)
    pallas_call x9, Pallas kernels, call(): pl.pallas_call(kernel, in_specs=[in_smem] * len(scalars) + [in_vmem] * le...  26.6 us
    ppermute x14, starting transfers between devices, exchange(): lax.ppermute(x, axis, [(i, i ^ mask) for i in range(lax.axis_size(axis))])  21.4 us
    ppermute x14, waiting for transfers between devices, exchange(): lax.ppermute(x, axis, [(i, i ^ mask) for i in range(lax.axis_size(axis))])  15.4 us
    ppermute x6, starting transfers between devices, to_peer(): return lax.ppermute(x, ('dom', 'sub'), pairs)  8.09 us
    ppermute x6, waiting for transfers between devices, to_peer(): return lax.ppermute(x, ('dom', 'sub'), pairs)  3.65 us
  transfers between devices with their start and end apart: 20, of which 8 were waited for; matrix products, arithmetic and copies ran while one was open for 1% of the time, Pallas kernels for 20%

profile of v7, /device:TPU:0, one launch (start us, length us, event | category | flops | bytes accessed | tf_op | source)
XLA Modules:
  0.0 78.6 jit_solution(11569328622657804065)
XLA Ops:
  1.3 0.8 %ids_kernel.1.refs_0_ = s16[17,3,512]{2,1,0:T(4,128)(2,1)S(1)} custom-call(s32[1,1]{1,0:T(1,128)S(6)} %copy.12.count, s32[1,8192]{1,0:T(1,128)} %bitcast.12, s32[1,8192]{1,0:T(1,128)} %bitcast.13, s32[1,8192]{1,0:T(1,128)} %bitcast.14, s32[1,512]{1,0:T(1,128)} %bitcast.15), custom_call_target="tpu_custom_call" | custom-call | flops 2097152 | bytes 131072 | tf_op jit(solution)/shard_map/ids_kernel/pallas_call | solution.py:311
  2.1 4.1 %collective-permute-start.1 = (s16[17,3,512]{2,1,0:T(4,128)(2,1)S(1)}, s16[17,3,512]{2,1,0:T(4,128)(2,1)S(1)}, u32[]{:S(2)}, u32[]{:S(2)}) collective-permute-start(s16[17,3,512]{2,1,0:T(4,128)(2,1)S(1)} %ids_kernel.1.refs_0_), channel_id=1, source_target_pairs={{0,16},{2,18},{4,20},{6,22},{8,24},{10,26},{12,28},{14,30},{16,0},... | collective-permute-start | bytes 156680 | tf_op jit(solution)/shard_map/ppermute | solution.py:274
  6.2 1.5 %collective-permute-start = (s16[17,3,512]{2,1,0:T(4,128)(2,1)S(1)}, s16[17,3,512]{2,1,0:T(4,128)(2,1)S(1)}, u32[]{:S(2)}, u32[]{:S(2)}) collective-permute-start(s16[17,3,512]{2,1,0:T(4,128)(2,1)S(1)} %ids_kernel.1.refs_0_), channel_id=1, source_target_pairs={{0,1},{1,0},{2,3},{3,2},{4,5},{5,4},{6,7},{7,6},{8,9},{9,8},{10,11... | collective-permute-start | bytes 156680 | tf_op jit(solution)/shard_map/ppermute | solution.py:274
  7.7 1.2 %rows_kernel.1.refs_0_ = bf16[256,512]{1,0:T(8,128)(2,1)S(1)} custom-call(f32[512,256]{1,0:T(8,128)} %table.2), custom_call_target="tpu_custom_call" | custom-call | flops 2097152 | bytes 131072 | tf_op jit(solution)/shard_map/rows_kernel/pallas_call | solution.py:311
  8.9 0.6 collective-permute-start.4
  9.5 0.1 collective-permute-start.3
  9.6 0.4 collective-permute-done.1.refs_2_
  10.0 1.7 %collective-permute-start.2 = (s16[17,3,512]{2,1,0:T(4,128)(2,1)S(1)}, s16[17,3,512]{2,1,0:T(4,128)(2,1)S(1)}, u32[]{:S(2)}, u32[]{:S(2)}) collective-permute-start(s16[17,3,512]{2,1,0:T(4,128)(2,1)S(1)} %collective-permute-done.1.refs_2_), channel_id=1, source_target_pairs={{0,1},{1,0},{2,3},{3,2},{4,5},{5,4},{6,7},{7,6},{8,9},{9,8},{10,11... | collective-permute-start | bytes 156680 | tf_op jit(solution)/shard_map/ppermute | solution.py:274
  11.7 0.1 pad_add_fusion.codes
  11.8 0.0 copy-start.1
  11.8 0.0 collective-permute-done.refs_1_
  11.8 6.2 %collective-permute-done.2.refs_3_ = s16[17,3,512]{2,1,0:T(4,128)(2,1)S(1)} collective-permute-done((s16[17,3,512]{2,1,0:T(4,128)(2,1)S(1)}, s16[17,3,512]{2,1,0:T(4,128)(2,1)S(1)}, u32[]{:S(2)}, u32[]{:S(2)}) %collective-permute-start.2) | collective-permute-done | bytes 52256 | tf_op jit(solution)/shard_map/ppermute | solution.py:274
  18.0 1.5 %plan_kernel.1 = (s32[37]{0:T(128)S(1)}, s32[16,3,512]{2,1,0:T(4,128)S(1)}, s32[4,1,512]{2,1,0:T(1,128)S(1)}) custom-call(s32[3]{0:T(128)S(1)} %pad_add_fusion.codes, s16[17,3,512]{2,1,0:T(4,128)(2,1)S(1)} %ids_kernel.1.refs_0_, s16[17,3,512]{2,1,0:T(4,128)(2,1)S(1)} %collective-permute-done.refs_1_, s16[17,3,512]{2,1,0:T(4,128)(2,1)S(1)} %collective-permute-done.1.refs_2_, ...), custom_call_target="tpu_custom_call" | custom-call | flops 34359738368 | bytes 2097152 | tf_op jit(solution)/shard_map/plan_kernel/pallas_call | solution.py:351
  19.5 3.7 %collective-permute-done.3.refs_2_ = bf16[256,512]{1,0:T(8,128)(2,1)S(1)} collective-permute-done((bf16[256,512]{1,0:T(8,128)(2,1)S(1)}, bf16[256,512]{1,0:T(8,128)(2,1)S(1)}, u32[]{:S(2)}, u32[]{:S(2)}) %collective-permute-start.3) | collective-permute-done | bytes 262176 | tf_op jit(solution)/shard_map/ppermute | solution.py:274
  23.2 1.5 %collective-permute-start.5 = (bf16[256,512]{1,0:T(8,128)(2,1)S(1)}, bf16[256,512]{1,0:T(8,128)(2,1)S(1)}, u32[]{:S(2)}, u32[]{:S(2)}) collective-permute-start(bf16[256,512]{1,0:T(8,128)(2,1)S(1)} %collective-permute-done.3.refs_2_), channel_id=1, source_target_pairs={{0,1},{1,0},{2,3},{3,2},{4,5},{5,4},{6,7},{7,6},{8,9},{9,8},{10,11... | collective-permute-start | bytes 786440 | tf_op jit(solution)/shard_map/ppermute | solution.py:274
  24.7 0.0 collective-permute-done.4.refs_1_
  24.7 0.0 copy-done.1
  24.7 4.0 %near_kernel.1 = (bf16[16,256,512]{2,1,0:T(8,128)(2,1)S(1)}, f32[16,256,512]{2,1,0:T(8,128)S(1)}) custom-call(s32[37]{0:T(128)S(1)} %get-tuple-element.66.plan, s32[16,3,512]{2,1,0:T(4,128)S(1)} %get-tuple-element.40.ids, f32[400,256]{1,0:T(8,128)S(1)} %copy-done.1, bf16[256,512]{1,0:T(8,128)(2,1)S(1)} %rows_kernel.1.refs_0_, ...), custom_call_target="tpu_custom_call" | custom-call | flops 4294967296 | bytes 131072 | tf_op jit(solution)/shard_map/near_kernel/pallas_call | solution.py:311
  28.7 1.6 %collective-permute-done.5.refs_3_ = bf16[256,512]{1,0:T(8,128)(2,1)S(1)} collective-permute-done((bf16[256,512]{1,0:T(8,128)(2,1)S(1)}, bf16[256,512]{1,0:T(8,128)(2,1)S(1)}, u32[]{:S(2)}, u32[]{:S(2)}) %collective-permute-start.5) | collective-permute-done | bytes 262176 | tf_op jit(solution)/shard_map/ppermute | solution.py:274
  30.4 9.8 %edge_kernel.1 = (bf16[16,512,512]{2,1,0:T(8,128)(2,1)S(1)}, bf16[16,512,512]{2,1,0:T(8,128)(2,1)S(1)}, bf16[4,1024,256]{2,1,0:T(8,128)(2,1)S(1)}, f32[512,256]{...) custom-call(s32[3]{0:T(128)S(1)} %pad_add_fusion.codes, ...), custom_call_target="tpu_custom_call" | custom-call | flops 11811160064 | bytes 131072 | tf_op jit(solution)/shard_map/edge_kernel/pallas_call | solution.py:311
  40.2 0.1 collective-permute-start.6
  40.2 0.1 multiply_convert_fusion.2
  40.3 4.2 %collective-permute-start.10 = (f16[512,256]{1,0:T(8,128)(2,1)S(1)}, f16[512,256]{1,0:T(8,128)(2,1)S(1)}, u32[]{:S(2)}, u32[]{:S(2)}) collective-permute-start(f16[512,256]{1,0:T(8,128)(2,1)S(1)} %multiply_convert_fusion.2), channel_id=1, source_target_pairs={{0,1},{1,0},{2,3},{3,2},{4,5},{5,4},{6,7},{7,6},{8,9},{9,8},{10,11... | collective-permute-start | bytes 786440 | tf_op jit(solution)/shard_map/ppermute | solution.py:274
  44.5 0.0 collective-permute-done.6
  44.6 1.5 %collective-permute-start.7 = (f32[64,256]{1,0:T(8,128)S(1)}, f32[64,256]{1,0:T(8,128)S(1)}, u32[]{:S(2)}, u32[]{:S(2)}) collective-permute-start(f32[64,256]{1,0:T(8,128)S(1)} %get-tuple-element.53), channel_id=1, source_target_pairs={{0,1},{1,0},{2,3},{3,2},{4,5},{5,4},{6,7},{7,6},{8,9},{9,8},{10,11... | collective-permute-start | bytes 196616 | tf_op jit(solution)/shard_map/ppermute | solution.py:342
  46.0 2.7 %collective-permute-start.8 = (f32[64,256]{1,0:T(8,128)S(1)}, f32[64,256]{1,0:T(8,128)S(1)}, u32[]{:S(2)}, u32[]{:S(2)}) collective-permute-start(f32[64,256]{1,0:T(8,128)S(1)} %get-tuple-element.54), channel_id=1, source_target_pairs={{0,4},{1,5},{2,6},{3,7},{4,0},{5,1},{6,2},{7,3},{8,12},{9,13},{10,... | collective-permute-start | bytes 196616 | tf_op jit(solution)/shard_map/ppermute | solution.py:342
  48.7 0.5 collective-permute-start.9
  49.2 3.0 %away_kernel.1 = f32[512,256]{1,0:T(8,128)S(1)} custom-call(s32[37]{0:T(128)S(1)} %get-tuple-element.66.plan, s32[16,3,512]{2,1,0:T(4,128)S(1)} %get-tuple-element.40.ids, s32[4,1,512]{2,1,0:T(1,128)S(1)} %get-tuple-element.41.negative_ids, bf16[16,512,512]{2,1,0:T(8,128)(2,1)S(1)} %get-tuple-element.57.grads, ...), custom_call_target="tpu_custom_call" | custom-call | bytes 131072 | tf_op jit(solution)/shard_map/away_kernel/pallas_call | solution.py:311
  52.2 0.0 collective-permute-done.10
  52.2 0.1 multiply_convert_fusion.1
  52.3 2.0 %collective-permute-done.7 = f32[64,256]{1,0:T(8,128)S(1)} collective-permute-done((f32[64,256]{1,0:T(8,128)S(1)}, f32[64,256]{1,0:T(8,128)S(1)}, u32[]{:S(2)}, u32[]{:S(2)}) %collective-permute-start.7) | collective-permute-done | bytes 65568 | tf_op jit(solution)/shard_map/ppermute | solution.py:342
  54.3 0.0 collective-permute-done.8
  54.3 0.0 collective-permute-done.9
  54.3 2.0 %collective-permute-start.13 = (f16[64,256]{1,0:T(8,128)(2,1)S(1)}, f16[64,256]{1,0:T(8,128)(2,1)S(1)}, u32[]{:S(2)}, u32[]{:S(2)}) collective-permute-start(f16[64,256]{1,0:T(8,128)(2,1)S(1)} %multiply_convert_fusion.3), channel_id=1, source_target_pairs={{0,24},{2,26},{4,28},{6,30},{8,16},{10,18},{12,20},{14,22},{16,8},... | collective-permute-start | bytes 98312 | tf_op jit(solution)/shard_map/ppermute | solution.py:274
  56.3 0.0 collective-permute-start.12
  56.3 2.5 %collective-permute-start.11 = (f16[64,256]{1,0:T(8,128)(2,1)S(1)}, f16[64,256]{1,0:T(8,128)(2,1)S(1)}, u32[]{:S(2)}, u32[]{:S(2)}) collective-permute-start(f16[64,256]{1,0:T(8,128)(2,1)S(1)} %multiply_convert_fusion.3), channel_id=1, source_target_pairs={{0,8},{2,10},{4,12},{6,14},{8,0},{10,2},{12,4},{14,6},{16,24},{18,... | collective-permute-start | bytes 98312 | tf_op jit(solution)/shard_map/ppermute | solution.py:274
  58.8 2.5 %own_other_kernel.1 = f32[512,256]{1,0:T(8,128)S(1)} custom-call(s32[37]{0:T(128)S(1)} %get-tuple-element.66.plan, s32[16,3,512]{2,1,0:T(4,128)S(1)} %get-tuple-element.40.ids, s32[4,1,512]{2,1,0:T(1,128)S(1)} %get-tuple-element.41.negative_ids, bf16[16,512,512]{2,1,0:T(8,128)(2,1)S(1)} %get-tuple-element.63.grads, ...), custom_call_target="tpu_custom_call" | custom-call | bytes 131072 | tf_op jit(solution)/shard_map/own_other_kernel/pallas_call | solution.py:311
  61.3 0.0 copy-start
  61.3 0.0 copy-start.2
  61.4 0.0 copy-start.3
  61.4 0.1 multiply_convert_fusion
  61.4 0.0 collective-permute-done.13
  61.4 0.0 collective-permute-done.12
  61.5 0.0 collective-permute-done.11
  61.5 1.7 %collective-permute-start.14 = (f16[512,256]{1,0:T(8,128)(2,1)S(1)}, f16[512,256]{1,0:T(8,128)(2,1)S(1)}, u32[]{:S(2)}, u32[]{:S(2)}) collective-permute-start(f16[512,256]{1,0:T(8,128)(2,1)S(1)} %multiply_convert_fusion.1), channel_id=1, source_target_pairs={{0,16},{2,18},{4,20},{6,22},{8,24},{10,26},{12,28},{14,30},{16,0},... | collective-permute-start | bytes 786440 | tf_op jit(solution)/shard_map/ppermute | solution.py:274
  63.2 1.4 %collective-permute-start.18 = (f16[512,256]{1,0:T(8,128)(2,1)S(1)}, f16[512,256]{1,0:T(8,128)(2,1)S(1)}, u32[]{:S(2)}, u32[]{:S(2)}) collective-permute-start(f16[512,256]{1,0:T(8,128)(2,1)S(1)} %multiply_convert_fusion), channel_id=1, source_target_pairs={{0,1},{1,0},{2,3},{3,2},{4,5},{5,4},{6,7},{7,6},{8,9},{9,8},{10,11... | collective-permute-start | bytes 786440 | tf_op jit(solution)/shard_map/ppermute | solution.py:274
  64.6 1.7 %collective-permute-start.17 = (f32[64,256]{1,0:T(8,128)S(1)}, f32[64,256]{1,0:T(8,128)S(1)}, u32[]{:S(2)}, u32[]{:S(2)}) collective-permute-start(f32[64,256]{1,0:T(8,128)S(1)} %add_multiply_fusion.1), channel_id=1, source_target_pairs={{0,5},{1,4},{2,7},{3,6},{4,1},{5,0},{6,3},{7,2},{8,13},{9,12},{10,... | collective-permute-start | bytes 196616 | tf_op jit(solution)/shard_map/ppermute | solution.py:342
  66.3 0.4 collective-permute-start.16
  66.7 1.4 %collective-permute-start.15 = (f32[64,256]{1,0:T(8,128)S(1)}, f32[64,256]{1,0:T(8,128)S(1)}, u32[]{:S(2)}, u32[]{:S(2)}) collective-permute-start(f32[64,256]{1,0:T(8,128)S(1)} %add_multiply_fusion.1), channel_id=1, source_target_pairs={{0,1},{1,0},{2,3},{3,2},{4,5},{5,4},{6,7},{7,6},{8,9},{9,8},{10,11... | collective-permute-start | bytes 196616 | tf_op jit(solution)/shard_map/ppermute | solution.py:342
  68.1 2.5 %own_kernel.1.own = f32[512,256]{1,0:T(8,128)S(1)} custom-call(s32[37]{0:T(128)S(1)} %get-tuple-element.66.plan, s32[16,3,512]{2,1,0:T(4,128)S(1)} %get-tuple-element.40.ids, s32[4,1,512]{2,1,0:T(1,128)S(1)} %get-tuple-element.41.negative_ids, bf16[16,512,512]{2,1,0:T(8,128)(2,1)S(1)} %get-tuple-element.63.grads, ...), custom_call_target="tpu_custom_call" | custom-call | bytes 131072 | tf_op jit(solution)/shard_map/own_kernel/pallas_call | solution.py:311
  70.6 0.0 collective-permute-done.17
  70.6 0.0 collective-permute-done.16
  70.7 1.6 %collective-permute-done.15 = f32[64,256]{1,0:T(8,128)S(1)} collective-permute-done((f32[64,256]{1,0:T(8,128)S(1)}, f32[64,256]{1,0:T(8,128)S(1)}, u32[]{:S(2)}, u32[]{:S(2)}) %collective-permute-start.15) | collective-permute-done | bytes 65568 | tf_op jit(solution)/shard_map/ppermute | solution.py:342
  72.3 3.2 %collective-permute-done.14 = f16[512,256]{1,0:T(8,128)(2,1)S(1)} collective-permute-done((f16[512,256]{1,0:T(8,128)(2,1)S(1)}, f16[512,256]{1,0:T(8,128)(2,1)S(1)}, u32[]{:S(2)}, u32[]{:S(2)}) %collective-permute-start.14) | collective-permute-done | bytes 262176 | tf_op jit(solution)/shard_map/ppermute | solution.py:274
  75.5 0.0 collective-permute-start.19
  75.5 0.0 collective-permute-done.18
  75.5 0.1 add_multiply_fusion.returned
  75.5 0.0 copy-done
  75.6 0.0 copy-done.2
  75.6 1.2 %entity_kernel.1 = (f32[512,256]{1,0:T(8,128)}, f32[1,512]{1,0:T(1,128)}) custom-call(f32[512,256]{1,0:T(8,128)S(1)} %copy-done, f32[1,512]{1,0:T(1,128)S(1)} %bitcast.10, f32[512,256]{1,0:T(8,128)S(1)} %add_multiply_fusion.returned, f32[512,256]{1,0:T(8,128)S(1)} %own_kernel.1.own), custom_call_target="tpu_custom_call" | custom-call | flops 2097152 | bytes 131072 | tf_op jit(solution)/shard_map/entity_kernel/pallas_call | solution.py:311
  76.7 0.3 collective-permute-done.19.theirs
  77.0 0.0 copy-done.3
  77.0 1.6 %relation_kernel.1 = f32[400,256]{1,0:T(8,128)} custom-call(s32[3]{0:T(128)S(1)} %pad_add_fusion.codes, f32[400,256]{1,0:T(8,128)S(1)} %copy-done.1, f32[1,400]{1,0:T(1,128)S(1)} %bitcast.11, f32[256,256]{1,0:T(8,128)S(1)} %pad_maximum_fusion.mine, f32[256,256]{1,0:T(8,128)S(1)} %collective-permute-done.19.theirs), custom_call_target="tpu_custom_call" | custom-call | bytes 131072 | tf_op jit(solution)/shard_map/relation_kernel/pallas_call | solution.py:311
  (4 shorter events, 0.1 us)
Async XLA Ops:
  2.1 7.9 %collective-permute-start.1 = (s16[17,3,512]{2,1,0:T(4,128)(2,1)S(1)}, s16[17,3,512]{2,1,0:T(4,128)(2,1)S(1)}, u32[]{:S(2)}, u32[]{:S(2)}) collective-permute-start(s16[17,3,512]{2,1,0:T(4,128)(2,1)S(1)} %ids_kernel.1.refs_0_), channel_id=1, source_target_pairs={{0,16},{2,18},{4,20},{6,22},{8,24},{10,26},{12,28},{14,30},{16,0},... | collective-permute-start | bytes 156680 | tf_op jit(solution)/shard_map/ppermute | solution.py:274
  6.2 5.6 %collective-permute-start = (s16[17,3,512]{2,1,0:T(4,128)(2,1)S(1)}, s16[17,3,512]{2,1,0:T(4,128)(2,1)S(1)}, u32[]{:S(2)}, u32[]{:S(2)}) collective-permute-start(s16[17,3,512]{2,1,0:T(4,128)(2,1)S(1)} %ids_kernel.1.refs_0_), channel_id=1, source_target_pairs={{0,1},{1,0},{2,3},{3,2},{4,5},{5,4},{6,7},{7,6},{8,9},{9,8},{10,11... | collective-permute-start | bytes 156680 | tf_op jit(solution)/shard_map/ppermute | solution.py:274
  8.9 15.8 %collective-permute-start.4 = (bf16[256,512]{1,0:T(8,128)(2,1)S(1)}, bf16[256,512]{1,0:T(8,128)(2,1)S(1)}, u32[]{:S(2)}, u32[]{:S(2)}) collective-permute-start(bf16[256,512]{1,0:T(8,128)(2,1)S(1)} %rows_kernel.1.refs_0_), channel_id=1, source_target_pairs={{0,1},{1,0},{2,3},{3,2},{4,5},{5,4},{6,7},{7,6},{8,9},{9,8},{10,11... | collective-permute-start | bytes 786440 | tf_op jit(solution)/shard_map/ppermute | solution.py:274
  9.5 13.7 %collective-permute-start.3 = (bf16[256,512]{1,0:T(8,128)(2,1)S(1)}, bf16[256,512]{1,0:T(8,128)(2,1)S(1)}, u32[]{:S(2)}, u32[]{:S(2)}) collective-permute-start(bf16[256,512]{1,0:T(8,128)(2,1)S(1)} %rows_kernel.1.refs_0_), channel_id=1, source_target_pairs={{0,16},{2,18},{4,20},{6,22},{8,24},{10,26},{12,28},{14,30},{16,0},... | collective-permute-start | bytes 786440 | tf_op jit(solution)/shard_map/ppermute | solution.py:274
  10.0 8.0 %collective-permute-start.2 = (s16[17,3,512]{2,1,0:T(4,128)(2,1)S(1)}, s16[17,3,512]{2,1,0:T(4,128)(2,1)S(1)}, u32[]{:S(2)}, u32[]{:S(2)}) collective-permute-start(s16[17,3,512]{2,1,0:T(4,128)(2,1)S(1)} %collective-permute-done.1.refs_2_), channel_id=1, source_target_pairs={{0,1},{1,0},{2,3},{3,2},{4,5},{5,4},{6,7},{7,6},{8,9},{9,8},{10,11... | collective-permute-start | bytes 156680 | tf_op jit(solution)/shard_map/ppermute | solution.py:274
  11.8 12.9 %copy-start.1 = (f32[400,256]{1,0:T(8,128)S(1)}, f32[400,256]{1,0:T(8,128)}, u32[]{:S(2)}) copy-start(f32[400,256]{1,0:T(8,128)} %relations.3) | copy-start | bytes 1228804
  23.2 7.1 %collective-permute-start.5 = (bf16[256,512]{1,0:T(8,128)(2,1)S(1)}, bf16[256,512]{1,0:T(8,128)(2,1)S(1)}, u32[]{:S(2)}, u32[]{:S(2)}) collective-permute-start(bf16[256,512]{1,0:T(8,128)(2,1)S(1)} %collective-permute-done.3.refs_2_), channel_id=1, source_target_pairs={{0,1},{1,0},{2,3},{3,2},{4,5},{5,4},{6,7},{7,6},{8,9},{9,8},{10,11... | collective-permute-start | bytes 786440 | tf_op jit(solution)/shard_map/ppermute | solution.py:274
  40.2 4.4 %collective-permute-start.6 = (f32[256,256]{1,0:T(8,128)S(1)}, f32[256,256]{1,0:T(8,128)S(1)}, u32[]{:S(2)}, u32[]{:S(2)}) collective-permute-start(f32[256,256]{1,0:T(8,128)S(1)} %get-tuple-element.48), channel_id=1, source_target_pairs={{0,2},{2,0},{4,6},{6,4},{8,10},{10,8},{12,14},{14,12},{16,18},{18,... | collective-permute-start | bytes 786440 | tf_op jit(solution)/shard_map/ppermute | solution.py:274
  40.3 11.9 %collective-permute-start.10 = (f16[512,256]{1,0:T(8,128)(2,1)S(1)}, f16[512,256]{1,0:T(8,128)(2,1)S(1)}, u32[]{:S(2)}, u32[]{:S(2)}) collective-permute-start(f16[512,256]{1,0:T(8,128)(2,1)S(1)} %multiply_convert_fusion.2), channel_id=1, source_target_pairs={{0,1},{1,0},{2,3},{3,2},{4,5},{5,4},{6,7},{7,6},{8,9},{9,8},{10,11... | collective-permute-start | bytes 786440 | tf_op jit(solution)/shard_map/ppermute | solution.py:274
  44.6 9.7 %collective-permute-start.7 = (f32[64,256]{1,0:T(8,128)S(1)}, f32[64,256]{1,0:T(8,128)S(1)}, u32[]{:S(2)}, u32[]{:S(2)}) collective-permute-start(f32[64,256]{1,0:T(8,128)S(1)} %get-tuple-element.53), channel_id=1, source_target_pairs={{0,1},{1,0},{2,3},{3,2},{4,5},{5,4},{6,7},{7,6},{8,9},{9,8},{10,11... | collective-permute-start | bytes 196616 | tf_op jit(solution)/shard_map/ppermute | solution.py:342
  46.0 8.3 %collective-permute-start.8 = (f32[64,256]{1,0:T(8,128)S(1)}, f32[64,256]{1,0:T(8,128)S(1)}, u32[]{:S(2)}, u32[]{:S(2)}) collective-permute-start(f32[64,256]{1,0:T(8,128)S(1)} %get-tuple-element.54), channel_id=1, source_target_pairs={{0,4},{1,5},{2,6},{3,7},{4,0},{5,1},{6,2},{7,3},{8,12},{9,13},{10,... | collective-permute-start | bytes 196616 | tf_op jit(solution)/shard_map/ppermute | solution.py:342
  48.7 5.6 %collective-permute-start.9 = (f32[64,256]{1,0:T(8,128)S(1)}, f32[64,256]{1,0:T(8,128)S(1)}, u32[]{:S(2)}, u32[]{:S(2)}) collective-permute-start(f32[64,256]{1,0:T(8,128)S(1)} %get-tuple-element.55), channel_id=1, source_target_pairs={{0,5},{1,4},{2,7},{3,6},{4,1},{5,0},{6,3},{7,2},{8,13},{9,12},{10,... | collective-permute-start | bytes 196616 | tf_op jit(solution)/shard_map/ppermute | solution.py:342
  54.3 7.1 %collective-permute-start.13 = (f16[64,256]{1,0:T(8,128)(2,1)S(1)}, f16[64,256]{1,0:T(8,128)(2,1)S(1)}, u32[]{:S(2)}, u32[]{:S(2)}) collective-permute-start(f16[64,256]{1,0:T(8,128)(2,1)S(1)} %multiply_convert_fusion.3), channel_id=1, source_target_pairs={{0,24},{2,26},{4,28},{6,30},{8,16},{10,18},{12,20},{14,22},{16,8},... | collective-permute-start | bytes 98312 | tf_op jit(solution)/shard_map/ppermute | solution.py:274
  56.3 5.1 %collective-permute-start.12 = (f16[64,256]{1,0:T(8,128)(2,1)S(1)}, f16[64,256]{1,0:T(8,128)(2,1)S(1)}, u32[]{:S(2)}, u32[]{:S(2)}) collective-permute-start(f16[64,256]{1,0:T(8,128)(2,1)S(1)} %multiply_convert_fusion.3), channel_id=1, source_target_pairs={{0,16},{2,18},{4,20},{6,22},{8,24},{10,26},{12,28},{14,30},{16,0},... | collective-permute-start | bytes 98312 | tf_op jit(solution)/shard_map/ppermute | solution.py:274
  56.3 5.2 %collective-permute-start.11 = (f16[64,256]{1,0:T(8,128)(2,1)S(1)}, f16[64,256]{1,0:T(8,128)(2,1)S(1)}, u32[]{:S(2)}, u32[]{:S(2)}) collective-permute-start(f16[64,256]{1,0:T(8,128)(2,1)S(1)} %multiply_convert_fusion.3), channel_id=1, source_target_pairs={{0,8},{2,10},{4,12},{6,14},{8,0},{10,2},{12,4},{14,6},{16,24},{18,... | collective-permute-start | bytes 98312 | tf_op jit(solution)/shard_map/ppermute | solution.py:274
  61.3 14.2 %copy-start = (f32[512,256]{1,0:T(8,128)S(1)}, f32[512,256]{1,0:T(8,128)}, u32[]{:S(2)}) copy-start(f32[512,256]{1,0:T(8,128)} %table.2) | copy-start | bytes 1572868
  61.3 14.2 %copy-start.2 = (f32[512]{0:T(512)S(1)}, f32[512]{0:T(512)}, u32[]{:S(2)}) copy-start(f32[512]{0:T(512)} %param.10) | copy-start | bytes 6148
  61.4 15.6 %copy-start.3 = (f32[400]{0:T(512)S(1)}, f32[400]{0:T(512)}, u32[]{:S(2)}) copy-start(f32[400]{0:T(512)} %param.12) | copy-start | bytes 4804
  61.5 14.0 %collective-permute-start.14 = (f16[512,256]{1,0:T(8,128)(2,1)S(1)}, f16[512,256]{1,0:T(8,128)(2,1)S(1)}, u32[]{:S(2)}, u32[]{:S(2)}) collective-permute-start(f16[512,256]{1,0:T(8,128)(2,1)S(1)} %multiply_convert_fusion.1), channel_id=1, source_target_pairs={{0,16},{2,18},{4,20},{6,22},{8,24},{10,26},{12,28},{14,30},{16,0},... | collective-permute-start | bytes 786440 | tf_op jit(solution)/shard_map/ppermute | solution.py:274
  63.2 12.2 %collective-permute-start.18 = (f16[512,256]{1,0:T(8,128)(2,1)S(1)}, f16[512,256]{1,0:T(8,128)(2,1)S(1)}, u32[]{:S(2)}, u32[]{:S(2)}) collective-permute-start(f16[512,256]{1,0:T(8,128)(2,1)S(1)} %multiply_convert_fusion), channel_id=1, source_target_pairs={{0,1},{1,0},{2,3},{3,2},{4,5},{5,4},{6,7},{7,6},{8,9},{9,8},{10,11... | collective-permute-start | bytes 786440 | tf_op jit(solution)/shard_map/ppermute | solution.py:274
  64.6 6.0 %collective-permute-start.17 = (f32[64,256]{1,0:T(8,128)S(1)}, f32[64,256]{1,0:T(8,128)S(1)}, u32[]{:S(2)}, u32[]{:S(2)}) collective-permute-start(f32[64,256]{1,0:T(8,128)S(1)} %add_multiply_fusion.1), channel_id=1, source_target_pairs={{0,5},{1,4},{2,7},{3,6},{4,1},{5,0},{6,3},{7,2},{8,13},{9,12},{10,... | collective-permute-start | bytes 196616 | tf_op jit(solution)/shard_map/ppermute | solution.py:342
  66.3 4.4 %collective-permute-start.16 = (f32[64,256]{1,0:T(8,128)S(1)}, f32[64,256]{1,0:T(8,128)S(1)}, u32[]{:S(2)}, u32[]{:S(2)}) collective-permute-start(f32[64,256]{1,0:T(8,128)S(1)} %add_multiply_fusion.1), channel_id=1, source_target_pairs={{0,4},{1,5},{2,6},{3,7},{4,0},{5,1},{6,2},{7,3},{8,12},{9,13},{10,... | collective-permute-start | bytes 196616 | tf_op jit(solution)/shard_map/ppermute | solution.py:342
  66.7 5.6 %collective-permute-start.15 = (f32[64,256]{1,0:T(8,128)S(1)}, f32[64,256]{1,0:T(8,128)S(1)}, u32[]{:S(2)}, u32[]{:S(2)}) collective-permute-start(f32[64,256]{1,0:T(8,128)S(1)} %add_multiply_fusion.1), channel_id=1, source_target_pairs={{0,1},{1,0},{2,3},{3,2},{4,5},{5,4},{6,7},{7,6},{8,9},{9,8},{10,11... | collective-permute-start | bytes 196616 | tf_op jit(solution)/shard_map/ppermute | solution.py:342
  75.5 1.5 %collective-permute-start.19 = (f32[256,256]{1,0:T(8,128)S(1)}, f32[256,256]{1,0:T(8,128)S(1)}, u32[]{:S(2)}, u32[]{:S(2)}) collective-permute-start(f32[256,256]{1,0:T(8,128)S(1)} %pad_maximum_fusion.mine), channel_id=1, source_target_pairs={{0,2},{2,0},{4,6},{6,4},{8,10},{10,8},{12,14},{14,12},{16,18},{18,... | collective-permute-start | bytes 786440 | tf_op jit(solution)/shard_map/ppermute | solution.py:274

commit v8 on v7

--- a/solution.py
+++ b/solution.py
@@ -416,21 +416,21 @@
     other_core = exchange(relation_part[chips], "dom", 1)
     partial = [relation_part[k] + other_core[k * chunk : (k + 1) * chunk] for k in range(chips)]
     away_other = [narrow(x) for x in away_other]
-    away_received = [widen(exchange(away_other[k - 1], "sub", k)) for k in range(1, n)]
-    partial, plan = lax.optimization_barrier((partial, plan))
+    partial, plan, away_other = lax.optimization_barrier((partial, plan, away_other))
     chunk_total = partial[0]
     for k in range(1, chips):
         chunk_total = chunk_total + to_chip(partial[k], k)
+    away_received = [widen(exchange(away_other[k - 1], "sub", k)) for k in range(1, n)]
     (away_total,) = scatter("away_kernel", 1, 0, 1, 0, plan, away_grad)
-    for x in away_received:
-        away_total = away_total + x
-    away_total = narrow(away_total)
     chunk_total = narrow(chunk_total, plane_scale)
     chunk_total, away_total, plan = lax.optimization_barrier((chunk_total, away_total, plan))
     terms = [chunk_total] + [exchange(chunk_total, "dom", mask) for mask in range(4, n_dom, 4)]
     terms = [widen(x, plane_scale) for x in terms]
     near_other = scatter("own_other_kernel", 0, rows, n - 1, n, plan, near_grad)
     near_other = [narrow(x) for x in near_other]
+    for x in away_received:
+        away_total = away_total + x
+    away_total = narrow(away_total)
     while len(terms) > 1:
         terms = [terms[k] + terms[k + 1] for k in range(0, len(terms), 2)]
     chunk_total, away_total, near_other, plan = lax.optimization_barrier((terms[0], away_total, near_other, plan))

time: 78.7 us -> 79.8 us (1.014); the launches traced: 78.6 us -> 80.8 us
  starting transfers between devices: 29.5 us -> 30.9 us
  waiting for transfers between devices: 19 us -> 19.8 us
    ppermute x14, starting transfers between devices: 21.4 us -> 23.3 us  [exchange(): lax.ppermute(x, axis, [(i, i ^ mask) for i in range(lax.axis_size(axis))])]
    ppermute x14, waiting for transfers between devices: 15.4 us -> 17.1 us  [exchange(): lax.ppermute(x, axis, [(i, i ^ mask) for i in range(lax.axis_size(axis))])]
    ppermute x6, waiting for transfers between devices: 3.65 us -> 2.71 us  [to_peer(): return lax.ppermute(x, ('dom', 'sub'), pairs)]
  transfers between devices with their start and end apart: 20 -> 20, of which waited for: 8 -> 10; matrix products, arithmetic and copies ran while one was open for 1% -> 0% of each run, Pallas kernels for 20% -> 20%
where the time goes in v8:
time: 79.8 us; the launch traced here: 80.8 us
  starting transfers between devices  30.9 us (39%)
  Pallas kernels  28.2 us (35%)
  waiting for transfers between devices  19.8 us (25%)
  between operations  1.49 us (2%)
    pallas_call x9, Pallas kernels, call(): pl.pallas_call(kernel, in_specs=[in_smem] * len(scalars) + [in_vmem] * le...  26.6 us
    ppermute x14, starting transfers between devices, exchange(): lax.ppermute(x, axis, [(i, i ^ mask) for i in range(lax.axis_size(axis))])  23.3 us
    ppermute x14, waiting for transfers between devices, exchange(): lax.ppermute(x, axis, [(i, i ^ mask) for i in range(lax.axis_size(axis))])  17.1 us
    ppermute x6, starting transfers between devices, to_peer(): return lax.ppermute(x, ('dom', 'sub'), pairs)  7.6 us
    ppermute x6, waiting for transfers between devices, to_peer(): return lax.ppermute(x, ('dom', 'sub'), pairs)  2.71 us
  transfers between devices with their start and end apart: 20, of which 10 were waited for; matrix products, arithmetic and copies ran while one was open for 0% of the time, Pallas kernels for 20%

profile of v8, /device:TPU:0, one launch (start us, length us, event | category | flops | bytes accessed | tf_op | source)
XLA Modules:
  0.0 80.8 jit_solution(1221999753723071754)
XLA Ops:
  1.3 0.8 %ids_kernel.1.refs_0_ = s16[17,3,512]{2,1,0:T(4,128)(2,1)S(1)} custom-call(s32[1,1]{1,0:T(1,128)S(6)} %copy.12.count, s32[1,8192]{1,0:T(1,128)} %bitcast.12, s32[1,8192]{1,0:T(1,128)} %bitcast.13, s32[1,8192]{1,0:T(1,128)} %bitcast.14, s32[1,512]{1,0:T(1,128)} %bitcast.15), custom_call_target="tpu_custom_call" | custom-call | flops 2097152 | bytes 131072 | tf_op jit(solution)/shard_map/ids_kernel/pallas_call | solution.py:311
  2.1 4.1 %collective-permute-start.1 = (s16[17,3,512]{2,1,0:T(4,128)(2,1)S(1)}, s16[17,3,512]{2,1,0:T(4,128)(2,1)S(1)}, u32[]{:S(2)}, u32[]{:S(2)}) collective-permute-start(s16[17,3,512]{2,1,0:T(4,128)(2,1)S(1)} %ids_kernel.1.refs_0_), channel_id=1, source_target_pairs={{0,16},{2,18},{4,20},{6,22},{8,24},{10,26},{12,28},{14,30},{16,0},... | collective-permute-start | bytes 156680 | tf_op jit(solution)/shard_map/ppermute | solution.py:274
  6.2 1.5 %collective-permute-start = (s16[17,3,512]{2,1,0:T(4,128)(2,1)S(1)}, s16[17,3,512]{2,1,0:T(4,128)(2,1)S(1)}, u32[]{:S(2)}, u32[]{:S(2)}) collective-permute-start(s16[17,3,512]{2,1,0:T(4,128)(2,1)S(1)} %ids_kernel.1.refs_0_), channel_id=1, source_target_pairs={{0,1},{1,0},{2,3},{3,2},{4,5},{5,4},{6,7},{7,6},{8,9},{9,8},{10,11... | collective-permute-start | bytes 156680 | tf_op jit(solution)/shard_map/ppermute | solution.py:274
  7.7 1.2 %rows_kernel.1.refs_0_ = bf16[256,512]{1,0:T(8,128)(2,1)S(1)} custom-call(f32[512,256]{1,0:T(8,128)} %table.2), custom_call_target="tpu_custom_call" | custom-call | flops 2097152 | bytes 131072 | tf_op jit(solution)/shard_map/rows_kernel/pallas_call | solution.py:311
  8.9 0.6 collective-permute-start.4
  9.5 0.1 collective-permute-start.3
  9.6 0.4 collective-permute-done.1.refs_2_
  10.0 1.7 %collective-permute-start.2 = (s16[17,3,512]{2,1,0:T(4,128)(2,1)S(1)}, s16[17,3,512]{2,1,0:T(4,128)(2,1)S(1)}, u32[]{:S(2)}, u32[]{:S(2)}) collective-permute-start(s16[17,3,512]{2,1,0:T(4,128)(2,1)S(1)} %collective-permute-done.1.refs_2_), channel_id=1, source_target_pairs={{0,1},{1,0},{2,3},{3,2},{4,5},{5,4},{6,7},{7,6},{8,9},{9,8},{10,11... | collective-permute-start | bytes 156680 | tf_op jit(solution)/shard_map/ppermute | solution.py:274
  11.7 0.1 pad_add_fusion.codes
  11.8 0.0 copy-start.1
  11.8 0.0 collective-permute-done.refs_1_
  11.8 6.2 %collective-permute-done.2.refs_3_ = s16[17,3,512]{2,1,0:T(4,128)(2,1)S(1)} collective-permute-done((s16[17,3,512]{2,1,0:T(4,128)(2,1)S(1)}, s16[17,3,512]{2,1,0:T(4,128)(2,1)S(1)}, u32[]{:S(2)}, u32[]{:S(2)}) %collective-permute-start.2) | collective-permute-done | bytes 52256 | tf_op jit(solution)/shard_map/ppermute | solution.py:274
  18.0 1.5 %plan_kernel.1 = (s32[37]{0:T(128)S(1)}, s32[16,3,512]{2,1,0:T(4,128)S(1)}, s32[4,1,512]{2,1,0:T(1,128)S(1)}) custom-call(s32[3]{0:T(128)S(1)} %pad_add_fusion.codes, s16[17,3,512]{2,1,0:T(4,128)(2,1)S(1)} %ids_kernel.1.refs_0_, s16[17,3,512]{2,1,0:T(4,128)(2,1)S(1)} %collective-permute-done.refs_1_, s16[17,3,512]{2,1,0:T(4,128)(2,1)S(1)} %collective-permute-done.1.refs_2_, ...), custom_call_target="tpu_custom_call" | custom-call | flops 34359738368 | bytes 2097152 | tf_op jit(solution)/shard_map/plan_kernel/pallas_call | solution.py:351
  19.5 3.7 %collective-permute-done.3.refs_2_ = bf16[256,512]{1,0:T(8,128)(2,1)S(1)} collective-permute-done((bf16[256,512]{1,0:T(8,128)(2,1)S(1)}, bf16[256,512]{1,0:T(8,128)(2,1)S(1)}, u32[]{:S(2)}, u32[]{:S(2)}) %collective-permute-start.3) | collective-permute-done | bytes 262176 | tf_op jit(solution)/shard_map/ppermute | solution.py:274
  23.2 1.5 %collective-permute-start.5 = (bf16[256,512]{1,0:T(8,128)(2,1)S(1)}, bf16[256,512]{1,0:T(8,128)(2,1)S(1)}, u32[]{:S(2)}, u32[]{:S(2)}) collective-permute-start(bf16[256,512]{1,0:T(8,128)(2,1)S(1)} %collective-permute-done.3.refs_2_), channel_id=1, source_target_pairs={{0,1},{1,0},{2,3},{3,2},{4,5},{5,4},{6,7},{7,6},{8,9},{9,8},{10,11... | collective-permute-start | bytes 786440 | tf_op jit(solution)/shard_map/ppermute | solution.py:274
  24.7 0.0 collective-permute-done.4.refs_1_
  24.7 0.0 copy-done.1
  24.7 4.0 %near_kernel.1 = (bf16[16,256,512]{2,1,0:T(8,128)(2,1)S(1)}, f32[16,256,512]{2,1,0:T(8,128)S(1)}) custom-call(s32[37]{0:T(128)S(1)} %get-tuple-element.68.plan, s32[16,3,512]{2,1,0:T(4,128)S(1)} %get-tuple-element.41.ids, f32[400,256]{1,0:T(8,128)S(1)} %copy-done.1, bf16[256,512]{1,0:T(8,128)(2,1)S(1)} %rows_kernel.1.refs_0_, ...), custom_call_target="tpu_custom_call" | custom-call | flops 4294967296 | bytes 131072 | tf_op jit(solution)/shard_map/near_kernel/pallas_call | solution.py:311
  28.7 1.6 %collective-permute-done.5.refs_3_ = bf16[256,512]{1,0:T(8,128)(2,1)S(1)} collective-permute-done((bf16[256,512]{1,0:T(8,128)(2,1)S(1)}, bf16[256,512]{1,0:T(8,128)(2,1)S(1)}, u32[]{:S(2)}, u32[]{:S(2)}) %collective-permute-start.5) | collective-permute-done | bytes 262176 | tf_op jit(solution)/shard_map/ppermute | solution.py:274
  30.4 9.8 %edge_kernel.1 = (bf16[16,512,512]{2,1,0:T(8,128)(2,1)S(1)}, bf16[16,512,512]{2,1,0:T(8,128)(2,1)S(1)}, bf16[4,1024,256]{2,1,0:T(8,128)(2,1)S(1)}, f32[512,256]{...) custom-call(s32[3]{0:T(128)S(1)} %pad_add_fusion.codes, ...), custom_call_target="tpu_custom_call" | custom-call | flops 11811160064 | bytes 131072 | tf_op jit(solution)/shard_map/edge_kernel/pallas_call | solution.py:311
  40.2 0.1 collective-permute-start.6
  40.2 0.1 multiply_convert_fusion.2
  40.3 1.5 %collective-permute-done.6 = f32[256,256]{1,0:T(8,128)S(1)} collective-permute-done((f32[256,256]{1,0:T(8,128)S(1)}, f32[256,256]{1,0:T(8,128)S(1)}, u32[]{:S(2)}, u32[]{:S(2)}) %collective-permute-start.6) | collective-permute-done | bytes 262176 | tf_op jit(solution)/shard_map/ppermute | solution.py:274
  41.8 1.9 %collective-permute-start.7 = (f32[64,256]{1,0:T(8,128)S(1)}, f32[64,256]{1,0:T(8,128)S(1)}, u32[]{:S(2)}, u32[]{:S(2)}) collective-permute-start(f32[64,256]{1,0:T(8,128)S(1)} %get-tuple-element.55), channel_id=1, source_target_pairs={{0,1},{1,0},{2,3},{3,2},{4,5},{5,4},{6,7},{7,6},{8,9},{9,8},{10,11... | collective-permute-start | bytes 196616 | tf_op jit(solution)/shard_map/ppermute | solution.py:342
  43.7 2.2 %collective-permute-start.8 = (f32[64,256]{1,0:T(8,128)S(1)}, f32[64,256]{1,0:T(8,128)S(1)}, u32[]{:S(2)}, u32[]{:S(2)}) collective-permute-start(f32[64,256]{1,0:T(8,128)S(1)} %get-tuple-element.56), channel_id=1, source_target_pairs={{0,4},{1,5},{2,6},{3,7},{4,0},{5,1},{6,2},{7,3},{8,12},{9,13},{10,... | collective-permute-start | bytes 196616 | tf_op jit(solution)/shard_map/ppermute | solution.py:342
  45.9 0.0 collective-permute-start.9
  45.9 1.5 %collective-permute-start.13 = (f16[512,256]{1,0:T(8,128)(2,1)S(1)}, f16[512,256]{1,0:T(8,128)(2,1)S(1)}, u32[]{:S(2)}, u32[]{:S(2)}) collective-permute-start(f16[512,256]{1,0:T(8,128)(2,1)S(1)} %multiply_convert_fusion.2), channel_id=1, source_target_pairs={{0,1},{1,0},{2,3},{3,2},{4,5},{5,4},{6,7},{7,6},{8,9},{9,8},{10,11... | collective-permute-start | bytes 786440 | tf_op jit(solution)/shard_map/ppermute | solution.py:274
  47.4 3.0 %away_kernel.1 = f32[512,256]{1,0:T(8,128)S(1)} custom-call(s32[37]{0:T(128)S(1)} %get-tuple-element.68.plan, s32[16,3,512]{2,1,0:T(4,128)S(1)} %get-tuple-element.41.ids, s32[4,1,512]{2,1,0:T(1,128)S(1)} %get-tuple-element.42.negative_ids, bf16[16,512,512]{2,1,0:T(8,128)(2,1)S(1)} %get-tuple-element.59.grads, ...), custom_call_target="tpu_custom_call" | custom-call | bytes 131072 | tf_op jit(solution)/shard_map/away_kernel/pallas_call | solution.py:311
  50.4 0.0 collective-permute-done.7
  50.4 0.0 collective-permute-done.8
  50.4 0.8 collective-permute-done.9
  51.2 7.6 %collective-permute-start.12 = (f16[64,256]{1,0:T(8,128)(2,1)S(1)}, f16[64,256]{1,0:T(8,128)(2,1)S(1)}, u32[]{:S(2)}, u32[]{:S(2)}) collective-permute-start(f16[64,256]{1,0:T(8,128)(2,1)S(1)} %multiply_convert_fusion.3), channel_id=1, source_target_pairs={{0,24},{2,26},{4,28},{6,30},{8,16},{10,18},{12,20},{14,22},{16,8},... | collective-permute-start | bytes 98312 | tf_op jit(solution)/shard_map/ppermute | solution.py:274
  58.8 0.0 collective-permute-start.11
  58.8 0.6 collective-permute-start.10
  59.4 2.5 %own_other_kernel.1 = f32[512,256]{1,0:T(8,128)S(1)} custom-call(s32[37]{0:T(128)S(1)} %get-tuple-element.68.plan, s32[16,3,512]{2,1,0:T(4,128)S(1)} %get-tuple-element.41.ids, s32[4,1,512]{2,1,0:T(1,128)S(1)} %get-tuple-element.42.negative_ids, bf16[16,512,512]{2,1,0:T(8,128)(2,1)S(1)} %get-tuple-element.65.grads, ...), custom_call_target="tpu_custom_call" | custom-call | bytes 131072 | tf_op jit(solution)/shard_map/own_other_kernel/pallas_call | solution.py:311
  62.0 0.0 copy-start
  62.0 0.0 copy-start.2
  62.0 0.0 copy-start.3
  62.0 0.1 multiply_convert_fusion
  62.1 0.0 collective-permute-done.12
  62.1 1.5 %collective-permute-done.11 = f16[64,256]{1,0:T(8,128)(2,1)S(1)} collective-permute-done((f16[64,256]{1,0:T(8,128)(2,1)S(1)}, f16[64,256]{1,0:T(8,128)(2,1)S(1)}, u32[]{:S(2)}, u32[]{:S(2)}) %collective-permute-start.11) | collective-permute-done | bytes 32800 | tf_op jit(solution)/shard_map/ppermute | solution.py:274
  63.6 0.0 collective-permute-done.10
  63.6 0.0 collective-permute-done.13
  63.7 0.1 multiply_convert_fusion.1
  63.8 2.1 %collective-permute-start.14 = (f16[512,256]{1,0:T(8,128)(2,1)S(1)}, f16[512,256]{1,0:T(8,128)(2,1)S(1)}, u32[]{:S(2)}, u32[]{:S(2)}) collective-permute-start(f16[512,256]{1,0:T(8,128)(2,1)S(1)} %multiply_convert_fusion.1), channel_id=1, source_target_pairs={{0,16},{2,18},{4,20},{6,22},{8,24},{10,26},{12,28},{14,30},{16,0},... | collective-permute-start | bytes 786440 | tf_op jit(solution)/shard_map/ppermute | solution.py:274
  65.8 2.0 %collective-permute-start.18 = (f16[512,256]{1,0:T(8,128)(2,1)S(1)}, f16[512,256]{1,0:T(8,128)(2,1)S(1)}, u32[]{:S(2)}, u32[]{:S(2)}) collective-permute-start(f16[512,256]{1,0:T(8,128)(2,1)S(1)} %multiply_convert_fusion), channel_id=1, source_target_pairs={{0,1},{1,0},{2,3},{3,2},{4,5},{5,4},{6,7},{7,6},{8,9},{9,8},{10,11... | collective-permute-start | bytes 786440 | tf_op jit(solution)/shard_map/ppermute | solution.py:274
  67.8 0.0 collective-permute-start.17
  67.8 1.5 %collective-permute-start.16 = (f32[64,256]{1,0:T(8,128)S(1)}, f32[64,256]{1,0:T(8,128)S(1)}, u32[]{:S(2)}, u32[]{:S(2)}) collective-permute-start(f32[64,256]{1,0:T(8,128)S(1)} %add_multiply_fusion.1), channel_id=1, source_target_pairs={{0,4},{1,5},{2,6},{3,7},{4,0},{5,1},{6,2},{7,3},{8,12},{9,13},{10,... | collective-permute-start | bytes 196616 | tf_op jit(solution)/shard_map/ppermute | solution.py:342
  69.3 2.0 %collective-permute-start.15 = (f32[64,256]{1,0:T(8,128)S(1)}, f32[64,256]{1,0:T(8,128)S(1)}, u32[]{:S(2)}, u32[]{:S(2)}) collective-permute-start(f32[64,256]{1,0:T(8,128)S(1)} %add_multiply_fusion.1), channel_id=1, source_target_pairs={{0,1},{1,0},{2,3},{3,2},{4,5},{5,4},{6,7},{7,6},{8,9},{9,8},{10,11... | collective-permute-start | bytes 196616 | tf_op jit(solution)/shard_map/ppermute | solution.py:342
  71.3 2.5 %own_kernel.1.own = f32[512,256]{1,0:T(8,128)S(1)} custom-call(s32[37]{0:T(128)S(1)} %get-tuple-element.68.plan, s32[16,3,512]{2,1,0:T(4,128)S(1)} %get-tuple-element.41.ids, s32[4,1,512]{2,1,0:T(1,128)S(1)} %get-tuple-element.42.negative_ids, bf16[16,512,512]{2,1,0:T(8,128)(2,1)S(1)} %get-tuple-element.65.grads, ...), custom_call_target="tpu_custom_call" | custom-call | bytes 131072 | tf_op jit(solution)/shard_map/own_kernel/pallas_call | solution.py:311
  73.8 0.0 collective-permute-done.17
  73.8 0.0 collective-permute-done.16
  73.9 1.9 %collective-permute-done.15 = f32[64,256]{1,0:T(8,128)S(1)} collective-permute-done((f32[64,256]{1,0:T(8,128)S(1)}, f32[64,256]{1,0:T(8,128)S(1)}, u32[]{:S(2)}, u32[]{:S(2)}) %collective-permute-start.15) | collective-permute-done | bytes 65568 | tf_op jit(solution)/shard_map/ppermute | solution.py:342
  75.8 1.9 %collective-permute-done.14 = f16[512,256]{1,0:T(8,128)(2,1)S(1)} collective-permute-done((f16[512,256]{1,0:T(8,128)(2,1)S(1)}, f16[512,256]{1,0:T(8,128)(2,1)S(1)}, u32[]{:S(2)}, u32[]{:S(2)}) %collective-permute-start.14) | collective-permute-done | bytes 262176 | tf_op jit(solution)/shard_map/ppermute | solution.py:274
  77.7 0.0 collective-permute-start.19
  77.7 0.0 collective-permute-done.18
  77.7 0.1 add_multiply_fusion.returned
  77.8 0.0 copy-done
  77.8 0.0 copy-done.2
  77.8 1.2 %entity_kernel.1 = (f32[512,256]{1,0:T(8,128)}, f32[1,512]{1,0:T(1,128)}) custom-call(f32[512,256]{1,0:T(8,128)S(1)} %copy-done, f32[1,512]{1,0:T(1,128)S(1)} %bitcast.10, f32[512,256]{1,0:T(8,128)S(1)} %add_multiply_fusion.returned, f32[512,256]{1,0:T(8,128)S(1)} %own_kernel.1.own), custom_call_target="tpu_custom_call" | custom-call | flops 2097152 | bytes 131072 | tf_op jit(solution)/shard_map/entity_kernel/pallas_call | solution.py:311
  79.0 0.3 collective-permute-done.19.theirs
  79.2 0.0 copy-done.3
  79.2 1.6 %relation_kernel.1 = f32[400,256]{1,0:T(8,128)} custom-call(s32[3]{0:T(128)S(1)} %pad_add_fusion.codes, f32[400,256]{1,0:T(8,128)S(1)} %copy-done.1, f32[1,400]{1,0:T(1,128)S(1)} %bitcast.11, f32[256,256]{1,0:T(8,128)S(1)} %pad_maximum_fusion.mine, f32[256,256]{1,0:T(8,128)S(1)} %collective-permute-done.19.theirs), custom_call_target="tpu_custom_call" | custom-call | bytes 131072 | tf_op jit(solution)/shard_map/relation_kernel/pallas_call | solution.py:311
  (4 shorter events, 0.1 us)
Async XLA Ops:
  2.1 7.9 %collective-permute-start.1 = (s16[17,3,512]{2,1,0:T(4,128)(2,1)S(1)}, s16[17,3,512]{2,1,0:T(4,128)(2,1)S(1)}, u32[]{:S(2)}, u32[]{:S(2)}) collective-permute-start(s16[17,3,512]{2,1,0:T(4,128)(2,1)S(1)} %ids_kernel.1.refs_0_), channel_id=1, source_target_pairs={{0,16},{2,18},{4,20},{6,22},{8,24},{10,26},{12,28},{14,30},{16,0},... | collective-permute-start | bytes 156680 | tf_op jit(solution)/shard_map/ppermute | solution.py:274
  6.2 5.6 %collective-permute-start = (s16[17,3,512]{2,1,0:T(4,128)(2,1)S(1)}, s16[17,3,512]{2,1,0:T(4,128)(2,1)S(1)}, u32[]{:S(2)}, u32[]{:S(2)}) collective-permute-start(s16[17,3,512]{2,1,0:T(4,128)(2,1)S(1)} %ids_kernel.1.refs_0_), channel_id=1, source_target_pairs={{0,1},{1,0},{2,3},{3,2},{4,5},{5,4},{6,7},{7,6},{8,9},{9,8},{10,11... | collective-permute-start | bytes 156680 | tf_op jit(solution)/shard_map/ppermute | solution.py:274
  8.9 15.8 %collective-permute-start.4 = (bf16[256,512]{1,0:T(8,128)(2,1)S(1)}, bf16[256,512]{1,0:T(8,128)(2,1)S(1)}, u32[]{:S(2)}, u32[]{:S(2)}) collective-permute-start(bf16[256,512]{1,0:T(8,128)(2,1)S(1)} %rows_kernel.1.refs_0_), channel_id=1, source_target_pairs={{0,1},{1,0},{2,3},{3,2},{4,5},{5,4},{6,7},{7,6},{8,9},{9,8},{10,11... | collective-permute-start | bytes 786440 | tf_op jit(solution)/shard_map/ppermute | solution.py:274
  9.5 13.7 %collective-permute-start.3 = (bf16[256,512]{1,0:T(8,128)(2,1)S(1)}, bf16[256,512]{1,0:T(8,128)(2,1)S(1)}, u32[]{:S(2)}, u32[]{:S(2)}) collective-permute-start(bf16[256,512]{1,0:T(8,128)(2,1)S(1)} %rows_kernel.1.refs_0_), channel_id=1, source_target_pairs={{0,16},{2,18},{4,20},{6,22},{8,24},{10,26},{12,28},{14,30},{16,0},... | collective-permute-start | bytes 786440 | tf_op jit(solution)/shard_map/ppermute | solution.py:274
  10.0 8.0 %collective-permute-start.2 = (s16[17,3,512]{2,1,0:T(4,128)(2,1)S(1)}, s16[17,3,512]{2,1,0:T(4,128)(2,1)S(1)}, u32[]{:S(2)}, u32[]{:S(2)}) collective-permute-start(s16[17,3,512]{2,1,0:T(4,128)(2,1)S(1)} %collective-permute-done.1.refs_2_), channel_id=1, source_target_pairs={{0,1},{1,0},{2,3},{3,2},{4,5},{5,4},{6,7},{7,6},{8,9},{9,8},{10,11... | collective-permute-start | bytes 156680 | tf_op jit(solution)/shard_map/ppermute | solution.py:274
  11.8 12.9 %copy-start.1 = (f32[400,256]{1,0:T(8,128)S(1)}, f32[400,256]{1,0:T(8,128)}, u32[]{:S(2)}) copy-start(f32[400,256]{1,0:T(8,128)} %relations.3) | copy-start | bytes 1228804
  23.2 7.1 %collective-permute-start.5 = (bf16[256,512]{1,0:T(8,128)(2,1)S(1)}, bf16[256,512]{1,0:T(8,128)(2,1)S(1)}, u32[]{:S(2)}, u32[]{:S(2)}) collective-permute-start(bf16[256,512]{1,0:T(8,128)(2,1)S(1)} %collective-permute-done.3.refs_2_), channel_id=1, source_target_pairs={{0,1},{1,0},{2,3},{3,2},{4,5},{5,4},{6,7},{7,6},{8,9},{9,8},{10,11... | collective-permute-start | bytes 786440 | tf_op jit(solution)/shard_map/ppermute | solution.py:274
  40.2 1.6 %collective-permute-start.6 = (f32[256,256]{1,0:T(8,128)S(1)}, f32[256,256]{1,0:T(8,128)S(1)}, u32[]{:S(2)}, u32[]{:S(2)}) collective-permute-start(f32[256,256]{1,0:T(8,128)S(1)} %get-tuple-element.49), channel_id=1, source_target_pairs={{0,2},{2,0},{4,6},{6,4},{8,10},{10,8},{12,14},{14,12},{16,18},{18,... | collective-permute-start | bytes 786440 | tf_op jit(solution)/shard_map/ppermute | solution.py:274
  41.8 8.6 %collective-permute-start.7 = (f32[64,256]{1,0:T(8,128)S(1)}, f32[64,256]{1,0:T(8,128)S(1)}, u32[]{:S(2)}, u32[]{:S(2)}) collective-permute-start(f32[64,256]{1,0:T(8,128)S(1)} %get-tuple-element.55), channel_id=1, source_target_pairs={{0,1},{1,0},{2,3},{3,2},{4,5},{5,4},{6,7},{7,6},{8,9},{9,8},{10,11... | collective-permute-start | bytes 196616 | tf_op jit(solution)/shard_map/ppermute | solution.py:342
  43.7 6.7 %collective-permute-start.8 = (f32[64,256]{1,0:T(8,128)S(1)}, f32[64,256]{1,0:T(8,128)S(1)}, u32[]{:S(2)}, u32[]{:S(2)}) collective-permute-start(f32[64,256]{1,0:T(8,128)S(1)} %get-tuple-element.56), channel_id=1, source_target_pairs={{0,4},{1,5},{2,6},{3,7},{4,0},{5,1},{6,2},{7,3},{8,12},{9,13},{10,... | collective-permute-start | bytes 196616 | tf_op jit(solution)/shard_map/ppermute | solution.py:342
  45.9 5.3 %collective-permute-start.9 = (f32[64,256]{1,0:T(8,128)S(1)}, f32[64,256]{1,0:T(8,128)S(1)}, u32[]{:S(2)}, u32[]{:S(2)}) collective-permute-start(f32[64,256]{1,0:T(8,128)S(1)} %get-tuple-element.57), channel_id=1, source_target_pairs={{0,5},{1,4},{2,7},{3,6},{4,1},{5,0},{6,3},{7,2},{8,13},{9,12},{10,... | collective-permute-start | bytes 196616 | tf_op jit(solution)/shard_map/ppermute | solution.py:342
  45.9 17.7 %collective-permute-start.13 = (f16[512,256]{1,0:T(8,128)(2,1)S(1)}, f16[512,256]{1,0:T(8,128)(2,1)S(1)}, u32[]{:S(2)}, u32[]{:S(2)}) collective-permute-start(f16[512,256]{1,0:T(8,128)(2,1)S(1)} %multiply_convert_fusion.2), channel_id=1, source_target_pairs={{0,1},{1,0},{2,3},{3,2},{4,5},{5,4},{6,7},{7,6},{8,9},{9,8},{10,11... | collective-permute-start | bytes 786440 | tf_op jit(solution)/shard_map/ppermute | solution.py:274
  51.2 10.9 %collective-permute-start.12 = (f16[64,256]{1,0:T(8,128)(2,1)S(1)}, f16[64,256]{1,0:T(8,128)(2,1)S(1)}, u32[]{:S(2)}, u32[]{:S(2)}) collective-permute-start(f16[64,256]{1,0:T(8,128)(2,1)S(1)} %multiply_convert_fusion.3), channel_id=1, source_target_pairs={{0,24},{2,26},{4,28},{6,30},{8,16},{10,18},{12,20},{14,22},{16,8},... | collective-permute-start | bytes 98312 | tf_op jit(solution)/shard_map/ppermute | solution.py:274
  58.8 4.8 %collective-permute-start.11 = (f16[64,256]{1,0:T(8,128)(2,1)S(1)}, f16[64,256]{1,0:T(8,128)(2,1)S(1)}, u32[]{:S(2)}, u32[]{:S(2)}) collective-permute-start(f16[64,256]{1,0:T(8,128)(2,1)S(1)} %multiply_convert_fusion.3), channel_id=1, source_target_pairs={{0,16},{2,18},{4,20},{6,22},{8,24},{10,26},{12,28},{14,30},{16,0},... | collective-permute-start | bytes 98312 | tf_op jit(solution)/shard_map/ppermute | solution.py:274
  58.8 4.8 %collective-permute-start.10 = (f16[64,256]{1,0:T(8,128)(2,1)S(1)}, f16[64,256]{1,0:T(8,128)(2,1)S(1)}, u32[]{:S(2)}, u32[]{:S(2)}) collective-permute-start(f16[64,256]{1,0:T(8,128)(2,1)S(1)} %multiply_convert_fusion.3), channel_id=1, source_target_pairs={{0,8},{2,10},{4,12},{6,14},{8,0},{10,2},{12,4},{14,6},{16,24},{18,... | collective-permute-start | bytes 98312 | tf_op jit(solution)/shard_map/ppermute | solution.py:274
  62.0 15.8 %copy-start = (f32[512,256]{1,0:T(8,128)S(1)}, f32[512,256]{1,0:T(8,128)}, u32[]{:S(2)}) copy-start(f32[512,256]{1,0:T(8,128)} %table.2) | copy-start | bytes 1572868
  62.0 15.8 %copy-start.2 = (f32[512]{0:T(512)S(1)}, f32[512]{0:T(512)}, u32[]{:S(2)}) copy-start(f32[512]{0:T(512)} %param.10) | copy-start | bytes 6148
  62.0 17.2 %copy-start.3 = (f32[400]{0:T(512)S(1)}, f32[400]{0:T(512)}, u32[]{:S(2)}) copy-start(f32[400]{0:T(512)} %param.12) | copy-start | bytes 4804
  63.8 13.9 %collective-permute-start.14 = (f16[512,256]{1,0:T(8,128)(2,1)S(1)}, f16[512,256]{1,0:T(8,128)(2,1)S(1)}, u32[]{:S(2)}, u32[]{:S(2)}) collective-permute-start(f16[512,256]{1,0:T(8,128)(2,1)S(1)} %multiply_convert_fusion.1), channel_id=1, source_target_pairs={{0,16},{2,18},{4,20},{6,22},{8,24},{10,26},{12,28},{14,30},{16,0},... | collective-permute-start | bytes 786440 | tf_op jit(solution)/shard_map/ppermute | solution.py:274
  65.8 11.8 %collective-permute-start.18 = (f16[512,256]{1,0:T(8,128)(2,1)S(1)}, f16[512,256]{1,0:T(8,128)(2,1)S(1)}, u32[]{:S(2)}, u32[]{:S(2)}) collective-permute-start(f16[512,256]{1,0:T(8,128)(2,1)S(1)} %multiply_convert_fusion), channel_id=1, source_target_pairs={{0,1},{1,0},{2,3},{3,2},{4,5},{5,4},{6,7},{7,6},{8,9},{9,8},{10,11... | collective-permute-start | bytes 786440 | tf_op jit(solution)/shard_map/ppermute | solution.py:274
  67.8 6.0 %collective-permute-start.17 = (f32[64,256]{1,0:T(8,128)S(1)}, f32[64,256]{1,0:T(8,128)S(1)}, u32[]{:S(2)}, u32[]{:S(2)}) collective-permute-start(f32[64,256]{1,0:T(8,128)S(1)} %add_multiply_fusion.1), channel_id=1, source_target_pairs={{0,5},{1,4},{2,7},{3,6},{4,1},{5,0},{6,3},{7,2},{8,13},{9,12},{10,... | collective-permute-start | bytes 196616 | tf_op jit(solution)/shard_map/ppermute | solution.py:342
  67.8 6.0 %collective-permute-start.16 = (f32[64,256]{1,0:T(8,128)S(1)}, f32[64,256]{1,0:T(8,128)S(1)}, u32[]{:S(2)}, u32[]{:S(2)}) collective-permute-start(f32[64,256]{1,0:T(8,128)S(1)} %add_multiply_fusion.1), channel_id=1, source_target_pairs={{0,4},{1,5},{2,6},{3,7},{4,0},{5,1},{6,2},{7,3},{8,12},{9,13},{10,... | collective-permute-start | bytes 196616 | tf_op jit(solution)/shard_map/ppermute | solution.py:342
  69.3 6.4 %collective-permute-start.15 = (f32[64,256]{1,0:T(8,128)S(1)}, f32[64,256]{1,0:T(8,128)S(1)}, u32[]{:S(2)}, u32[]{:S(2)}) collective-permute-start(f32[64,256]{1,0:T(8,128)S(1)} %add_multiply_fusion.1), channel_id=1, source_target_pairs={{0,1},{1,0},{2,3},{3,2},{4,5},{5,4},{6,7},{7,6},{8,9},{9,8},{10,11... | collective-permute-start | bytes 196616 | tf_op jit(solution)/shard_map/ppermute | solution.py:342
  77.7 1.5 %collective-permute-start.19 = (f32[256,256]{1,0:T(8,128)S(1)}, f32[256,256]{1,0:T(8,128)S(1)}, u32[]{:S(2)}, u32[]{:S(2)}) collective-permute-start(f32[256,256]{1,0:T(8,128)S(1)} %pad_maximum_fusion.mine), channel_id=1, source_target_pairs={{0,2},{2,0},{4,6},{6,4},{8,10},{10,8},{12,14},{14,12},{16,18},{18,... | collective-permute-start | bytes 786440 | tf_op jit(solution)/shard_map/ppermute | solution.py:274

commit v9 on v8

--- a/solution.py
+++ b/solution.py
@@ -63,7 +63,7 @@
     out[...] = table[...].T.astype(bf16)
 
 
-def ids_kernel(count, heads, tails, kinds, negatives, ids_out):
+def ids_kernel(count, heads, tails, kinds, negatives, ids_out, upper_out):
     blocks, _, width = ids_out.shape
     for j in range(blocks - 1):
         at = slice(j * width, (j + 1) * width)
@@ -71,40 +71,53 @@
         ids_out[j] = block.astype(jnp.int16)
     last = jnp.concatenate([negatives[...], jnp.full((2, width), count[0, 0], i32)], axis=0)
     ids_out[blocks - 1] = last.astype(jnp.int16)
+    upper_out[...] = ids_out[blocks - upper_out.shape[0] :]
 
 
 def plan_kernel(n, codes, *refs):
     sources, (plan, step_ids, negative_ids) = refs[:-3], refs[-3:]
     team = len(sources)
     most, _, width = step_ids.shape
+    offset = most + 1 - sources[-1].shape[0]
     me = codes[0]
-    counts, blocks = [], []
+    counts, blocks, movable = [], [], []
     for k, ids in enumerate(sources):
-        last = ids[most].astype(i32)
+        last = ids[ids.shape[0] - 1].astype(i32)
         counts.append(jnp.max(last[1:2]))
         blocks.append(lax.div(counts[k] + (width - 1), i32(width)))
+        movable.append(jnp.maximum(blocks[k] - offset, 0))
         negative_ids[k] = last[0:1] ^ codes[1]
-    total = sum(blocks)
-    low = lax.div(me * total, i32(team))
-    high = lax.div((me + 1) * total, i32(team))
+    surplus = sum(blocks[:n]) - sum(blocks[n:])
+    starts, lengths = [], []
+    for k in range(team):
+        side = range(n) if k < n else range(n, team)
+        moved = jnp.maximum(lax.div(surplus if k < n else -surplus, i32(2)), 0)
+        later = [jnp.where((me ^ j) > (me ^ k), movable[j], 0) for j in side if j != k]
+        moved = jnp.clip(moved - sum(later), 0, movable[k])
+        starts.append(0 if k < n else blocks[k] - moved)
+        lengths.append(blocks[k] - moved if k < n else moved)
+    total = sum(lengths)
+    place = codes[3]
+    low = lax.div(place * total, i32(n))
+    high = lax.div((place + 1) * total, i32(n))
     plan[2 * most] = high - low
     before = []
     for k in range(team):
-        ahead = [jnp.where((me ^ j) < (me ^ k), blocks[j], 0) for j in range(team) if j != k]
+        ahead = [jnp.where((me ^ j) < (me ^ k), lengths[j], 0) for j in range(team) if j != k]
         before.append(sum(ahead))
-        seen = (before[k] < high) & (before[k] + blocks[k] > low)
+        seen = (lengths[k] > 0) & (before[k] < high) & (before[k] + lengths[k] > low)
         plan[2 * most + 1 + k] = seen.astype(i32)
 
     def one_step(i, carry):
-        line = jnp.minimum(low + i, high - 1)
+        line = low + i
         for k, ids in enumerate(sources):
 
-            @pl.when((line >= before[k]) & (line < before[k] + blocks[k]))
+            @pl.when((line >= before[k]) & (line < before[k] + lengths[k]))
             def _(k=k, ids=ids):
-                nth = line - before[k]
+                nth = line - before[k] + starts[k]
                 plan[i] = k
                 plan[most + i] = jnp.clip(counts[k] - nth * width, 0, width)
-                entries = ids[nth].astype(i32)
+                entries = ids[nth - (most + 1 - ids.shape[0])].astype(i32)
                 near, away = (0, 1) if k < n else (1, 0)
                 step_ids[i, 0:1] = entries[near : near + 1] ^ codes[1]
                 step_ids[i, 1:2] = entries[away : away + 1] ^ codes[1]
@@ -301,7 +314,7 @@
     chunk = rel_rows // (2 * chips)
     me = lax.shift_right_logical(me_dom, pair.bit_length() - 1) * n + me_sub
     chunk_code = (me_dom & 1) * chips + ((me_dom >> 1) & 1) * n + me_sub
-    codes = jnp.stack([me, me_sub * rows, chunk_code * chunk]).astype(i32)
+    codes = jnp.stack([me, me_sub * rows, chunk_code * chunk, me_sub]).astype(i32)
 
     in_vmem = pl.BlockSpec(memory_space=pltpu.VMEM)
     in_smem = pl.BlockSpec(memory_space=pltpu.SMEM)
@@ -319,10 +332,10 @@
             name=name,
         )(*scalars, *(pltpu.with_memory_space_constraint(x, pltpu.HBM if fetch else pltpu.VMEM) for x in arrays))
 
-    (ids,) = call(
+    ids, upper = call(
         ids_kernel,
         "ids_kernel",
-        [((most + 1, 3, width), jnp.int16)],
+        [((most + 1, 3, width), jnp.int16), ((most + 1 - most // 2, 3, width), jnp.int16)],
         [],
         1,
         (edge_counts,),
@@ -334,7 +347,7 @@
         ),
         fetch=True,
     )
-    ids, table = lax.optimization_barrier((ids, entity_table))
+    ids, upper, table = lax.optimization_barrier((ids, upper, entity_table))
     (local,) = call(rows_kernel, "rows_kernel", [((dims, rows), bf16)], [], 1, (), (table,), fetch=True)
 
     def to_peer(x, across, aside):
@@ -344,7 +357,7 @@
     def along_sub(x):
         return [x] + [exchange(x, "sub", k) for k in range(1, n)]
 
-    all_ids = along_sub(ids) + along_sub(exchange(ids, "dom", pair))
+    all_ids = along_sub(ids) + along_sub(exchange(upper, "dom", pair))
     near_slab = along_sub(local)
     away_first = exchange(local, "dom", pair)
 

time: 79.8 us -> 77.3 us (0.969); the launches traced: 80.8 us -> 77 us
  starting transfers between devices: 30.9 us -> 23.6 us
  Pallas kernels: 28.2 us -> 35 us
  waiting for transfers between devices: 19.8 us -> 16.5 us
    ppermute x14, starting transfers between devices: 23.3 us -> 16.5 us  [exchange(): lax.ppermute(x, axis, [(i, i ^ mask) for i in range(lax.axis_size(axis))])]
    pallas_call x9, Pallas kernels: 26.6 us -> 33.3 us  [call(): pl.pallas_call(kernel, in_specs=[in_smem] * len(scalars) + [in_vmem] * le...]
    ppermute x6, waiting for transfers between devices: 2.71 us -> 0.33 us  [to_peer(): return lax.ppermute(x, ('dom', 'sub'), pairs)]
    ppermute x14, waiting for transfers between devices: 17.1 us -> 16.1 us  [exchange(): lax.ppermute(x, axis, [(i, i ^ mask) for i in range(lax.axis_size(axis))])]
  transfers between devices with their start and end apart: 20 -> 20, of which waited for: 10 -> 9; matrix products, arithmetic and copies ran while one was open for 0% -> 0% of each run, Pallas kernels for 20% -> 25%
where the time goes in v9:
time: 77.3 us; the launch traced here: 77 us
  Pallas kernels  35 us (45%)
  starting transfers between devices  23.6 us (31%)
  waiting for transfers between devices  16.5 us (21%)
  between operations  1.49 us (2%)
    pallas_call x9, Pallas kernels, call(): pl.pallas_call(kernel, in_specs=[in_smem] * len(scalars) + [in_vmem] * le...  33.3 us
    ppermute x14, starting transfers between devices, exchange(): lax.ppermute(x, axis, [(i, i ^ mask) for i in range(lax.axis_size(axis))])  16.5 us
    ppermute x14, waiting for transfers between devices, exchange(): lax.ppermute(x, axis, [(i, i ^ mask) for i in range(lax.axis_size(axis))])  16.1 us
    ppermute x6, starting transfers between devices, to_peer(): return lax.ppermute(x, ('dom', 'sub'), pairs)  7.04 us
    pallas_call x1, Pallas kernels, on_device(): pl.pallas_call(functools.partial(plan_kernel, n), in_specs=[in_smem] + [i...  1.68 us
  transfers between devices with their start and end apart: 20, of which 9 were waited for; matrix products, arithmetic and copies ran while one was open for 0% of the time, Pallas kernels for 25%

profile of v9, /device:TPU:0, one launch (start us, length us, event | category | flops | bytes accessed | tf_op | source)
XLA Modules:
  0.0 77.0 jit_solution(6219912022412638405)
XLA Ops:
  1.3 0.8 %ids_kernel.1 = (s16[17,3,512]{2,1,0:T(4,128)(2,1)S(1)}, s16[9,3,512]{2,1,0:T(4,128)(2,1)S(1)}) custom-call(s32[1,1]{1,0:T(1,128)S(6)} %copy.12.count, s32[1,8192]{1,0:T(1,128)} %bitcast.13, s32[1,8192]{1,0:T(1,128)} %bitcast.14, s32[1,8192]{1,0:T(1,128)} %bitcast.15, s32[1,512]{1,0:T(1,128)} %bitcast.16), custom_call_target="tpu_custom_call" | custom-call | flops 2097152 | bytes 131072 | tf_op jit(solution)/shard_map/ids_kernel/pallas_call | solution.py:324
  2.1 4.1 %collective-permute-start.1 = (s16[9,3,512]{2,1,0:T(4,128)(2,1)S(1)}, s16[9,3,512]{2,1,0:T(4,128)(2,1)S(1)}, u32[]{:S(2)}, u32[]{:S(2)}) collective-permute-start(s16[9,3,512]{2,1,0:T(4,128)(2,1)S(1)} %get-tuple-element.45), channel_id=1, source_target_pairs={{0,16},{2,18},{4,20},{6,22},{8,24},{10,26},{12,28},{14,30},{16,0},... | collective-permute-start | bytes 82952 | tf_op jit(solution)/shard_map/ppermute | solution.py:287
  6.2 1.2 %rows_kernel.1.refs_0_ = bf16[256,512]{1,0:T(8,128)(2,1)S(1)} custom-call(f32[512,256]{1,0:T(8,128)} %table.2), custom_call_target="tpu_custom_call" | custom-call | flops 2097152 | bytes 131072 | tf_op jit(solution)/shard_map/rows_kernel/pallas_call | solution.py:324
  7.4 1.6 %collective-permute-start.4 = (bf16[256,512]{1,0:T(8,128)(2,1)S(1)}, bf16[256,512]{1,0:T(8,128)(2,1)S(1)}, u32[]{:S(2)}, u32[]{:S(2)}) collective-permute-start(bf16[256,512]{1,0:T(8,128)(2,1)S(1)} %rows_kernel.1.refs_0_), channel_id=1, source_target_pairs={{0,1},{1,0},{2,3},{3,2},{4,5},{5,4},{6,7},{7,6},{8,9},{9,8},{10,11... | collective-permute-start | bytes 786440 | tf_op jit(solution)/shard_map/ppermute | solution.py:287
  9.0 0.3 collective-permute-start.3
  9.3 0.2 collective-permute-start
  9.5 0.0 collective-permute-done.1.refs_2_
  9.5 1.8 %collective-permute-start.2 = (s16[9,3,512]{2,1,0:T(4,128)(2,1)S(1)}, s16[9,3,512]{2,1,0:T(4,128)(2,1)S(1)}, u32[]{:S(2)}, u32[]{:S(2)}) collective-permute-start(s16[9,3,512]{2,1,0:T(4,128)(2,1)S(1)} %collective-permute-done.1.refs_2_), channel_id=1, source_target_pairs={{0,1},{1,0},{2,3},{3,2},{4,5},{5,4},{6,7},{7,6},{8,9},{9,8},{10,11... | collective-permute-start | bytes 82952 | tf_op jit(solution)/shard_map/ppermute | solution.py:287
  11.4 0.1 pad_add_fusion.codes
  11.4 0.0 copy-start.1
  11.4 5.7 %collective-permute-done.refs_1_ = s16[17,3,512]{2,1,0:T(4,128)(2,1)S(1)} collective-permute-done((s16[17,3,512]{2,1,0:T(4,128)(2,1)S(1)}, s16[17,3,512]{2,1,0:T(4,128)(2,1)S(1)}, u32[]{:S(2)}, u32[]{:S(2)}) %collective-permute-start) | collective-permute-done | bytes 52256 | tf_op jit(solution)/shard_map/ppermute | solution.py:287
  17.1 0.4 collective-permute-done.2.refs_3_
  17.5 1.7 %plan_kernel.1 = (s32[37]{0:T(128)S(1)}, s32[16,3,512]{2,1,0:T(4,128)S(1)}, s32[4,1,512]{2,1,0:T(1,128)S(1)}) custom-call(s32[4]{0:T(128)S(1)} %pad_add_fusion.codes, s16[17,3,512]{2,1,0:T(4,128)(2,1)S(1)} %get-tuple-element.44.refs_0_, s16[17,3,512]{2,1,0:T(4,128)(2,1)S(1)} %collective-permute-done.refs_1_, ...), custom_call_target="tpu_custom_call" | custom-call | flops 34359738368 | bytes 2097152 | tf_op jit(solution)/shard_map/plan_kernel/pallas_call | solution.py:364
  19.2 3.8 %collective-permute-done.3.refs_2_ = bf16[256,512]{1,0:T(8,128)(2,1)S(1)} collective-permute-done((bf16[256,512]{1,0:T(8,128)(2,1)S(1)}, bf16[256,512]{1,0:T(8,128)(2,1)S(1)}, u32[]{:S(2)}, u32[]{:S(2)}) %collective-permute-start.3) | collective-permute-done | bytes 262176 | tf_op jit(solution)/shard_map/ppermute | solution.py:287
  23.0 0.5 collective-permute-start.5
  23.5 0.0 collective-permute-done.4.refs_1_
  23.5 0.0 copy-done.1
  23.5 5.2 %near_kernel.1 = (bf16[16,256,512]{2,1,0:T(8,128)(2,1)S(1)}, f32[16,256,512]{2,1,0:T(8,128)S(1)}) custom-call(s32[37]{0:T(128)S(1)} %get-tuple-element.74.plan, s32[16,3,512]{2,1,0:T(4,128)S(1)} %get-tuple-element.47.ids, f32[400,256]{1,0:T(8,128)S(1)} %copy-done.1, bf16[256,512]{1,0:T(8,128)(2,1)S(1)} %rows_kernel.1.refs_0_, ...), custom_call_target="tpu_custom_call" | custom-call | flops 4294967296 | bytes 131072 | tf_op jit(solution)/shard_map/near_kernel/pallas_call | solution.py:324
  28.7 1.4 %collective-permute-done.5.refs_3_ = bf16[256,512]{1,0:T(8,128)(2,1)S(1)} collective-permute-done((bf16[256,512]{1,0:T(8,128)(2,1)S(1)}, bf16[256,512]{1,0:T(8,128)(2,1)S(1)}, u32[]{:S(2)}, u32[]{:S(2)}) %collective-permute-start.5) | collective-permute-done | bytes 262176 | tf_op jit(solution)/shard_map/ppermute | solution.py:287
  30.1 13.0 %edge_kernel.1 = (bf16[16,512,512]{2,1,0:T(8,128)(2,1)S(1)}, bf16[16,512,512]{2,1,0:T(8,128)(2,1)S(1)}, bf16[4,1024,256]{2,1,0:T(8,128)(2,1)S(1)}, f32[512,256]{...) custom-call(s32[4]{0:T(128)S(1)} %pad_add_fusion.codes, ...), custom_call_target="tpu_custom_call" | custom-call | flops 11811160064 | bytes 131072 | tf_op jit(solution)/shard_map/edge_kernel/pallas_call | solution.py:324
  43.2 0.1 collective-permute-start.6
  43.2 0.1 multiply_convert_fusion.2
  43.3 1.5 %collective-permute-done.6 = f32[256,256]{1,0:T(8,128)S(1)} collective-permute-done((f32[256,256]{1,0:T(8,128)S(1)}, f32[256,256]{1,0:T(8,128)S(1)}, u32[]{:S(2)}, u32[]{:S(2)}) %collective-permute-start.6) | collective-permute-done | bytes 262176 | tf_op jit(solution)/shard_map/ppermute | solution.py:287
  44.8 1.6 %collective-permute-start.7 = (f32[64,256]{1,0:T(8,128)S(1)}, f32[64,256]{1,0:T(8,128)S(1)}, u32[]{:S(2)}, u32[]{:S(2)}) collective-permute-start(f32[64,256]{1,0:T(8,128)S(1)} %get-tuple-element.61), channel_id=1, source_target_pairs={{0,1},{1,0},{2,3},{3,2},{4,5},{5,4},{6,7},{7,6},{8,9},{9,8},{10,11... | collective-permute-start | bytes 196616 | tf_op jit(solution)/shard_map/ppermute | solution.py:355
  46.4 1.5 %collective-permute-start.8 = (f32[64,256]{1,0:T(8,128)S(1)}, f32[64,256]{1,0:T(8,128)S(1)}, u32[]{:S(2)}, u32[]{:S(2)}) collective-permute-start(f32[64,256]{1,0:T(8,128)S(1)} %get-tuple-element.62), channel_id=1, source_target_pairs={{0,4},{1,5},{2,6},{3,7},{4,0},{5,1},{6,2},{7,3},{8,12},{9,13},{10,... | collective-permute-start | bytes 196616 | tf_op jit(solution)/shard_map/ppermute | solution.py:355
  47.9 0.5 collective-permute-start.9
  48.4 1.5 %collective-permute-start.13 = (f16[512,256]{1,0:T(8,128)(2,1)S(1)}, f16[512,256]{1,0:T(8,128)(2,1)S(1)}, u32[]{:S(2)}, u32[]{:S(2)}) collective-permute-start(f16[512,256]{1,0:T(8,128)(2,1)S(1)} %multiply_convert_fusion.2), channel_id=1, source_target_pairs={{0,1},{1,0},{2,3},{3,2},{4,5},{5,4},{6,7},{7,6},{8,9},{9,8},{10,11... | collective-permute-start | bytes 786440 | tf_op jit(solution)/shard_map/ppermute | solution.py:287
  49.9 3.7 %away_kernel.1 = f32[512,256]{1,0:T(8,128)S(1)} custom-call(s32[37]{0:T(128)S(1)} %get-tuple-element.74.plan, s32[16,3,512]{2,1,0:T(4,128)S(1)} %get-tuple-element.47.ids, s32[4,1,512]{2,1,0:T(1,128)S(1)} %get-tuple-element.48.negative_ids, bf16[16,512,512]{2,1,0:T(8,128)(2,1)S(1)} %get-tuple-element.65.grads, ...), custom_call_target="tpu_custom_call" | custom-call | bytes 131072 | tf_op jit(solution)/shard_map/away_kernel/pallas_call | solution.py:324
  53.6 0.0 collective-permute-done.7
  53.6 0.0 collective-permute-done.8
  53.6 0.0 collective-permute-done.9
  53.7 4.1 %collective-permute-start.12 = (f16[64,256]{1,0:T(8,128)(2,1)S(1)}, f16[64,256]{1,0:T(8,128)(2,1)S(1)}, u32[]{:S(2)}, u32[]{:S(2)}) collective-permute-start(f16[64,256]{1,0:T(8,128)(2,1)S(1)} %multiply_convert_fusion.3), channel_id=1, source_target_pairs={{0,24},{2,26},{4,28},{6,30},{8,16},{10,18},{12,20},{14,22},{16,8},... | collective-permute-start | bytes 98312 | tf_op jit(solution)/shard_map/ppermute | solution.py:287
  57.8 0.0 collective-permute-start.11
  57.8 0.6 collective-permute-start.10
  58.5 3.3 %own_other_kernel.1 = f32[512,256]{1,0:T(8,128)S(1)} custom-call(s32[37]{0:T(128)S(1)} %get-tuple-element.74.plan, s32[16,3,512]{2,1,0:T(4,128)S(1)} %get-tuple-element.47.ids, s32[4,1,512]{2,1,0:T(1,128)S(1)} %get-tuple-element.48.negative_ids, bf16[16,512,512]{2,1,0:T(8,128)(2,1)S(1)} %get-tuple-element.71.grads, ...), custom_call_target="tpu_custom_call" | custom-call | bytes 131072 | tf_op jit(solution)/shard_map/own_other_kernel/pallas_call | solution.py:324
  61.7 0.0 copy-start
  61.8 0.0 copy-start.2
  61.8 0.0 copy-start.3
  61.8 0.1 multiply_convert_fusion
  61.8 0.0 collective-permute-done.12
  61.9 2.3 %collective-permute-done.11 = f16[64,256]{1,0:T(8,128)(2,1)S(1)} collective-permute-done((f16[64,256]{1,0:T(8,128)(2,1)S(1)}, f16[64,256]{1,0:T(8,128)(2,1)S(1)}, u32[]{:S(2)}, u32[]{:S(2)}) %collective-permute-start.11) | collective-permute-done | bytes 32800 | tf_op jit(solution)/shard_map/ppermute | solution.py:287
  64.2 0.0 collective-permute-done.10
  64.2 0.0 collective-permute-done.13
  64.2 0.1 multiply_convert_fusion.1
  64.3 0.9 %collective-permute-start.14 = (f16[512,256]{1,0:T(8,128)(2,1)S(1)}, f16[512,256]{1,0:T(8,128)(2,1)S(1)}, u32[]{:S(2)}, u32[]{:S(2)}) collective-permute-start(f16[512,256]{1,0:T(8,128)(2,1)S(1)} %multiply_convert_fusion.1), channel_id=1, source_target_pairs={{0,16},{2,18},{4,20},{6,22},{8,24},{10,26},{12,28},{14,30},{16,0},... | collective-permute-start | bytes 786440 | tf_op jit(solution)/shard_map/ppermute | solution.py:287
  65.2 0.7 collective-permute-start.18
  65.9 0.5 collective-permute-start.17
  66.4 2.4 %collective-permute-start.16 = (f32[64,256]{1,0:T(8,128)S(1)}, f32[64,256]{1,0:T(8,128)S(1)}, u32[]{:S(2)}, u32[]{:S(2)}) collective-permute-start(f32[64,256]{1,0:T(8,128)S(1)} %add_multiply_fusion.1), channel_id=1, source_target_pairs={{0,4},{1,5},{2,6},{3,7},{4,0},{5,1},{6,2},{7,3},{8,12},{9,13},{10,... | collective-permute-start | bytes 196616 | tf_op jit(solution)/shard_map/ppermute | solution.py:355
  68.7 0.7 collective-permute-start.15
  69.4 3.3 %own_kernel.1.own = f32[512,256]{1,0:T(8,128)S(1)} custom-call(s32[37]{0:T(128)S(1)} %get-tuple-element.74.plan, s32[16,3,512]{2,1,0:T(4,128)S(1)} %get-tuple-element.47.ids, s32[4,1,512]{2,1,0:T(1,128)S(1)} %get-tuple-element.48.negative_ids, bf16[16,512,512]{2,1,0:T(8,128)(2,1)S(1)} %get-tuple-element.71.grads, ...), custom_call_target="tpu_custom_call" | custom-call | bytes 131072 | tf_op jit(solution)/shard_map/own_kernel/pallas_call | solution.py:324
  72.7 0.0 collective-permute-done.17
  72.7 0.0 collective-permute-done.16
  72.7 0.3 collective-permute-done.15
  73.0 0.8 %collective-permute-done.14 = f16[512,256]{1,0:T(8,128)(2,1)S(1)} collective-permute-done((f16[512,256]{1,0:T(8,128)(2,1)S(1)}, f16[512,256]{1,0:T(8,128)(2,1)S(1)}, u32[]{:S(2)}, u32[]{:S(2)}) %collective-permute-start.14) | collective-permute-done | bytes 262176 | tf_op jit(solution)/shard_map/ppermute | solution.py:287
  73.9 0.0 collective-permute-start.19
  73.9 0.0 collective-permute-done.18
  73.9 0.1 add_multiply_fusion.returned
  73.9 0.0 copy-done
  74.0 0.0 copy-done.2
  74.0 1.2 %entity_kernel.1 = (f32[512,256]{1,0:T(8,128)}, f32[1,512]{1,0:T(1,128)}) custom-call(f32[512,256]{1,0:T(8,128)S(1)} %copy-done, f32[1,512]{1,0:T(1,128)S(1)} %bitcast.11, f32[512,256]{1,0:T(8,128)S(1)} %add_multiply_fusion.returned, f32[512,256]{1,0:T(8,128)S(1)} %own_kernel.1.own), custom_call_target="tpu_custom_call" | custom-call | flops 2097152 | bytes 131072 | tf_op jit(solution)/shard_map/entity_kernel/pallas_call | solution.py:324
  75.1 0.3 collective-permute-done.19.theirs
  75.4 0.0 copy-done.3
  75.4 1.6 %relation_kernel.1 = f32[400,256]{1,0:T(8,128)} custom-call(s32[4]{0:T(128)S(1)} %pad_add_fusion.codes, f32[400,256]{1,0:T(8,128)S(1)} %copy-done.1, f32[1,400]{1,0:T(1,128)S(1)} %bitcast.12, f32[256,256]{1,0:T(8,128)S(1)} %pad_maximum_fusion.mine, f32[256,256]{1,0:T(8,128)S(1)} %collective-permute-done.19.theirs), custom_call_target="tpu_custom_call" | custom-call | bytes 131072 | tf_op jit(solution)/shard_map/relation_kernel/pallas_call | solution.py:324
  (4 shorter events, 0.1 us)
Async XLA Ops:
  2.1 7.4 %collective-permute-start.1 = (s16[9,3,512]{2,1,0:T(4,128)(2,1)S(1)}, s16[9,3,512]{2,1,0:T(4,128)(2,1)S(1)}, u32[]{:S(2)}, u32[]{:S(2)}) collective-permute-start(s16[9,3,512]{2,1,0:T(4,128)(2,1)S(1)} %get-tuple-element.45), channel_id=1, source_target_pairs={{0,16},{2,18},{4,20},{6,22},{8,24},{10,26},{12,28},{14,30},{16,0},... | collective-permute-start | bytes 82952 | tf_op jit(solution)/shard_map/ppermute | solution.py:287
  7.4 16.1 %collective-permute-start.4 = (bf16[256,512]{1,0:T(8,128)(2,1)S(1)}, bf16[256,512]{1,0:T(8,128)(2,1)S(1)}, u32[]{:S(2)}, u32[]{:S(2)}) collective-permute-start(bf16[256,512]{1,0:T(8,128)(2,1)S(1)} %rows_kernel.1.refs_0_), channel_id=1, source_target_pairs={{0,1},{1,0},{2,3},{3,2},{4,5},{5,4},{6,7},{7,6},{8,9},{9,8},{10,11... | collective-permute-start | bytes 786440 | tf_op jit(solution)/shard_map/ppermute | solution.py:287
  9.0 14.0 %collective-permute-start.3 = (bf16[256,512]{1,0:T(8,128)(2,1)S(1)}, bf16[256,512]{1,0:T(8,128)(2,1)S(1)}, u32[]{:S(2)}, u32[]{:S(2)}) collective-permute-start(bf16[256,512]{1,0:T(8,128)(2,1)S(1)} %rows_kernel.1.refs_0_), channel_id=1, source_target_pairs={{0,16},{2,18},{4,20},{6,22},{8,24},{10,26},{12,28},{14,30},{16,0},... | collective-permute-start | bytes 786440 | tf_op jit(solution)/shard_map/ppermute | solution.py:287
  9.3 7.8 %collective-permute-start = (s16[17,3,512]{2,1,0:T(4,128)(2,1)S(1)}, s16[17,3,512]{2,1,0:T(4,128)(2,1)S(1)}, u32[]{:S(2)}, u32[]{:S(2)}) collective-permute-start(s16[17,3,512]{2,1,0:T(4,128)(2,1)S(1)} %get-tuple-element.44.refs_0_), channel_id=1, source_target_pairs={{0,1},{1,0},{2,3},{3,2},{4,5},{5,4},{6,7},{7,6},{8,9},{9,8},{10,11... | collective-permute-start | bytes 156680 | tf_op jit(solution)/shard_map/ppermute | solution.py:287
  9.5 8.0 %collective-permute-start.2 = (s16[9,3,512]{2,1,0:T(4,128)(2,1)S(1)}, s16[9,3,512]{2,1,0:T(4,128)(2,1)S(1)}, u32[]{:S(2)}, u32[]{:S(2)}) collective-permute-start(s16[9,3,512]{2,1,0:T(4,128)(2,1)S(1)} %collective-permute-done.1.refs_2_), channel_id=1, source_target_pairs={{0,1},{1,0},{2,3},{3,2},{4,5},{5,4},{6,7},{7,6},{8,9},{9,8},{10,11... | collective-permute-start | bytes 82952 | tf_op jit(solution)/shard_map/ppermute | solution.py:287
  11.4 12.1 %copy-start.1 = (f32[400,256]{1,0:T(8,128)S(1)}, f32[400,256]{1,0:T(8,128)}, u32[]{:S(2)}) copy-start(f32[400,256]{1,0:T(8,128)} %relations.3) | copy-start | bytes 1228804
  23.0 7.1 %collective-permute-start.5 = (bf16[256,512]{1,0:T(8,128)(2,1)S(1)}, bf16[256,512]{1,0:T(8,128)(2,1)S(1)}, u32[]{:S(2)}, u32[]{:S(2)}) collective-permute-start(bf16[256,512]{1,0:T(8,128)(2,1)S(1)} %collective-permute-done.3.refs_2_), channel_id=1, source_target_pairs={{0,1},{1,0},{2,3},{3,2},{4,5},{5,4},{6,7},{7,6},{8,9},{9,8},{10,11... | collective-permute-start | bytes 786440 | tf_op jit(solution)/shard_map/ppermute | solution.py:287
  43.2 1.6 %collective-permute-start.6 = (f32[256,256]{1,0:T(8,128)S(1)}, f32[256,256]{1,0:T(8,128)S(1)}, u32[]{:S(2)}, u32[]{:S(2)}) collective-permute-start(f32[256,256]{1,0:T(8,128)S(1)} %get-tuple-element.55), channel_id=1, source_target_pairs={{0,2},{2,0},{4,6},{6,4},{8,10},{10,8},{12,14},{14,12},{16,18},{18,... | collective-permute-start | bytes 786440 | tf_op jit(solution)/shard_map/ppermute | solution.py:287
  44.8 8.8 %collective-permute-start.7 = (f32[64,256]{1,0:T(8,128)S(1)}, f32[64,256]{1,0:T(8,128)S(1)}, u32[]{:S(2)}, u32[]{:S(2)}) collective-permute-start(f32[64,256]{1,0:T(8,128)S(1)} %get-tuple-element.61), channel_id=1, source_target_pairs={{0,1},{1,0},{2,3},{3,2},{4,5},{5,4},{6,7},{7,6},{8,9},{9,8},{10,11... | collective-permute-start | bytes 196616 | tf_op jit(solution)/shard_map/ppermute | solution.py:355
  46.4 7.2 %collective-permute-start.8 = (f32[64,256]{1,0:T(8,128)S(1)}, f32[64,256]{1,0:T(8,128)S(1)}, u32[]{:S(2)}, u32[]{:S(2)}) collective-permute-start(f32[64,256]{1,0:T(8,128)S(1)} %get-tuple-element.62), channel_id=1, source_target_pairs={{0,4},{1,5},{2,6},{3,7},{4,0},{5,1},{6,2},{7,3},{8,12},{9,13},{10,... | collective-permute-start | bytes 196616 | tf_op jit(solution)/shard_map/ppermute | solution.py:355
  47.9 5.7 %collective-permute-start.9 = (f32[64,256]{1,0:T(8,128)S(1)}, f32[64,256]{1,0:T(8,128)S(1)}, u32[]{:S(2)}, u32[]{:S(2)}) collective-permute-start(f32[64,256]{1,0:T(8,128)S(1)} %get-tuple-element.63), channel_id=1, source_target_pairs={{0,5},{1,4},{2,7},{3,6},{4,1},{5,0},{6,3},{7,2},{8,13},{9,12},{10,... | collective-permute-start | bytes 196616 | tf_op jit(solution)/shard_map/ppermute | solution.py:355
  48.4 15.8 %collective-permute-start.13 = (f16[512,256]{1,0:T(8,128)(2,1)S(1)}, f16[512,256]{1,0:T(8,128)(2,1)S(1)}, u32[]{:S(2)}, u32[]{:S(2)}) collective-permute-start(f16[512,256]{1,0:T(8,128)(2,1)S(1)} %multiply_convert_fusion.2), channel_id=1, source_target_pairs={{0,1},{1,0},{2,3},{3,2},{4,5},{5,4},{6,7},{7,6},{8,9},{9,8},{10,11... | collective-permute-start | bytes 786440 | tf_op jit(solution)/shard_map/ppermute | solution.py:287
  53.7 8.2 %collective-permute-start.12 = (f16[64,256]{1,0:T(8,128)(2,1)S(1)}, f16[64,256]{1,0:T(8,128)(2,1)S(1)}, u32[]{:S(2)}, u32[]{:S(2)}) collective-permute-start(f16[64,256]{1,0:T(8,128)(2,1)S(1)} %multiply_convert_fusion.3), channel_id=1, source_target_pairs={{0,24},{2,26},{4,28},{6,30},{8,16},{10,18},{12,20},{14,22},{16,8},... | collective-permute-start | bytes 98312 | tf_op jit(solution)/shard_map/ppermute | solution.py:287
  57.8 6.4 %collective-permute-start.11 = (f16[64,256]{1,0:T(8,128)(2,1)S(1)}, f16[64,256]{1,0:T(8,128)(2,1)S(1)}, u32[]{:S(2)}, u32[]{:S(2)}) collective-permute-start(f16[64,256]{1,0:T(8,128)(2,1)S(1)} %multiply_convert_fusion.3), channel_id=1, source_target_pairs={{0,16},{2,18},{4,20},{6,22},{8,24},{10,26},{12,28},{14,30},{16,0},... | collective-permute-start | bytes 98312 | tf_op jit(solution)/shard_map/ppermute | solution.py:287
  57.8 6.4 %collective-permute-start.10 = (f16[64,256]{1,0:T(8,128)(2,1)S(1)}, f16[64,256]{1,0:T(8,128)(2,1)S(1)}, u32[]{:S(2)}, u32[]{:S(2)}) collective-permute-start(f16[64,256]{1,0:T(8,128)(2,1)S(1)} %multiply_convert_fusion.3), channel_id=1, source_target_pairs={{0,8},{2,10},{4,12},{6,14},{8,0},{10,2},{12,4},{14,6},{16,24},{18,... | collective-permute-start | bytes 98312 | tf_op jit(solution)/shard_map/ppermute | solution.py:287
  61.7 12.2 %copy-start = (f32[512,256]{1,0:T(8,128)S(1)}, f32[512,256]{1,0:T(8,128)}, u32[]{:S(2)}) copy-start(f32[512,256]{1,0:T(8,128)} %table.2) | copy-start | bytes 1572868
  61.8 12.2 %copy-start.2 = (f32[512]{0:T(512)S(1)}, f32[512]{0:T(512)}, u32[]{:S(2)}) copy-start(f32[512]{0:T(512)} %param.10) | copy-start | bytes 6148
  61.8 13.6 %copy-start.3 = (f32[400]{0:T(512)S(1)}, f32[400]{0:T(512)}, u32[]{:S(2)}) copy-start(f32[400]{0:T(512)} %param.12) | copy-start | bytes 4804
  64.3 9.5 %collective-permute-start.14 = (f16[512,256]{1,0:T(8,128)(2,1)S(1)}, f16[512,256]{1,0:T(8,128)(2,1)S(1)}, u32[]{:S(2)}, u32[]{:S(2)}) collective-permute-start(f16[512,256]{1,0:T(8,128)(2,1)S(1)} %multiply_convert_fusion.1), channel_id=1, source_target_pairs={{0,16},{2,18},{4,20},{6,22},{8,24},{10,26},{12,28},{14,30},{16,0},... | collective-permute-start | bytes 786440 | tf_op jit(solution)/shard_map/ppermute | solution.py:287
  65.2 8.6 %collective-permute-start.18 = (f16[512,256]{1,0:T(8,128)(2,1)S(1)}, f16[512,256]{1,0:T(8,128)(2,1)S(1)}, u32[]{:S(2)}, u32[]{:S(2)}) collective-permute-start(f16[512,256]{1,0:T(8,128)(2,1)S(1)} %multiply_convert_fusion), channel_id=1, source_target_pairs={{0,1},{1,0},{2,3},{3,2},{4,5},{5,4},{6,7},{7,6},{8,9},{9,8},{10,11... | collective-permute-start | bytes 786440 | tf_op jit(solution)/shard_map/ppermute | solution.py:287
  65.9 6.8 %collective-permute-start.17 = (f32[64,256]{1,0:T(8,128)S(1)}, f32[64,256]{1,0:T(8,128)S(1)}, u32[]{:S(2)}, u32[]{:S(2)}) collective-permute-start(f32[64,256]{1,0:T(8,128)S(1)} %add_multiply_fusion.1), channel_id=1, source_target_pairs={{0,5},{1,4},{2,7},{3,6},{4,1},{5,0},{6,3},{7,2},{8,13},{9,12},{10,... | collective-permute-start | bytes 196616 | tf_op jit(solution)/shard_map/ppermute | solution.py:355
  66.4 6.3 %collective-permute-start.16 = (f32[64,256]{1,0:T(8,128)S(1)}, f32[64,256]{1,0:T(8,128)S(1)}, u32[]{:S(2)}, u32[]{:S(2)}) collective-permute-start(f32[64,256]{1,0:T(8,128)S(1)} %add_multiply_fusion.1), channel_id=1, source_target_pairs={{0,4},{1,5},{2,6},{3,7},{4,0},{5,1},{6,2},{7,3},{8,12},{9,13},{10,... | collective-permute-start | bytes 196616 | tf_op jit(solution)/shard_map/ppermute | solution.py:355
  68.7 4.3 %collective-permute-start.15 = (f32[64,256]{1,0:T(8,128)S(1)}, f32[64,256]{1,0:T(8,128)S(1)}, u32[]{:S(2)}, u32[]{:S(2)}) collective-permute-start(f32[64,256]{1,0:T(8,128)S(1)} %add_multiply_fusion.1), channel_id=1, source_target_pairs={{0,1},{1,0},{2,3},{3,2},{4,5},{5,4},{6,7},{7,6},{8,9},{9,8},{10,11... | collective-permute-start | bytes 196616 | tf_op jit(solution)/shard_map/ppermute | solution.py:355
  73.9 1.5 %collective-permute-start.19 = (f32[256,256]{1,0:T(8,128)S(1)}, f32[256,256]{1,0:T(8,128)S(1)}, u32[]{:S(2)}, u32[]{:S(2)}) collective-permute-start(f32[256,256]{1,0:T(8,128)S(1)} %pad_maximum_fusion.mine), channel_id=1, source_target_pairs={{0,2},{2,0},{4,6},{6,4},{8,10},{10,8},{12,14},{14,12},{16,18},{18,... | collective-permute-start | bytes 786440 | tf_op jit(solution)/shard_map/ppermute | solution.py:287

commit v10 on v9

--- a/solution.py
+++ b/solution.py
@@ -357,9 +357,10 @@
     def along_sub(x):
         return [x] + [exchange(x, "sub", k) for k in range(1, n)]
 
-    all_ids = along_sub(ids) + along_sub(exchange(upper, "dom", pair))
+    away_first = exchange(local, "dom", pair)
+    across, local = lax.optimization_barrier((exchange(upper, "dom", pair), local))
+    all_ids = along_sub(ids) + along_sub(across)
     near_slab = along_sub(local)
-    away_first = exchange(local, "dom", pair)
 
     plan, step_ids, negative_ids = pl.pallas_call(
         functools.partial(plan_kernel, n),

time: 77.3 us -> 80.9 us (1.047)
  Pallas kernels: 35 us -> 43.3 us
  waiting for transfers between devices: 16.5 us -> 13.7 us
  starting transfers between devices: 23.6 us -> 22.3 us
    pallas_call x9, Pallas kernels: 33.3 us -> 41.5 us  [call(): pl.pallas_call(kernel, in_specs=[in_smem] * len(scalars) + [in_vmem] * le...]
    ppermute x14, waiting for transfers between devices: 16.1 us -> 13.7 us  [exchange(): lax.ppermute(x, axis, [(i, i ^ mask) for i in range(lax.axis_size(axis))])]
    ppermute x14, starting transfers between devices: 16.5 us -> 15.2 us  [exchange(): lax.ppermute(x, axis, [(i, i ^ mask) for i in range(lax.axis_size(axis))])]
  transfers between devices with their start and end apart: 20 -> 20, of which waited for: 9 -> 6; matrix products, arithmetic and copies ran while one was open for 0% -> 0% of each run, Pallas kernels for 25% -> 29%
where the time goes in v10:
time: 80.9 us; the launch traced here: 81.3 us
  Pallas kernels  43.3 us (54%)
  starting transfers between devices  22.3 us (28%)
  waiting for transfers between devices  13.7 us (17%)
  between operations  1.55 us (2%)
    pallas_call x9, Pallas kernels, call(): pl.pallas_call(kernel, in_specs=[in_smem] * len(scalars) + [in_vmem] * le...  41.5 us
    ppermute x14, starting transfers between devices, exchange(): lax.ppermute(x, axis, [(i, i ^ mask) for i in range(lax.axis_size(axis))])  15.2 us
    ppermute x14, waiting for transfers between devices, exchange(): lax.ppermute(x, axis, [(i, i ^ mask) for i in range(lax.axis_size(axis))])  13.7 us
    ppermute x6, starting transfers between devices, to_peer(): return lax.ppermute(x, ('dom', 'sub'), pairs)  7.04 us
    pallas_call x1, Pallas kernels, on_device(): pl.pallas_call(functools.partial(plan_kernel, n), in_specs=[in_smem] + [i...  1.77 us
  transfers between devices with their start and end apart: 20, of which 6 were waited for; matrix products, arithmetic and copies ran while one was open for 0% of the time, Pallas kernels for 29%

profile of v10, /device:TPU:0, one launch (start us, length us, event | category | flops | bytes accessed | tf_op | source)
XLA Modules:
  0.0 81.3 jit_solution(1387548075946393187)
XLA Ops:
  1.3 0.8 %ids_kernel.1 = (s16[17,3,512]{2,1,0:T(4,128)(2,1)S(1)}, s16[9,3,512]{2,1,0:T(4,128)(2,1)S(1)}) custom-call(s32[1,1]{1,0:T(1,128)S(6)} %copy.12.count, s32[1,8192]{1,0:T(1,128)} %bitcast.13, s32[1,8192]{1,0:T(1,128)} %bitcast.14, s32[1,8192]{1,0:T(1,128)} %bitcast.15, s32[1,512]{1,0:T(1,128)} %bitcast.16), custom_call_target="tpu_custom_call" | custom-call | flops 2097152 | bytes 131072 | tf_op jit(solution)/shard_map/ids_kernel/pallas_call | solution.py:324
  2.1 4.1 %collective-permute-start.1 = (s16[9,3,512]{2,1,0:T(4,128)(2,1)S(1)}, s16[9,3,512]{2,1,0:T(4,128)(2,1)S(1)}, u32[]{:S(2)}, u32[]{:S(2)}) collective-permute-start(s16[9,3,512]{2,1,0:T(4,128)(2,1)S(1)} %get-tuple-element.47), channel_id=1, source_target_pairs={{0,16},{2,18},{4,20},{6,22},{8,24},{10,26},{12,28},{14,30},{16,0},... | collective-permute-start | bytes 82952 | tf_op jit(solution)/shard_map/ppermute | solution.py:287
  6.2 1.5 %collective-permute-start = (s16[17,3,512]{2,1,0:T(4,128)(2,1)S(1)}, s16[17,3,512]{2,1,0:T(4,128)(2,1)S(1)}, u32[]{:S(2)}, u32[]{:S(2)}) collective-permute-start(s16[17,3,512]{2,1,0:T(4,128)(2,1)S(1)} %get-tuple-element.46.refs_0_), channel_id=1, source_target_pairs={{0,1},{1,0},{2,3},{3,2},{4,5},{5,4},{6,7},{7,6},{8,9},{9,8},{10,11... | collective-permute-start | bytes 156680 | tf_op jit(solution)/shard_map/ppermute | solution.py:287
  7.7 1.2 %rows_kernel.1.refs_0_ = bf16[256,512]{1,0:T(8,128)(2,1)S(1)} custom-call(f32[512,256]{1,0:T(8,128)} %table.2), custom_call_target="tpu_custom_call" | custom-call | flops 2097152 | bytes 131072 | tf_op jit(solution)/shard_map/rows_kernel/pallas_call | solution.py:324
  8.9 0.4 collective-permute-start.3
  9.3 0.0 collective-permute-done.1.refs_2_
  9.3 1.0 %collective-permute-start.2 = (s16[9,3,512]{2,1,0:T(4,128)(2,1)S(1)}, s16[9,3,512]{2,1,0:T(4,128)(2,1)S(1)}, u32[]{:S(2)}, u32[]{:S(2)}) collective-permute-start(s16[9,3,512]{2,1,0:T(4,128)(2,1)S(1)} %collective-permute-done.1.refs_2_), channel_id=1, source_target_pairs={{0,1},{1,0},{2,3},{3,2},{4,5},{5,4},{6,7},{7,6},{8,9},{9,8},{10,11... | collective-permute-start | bytes 82952 | tf_op jit(solution)/shard_map/ppermute | solution.py:287
  10.3 0.1 pad_add_fusion.codes
  10.4 0.0 copy-start.1
  10.4 1.1 %collective-permute-start.4 = (bf16[256,512]{1,0:T(8,128)(2,1)S(1)}, bf16[256,512]{1,0:T(8,128)(2,1)S(1)}, u32[]{:S(2)}, u32[]{:S(2)}) collective-permute-start(bf16[256,512]{1,0:T(8,128)(2,1)S(1)} %rows_kernel.1.refs_0_), channel_id=1, source_target_pairs={{0,1},{1,0},{2,3},{3,2},{4,5},{5,4},{6,7},{7,6},{8,9},{9,8},{10,11... | collective-permute-start | bytes 786440 | tf_op jit(solution)/shard_map/ppermute | solution.py:287
  11.4 0.0 collective-permute-done.refs_1_
  11.4 2.3 %collective-permute-done.2.refs_3_ = s16[9,3,512]{2,1,0:T(4,128)(2,1)S(1)} collective-permute-done((s16[9,3,512]{2,1,0:T(4,128)(2,1)S(1)}, s16[9,3,512]{2,1,0:T(4,128)(2,1)S(1)}, u32[]{:S(2)}, u32[]{:S(2)}) %collective-permute-start.2) | collective-permute-done | bytes 27680 | tf_op jit(solution)/shard_map/ppermute | solution.py:287
  13.7 1.8 %plan_kernel.1 = (s32[37]{0:T(128)S(1)}, s32[16,3,512]{2,1,0:T(4,128)S(1)}, s32[4,1,512]{2,1,0:T(1,128)S(1)}) custom-call(s32[4]{0:T(128)S(1)} %pad_add_fusion.codes, s16[17,3,512]{2,1,0:T(4,128)(2,1)S(1)} %get-tuple-element.46.refs_0_, s16[17,3,512]{2,1,0:T(4,128)(2,1)S(1)} %collective-permute-done.refs_1_, ...), custom_call_target="tpu_custom_call" | custom-call | flops 34359738368 | bytes 2097152 | tf_op jit(solution)/shard_map/plan_kernel/pallas_call | solution.py:365
  15.5 7.5 %collective-permute-done.3.refs_2_ = bf16[256,512]{1,0:T(8,128)(2,1)S(1)} collective-permute-done((bf16[256,512]{1,0:T(8,128)(2,1)S(1)}, bf16[256,512]{1,0:T(8,128)(2,1)S(1)}, u32[]{:S(2)}, u32[]{:S(2)}) %collective-permute-start.3) | collective-permute-done | bytes 262176 | tf_op jit(solution)/shard_map/ppermute | solution.py:287
  23.0 0.5 collective-permute-start.5
  23.5 0.0 collective-permute-done.4.refs_1_
  23.5 0.0 copy-done.1
  23.5 6.5 %near_kernel.1 = (bf16[16,256,512]{2,1,0:T(8,128)(2,1)S(1)}, f32[16,256,512]{2,1,0:T(8,128)S(1)}) custom-call(s32[37]{0:T(128)S(1)} %get-tuple-element.78.plan, s32[16,3,512]{2,1,0:T(4,128)S(1)} %get-tuple-element.51.ids, f32[400,256]{1,0:T(8,128)S(1)} %copy-done.1, bf16[256,512]{1,0:T(8,128)(2,1)S(1)} %rows_kernel.1.refs_0_, ...), custom_call_target="tpu_custom_call" | custom-call | flops 4294967296 | bytes 131072 | tf_op jit(solution)/shard_map/near_kernel/pallas_call | solution.py:324
  30.0 0.2 collective-permute-done.5.refs_3_
  30.1 17.3 %edge_kernel.1 = (bf16[16,512,512]{2,1,0:T(8,128)(2,1)S(1)}, bf16[16,512,512]{2,1,0:T(8,128)(2,1)S(1)}, bf16[4,1024,256]{2,1,0:T(8,128)(2,1)S(1)}, f32[512,256]{...) custom-call(s32[4]{0:T(128)S(1)} %pad_add_fusion.codes, ...), custom_call_target="tpu_custom_call" | custom-call | flops 11811160064 | bytes 131072 | tf_op jit(solution)/shard_map/edge_kernel/pallas_call | solution.py:324
  47.4 0.1 collective-permute-start.6
  47.5 0.1 multiply_convert_fusion.2
  47.6 1.5 %collective-permute-done.6 = f32[256,256]{1,0:T(8,128)S(1)} collective-permute-done((f32[256,256]{1,0:T(8,128)S(1)}, f32[256,256]{1,0:T(8,128)S(1)}, u32[]{:S(2)}, u32[]{:S(2)}) %collective-permute-start.6) | collective-permute-done | bytes 262176 | tf_op jit(solution)/shard_map/ppermute | solution.py:287
  49.1 1.7 %collective-permute-start.7 = (f32[64,256]{1,0:T(8,128)S(1)}, f32[64,256]{1,0:T(8,128)S(1)}, u32[]{:S(2)}, u32[]{:S(2)}) collective-permute-start(f32[64,256]{1,0:T(8,128)S(1)} %get-tuple-element.65), channel_id=1, source_target_pairs={{0,1},{1,0},{2,3},{3,2},{4,5},{5,4},{6,7},{7,6},{8,9},{9,8},{10,11... | collective-permute-start | bytes 196616 | tf_op jit(solution)/shard_map/ppermute | solution.py:355
  50.8 0.0 collective-permute-start.8
  50.8 1.8 %collective-permute-start.9 = (f32[64,256]{1,0:T(8,128)S(1)}, f32[64,256]{1,0:T(8,128)S(1)}, u32[]{:S(2)}, u32[]{:S(2)}) collective-permute-start(f32[64,256]{1,0:T(8,128)S(1)} %get-tuple-element.67), channel_id=1, source_target_pairs={{0,5},{1,4},{2,7},{3,6},{4,1},{5,0},{6,3},{7,2},{8,13},{9,12},{10,... | collective-permute-start | bytes 196616 | tf_op jit(solution)/shard_map/ppermute | solution.py:355
  52.6 1.7 %collective-permute-start.13 = (f16[512,256]{1,0:T(8,128)(2,1)S(1)}, f16[512,256]{1,0:T(8,128)(2,1)S(1)}, u32[]{:S(2)}, u32[]{:S(2)}) collective-permute-start(f16[512,256]{1,0:T(8,128)(2,1)S(1)} %multiply_convert_fusion.2), channel_id=1, source_target_pairs={{0,1},{1,0},{2,3},{3,2},{4,5},{5,4},{6,7},{7,6},{8,9},{9,8},{10,11... | collective-permute-start | bytes 786440 | tf_op jit(solution)/shard_map/ppermute | solution.py:287
  54.3 4.9 %away_kernel.1 = f32[512,256]{1,0:T(8,128)S(1)} custom-call(s32[37]{0:T(128)S(1)} %get-tuple-element.78.plan, s32[16,3,512]{2,1,0:T(4,128)S(1)} %get-tuple-element.51.ids, s32[4,1,512]{2,1,0:T(1,128)S(1)} %get-tuple-element.52.negative_ids, bf16[16,512,512]{2,1,0:T(8,128)(2,1)S(1)} %get-tuple-element.69.grads, ...), custom_call_target="tpu_custom_call" | custom-call | bytes 131072 | tf_op jit(solution)/shard_map/away_kernel/pallas_call | solution.py:324
  59.2 0.0 collective-permute-done.7
  59.2 0.0 collective-permute-done.8
  59.2 0.0 collective-permute-done.9
  59.3 0.1 collective-permute-start.12
  59.3 0.1 collective-permute-start.11
  59.4 4.3 %collective-permute-start.10 = (f16[64,256]{1,0:T(8,128)(2,1)S(1)}, f16[64,256]{1,0:T(8,128)(2,1)S(1)}, u32[]{:S(2)}, u32[]{:S(2)}) collective-permute-start(f16[64,256]{1,0:T(8,128)(2,1)S(1)} %multiply_convert_fusion.3), channel_id=1, source_target_pairs={{0,8},{2,10},{4,12},{6,14},{8,0},{10,2},{12,4},{14,6},{16,24},{18,... | collective-permute-start | bytes 98312 | tf_op jit(solution)/shard_map/ppermute | solution.py:287
  63.7 4.0 %own_other_kernel.1 = f32[512,256]{1,0:T(8,128)S(1)} custom-call(s32[37]{0:T(128)S(1)} %get-tuple-element.78.plan, s32[16,3,512]{2,1,0:T(4,128)S(1)} %get-tuple-element.51.ids, s32[4,1,512]{2,1,0:T(1,128)S(1)} %get-tuple-element.52.negative_ids, bf16[16,512,512]{2,1,0:T(8,128)(2,1)S(1)} %get-tuple-element.75.grads, ...), custom_call_target="tpu_custom_call" | custom-call | bytes 131072 | tf_op jit(solution)/shard_map/own_other_kernel/pallas_call | solution.py:324
  67.7 0.0 copy-start
  67.8 0.0 copy-start.2
  67.8 0.0 copy-start.3
  67.8 0.1 multiply_convert_fusion
  67.8 0.0 collective-permute-done.12
  67.8 0.0 collective-permute-done.11
  67.9 0.0 collective-permute-done.10
  67.9 0.0 collective-permute-done.13
  67.9 0.1 multiply_convert_fusion.1
  68.0 0.1 collective-permute-start.14
  68.1 0.4 collective-permute-start.18
  68.5 0.0 collective-permute-start.17
  68.5 3.1 %collective-permute-start.16 = (f32[64,256]{1,0:T(8,128)S(1)}, f32[64,256]{1,0:T(8,128)S(1)}, u32[]{:S(2)}, u32[]{:S(2)}) collective-permute-start(f32[64,256]{1,0:T(8,128)S(1)} %add_multiply_fusion.1), channel_id=1, source_target_pairs={{0,4},{1,5},{2,6},{3,7},{4,0},{5,1},{6,2},{7,3},{8,12},{9,13},{10,... | collective-permute-start | bytes 196616 | tf_op jit(solution)/shard_map/ppermute | solution.py:355
  71.7 0.3 collective-permute-start.15
  72.0 4.0 %own_kernel.1.own = f32[512,256]{1,0:T(8,128)S(1)} custom-call(s32[37]{0:T(128)S(1)} %get-tuple-element.78.plan, s32[16,3,512]{2,1,0:T(4,128)S(1)} %get-tuple-element.51.ids, s32[4,1,512]{2,1,0:T(1,128)S(1)} %get-tuple-element.52.negative_ids, bf16[16,512,512]{2,1,0:T(8,128)(2,1)S(1)} %get-tuple-element.75.grads, ...), custom_call_target="tpu_custom_call" | custom-call | bytes 131072 | tf_op jit(solution)/shard_map/own_kernel/pallas_call | solution.py:324
  76.0 0.0 collective-permute-done.17
  76.0 0.0 collective-permute-done.16
  76.0 0.0 collective-permute-done.15
  76.1 2.0 %collective-permute-done.14 = f16[512,256]{1,0:T(8,128)(2,1)S(1)} collective-permute-done((f16[512,256]{1,0:T(8,128)(2,1)S(1)}, f16[512,256]{1,0:T(8,128)(2,1)S(1)}, u32[]{:S(2)}, u32[]{:S(2)}) %collective-permute-start.14) | collective-permute-done | bytes 262176 | tf_op jit(solution)/shard_map/ppermute | solution.py:287
  78.1 0.0 collective-permute-start.19
  78.1 0.0 collective-permute-done.18
  78.1 0.1 add_multiply_fusion.returned
  78.2 0.0 copy-done
  78.2 0.0 copy-done.2
  78.2 1.2 %entity_kernel.1 = (f32[512,256]{1,0:T(8,128)}, f32[1,512]{1,0:T(1,128)}) custom-call(f32[512,256]{1,0:T(8,128)S(1)} %copy-done, f32[1,512]{1,0:T(1,128)S(1)} %bitcast.11, f32[512,256]{1,0:T(8,128)S(1)} %add_multiply_fusion.returned, f32[512,256]{1,0:T(8,128)S(1)} %own_kernel.1.own), custom_call_target="tpu_custom_call" | custom-call | flops 2097152 | bytes 131072 | tf_op jit(solution)/shard_map/entity_kernel/pallas_call | solution.py:324
  79.4 0.3 collective-permute-done.19.theirs
  79.7 0.0 copy-done.3
  79.7 1.6 %relation_kernel.1 = f32[400,256]{1,0:T(8,128)} custom-call(s32[4]{0:T(128)S(1)} %pad_add_fusion.codes, f32[400,256]{1,0:T(8,128)S(1)} %copy-done.1, f32[1,400]{1,0:T(1,128)S(1)} %bitcast.12, f32[256,256]{1,0:T(8,128)S(1)} %pad_maximum_fusion.mine, f32[256,256]{1,0:T(8,128)S(1)} %collective-permute-done.19.theirs), custom_call_target="tpu_custom_call" | custom-call | bytes 131072 | tf_op jit(solution)/shard_map/relation_kernel/pallas_call | solution.py:324
  (4 shorter events, 0.1 us)
Async XLA Ops:
  2.1 7.2 %collective-permute-start.1 = (s16[9,3,512]{2,1,0:T(4,128)(2,1)S(1)}, s16[9,3,512]{2,1,0:T(4,128)(2,1)S(1)}, u32[]{:S(2)}, u32[]{:S(2)}) collective-permute-start(s16[9,3,512]{2,1,0:T(4,128)(2,1)S(1)} %get-tuple-element.47), channel_id=1, source_target_pairs={{0,16},{2,18},{4,20},{6,22},{8,24},{10,26},{12,28},{14,30},{16,0},... | collective-permute-start | bytes 82952 | tf_op jit(solution)/shard_map/ppermute | solution.py:287
  6.2 5.2 %collective-permute-start = (s16[17,3,512]{2,1,0:T(4,128)(2,1)S(1)}, s16[17,3,512]{2,1,0:T(4,128)(2,1)S(1)}, u32[]{:S(2)}, u32[]{:S(2)}) collective-permute-start(s16[17,3,512]{2,1,0:T(4,128)(2,1)S(1)} %get-tuple-element.46.refs_0_), channel_id=1, source_target_pairs={{0,1},{1,0},{2,3},{3,2},{4,5},{5,4},{6,7},{7,6},{8,9},{9,8},{10,11... | collective-permute-start | bytes 156680 | tf_op jit(solution)/shard_map/ppermute | solution.py:287
  8.9 14.1 %collective-permute-start.3 = (bf16[256,512]{1,0:T(8,128)(2,1)S(1)}, bf16[256,512]{1,0:T(8,128)(2,1)S(1)}, u32[]{:S(2)}, u32[]{:S(2)}) collective-permute-start(bf16[256,512]{1,0:T(8,128)(2,1)S(1)} %rows_kernel.1.refs_0_), channel_id=1, source_target_pairs={{0,16},{2,18},{4,20},{6,22},{8,24},{10,26},{12,28},{14,30},{16,0},... | collective-permute-start | bytes 786440 | tf_op jit(solution)/shard_map/ppermute | solution.py:287
  9.3 4.4 %collective-permute-start.2 = (s16[9,3,512]{2,1,0:T(4,128)(2,1)S(1)}, s16[9,3,512]{2,1,0:T(4,128)(2,1)S(1)}, u32[]{:S(2)}, u32[]{:S(2)}) collective-permute-start(s16[9,3,512]{2,1,0:T(4,128)(2,1)S(1)} %collective-permute-done.1.refs_2_), channel_id=1, source_target_pairs={{0,1},{1,0},{2,3},{3,2},{4,5},{5,4},{6,7},{7,6},{8,9},{9,8},{10,11... | collective-permute-start | bytes 82952 | tf_op jit(solution)/shard_map/ppermute | solution.py:287
  10.4 13.1 %copy-start.1 = (f32[400,256]{1,0:T(8,128)S(1)}, f32[400,256]{1,0:T(8,128)}, u32[]{:S(2)}) copy-start(f32[400,256]{1,0:T(8,128)} %relations.3) | copy-start | bytes 1228804
  10.4 13.1 %collective-permute-start.4 = (bf16[256,512]{1,0:T(8,128)(2,1)S(1)}, bf16[256,512]{1,0:T(8,128)(2,1)S(1)}, u32[]{:S(2)}, u32[]{:S(2)}) collective-permute-start(bf16[256,512]{1,0:T(8,128)(2,1)S(1)} %rows_kernel.1.refs_0_), channel_id=1, source_target_pairs={{0,1},{1,0},{2,3},{3,2},{4,5},{5,4},{6,7},{7,6},{8,9},{9,8},{10,11... | collective-permute-start | bytes 786440 | tf_op jit(solution)/shard_map/ppermute | solution.py:287
  23.0 7.1 %collective-permute-start.5 = (bf16[256,512]{1,0:T(8,128)(2,1)S(1)}, bf16[256,512]{1,0:T(8,128)(2,1)S(1)}, u32[]{:S(2)}, u32[]{:S(2)}) collective-permute-start(bf16[256,512]{1,0:T(8,128)(2,1)S(1)} %collective-permute-done.3.refs_2_), channel_id=1, source_target_pairs={{0,1},{1,0},{2,3},{3,2},{4,5},{5,4},{6,7},{7,6},{8,9},{9,8},{10,11... | collective-permute-start | bytes 786440 | tf_op jit(solution)/shard_map/ppermute | solution.py:287
  47.4 1.6 %collective-permute-start.6 = (f32[256,256]{1,0:T(8,128)S(1)}, f32[256,256]{1,0:T(8,128)S(1)}, u32[]{:S(2)}, u32[]{:S(2)}) collective-permute-start(f32[256,256]{1,0:T(8,128)S(1)} %get-tuple-element.59), channel_id=1, source_target_pairs={{0,2},{2,0},{4,6},{6,4},{8,10},{10,8},{12,14},{14,12},{16,18},{18,... | collective-permute-start | bytes 786440 | tf_op jit(solution)/shard_map/ppermute | solution.py:287
  49.1 10.1 %collective-permute-start.7 = (f32[64,256]{1,0:T(8,128)S(1)}, f32[64,256]{1,0:T(8,128)S(1)}, u32[]{:S(2)}, u32[]{:S(2)}) collective-permute-start(f32[64,256]{1,0:T(8,128)S(1)} %get-tuple-element.65), channel_id=1, source_target_pairs={{0,1},{1,0},{2,3},{3,2},{4,5},{5,4},{6,7},{7,6},{8,9},{9,8},{10,11... | collective-permute-start | bytes 196616 | tf_op jit(solution)/shard_map/ppermute | solution.py:355
  50.8 8.4 %collective-permute-start.8 = (f32[64,256]{1,0:T(8,128)S(1)}, f32[64,256]{1,0:T(8,128)S(1)}, u32[]{:S(2)}, u32[]{:S(2)}) collective-permute-start(f32[64,256]{1,0:T(8,128)S(1)} %get-tuple-element.66), channel_id=1, source_target_pairs={{0,4},{1,5},{2,6},{3,7},{4,0},{5,1},{6,2},{7,3},{8,12},{9,13},{10,... | collective-permute-start | bytes 196616 | tf_op jit(solution)/shard_map/ppermute | solution.py:355
  50.8 8.4 %collective-permute-start.9 = (f32[64,256]{1,0:T(8,128)S(1)}, f32[64,256]{1,0:T(8,128)S(1)}, u32[]{:S(2)}, u32[]{:S(2)}) collective-permute-start(f32[64,256]{1,0:T(8,128)S(1)} %get-tuple-element.67), channel_id=1, source_target_pairs={{0,5},{1,4},{2,7},{3,6},{4,1},{5,0},{6,3},{7,2},{8,13},{9,12},{10,... | collective-permute-start | bytes 196616 | tf_op jit(solution)/shard_map/ppermute | solution.py:355
  52.6 15.3 %collective-permute-start.13 = (f16[512,256]{1,0:T(8,128)(2,1)S(1)}, f16[512,256]{1,0:T(8,128)(2,1)S(1)}, u32[]{:S(2)}, u32[]{:S(2)}) collective-permute-start(f16[512,256]{1,0:T(8,128)(2,1)S(1)} %multiply_convert_fusion.2), channel_id=1, source_target_pairs={{0,1},{1,0},{2,3},{3,2},{4,5},{5,4},{6,7},{7,6},{8,9},{9,8},{10,11... | collective-permute-start | bytes 786440 | tf_op jit(solution)/shard_map/ppermute | solution.py:287
  59.3 8.6 %collective-permute-start.12 = (f16[64,256]{1,0:T(8,128)(2,1)S(1)}, f16[64,256]{1,0:T(8,128)(2,1)S(1)}, u32[]{:S(2)}, u32[]{:S(2)}) collective-permute-start(f16[64,256]{1,0:T(8,128)(2,1)S(1)} %multiply_convert_fusion.3), channel_id=1, source_target_pairs={{0,24},{2,26},{4,28},{6,30},{8,16},{10,18},{12,20},{14,22},{16,8},... | collective-permute-start | bytes 98312 | tf_op jit(solution)/shard_map/ppermute | solution.py:287
  59.3 8.5 %collective-permute-start.11 = (f16[64,256]{1,0:T(8,128)(2,1)S(1)}, f16[64,256]{1,0:T(8,128)(2,1)S(1)}, u32[]{:S(2)}, u32[]{:S(2)}) collective-permute-start(f16[64,256]{1,0:T(8,128)(2,1)S(1)} %multiply_convert_fusion.3), channel_id=1, source_target_pairs={{0,16},{2,18},{4,20},{6,22},{8,24},{10,26},{12,28},{14,30},{16,0},... | collective-permute-start | bytes 98312 | tf_op jit(solution)/shard_map/ppermute | solution.py:287
  59.4 8.5 %collective-permute-start.10 = (f16[64,256]{1,0:T(8,128)(2,1)S(1)}, f16[64,256]{1,0:T(8,128)(2,1)S(1)}, u32[]{:S(2)}, u32[]{:S(2)}) collective-permute-start(f16[64,256]{1,0:T(8,128)(2,1)S(1)} %multiply_convert_fusion.3), channel_id=1, source_target_pairs={{0,8},{2,10},{4,12},{6,14},{8,0},{10,2},{12,4},{14,6},{16,24},{18,... | collective-permute-start | bytes 98312 | tf_op jit(solution)/shard_map/ppermute | solution.py:287
  67.7 10.5 %copy-start = (f32[512,256]{1,0:T(8,128)S(1)}, f32[512,256]{1,0:T(8,128)}, u32[]{:S(2)}) copy-start(f32[512,256]{1,0:T(8,128)} %table.2) | copy-start | bytes 1572868
  67.8 10.5 %copy-start.2 = (f32[512]{0:T(512)S(1)}, f32[512]{0:T(512)}, u32[]{:S(2)}) copy-start(f32[512]{0:T(512)} %param.10) | copy-start | bytes 6148
  67.8 11.9 %copy-start.3 = (f32[400]{0:T(512)S(1)}, f32[400]{0:T(512)}, u32[]{:S(2)}) copy-start(f32[400]{0:T(512)} %param.12) | copy-start | bytes 4804
  68.0 10.1 %collective-permute-start.14 = (f16[512,256]{1,0:T(8,128)(2,1)S(1)}, f16[512,256]{1,0:T(8,128)(2,1)S(1)}, u32[]{:S(2)}, u32[]{:S(2)}) collective-permute-start(f16[512,256]{1,0:T(8,128)(2,1)S(1)} %multiply_convert_fusion.1), channel_id=1, source_target_pairs={{0,16},{2,18},{4,20},{6,22},{8,24},{10,26},{12,28},{14,30},{16,0},... | collective-permute-start | bytes 786440 | tf_op jit(solution)/shard_map/ppermute | solution.py:287
  68.1 10.0 %collective-permute-start.18 = (f16[512,256]{1,0:T(8,128)(2,1)S(1)}, f16[512,256]{1,0:T(8,128)(2,1)S(1)}, u32[]{:S(2)}, u32[]{:S(2)}) collective-permute-start(f16[512,256]{1,0:T(8,128)(2,1)S(1)} %multiply_convert_fusion), channel_id=1, source_target_pairs={{0,1},{1,0},{2,3},{3,2},{4,5},{5,4},{6,7},{7,6},{8,9},{9,8},{10,11... | collective-permute-start | bytes 786440 | tf_op jit(solution)/shard_map/ppermute | solution.py:287
  68.5 7.5 %collective-permute-start.17 = (f32[64,256]{1,0:T(8,128)S(1)}, f32[64,256]{1,0:T(8,128)S(1)}, u32[]{:S(2)}, u32[]{:S(2)}) collective-permute-start(f32[64,256]{1,0:T(8,128)S(1)} %add_multiply_fusion.1), channel_id=1, source_target_pairs={{0,5},{1,4},{2,7},{3,6},{4,1},{5,0},{6,3},{7,2},{8,13},{9,12},{10,... | collective-permute-start | bytes 196616 | tf_op jit(solution)/shard_map/ppermute | solution.py:355
  68.5 7.5 %collective-permute-start.16 = (f32[64,256]{1,0:T(8,128)S(1)}, f32[64,256]{1,0:T(8,128)S(1)}, u32[]{:S(2)}, u32[]{:S(2)}) collective-permute-start(f32[64,256]{1,0:T(8,128)S(1)} %add_multiply_fusion.1), channel_id=1, source_target_pairs={{0,4},{1,5},{2,6},{3,7},{4,0},{5,1},{6,2},{7,3},{8,12},{9,13},{10,... | collective-permute-start | bytes 196616 | tf_op jit(solution)/shard_map/ppermute | solution.py:355
  71.7 4.4 %collective-permute-start.15 = (f32[64,256]{1,0:T(8,128)S(1)}, f32[64,256]{1,0:T(8,128)S(1)}, u32[]{:S(2)}, u32[]{:S(2)}) collective-permute-start(f32[64,256]{1,0:T(8,128)S(1)} %add_multiply_fusion.1), channel_id=1, source_target_pairs={{0,1},{1,0},{2,3},{3,2},{4,5},{5,4},{6,7},{7,6},{8,9},{9,8},{10,11... | collective-permute-start | bytes 196616 | tf_op jit(solution)/shard_map/ppermute | solution.py:355
  78.1 1.5 %collective-permute-start.19 = (f32[256,256]{1,0:T(8,128)S(1)}, f32[256,256]{1,0:T(8,128)S(1)}, u32[]{:S(2)}, u32[]{:S(2)}) collective-permute-start(f32[256,256]{1,0:T(8,128)S(1)} %pad_maximum_fusion.mine), channel_id=1, source_target_pairs={{0,2},{2,0},{4,6},{6,4},{8,10},{10,8},{12,14},{14,12},{16,18},{18,... | collective-permute-start | bytes 786440 | tf_op jit(solution)/shard_map/ppermute | solution.py:287

commit v11 on v8

--- a/solution.py
+++ b/solution.py
@@ -256,18 +256,28 @@
     new_state[...] = jnp.broadcast_to(after, (table.shape[0], lanes)).T[:1]
 
 
-def relation_kernel(chunk, codes, relations, state, mine, theirs, out, grad, column):
-    chunks = mine.shape[0] // chunk
-    for k in range(2 * chunks):
-        part = (mine, theirs)[k // chunks]
-        start = (k % chunks) * chunk
-        grad[pl.ds(pl.multiple_of(codes[2] ^ (k * chunk), chunk), chunk), :] = part[start : start + chunk, :]
+def update_chunks(chunk, first, codes, grads, column, rows):
+    for k in range(grads.shape[0] // chunk):
+        at = pl.ds(pl.multiple_of(codes[2] ^ ((first + k) * chunk), chunk), chunk)
+        g = grads[k * chunk : (k + 1) * chunk, :]
+        total = column[at, :1] + jnp.mean(g * g, axis=-1, keepdims=True)
+        rows[at, :] = rows[at, :] - learn_rate * g / jnp.sqrt(total)
+
+
+def relation_mine_kernel(chunk, codes, relations, state, mine, rows, column, wide):
     count = relations.shape[0]
-    column[...] = jnp.ones_like(column)
-    column[:, :count] = jnp.broadcast_to(state[...], (column.shape[0], count))
-    g = grad[:count, :]
-    total = column[...].T[:count, :1] + jnp.mean(g * g, axis=-1, keepdims=True)
-    out[...] = relations[...] - learn_rate * g / jnp.sqrt(total)
+    wide[...] = jnp.ones_like(wide)
+    wide[:, :count] = jnp.broadcast_to(state[...], (wide.shape[0], count))
+    column[...] = wide[...].T
+    rows[...] = jnp.zeros_like(rows)
+    rows[:count, :] = relations[...]
+    update_chunks(chunk, 0, codes, mine, column, rows)
+
+
+def relation_theirs_kernel(chunk, codes, before, column, theirs, out, rows):
+    rows[...] = before[...]
+    update_chunks(chunk, theirs.shape[0] // chunk, codes, theirs, column, rows)
+    out[...] = rows[: out.shape[0], :]
 
 
 def exchange(x, axis, mask):
@@ -438,16 +448,25 @@
     near_received = [widen(exchange(near_other[k - 1], "sub", k)) for k in range(1, n)]
     mine = jnp.concatenate([chunk_total] + [to_chip(chunk_total, k) for k in range(1, chips)], axis=0)
     (near_sum,) = scatter("own_kernel", 0, 0, 1, n, plan, near_grad)
-    returned, mine, near_sum = lax.optimization_barrier((returned, mine, near_sum))
+    half_done, column = call(
+        functools.partial(relation_mine_kernel, chunk),
+        "relation_mine_kernel",
+        [((rel_rows, dims), f32), ((rel_rows, 128), f32)],
+        [pltpu.VMEM((128, rel_rows), f32)],
+        0,
+        (codes,),
+        (relations, relation_state.reshape(1, -1), mine),
+    )
+    returned, mine, near_sum, half_done = lax.optimization_barrier((returned, mine, near_sum, half_done))
     theirs = exchange(mine, "dom", 1)
     (new_relations,) = call(
-        functools.partial(relation_kernel, chunk),
-        "relation_kernel",
+        functools.partial(relation_theirs_kernel, chunk),
+        "relation_theirs_kernel",
         [(relations.shape, f32)],
-        [pltpu.VMEM((rel_rows, dims), f32), pltpu.VMEM((128, rel_rows), f32)],
+        [pltpu.VMEM((rel_rows, dims), f32)],
         0,
         (codes,),
-        (relations, relation_state.reshape(1, -1), mine, theirs),
+        (half_done, column, theirs),
         held=False,
     )
     returned = widen(returned)

time: 79.8 us -> 83.6 us (1.048)
  waiting for transfers between devices: 19.8 us -> 24.1 us
  starting transfers between devices: 30.9 us -> 28.8 us
    ppermute x14, waiting for transfers between devices: 17.1 us -> 23.3 us  [exchange(): lax.ppermute(x, axis, [(i, i ^ mask) for i in range(lax.axis_size(axis))])]
    ppermute x14, starting transfers between devices: 23.3 us -> 20.3 us  [exchange(): lax.ppermute(x, axis, [(i, i ^ mask) for i in range(lax.axis_size(axis))])]
    ppermute x6, waiting for transfers between devices: 2.71 us -> 0.77 us  [to_peer(): return lax.ppermute(x, ('dom', 'sub'), pairs)]
    ppermute x6, starting transfers between devices: 7.6 us -> 8.55 us  [to_peer(): return lax.ppermute(x, ('dom', 'sub'), pairs)]
    pallas_call x9 -> x10, Pallas kernels: 26.6 us -> 27.4 us  [call(): pl.pallas_call(kernel, in_specs=[in_smem] * len(scalars) + [in_vmem] * le...]
  transfers between devices with their start and end apart: 20 -> 20, of which waited for: 10 -> 9; matrix products, arithmetic and copies ran while one was open for 0% -> 0% of each run, Pallas kernels for 20% -> 20%
where the time goes in v11:
time: 83.6 us; the launch traced here: 83.9 us
  Pallas kernels  29 us (35%)
  starting transfers between devices  28.8 us (34%)
  waiting for transfers between devices  24.1 us (29%)
  between operations  1.53 us (2%)
    pallas_call x10, Pallas kernels, call(): pl.pallas_call(kernel, in_specs=[in_smem] * len(scalars) + [in_vmem] * le...  27.4 us
    ppermute x14, waiting for transfers between devices, exchange(): lax.ppermute(x, axis, [(i, i ^ mask) for i in range(lax.axis_size(axis))])  23.3 us
    ppermute x14, starting transfers between devices, exchange(): lax.ppermute(x, axis, [(i, i ^ mask) for i in range(lax.axis_size(axis))])  20.3 us
    ppermute x6, starting transfers between devices, to_peer(): return lax.ppermute(x, ('dom', 'sub'), pairs)  8.55 us
  transfers between devices with their start and end apart: 20, of which 9 were waited for; matrix products, arithmetic and copies ran while one was open for 0% of the time, Pallas kernels for 20%

profile of v11, /device:TPU:0, one launch (start us, length us, event | category | flops | bytes accessed | tf_op | source)
XLA Modules:
  0.0 83.9 jit_solution(2549855116465044115)
XLA Ops:
  1.3 0.8 ids_kernel.1.refs_0_
  2.1 4.1 %collective-permute-start.1 = (s16[17,3,512]{2,1,0:T(4,128)(2,1)S(1)}, s16[17,3,512]{2,1,0:T(4,128)(2,1)S(1)}, u32[]{:S(2)}, u32[]{:S(2)}) collective-permute-start(s16[17,3,512]{2,1,0:T(4,128)(2,1)S(1)} %ids_kernel.1.refs_0_), channel_id=1, source_target_pairs={{0,16},{2,18},{4,20},{6,22},{8,24},{10,26},{12,28},{14,30},{16,0},... | collective-permute-start | bytes 156680 | tf_op jit(solution)/shard_map/ppermute | solution.py:284
  6.2 1.5 %collective-permute-start = (s16[17,3,512]{2,1,0:T(4,128)(2,1)S(1)}, s16[17,3,512]{2,1,0:T(4,128)(2,1)S(1)}, u32[]{:S(2)}, u32[]{:S(2)}) collective-permute-start(s16[17,3,512]{2,1,0:T(4,128)(2,1)S(1)} %ids_kernel.1.refs_0_), channel_id=1, source_target_pairs={{0,1},{1,0},{2,3},{3,2},{4,5},{5,4},{6,7},{7,6},{8,9},{9,8},{10,11... | collective-permute-start | bytes 156680 | tf_op jit(solution)/shard_map/ppermute | solution.py:284
  7.7 1.2 %rows_kernel.1.refs_0_ = bf16[256,512]{1,0:T(8,128)(2,1)S(1)} custom-call(f32[512,256]{1,0:T(8,128)} %table.2), custom_call_target="tpu_custom_call" | custom-call | flops 2097152 | bytes 131072 | tf_op jit(solution)/shard_map/rows_kernel/pallas_call | solution.py:321
  8.9 0.6 collective-permute-start.4
  9.5 0.1 collective-permute-start.3
  9.6 0.4 collective-permute-done.1.refs_2_
  10.0 1.7 %collective-permute-start.2 = (s16[17,3,512]{2,1,0:T(4,128)(2,1)S(1)}, s16[17,3,512]{2,1,0:T(4,128)(2,1)S(1)}, u32[]{:S(2)}, u32[]{:S(2)}) collective-permute-start(s16[17,3,512]{2,1,0:T(4,128)(2,1)S(1)} %collective-permute-done.1.refs_2_), channel_id=1, source_target_pairs={{0,1},{1,0},{2,3},{3,2},{4,5},{5,4},{6,7},{7,6},{8,9},{9,8},{10,11... | collective-permute-start | bytes 156680 | tf_op jit(solution)/shard_map/ppermute | solution.py:284
  11.7 0.1 pad_add_fusion.codes
  11.8 0.0 copy-start.1
  11.8 0.0 collective-permute-done.refs_1_
  11.8 6.2 %collective-permute-done.2.refs_3_ = s16[17,3,512]{2,1,0:T(4,128)(2,1)S(1)} collective-permute-done((s16[17,3,512]{2,1,0:T(4,128)(2,1)S(1)}, s16[17,3,512]{2,1,0:T(4,128)(2,1)S(1)}, u32[]{:S(2)}, u32[]{:S(2)}) %collective-permute-start.2) | collective-permute-done | bytes 52256 | tf_op jit(solution)/shard_map/ppermute | solution.py:284
  18.0 1.5 %plan_kernel.1 = (s32[37]{0:T(128)S(1)}, s32[16,3,512]{2,1,0:T(4,128)S(1)}, s32[4,1,512]{2,1,0:T(1,128)S(1)}) custom-call(s32[3]{0:T(128)S(1)} %pad_add_fusion.codes, s16[17,3,512]{2,1,0:T(4,128)(2,1)S(1)} %ids_kernel.1.refs_0_, s16[17,3,512]{2,1,0:T(4,128)(2,1)S(1)} %collective-permute-done.refs_1_, s16[17,3,512]{2,1,0:T(4,128)(2,1)S(1)} %collective-permute-done.1.refs_2_, ...), custom_call_target="tpu_custom_call" | custom-call | flops 34359738368 | bytes 2097152 | tf_op jit(solution)/shard_map/plan_kernel/pallas_call | solution.py:361
  19.5 3.7 %collective-permute-done.3.refs_2_ = bf16[256,512]{1,0:T(8,128)(2,1)S(1)} collective-permute-done((bf16[256,512]{1,0:T(8,128)(2,1)S(1)}, bf16[256,512]{1,0:T(8,128)(2,1)S(1)}, u32[]{:S(2)}, u32[]{:S(2)}) %collective-permute-start.3) | collective-permute-done | bytes 262176 | tf_op jit(solution)/shard_map/ppermute | solution.py:284
  23.2 1.5 %collective-permute-start.5 = (bf16[256,512]{1,0:T(8,128)(2,1)S(1)}, bf16[256,512]{1,0:T(8,128)(2,1)S(1)}, u32[]{:S(2)}, u32[]{:S(2)}) collective-permute-start(bf16[256,512]{1,0:T(8,128)(2,1)S(1)} %collective-permute-done.3.refs_2_), channel_id=1, source_target_pairs={{0,1},{1,0},{2,3},{3,2},{4,5},{5,4},{6,7},{7,6},{8,9},{9,8},{10,11... | collective-permute-start | bytes 786440 | tf_op jit(solution)/shard_map/ppermute | solution.py:284
  24.7 0.0 collective-permute-done.4.refs_1_
  24.7 0.0 copy-done.1
  24.7 4.0 %near_kernel.1 = (bf16[16,256,512]{2,1,0:T(8,128)(2,1)S(1)}, f32[16,256,512]{2,1,0:T(8,128)S(1)}) custom-call(s32[37]{0:T(128)S(1)} %get-tuple-element.71.plan, s32[16,3,512]{2,1,0:T(4,128)S(1)} %get-tuple-element.44.ids, f32[400,256]{1,0:T(8,128)S(1)} %copy-done.1, bf16[256,512]{1,0:T(8,128)(2,1)S(1)} %rows_kernel.1.refs_0_, ...), custom_call_target="tpu_custom_call" | custom-call | flops 4294967296 | bytes 131072 | tf_op jit(solution)/shard_map/near_kernel/pallas_call | solution.py:321
  28.7 1.6 %collective-permute-done.5.refs_3_ = bf16[256,512]{1,0:T(8,128)(2,1)S(1)} collective-permute-done((bf16[256,512]{1,0:T(8,128)(2,1)S(1)}, bf16[256,512]{1,0:T(8,128)(2,1)S(1)}, u32[]{:S(2)}, u32[]{:S(2)}) %collective-permute-start.5) | collective-permute-done | bytes 262176 | tf_op jit(solution)/shard_map/ppermute | solution.py:284
  30.4 9.8 %edge_kernel.1 = (bf16[16,512,512]{2,1,0:T(8,128)(2,1)S(1)}, bf16[16,512,512]{2,1,0:T(8,128)(2,1)S(1)}, bf16[4,1024,256]{2,1,0:T(8,128)(2,1)S(1)}, f32[512,256]{...) custom-call(s32[3]{0:T(128)S(1)} %pad_add_fusion.codes, ...), custom_call_target="tpu_custom_call" | custom-call | flops 11811160064 | bytes 131072 | tf_op jit(solution)/shard_map/edge_kernel/pallas_call | solution.py:321
  40.2 0.1 collective-permute-start.6
  40.2 0.1 multiply_convert_fusion.2
  40.3 1.5 %collective-permute-done.6 = f32[256,256]{1,0:T(8,128)S(1)} collective-permute-done((f32[256,256]{1,0:T(8,128)S(1)}, f32[256,256]{1,0:T(8,128)S(1)}, u32[]{:S(2)}, u32[]{:S(2)}) %collective-permute-start.6) | collective-permute-done | bytes 262176 | tf_op jit(solution)/shard_map/ppermute | solution.py:284
  41.8 2.6 %collective-permute-start.7 = (f32[64,256]{1,0:T(8,128)S(1)}, f32[64,256]{1,0:T(8,128)S(1)}, u32[]{:S(2)}, u32[]{:S(2)}) collective-permute-start(f32[64,256]{1,0:T(8,128)S(1)} %get-tuple-element.58), channel_id=1, source_target_pairs={{0,1},{1,0},{2,3},{3,2},{4,5},{5,4},{6,7},{7,6},{8,9},{9,8},{10,11... | collective-permute-start | bytes 196616 | tf_op jit(solution)/shard_map/ppermute | solution.py:352
  44.4 2.4 %collective-permute-start.8 = (f32[64,256]{1,0:T(8,128)S(1)}, f32[64,256]{1,0:T(8,128)S(1)}, u32[]{:S(2)}, u32[]{:S(2)}) collective-permute-start(f32[64,256]{1,0:T(8,128)S(1)} %get-tuple-element.59), channel_id=1, source_target_pairs={{0,4},{1,5},{2,6},{3,7},{4,0},{5,1},{6,2},{7,3},{8,12},{9,13},{10,... | collective-permute-start | bytes 196616 | tf_op jit(solution)/shard_map/ppermute | solution.py:352
  46.8 0.0 collective-permute-start.9
  46.8 1.5 %collective-permute-start.13 = (f16[512,256]{1,0:T(8,128)(2,1)S(1)}, f16[512,256]{1,0:T(8,128)(2,1)S(1)}, u32[]{:S(2)}, u32[]{:S(2)}) collective-permute-start(f16[512,256]{1,0:T(8,128)(2,1)S(1)} %multiply_convert_fusion.2), channel_id=1, source_target_pairs={{0,1},{1,0},{2,3},{3,2},{4,5},{5,4},{6,7},{7,6},{8,9},{9,8},{10,11... | collective-permute-start | bytes 786440 | tf_op jit(solution)/shard_map/ppermute | solution.py:284
  48.3 3.0 %away_kernel.1 = f32[512,256]{1,0:T(8,128)S(1)} custom-call(s32[37]{0:T(128)S(1)} %get-tuple-element.71.plan, s32[16,3,512]{2,1,0:T(4,128)S(1)} %get-tuple-element.44.ids, s32[4,1,512]{2,1,0:T(1,128)S(1)} %get-tuple-element.45.negative_ids, bf16[16,512,512]{2,1,0:T(8,128)(2,1)S(1)} %get-tuple-element.62.grads, ...), custom_call_target="tpu_custom_call" | custom-call | bytes 131072 | tf_op jit(solution)/shard_map/away_kernel/pallas_call | solution.py:321
  51.2 0.0 collective-permute-done.7
  51.2 0.0 collective-permute-done.8
  51.3 0.8 collective-permute-done.9
  52.0 6.1 %collective-permute-start.12 = (f16[64,256]{1,0:T(8,128)(2,1)S(1)}, f16[64,256]{1,0:T(8,128)(2,1)S(1)}, u32[]{:S(2)}, u32[]{:S(2)}) collective-permute-start(f16[64,256]{1,0:T(8,128)(2,1)S(1)} %multiply_convert_fusion.3), channel_id=1, source_target_pairs={{0,24},{2,26},{4,28},{6,30},{8,16},{10,18},{12,20},{14,22},{16,8},... | collective-permute-start | bytes 98312 | tf_op jit(solution)/shard_map/ppermute | solution.py:284
  58.1 0.0 collective-permute-start.11
  58.1 0.6 collective-permute-start.10
  58.8 2.5 %own_other_kernel.1 = f32[512,256]{1,0:T(8,128)S(1)} custom-call(s32[37]{0:T(128)S(1)} %get-tuple-element.71.plan, s32[16,3,512]{2,1,0:T(4,128)S(1)} %get-tuple-element.44.ids, s32[4,1,512]{2,1,0:T(1,128)S(1)} %get-tuple-element.45.negative_ids, bf16[16,512,512]{2,1,0:T(8,128)(2,1)S(1)} %get-tuple-element.68.grads, ...), custom_call_target="tpu_custom_call" | custom-call | bytes 131072 | tf_op jit(solution)/shard_map/own_other_kernel/pallas_call | solution.py:321
  61.3 0.0 copy-start.2
  61.3 0.0 copy-start
  61.3 0.0 copy-start.3
  61.3 0.1 multiply_convert_fusion
  61.4 0.0 collective-permute-done.12
  61.4 1.5 %collective-permute-done.11 = f16[64,256]{1,0:T(8,128)(2,1)S(1)} collective-permute-done((f16[64,256]{1,0:T(8,128)(2,1)S(1)}, f16[64,256]{1,0:T(8,128)(2,1)S(1)}, u32[]{:S(2)}, u32[]{:S(2)}) %collective-permute-start.11) | collective-permute-done | bytes 32800 | tf_op jit(solution)/shard_map/ppermute | solution.py:284
  62.9 0.0 collective-permute-done.10
  62.9 0.0 collective-permute-done.13
  63.0 0.1 multiply_convert_fusion.1
  63.1 0.3 collective-permute-start.17
  63.4 1.3 %collective-permute-start.16 = (f32[64,256]{1,0:T(8,128)S(1)}, f32[64,256]{1,0:T(8,128)S(1)}, u32[]{:S(2)}, u32[]{:S(2)}) collective-permute-start(f32[64,256]{1,0:T(8,128)S(1)} %add_multiply_fusion.1), channel_id=1, source_target_pairs={{0,4},{1,5},{2,6},{3,7},{4,0},{5,1},{6,2},{7,3},{8,12},{9,13},{10,... | collective-permute-start | bytes 196616 | tf_op jit(solution)/shard_map/ppermute | solution.py:352
  64.7 1.9 %collective-permute-start.15 = (f32[64,256]{1,0:T(8,128)S(1)}, f32[64,256]{1,0:T(8,128)S(1)}, u32[]{:S(2)}, u32[]{:S(2)}) collective-permute-start(f32[64,256]{1,0:T(8,128)S(1)} %add_multiply_fusion.1), channel_id=1, source_target_pairs={{0,1},{1,0},{2,3},{3,2},{4,5},{5,4},{6,7},{7,6},{8,9},{9,8},{10,11... | collective-permute-start | bytes 196616 | tf_op jit(solution)/shard_map/ppermute | solution.py:352
  66.6 2.5 %own_kernel.1.own = f32[512,256]{1,0:T(8,128)S(1)} custom-call(s32[37]{0:T(128)S(1)} %get-tuple-element.71.plan, s32[16,3,512]{2,1,0:T(4,128)S(1)} %get-tuple-element.44.ids, s32[4,1,512]{2,1,0:T(1,128)S(1)} %get-tuple-element.45.negative_ids, bf16[16,512,512]{2,1,0:T(8,128)(2,1)S(1)} %get-tuple-element.68.grads, ...), custom_call_target="tpu_custom_call" | custom-call | bytes 131072 | tf_op jit(solution)/shard_map/own_kernel/pallas_call | solution.py:321
  69.2 2.5 %collective-permute-start.14 = (f16[512,256]{1,0:T(8,128)(2,1)S(1)}, f16[512,256]{1,0:T(8,128)(2,1)S(1)}, u32[]{:S(2)}, u32[]{:S(2)}) collective-permute-start(f16[512,256]{1,0:T(8,128)(2,1)S(1)} %multiply_convert_fusion.1), channel_id=1, source_target_pairs={{0,16},{2,18},{4,20},{6,22},{8,24},{10,26},{12,28},{14,30},{16,0},... | collective-permute-start | bytes 786440 | tf_op jit(solution)/shard_map/ppermute | solution.py:284
  71.7 0.0 collective-permute-start.18
  71.7 0.0 collective-permute-done.15
  71.7 0.0 collective-permute-done.16
  71.8 0.0 collective-permute-done.17
  71.8 0.0 copy-done.2
  71.8 0.9 %relation_mine_kernel.1 = (f32[512,256]{1,0:T(8,128)S(1)}, f32[512,128]{1,0:T(8,128)S(1)}) custom-call(s32[3]{0:T(128)S(1)} %pad_add_fusion.codes, f32[400,256]{1,0:T(8,128)S(1)} %copy-done.1, f32[1,400]{1,0:T(1,128)S(1)} %bitcast.10, f32[256,256]{1,0:T(8,128)S(1)} %constant_dynamic-update-slice_fusion.mine), custom_call_target="tpu_custom_call" | custom-call | bytes 131072 | tf_op jit(solution)/shard_map/relation_mine_kernel/pallas_call | solution.py:321
  72.7 8.2 %collective-permute-done.14 = f16[512,256]{1,0:T(8,128)(2,1)S(1)} collective-permute-done((f16[512,256]{1,0:T(8,128)(2,1)S(1)}, f16[512,256]{1,0:T(8,128)(2,1)S(1)}, u32[]{:S(2)}, u32[]{:S(2)}) %collective-permute-start.14) | collective-permute-done | bytes 262176 | tf_op jit(solution)/shard_map/ppermute | solution.py:284
  80.8 0.0 collective-permute-start.19
  80.8 0.0 collective-permute-done.18
  80.8 0.1 add_multiply_fusion.returned
  80.9 0.0 copy-done
  80.9 0.0 copy-done.3
  80.9 1.2 %entity_kernel.1 = (f32[512,256]{1,0:T(8,128)}, f32[1,512]{1,0:T(1,128)}) custom-call(f32[512,256]{1,0:T(8,128)S(1)} %copy-done, f32[1,512]{1,0:T(1,128)S(1)} %bitcast.11, f32[512,256]{1,0:T(8,128)S(1)} %add_multiply_fusion.returned, f32[512,256]{1,0:T(8,128)S(1)} %own_kernel.1.own), custom_call_target="tpu_custom_call" | custom-call | flops 2097152 | bytes 131072 | tf_op jit(solution)/shard_map/entity_kernel/pallas_call | solution.py:321
  82.1 0.3 collective-permute-done.19.theirs
  82.4 1.6 %relation_theirs_kernel.1 = f32[400,256]{1,0:T(8,128)} custom-call(s32[3]{0:T(128)S(1)} %pad_add_fusion.codes, f32[512,256]{1,0:T(8,128)S(1)} %get-tuple-element.78.before, f32[512,128]{1,0:T(8,128)S(1)} %get-tuple-element.79.column, f32[256,256]{1,0:T(8,128)S(1)} %collective-permute-done.19.theirs), custom_call_target="tpu_custom_call" | custom-call | bytes 131072 | tf_op jit(solution)/shard_map/relation_theirs_kernel/pallas_call | solution.py:321
  (7 shorter events, 0.1 us)
Async XLA Ops:
  2.1 7.9 %collective-permute-start.1 = (s16[17,3,512]{2,1,0:T(4,128)(2,1)S(1)}, s16[17,3,512]{2,1,0:T(4,128)(2,1)S(1)}, u32[]{:S(2)}, u32[]{:S(2)}) collective-permute-start(s16[17,3,512]{2,1,0:T(4,128)(2,1)S(1)} %ids_kernel.1.refs_0_), channel_id=1, source_target_pairs={{0,16},{2,18},{4,20},{6,22},{8,24},{10,26},{12,28},{14,30},{16,0},... | collective-permute-start | bytes 156680 | tf_op jit(solution)/shard_map/ppermute | solution.py:284
  6.2 5.6 %collective-permute-start = (s16[17,3,512]{2,1,0:T(4,128)(2,1)S(1)}, s16[17,3,512]{2,1,0:T(4,128)(2,1)S(1)}, u32[]{:S(2)}, u32[]{:S(2)}) collective-permute-start(s16[17,3,512]{2,1,0:T(4,128)(2,1)S(1)} %ids_kernel.1.refs_0_), channel_id=1, source_target_pairs={{0,1},{1,0},{2,3},{3,2},{4,5},{5,4},{6,7},{7,6},{8,9},{9,8},{10,11... | collective-permute-start | bytes 156680 | tf_op jit(solution)/shard_map/ppermute | solution.py:284
  8.9 15.8 %collective-permute-start.4 = (bf16[256,512]{1,0:T(8,128)(2,1)S(1)}, bf16[256,512]{1,0:T(8,128)(2,1)S(1)}, u32[]{:S(2)}, u32[]{:S(2)}) collective-permute-start(bf16[256,512]{1,0:T(8,128)(2,1)S(1)} %rows_kernel.1.refs_0_), channel_id=1, source_target_pairs={{0,1},{1,0},{2,3},{3,2},{4,5},{5,4},{6,7},{7,6},{8,9},{9,8},{10,11... | collective-permute-start | bytes 786440 | tf_op jit(solution)/shard_map/ppermute | solution.py:284
  9.5 13.7 %collective-permute-start.3 = (bf16[256,512]{1,0:T(8,128)(2,1)S(1)}, bf16[256,512]{1,0:T(8,128)(2,1)S(1)}, u32[]{:S(2)}, u32[]{:S(2)}) collective-permute-start(bf16[256,512]{1,0:T(8,128)(2,1)S(1)} %rows_kernel.1.refs_0_), channel_id=1, source_target_pairs={{0,16},{2,18},{4,20},{6,22},{8,24},{10,26},{12,28},{14,30},{16,0},... | collective-permute-start | bytes 786440 | tf_op jit(solution)/shard_map/ppermute | solution.py:284
  10.0 8.0 %collective-permute-start.2 = (s16[17,3,512]{2,1,0:T(4,128)(2,1)S(1)}, s16[17,3,512]{2,1,0:T(4,128)(2,1)S(1)}, u32[]{:S(2)}, u32[]{:S(2)}) collective-permute-start(s16[17,3,512]{2,1,0:T(4,128)(2,1)S(1)} %collective-permute-done.1.refs_2_), channel_id=1, source_target_pairs={{0,1},{1,0},{2,3},{3,2},{4,5},{5,4},{6,7},{7,6},{8,9},{9,8},{10,11... | collective-permute-start | bytes 156680 | tf_op jit(solution)/shard_map/ppermute | solution.py:284
  11.8 12.9 %copy-start.1 = (f32[400,256]{1,0:T(8,128)S(1)}, f32[400,256]{1,0:T(8,128)}, u32[]{:S(2)}) copy-start(f32[400,256]{1,0:T(8,128)} %relations.3) | copy-start | bytes 1228804
  23.2 7.1 %collective-permute-start.5 = (bf16[256,512]{1,0:T(8,128)(2,1)S(1)}, bf16[256,512]{1,0:T(8,128)(2,1)S(1)}, u32[]{:S(2)}, u32[]{:S(2)}) collective-permute-start(bf16[256,512]{1,0:T(8,128)(2,1)S(1)} %collective-permute-done.3.refs_2_), channel_id=1, source_target_pairs={{0,1},{1,0},{2,3},{3,2},{4,5},{5,4},{6,7},{7,6},{8,9},{9,8},{10,11... | collective-permute-start | bytes 786440 | tf_op jit(solution)/shard_map/ppermute | solution.py:284
  40.2 1.6 %collective-permute-start.6 = (f32[256,256]{1,0:T(8,128)S(1)}, f32[256,256]{1,0:T(8,128)S(1)}, u32[]{:S(2)}, u32[]{:S(2)}) collective-permute-start(f32[256,256]{1,0:T(8,128)S(1)} %get-tuple-element.52), channel_id=1, source_target_pairs={{0,2},{2,0},{4,6},{6,4},{8,10},{10,8},{12,14},{14,12},{16,18},{18,... | collective-permute-start | bytes 786440 | tf_op jit(solution)/shard_map/ppermute | solution.py:284
  41.8 9.4 %collective-permute-start.7 = (f32[64,256]{1,0:T(8,128)S(1)}, f32[64,256]{1,0:T(8,128)S(1)}, u32[]{:S(2)}, u32[]{:S(2)}) collective-permute-start(f32[64,256]{1,0:T(8,128)S(1)} %get-tuple-element.58), channel_id=1, source_target_pairs={{0,1},{1,0},{2,3},{3,2},{4,5},{5,4},{6,7},{7,6},{8,9},{9,8},{10,11... | collective-permute-start | bytes 196616 | tf_op jit(solution)/shard_map/ppermute | solution.py:352
  44.4 6.8 %collective-permute-start.8 = (f32[64,256]{1,0:T(8,128)S(1)}, f32[64,256]{1,0:T(8,128)S(1)}, u32[]{:S(2)}, u32[]{:S(2)}) collective-permute-start(f32[64,256]{1,0:T(8,128)S(1)} %get-tuple-element.59), channel_id=1, source_target_pairs={{0,4},{1,5},{2,6},{3,7},{4,0},{5,1},{6,2},{7,3},{8,12},{9,13},{10,... | collective-permute-start | bytes 196616 | tf_op jit(solution)/shard_map/ppermute | solution.py:352
  46.8 5.2 %collective-permute-start.9 = (f32[64,256]{1,0:T(8,128)S(1)}, f32[64,256]{1,0:T(8,128)S(1)}, u32[]{:S(2)}, u32[]{:S(2)}) collective-permute-start(f32[64,256]{1,0:T(8,128)S(1)} %get-tuple-element.60), channel_id=1, source_target_pairs={{0,5},{1,4},{2,7},{3,6},{4,1},{5,0},{6,3},{7,2},{8,13},{9,12},{10,... | collective-permute-start | bytes 196616 | tf_op jit(solution)/shard_map/ppermute | solution.py:352
  46.8 16.2 %collective-permute-start.13 = (f16[512,256]{1,0:T(8,128)(2,1)S(1)}, f16[512,256]{1,0:T(8,128)(2,1)S(1)}, u32[]{:S(2)}, u32[]{:S(2)}) collective-permute-start(f16[512,256]{1,0:T(8,128)(2,1)S(1)} %multiply_convert_fusion.2), channel_id=1, source_target_pairs={{0,1},{1,0},{2,3},{3,2},{4,5},{5,4},{6,7},{7,6},{8,9},{9,8},{10,11... | collective-permute-start | bytes 786440 | tf_op jit(solution)/shard_map/ppermute | solution.py:284
  52.0 9.4 %collective-permute-start.12 = (f16[64,256]{1,0:T(8,128)(2,1)S(1)}, f16[64,256]{1,0:T(8,128)(2,1)S(1)}, u32[]{:S(2)}, u32[]{:S(2)}) collective-permute-start(f16[64,256]{1,0:T(8,128)(2,1)S(1)} %multiply_convert_fusion.3), channel_id=1, source_target_pairs={{0,24},{2,26},{4,28},{6,30},{8,16},{10,18},{12,20},{14,22},{16,8},... | collective-permute-start | bytes 98312 | tf_op jit(solution)/shard_map/ppermute | solution.py:284
  58.1 4.8 %collective-permute-start.11 = (f16[64,256]{1,0:T(8,128)(2,1)S(1)}, f16[64,256]{1,0:T(8,128)(2,1)S(1)}, u32[]{:S(2)}, u32[]{:S(2)}) collective-permute-start(f16[64,256]{1,0:T(8,128)(2,1)S(1)} %multiply_convert_fusion.3), channel_id=1, source_target_pairs={{0,16},{2,18},{4,20},{6,22},{8,24},{10,26},{12,28},{14,30},{16,0},... | collective-permute-start | bytes 98312 | tf_op jit(solution)/shard_map/ppermute | solution.py:284
  58.1 4.8 %collective-permute-start.10 = (f16[64,256]{1,0:T(8,128)(2,1)S(1)}, f16[64,256]{1,0:T(8,128)(2,1)S(1)}, u32[]{:S(2)}, u32[]{:S(2)}) collective-permute-start(f16[64,256]{1,0:T(8,128)(2,1)S(1)} %multiply_convert_fusion.3), channel_id=1, source_target_pairs={{0,8},{2,10},{4,12},{6,14},{8,0},{10,2},{12,4},{14,6},{16,24},{18,... | collective-permute-start | bytes 98312 | tf_op jit(solution)/shard_map/ppermute | solution.py:284
  61.3 10.5 %copy-start.2 = (f32[400]{0:T(512)S(1)}, f32[400]{0:T(512)}, u32[]{:S(2)}) copy-start(f32[400]{0:T(512)} %param.12) | copy-start | bytes 4804
  61.3 19.6 %copy-start = (f32[512,256]{1,0:T(8,128)S(1)}, f32[512,256]{1,0:T(8,128)}, u32[]{:S(2)}) copy-start(f32[512,256]{1,0:T(8,128)} %table.2) | copy-start | bytes 1572868
  61.3 19.6 %copy-start.3 = (f32[512]{0:T(512)S(1)}, f32[512]{0:T(512)}, u32[]{:S(2)}) copy-start(f32[512]{0:T(512)} %param.10) | copy-start | bytes 6148
  63.1 8.7 %collective-permute-start.17 = (f32[64,256]{1,0:T(8,128)S(1)}, f32[64,256]{1,0:T(8,128)S(1)}, u32[]{:S(2)}, u32[]{:S(2)}) collective-permute-start(f32[64,256]{1,0:T(8,128)S(1)} %add_multiply_fusion.1), channel_id=1, source_target_pairs={{0,5},{1,4},{2,7},{3,6},{4,1},{5,0},{6,3},{7,2},{8,13},{9,12},{10,... | collective-permute-start | bytes 196616 | tf_op jit(solution)/shard_map/ppermute | solution.py:352
  63.4 8.3 %collective-permute-start.16 = (f32[64,256]{1,0:T(8,128)S(1)}, f32[64,256]{1,0:T(8,128)S(1)}, u32[]{:S(2)}, u32[]{:S(2)}) collective-permute-start(f32[64,256]{1,0:T(8,128)S(1)} %add_multiply_fusion.1), channel_id=1, source_target_pairs={{0,4},{1,5},{2,6},{3,7},{4,0},{5,1},{6,2},{7,3},{8,12},{9,13},{10,... | collective-permute-start | bytes 196616 | tf_op jit(solution)/shard_map/ppermute | solution.py:352
  64.7 7.0 %collective-permute-start.15 = (f32[64,256]{1,0:T(8,128)S(1)}, f32[64,256]{1,0:T(8,128)S(1)}, u32[]{:S(2)}, u32[]{:S(2)}) collective-permute-start(f32[64,256]{1,0:T(8,128)S(1)} %add_multiply_fusion.1), channel_id=1, source_target_pairs={{0,1},{1,0},{2,3},{3,2},{4,5},{5,4},{6,7},{7,6},{8,9},{9,8},{10,11... | collective-permute-start | bytes 196616 | tf_op jit(solution)/shard_map/ppermute | solution.py:352
  69.2 11.6 %collective-permute-start.14 = (f16[512,256]{1,0:T(8,128)(2,1)S(1)}, f16[512,256]{1,0:T(8,128)(2,1)S(1)}, u32[]{:S(2)}, u32[]{:S(2)}) collective-permute-start(f16[512,256]{1,0:T(8,128)(2,1)S(1)} %multiply_convert_fusion.1), channel_id=1, source_target_pairs={{0,16},{2,18},{4,20},{6,22},{8,24},{10,26},{12,28},{14,30},{16,0},... | collective-permute-start | bytes 786440 | tf_op jit(solution)/shard_map/ppermute | solution.py:284
  71.7 9.1 %collective-permute-start.18 = (f16[512,256]{1,0:T(8,128)(2,1)S(1)}, f16[512,256]{1,0:T(8,128)(2,1)S(1)}, u32[]{:S(2)}, u32[]{:S(2)}) collective-permute-start(f16[512,256]{1,0:T(8,128)(2,1)S(1)} %multiply_convert_fusion), channel_id=1, source_target_pairs={{0,1},{1,0},{2,3},{3,2},{4,5},{5,4},{6,7},{7,6},{8,9},{9,8},{10,11... | collective-permute-start | bytes 786440 | tf_op jit(solution)/shard_map/ppermute | solution.py:284
  80.8 1.5 %collective-permute-start.19 = (f32[256,256]{1,0:T(8,128)S(1)}, f32[256,256]{1,0:T(8,128)S(1)}, u32[]{:S(2)}, u32[]{:S(2)}) collective-permute-start(f32[256,256]{1,0:T(8,128)S(1)} %constant_dynamic-update-slice_fusion.mine), channel_id=1, source_target_pairs={{0,2},{2,0},{4,6},{6,4},{8,10},{10,8},{12,14},{14,12},{16,18},{18,... | collective-permute-start | bytes 786440 | tf_op jit(solution)/shard_map/ppermute | solution.py:284

commit v12 on v8

--- a/solution.py
+++ b/solution.py
@@ -229,16 +229,17 @@
     def hot_of(i):
         return one_hot(ids[i][row : row + 1] - start, height)
 
-    def two_blocks(i, carry):
-        hot = jnp.concatenate([hot_of(2 * i), hot_of(2 * i + 1)], axis=1)
-        scatter_add(sums, hot, jnp.concatenate([grads[2 * i], grads[2 * i + 1]], axis=1))
+    def four_blocks(i, carry):
+        hot = jnp.concatenate([hot_of(4 * i + k) for k in range(4)], axis=1)
+        scatter_add(sums, hot, jnp.concatenate([grads[4 * i + k] for k in range(4)], axis=1))
         return carry
 
-    lax.fori_loop(0, steps >> 1, two_blocks, 0)
-
-    @pl.when((steps & 1) == 1)
-    def _():
-        scatter_add(sums, hot_of(steps - 1), grads[steps - 1])
+    def one_block(i, carry):
+        scatter_add(sums, hot_of(i), grads[i])
+        return carry
+
+    lax.fori_loop(0, steps >> 2, four_blocks, 0)
+    lax.fori_loop((steps >> 2) << 2, steps, one_block, 0)
 
     for k in range(first, first + negative_ids.shape[0] // 2):
 

time: 79.8 us -> 78.9 us (0.989); the launches traced: 80.8 us -> 78.3 us
  starting transfers between devices: 30.9 us -> 29.2 us
    ppermute x14, starting transfers between devices: 23.3 us -> 19.9 us  [exchange(): lax.ppermute(x, axis, [(i, i ^ mask) for i in range(lax.axis_size(axis))])]
    ppermute x6, starting transfers between devices: 7.6 us -> 9.25 us  [to_peer(): return lax.ppermute(x, ('dom', 'sub'), pairs)]
where the time goes in v12:
time: 78.9 us; the launch traced here: 78.3 us
  starting transfers between devices  29.2 us (37%)
  Pallas kernels  27.6 us (35%)
  waiting for transfers between devices  19.6 us (25%)
  between operations  1.49 us (2%)
    pallas_call x9, Pallas kernels, call(): pl.pallas_call(kernel, in_specs=[in_smem] * len(scalars) + [in_vmem] * le...  26 us
    ppermute x14, starting transfers between devices, exchange(): lax.ppermute(x, axis, [(i, i ^ mask) for i in range(lax.axis_size(axis))])  19.9 us
    ppermute x14, waiting for transfers between devices, exchange(): lax.ppermute(x, axis, [(i, i ^ mask) for i in range(lax.axis_size(axis))])  17.6 us
    ppermute x6, starting transfers between devices, to_peer(): return lax.ppermute(x, ('dom', 'sub'), pairs)  9.25 us
    ppermute x6, waiting for transfers between devices, to_peer(): return lax.ppermute(x, ('dom', 'sub'), pairs)  1.96 us
  transfers between devices with their start and end apart: 20, of which 10 were waited for; matrix products, arithmetic and copies ran while one was open for 0% of the time, Pallas kernels for 20%

profile of v12, /device:TPU:0, one launch (start us, length us, event | category | flops | bytes accessed | tf_op | source)
XLA Modules:
  0.0 78.3 jit_solution(7872457338007086456)
XLA Ops:
  1.3 0.8 %ids_kernel.1.refs_0_ = s16[17,3,512]{2,1,0:T(4,128)(2,1)S(1)} custom-call(s32[1,1]{1,0:T(1,128)S(6)} %copy.12.count, s32[1,8192]{1,0:T(1,128)} %bitcast.12, s32[1,8192]{1,0:T(1,128)} %bitcast.13, s32[1,8192]{1,0:T(1,128)} %bitcast.14, s32[1,512]{1,0:T(1,128)} %bitcast.15), custom_call_target="tpu_custom_call" | custom-call | flops 2097152 | bytes 131072 | tf_op jit(solution)/shard_map/ids_kernel/pallas_call | solution.py:312
  2.1 4.1 %collective-permute-start.1 = (s16[17,3,512]{2,1,0:T(4,128)(2,1)S(1)}, s16[17,3,512]{2,1,0:T(4,128)(2,1)S(1)}, u32[]{:S(2)}, u32[]{:S(2)}) collective-permute-start(s16[17,3,512]{2,1,0:T(4,128)(2,1)S(1)} %ids_kernel.1.refs_0_), channel_id=1, source_target_pairs={{0,16},{2,18},{4,20},{6,22},{8,24},{10,26},{12,28},{14,30},{16,0},... | collective-permute-start | bytes 156680 | tf_op jit(solution)/shard_map/ppermute | solution.py:275
  6.2 1.5 %collective-permute-start = (s16[17,3,512]{2,1,0:T(4,128)(2,1)S(1)}, s16[17,3,512]{2,1,0:T(4,128)(2,1)S(1)}, u32[]{:S(2)}, u32[]{:S(2)}) collective-permute-start(s16[17,3,512]{2,1,0:T(4,128)(2,1)S(1)} %ids_kernel.1.refs_0_), channel_id=1, source_target_pairs={{0,1},{1,0},{2,3},{3,2},{4,5},{5,4},{6,7},{7,6},{8,9},{9,8},{10,11... | collective-permute-start | bytes 156680 | tf_op jit(solution)/shard_map/ppermute | solution.py:275
  7.7 1.2 %rows_kernel.1.refs_0_ = bf16[256,512]{1,0:T(8,128)(2,1)S(1)} custom-call(f32[512,256]{1,0:T(8,128)} %table.2), custom_call_target="tpu_custom_call" | custom-call | flops 2097152 | bytes 131072 | tf_op jit(solution)/shard_map/rows_kernel/pallas_call | solution.py:312
  8.9 0.6 collective-permute-start.4
  9.5 0.1 collective-permute-start.3
  9.6 0.4 collective-permute-done.1.refs_2_
  10.0 1.7 %collective-permute-start.2 = (s16[17,3,512]{2,1,0:T(4,128)(2,1)S(1)}, s16[17,3,512]{2,1,0:T(4,128)(2,1)S(1)}, u32[]{:S(2)}, u32[]{:S(2)}) collective-permute-start(s16[17,3,512]{2,1,0:T(4,128)(2,1)S(1)} %collective-permute-done.1.refs_2_), channel_id=1, source_target_pairs={{0,1},{1,0},{2,3},{3,2},{4,5},{5,4},{6,7},{7,6},{8,9},{9,8},{10,11... | collective-permute-start | bytes 156680 | tf_op jit(solution)/shard_map/ppermute | solution.py:275
  11.7 0.1 pad_add_fusion.codes
  11.8 0.0 copy-start.1
  11.8 0.0 collective-permute-done.refs_1_
  11.8 6.2 %collective-permute-done.2.refs_3_ = s16[17,3,512]{2,1,0:T(4,128)(2,1)S(1)} collective-permute-done((s16[17,3,512]{2,1,0:T(4,128)(2,1)S(1)}, s16[17,3,512]{2,1,0:T(4,128)(2,1)S(1)}, u32[]{:S(2)}, u32[]{:S(2)}) %collective-permute-start.2) | collective-permute-done | bytes 52256 | tf_op jit(solution)/shard_map/ppermute | solution.py:275
  18.0 1.5 %plan_kernel.1 = (s32[37]{0:T(128)S(1)}, s32[16,3,512]{2,1,0:T(4,128)S(1)}, s32[4,1,512]{2,1,0:T(1,128)S(1)}) custom-call(s32[3]{0:T(128)S(1)} %pad_add_fusion.codes, s16[17,3,512]{2,1,0:T(4,128)(2,1)S(1)} %ids_kernel.1.refs_0_, s16[17,3,512]{2,1,0:T(4,128)(2,1)S(1)} %collective-permute-done.refs_1_, s16[17,3,512]{2,1,0:T(4,128)(2,1)S(1)} %collective-permute-done.1.refs_2_, ...), custom_call_target="tpu_custom_call" | custom-call | flops 34359738368 | bytes 2097152 | tf_op jit(solution)/shard_map/plan_kernel/pallas_call | solution.py:352
  19.5 3.7 %collective-permute-done.3.refs_2_ = bf16[256,512]{1,0:T(8,128)(2,1)S(1)} collective-permute-done((bf16[256,512]{1,0:T(8,128)(2,1)S(1)}, bf16[256,512]{1,0:T(8,128)(2,1)S(1)}, u32[]{:S(2)}, u32[]{:S(2)}) %collective-permute-start.3) | collective-permute-done | bytes 262176 | tf_op jit(solution)/shard_map/ppermute | solution.py:275
  23.2 1.5 %collective-permute-start.5 = (bf16[256,512]{1,0:T(8,128)(2,1)S(1)}, bf16[256,512]{1,0:T(8,128)(2,1)S(1)}, u32[]{:S(2)}, u32[]{:S(2)}) collective-permute-start(bf16[256,512]{1,0:T(8,128)(2,1)S(1)} %collective-permute-done.3.refs_2_), channel_id=1, source_target_pairs={{0,1},{1,0},{2,3},{3,2},{4,5},{5,4},{6,7},{7,6},{8,9},{9,8},{10,11... | collective-permute-start | bytes 786440 | tf_op jit(solution)/shard_map/ppermute | solution.py:275
  24.7 0.0 collective-permute-done.4.refs_1_
  24.7 0.0 copy-done.1
  24.7 4.0 %near_kernel.1 = (bf16[16,256,512]{2,1,0:T(8,128)(2,1)S(1)}, f32[16,256,512]{2,1,0:T(8,128)S(1)}) custom-call(s32[37]{0:T(128)S(1)} %get-tuple-element.68.plan, s32[16,3,512]{2,1,0:T(4,128)S(1)} %get-tuple-element.41.ids, f32[400,256]{1,0:T(8,128)S(1)} %copy-done.1, bf16[256,512]{1,0:T(8,128)(2,1)S(1)} %rows_kernel.1.refs_0_, ...), custom_call_target="tpu_custom_call" | custom-call | flops 4294967296 | bytes 131072 | tf_op jit(solution)/shard_map/near_kernel/pallas_call | solution.py:312
  28.7 1.6 %collective-permute-done.5.refs_3_ = bf16[256,512]{1,0:T(8,128)(2,1)S(1)} collective-permute-done((bf16[256,512]{1,0:T(8,128)(2,1)S(1)}, bf16[256,512]{1,0:T(8,128)(2,1)S(1)}, u32[]{:S(2)}, u32[]{:S(2)}) %collective-permute-start.5) | collective-permute-done | bytes 262176 | tf_op jit(solution)/shard_map/ppermute | solution.py:275
  30.4 9.8 %edge_kernel.1 = (bf16[16,512,512]{2,1,0:T(8,128)(2,1)S(1)}, bf16[16,512,512]{2,1,0:T(8,128)(2,1)S(1)}, bf16[4,1024,256]{2,1,0:T(8,128)(2,1)S(1)}, f32[512,256]{...) custom-call(s32[3]{0:T(128)S(1)} %pad_add_fusion.codes, ...), custom_call_target="tpu_custom_call" | custom-call | flops 11811160064 | bytes 131072 | tf_op jit(solution)/shard_map/edge_kernel/pallas_call | solution.py:312
  40.2 0.1 collective-permute-start.6
  40.2 0.1 multiply_convert_fusion.2
  40.3 1.5 %collective-permute-done.6 = f32[256,256]{1,0:T(8,128)S(1)} collective-permute-done((f32[256,256]{1,0:T(8,128)S(1)}, f32[256,256]{1,0:T(8,128)S(1)}, u32[]{:S(2)}, u32[]{:S(2)}) %collective-permute-start.6) | collective-permute-done | bytes 262176 | tf_op jit(solution)/shard_map/ppermute | solution.py:275
  41.8 4.2 %collective-permute-start.7 = (f32[64,256]{1,0:T(8,128)S(1)}, f32[64,256]{1,0:T(8,128)S(1)}, u32[]{:S(2)}, u32[]{:S(2)}) collective-permute-start(f32[64,256]{1,0:T(8,128)S(1)} %get-tuple-element.55), channel_id=1, source_target_pairs={{0,1},{1,0},{2,3},{3,2},{4,5},{5,4},{6,7},{7,6},{8,9},{9,8},{10,11... | collective-permute-start | bytes 196616 | tf_op jit(solution)/shard_map/ppermute | solution.py:343
  46.0 0.0 collective-permute-start.8
  46.0 1.5 %collective-permute-start.9 = (f32[64,256]{1,0:T(8,128)S(1)}, f32[64,256]{1,0:T(8,128)S(1)}, u32[]{:S(2)}, u32[]{:S(2)}) collective-permute-start(f32[64,256]{1,0:T(8,128)S(1)} %get-tuple-element.57), channel_id=1, source_target_pairs={{0,5},{1,4},{2,7},{3,6},{4,1},{5,0},{6,3},{7,2},{8,13},{9,12},{10,... | collective-permute-start | bytes 196616 | tf_op jit(solution)/shard_map/ppermute | solution.py:343
  47.6 1.9 %collective-permute-start.13 = (f16[512,256]{1,0:T(8,128)(2,1)S(1)}, f16[512,256]{1,0:T(8,128)(2,1)S(1)}, u32[]{:S(2)}, u32[]{:S(2)}) collective-permute-start(f16[512,256]{1,0:T(8,128)(2,1)S(1)} %multiply_convert_fusion.2), channel_id=1, source_target_pairs={{0,1},{1,0},{2,3},{3,2},{4,5},{5,4},{6,7},{7,6},{8,9},{9,8},{10,11... | collective-permute-start | bytes 786440 | tf_op jit(solution)/shard_map/ppermute | solution.py:275
  49.5 2.8 %away_kernel.1 = f32[512,256]{1,0:T(8,128)S(1)} custom-call(s32[37]{0:T(128)S(1)} %get-tuple-element.68.plan, s32[16,3,512]{2,1,0:T(4,128)S(1)} %get-tuple-element.41.ids, s32[4,1,512]{2,1,0:T(1,128)S(1)} %get-tuple-element.42.negative_ids, bf16[16,512,512]{2,1,0:T(8,128)(2,1)S(1)} %get-tuple-element.59.grads, ...), custom_call_target="tpu_custom_call" | custom-call | bytes 131072 | tf_op jit(solution)/shard_map/away_kernel/pallas_call | solution.py:312
  52.3 0.0 collective-permute-done.7
  52.3 0.0 collective-permute-done.8
  52.3 0.0 collective-permute-done.9
  52.3 5.3 %collective-permute-start.12 = (f16[64,256]{1,0:T(8,128)(2,1)S(1)}, f16[64,256]{1,0:T(8,128)(2,1)S(1)}, u32[]{:S(2)}, u32[]{:S(2)}) collective-permute-start(f16[64,256]{1,0:T(8,128)(2,1)S(1)} %multiply_convert_fusion.3), channel_id=1, source_target_pairs={{0,24},{2,26},{4,28},{6,30},{8,16},{10,18},{12,20},{14,22},{16,8},... | collective-permute-start | bytes 98312 | tf_op jit(solution)/shard_map/ppermute | solution.py:275
  57.6 0.0 collective-permute-start.11
  57.6 0.6 collective-permute-start.10
  58.3 2.3 %own_other_kernel.1 = f32[512,256]{1,0:T(8,128)S(1)} custom-call(s32[37]{0:T(128)S(1)} %get-tuple-element.68.plan, s32[16,3,512]{2,1,0:T(4,128)S(1)} %get-tuple-element.41.ids, s32[4,1,512]{2,1,0:T(1,128)S(1)} %get-tuple-element.42.negative_ids, bf16[16,512,512]{2,1,0:T(8,128)(2,1)S(1)} %get-tuple-element.65.grads, ...), custom_call_target="tpu_custom_call" | custom-call | bytes 131072 | tf_op jit(solution)/shard_map/own_other_kernel/pallas_call | solution.py:312
  60.6 0.0 copy-start
  60.6 0.0 copy-start.2
  60.6 0.0 copy-start.3
  60.6 0.1 multiply_convert_fusion
  60.7 0.0 collective-permute-done.12
  60.7 1.7 %collective-permute-done.11 = f16[64,256]{1,0:T(8,128)(2,1)S(1)} collective-permute-done((f16[64,256]{1,0:T(8,128)(2,1)S(1)}, f16[64,256]{1,0:T(8,128)(2,1)S(1)}, u32[]{:S(2)}, u32[]{:S(2)}) %collective-permute-start.11) | collective-permute-done | bytes 32800 | tf_op jit(solution)/shard_map/ppermute | solution.py:275
  62.4 0.0 collective-permute-done.10
  62.5 0.0 collective-permute-done.13
  62.5 0.1 multiply_convert_fusion.1
  62.6 2.1 %collective-permute-start.14 = (f16[512,256]{1,0:T(8,128)(2,1)S(1)}, f16[512,256]{1,0:T(8,128)(2,1)S(1)}, u32[]{:S(2)}, u32[]{:S(2)}) collective-permute-start(f16[512,256]{1,0:T(8,128)(2,1)S(1)} %multiply_convert_fusion.1), channel_id=1, source_target_pairs={{0,16},{2,18},{4,20},{6,22},{8,24},{10,26},{12,28},{14,30},{16,0},... | collective-permute-start | bytes 786440 | tf_op jit(solution)/shard_map/ppermute | solution.py:275
  64.7 0.4 collective-permute-start.18
  65.0 1.1 %collective-permute-start.17 = (f32[64,256]{1,0:T(8,128)S(1)}, f32[64,256]{1,0:T(8,128)S(1)}, u32[]{:S(2)}, u32[]{:S(2)}) collective-permute-start(f32[64,256]{1,0:T(8,128)S(1)} %add_multiply_fusion.1), channel_id=1, source_target_pairs={{0,5},{1,4},{2,7},{3,6},{4,1},{5,0},{6,3},{7,2},{8,13},{9,12},{10,... | collective-permute-start | bytes 196616 | tf_op jit(solution)/shard_map/ppermute | solution.py:343
  66.2 2.0 %collective-permute-start.16 = (f32[64,256]{1,0:T(8,128)S(1)}, f32[64,256]{1,0:T(8,128)S(1)}, u32[]{:S(2)}, u32[]{:S(2)}) collective-permute-start(f32[64,256]{1,0:T(8,128)S(1)} %add_multiply_fusion.1), channel_id=1, source_target_pairs={{0,4},{1,5},{2,6},{3,7},{4,0},{5,1},{6,2},{7,3},{8,12},{9,13},{10,... | collective-permute-start | bytes 196616 | tf_op jit(solution)/shard_map/ppermute | solution.py:343
  68.1 0.4 collective-permute-start.15
  68.5 2.3 %own_kernel.1.own = f32[512,256]{1,0:T(8,128)S(1)} custom-call(s32[37]{0:T(128)S(1)} %get-tuple-element.68.plan, s32[16,3,512]{2,1,0:T(4,128)S(1)} %get-tuple-element.41.ids, s32[4,1,512]{2,1,0:T(1,128)S(1)} %get-tuple-element.42.negative_ids, bf16[16,512,512]{2,1,0:T(8,128)(2,1)S(1)} %get-tuple-element.65.grads, ...), custom_call_target="tpu_custom_call" | custom-call | bytes 131072 | tf_op jit(solution)/shard_map/own_kernel/pallas_call | solution.py:312
  70.9 0.0 collective-permute-done.17
  70.9 0.2 collective-permute-done.16
  71.1 1.7 %collective-permute-done.15 = f32[64,256]{1,0:T(8,128)S(1)} collective-permute-done((f32[64,256]{1,0:T(8,128)S(1)}, f32[64,256]{1,0:T(8,128)S(1)}, u32[]{:S(2)}, u32[]{:S(2)}) %collective-permute-start.15) | collective-permute-done | bytes 65568 | tf_op jit(solution)/shard_map/ppermute | solution.py:343
  72.9 2.2 %collective-permute-done.14 = f16[512,256]{1,0:T(8,128)(2,1)S(1)} collective-permute-done((f16[512,256]{1,0:T(8,128)(2,1)S(1)}, f16[512,256]{1,0:T(8,128)(2,1)S(1)}, u32[]{:S(2)}, u32[]{:S(2)}) %collective-permute-start.14) | collective-permute-done | bytes 262176 | tf_op jit(solution)/shard_map/ppermute | solution.py:275
  75.1 0.0 collective-permute-start.19
  75.1 0.0 collective-permute-done.18
  75.1 0.1 add_multiply_fusion.returned
  75.2 0.0 copy-done
  75.2 0.0 copy-done.2
  75.2 1.2 %entity_kernel.1 = (f32[512,256]{1,0:T(8,128)}, f32[1,512]{1,0:T(1,128)}) custom-call(f32[512,256]{1,0:T(8,128)S(1)} %copy-done, f32[1,512]{1,0:T(1,128)S(1)} %bitcast.10, f32[512,256]{1,0:T(8,128)S(1)} %add_multiply_fusion.returned, f32[512,256]{1,0:T(8,128)S(1)} %own_kernel.1.own), custom_call_target="tpu_custom_call" | custom-call | flops 2097152 | bytes 131072 | tf_op jit(solution)/shard_map/entity_kernel/pallas_call | solution.py:312
  76.4 0.3 collective-permute-done.19.theirs
  76.6 0.0 copy-done.3
  76.6 1.6 %relation_kernel.1 = f32[400,256]{1,0:T(8,128)} custom-call(s32[3]{0:T(128)S(1)} %pad_add_fusion.codes, f32[400,256]{1,0:T(8,128)S(1)} %copy-done.1, f32[1,400]{1,0:T(1,128)S(1)} %bitcast.11, f32[256,256]{1,0:T(8,128)S(1)} %pad_maximum_fusion.mine, f32[256,256]{1,0:T(8,128)S(1)} %collective-permute-done.19.theirs), custom_call_target="tpu_custom_call" | custom-call | bytes 131072 | tf_op jit(solution)/shard_map/relation_kernel/pallas_call | solution.py:312
  (4 shorter events, 0.1 us)
Async XLA Ops:
  2.1 7.9 %collective-permute-start.1 = (s16[17,3,512]{2,1,0:T(4,128)(2,1)S(1)}, s16[17,3,512]{2,1,0:T(4,128)(2,1)S(1)}, u32[]{:S(2)}, u32[]{:S(2)}) collective-permute-start(s16[17,3,512]{2,1,0:T(4,128)(2,1)S(1)} %ids_kernel.1.refs_0_), channel_id=1, source_target_pairs={{0,16},{2,18},{4,20},{6,22},{8,24},{10,26},{12,28},{14,30},{16,0},... | collective-permute-start | bytes 156680 | tf_op jit(solution)/shard_map/ppermute | solution.py:275
  6.2 5.6 %collective-permute-start = (s16[17,3,512]{2,1,0:T(4,128)(2,1)S(1)}, s16[17,3,512]{2,1,0:T(4,128)(2,1)S(1)}, u32[]{:S(2)}, u32[]{:S(2)}) collective-permute-start(s16[17,3,512]{2,1,0:T(4,128)(2,1)S(1)} %ids_kernel.1.refs_0_), channel_id=1, source_target_pairs={{0,1},{1,0},{2,3},{3,2},{4,5},{5,4},{6,7},{7,6},{8,9},{9,8},{10,11... | collective-permute-start | bytes 156680 | tf_op jit(solution)/shard_map/ppermute | solution.py:275
  8.9 15.8 %collective-permute-start.4 = (bf16[256,512]{1,0:T(8,128)(2,1)S(1)}, bf16[256,512]{1,0:T(8,128)(2,1)S(1)}, u32[]{:S(2)}, u32[]{:S(2)}) collective-permute-start(bf16[256,512]{1,0:T(8,128)(2,1)S(1)} %rows_kernel.1.refs_0_), channel_id=1, source_target_pairs={{0,1},{1,0},{2,3},{3,2},{4,5},{5,4},{6,7},{7,6},{8,9},{9,8},{10,11... | collective-permute-start | bytes 786440 | tf_op jit(solution)/shard_map/ppermute | solution.py:275
  9.5 13.7 %collective-permute-start.3 = (bf16[256,512]{1,0:T(8,128)(2,1)S(1)}, bf16[256,512]{1,0:T(8,128)(2,1)S(1)}, u32[]{:S(2)}, u32[]{:S(2)}) collective-permute-start(bf16[256,512]{1,0:T(8,128)(2,1)S(1)} %rows_kernel.1.refs_0_), channel_id=1, source_target_pairs={{0,16},{2,18},{4,20},{6,22},{8,24},{10,26},{12,28},{14,30},{16,0},... | collective-permute-start | bytes 786440 | tf_op jit(solution)/shard_map/ppermute | solution.py:275
  10.0 8.0 %collective-permute-start.2 = (s16[17,3,512]{2,1,0:T(4,128)(2,1)S(1)}, s16[17,3,512]{2,1,0:T(4,128)(2,1)S(1)}, u32[]{:S(2)}, u32[]{:S(2)}) collective-permute-start(s16[17,3,512]{2,1,0:T(4,128)(2,1)S(1)} %collective-permute-done.1.refs_2_), channel_id=1, source_target_pairs={{0,1},{1,0},{2,3},{3,2},{4,5},{5,4},{6,7},{7,6},{8,9},{9,8},{10,11... | collective-permute-start | bytes 156680 | tf_op jit(solution)/shard_map/ppermute | solution.py:275
  11.8 12.9 %copy-start.1 = (f32[400,256]{1,0:T(8,128)S(1)}, f32[400,256]{1,0:T(8,128)}, u32[]{:S(2)}) copy-start(f32[400,256]{1,0:T(8,128)} %relations.3) | copy-start | bytes 1228804
  23.2 7.1 %collective-permute-start.5 = (bf16[256,512]{1,0:T(8,128)(2,1)S(1)}, bf16[256,512]{1,0:T(8,128)(2,1)S(1)}, u32[]{:S(2)}, u32[]{:S(2)}) collective-permute-start(bf16[256,512]{1,0:T(8,128)(2,1)S(1)} %collective-permute-done.3.refs_2_), channel_id=1, source_target_pairs={{0,1},{1,0},{2,3},{3,2},{4,5},{5,4},{6,7},{7,6},{8,9},{9,8},{10,11... | collective-permute-start | bytes 786440 | tf_op jit(solution)/shard_map/ppermute | solution.py:275
  40.2 1.6 %collective-permute-start.6 = (f32[256,256]{1,0:T(8,128)S(1)}, f32[256,256]{1,0:T(8,128)S(1)}, u32[]{:S(2)}, u32[]{:S(2)}) collective-permute-start(f32[256,256]{1,0:T(8,128)S(1)} %get-tuple-element.49), channel_id=1, source_target_pairs={{0,2},{2,0},{4,6},{6,4},{8,10},{10,8},{12,14},{14,12},{16,18},{18,... | collective-permute-start | bytes 786440 | tf_op jit(solution)/shard_map/ppermute | solution.py:275
  41.8 10.5 %collective-permute-start.7 = (f32[64,256]{1,0:T(8,128)S(1)}, f32[64,256]{1,0:T(8,128)S(1)}, u32[]{:S(2)}, u32[]{:S(2)}) collective-permute-start(f32[64,256]{1,0:T(8,128)S(1)} %get-tuple-element.55), channel_id=1, source_target_pairs={{0,1},{1,0},{2,3},{3,2},{4,5},{5,4},{6,7},{7,6},{8,9},{9,8},{10,11... | collective-permute-start | bytes 196616 | tf_op jit(solution)/shard_map/ppermute | solution.py:343
  46.0 6.3 %collective-permute-start.8 = (f32[64,256]{1,0:T(8,128)S(1)}, f32[64,256]{1,0:T(8,128)S(1)}, u32[]{:S(2)}, u32[]{:S(2)}) collective-permute-start(f32[64,256]{1,0:T(8,128)S(1)} %get-tuple-element.56), channel_id=1, source_target_pairs={{0,4},{1,5},{2,6},{3,7},{4,0},{5,1},{6,2},{7,3},{8,12},{9,13},{10,... | collective-permute-start | bytes 196616 | tf_op jit(solution)/shard_map/ppermute | solution.py:343
  46.0 6.3 %collective-permute-start.9 = (f32[64,256]{1,0:T(8,128)S(1)}, f32[64,256]{1,0:T(8,128)S(1)}, u32[]{:S(2)}, u32[]{:S(2)}) collective-permute-start(f32[64,256]{1,0:T(8,128)S(1)} %get-tuple-element.57), channel_id=1, source_target_pairs={{0,5},{1,4},{2,7},{3,6},{4,1},{5,0},{6,3},{7,2},{8,13},{9,12},{10,... | collective-permute-start | bytes 196616 | tf_op jit(solution)/shard_map/ppermute | solution.py:343
  47.6 14.9 %collective-permute-start.13 = (f16[512,256]{1,0:T(8,128)(2,1)S(1)}, f16[512,256]{1,0:T(8,128)(2,1)S(1)}, u32[]{:S(2)}, u32[]{:S(2)}) collective-permute-start(f16[512,256]{1,0:T(8,128)(2,1)S(1)} %multiply_convert_fusion.2), channel_id=1, source_target_pairs={{0,1},{1,0},{2,3},{3,2},{4,5},{5,4},{6,7},{7,6},{8,9},{9,8},{10,11... | collective-permute-start | bytes 786440 | tf_op jit(solution)/shard_map/ppermute | solution.py:275
  52.3 8.4 %collective-permute-start.12 = (f16[64,256]{1,0:T(8,128)(2,1)S(1)}, f16[64,256]{1,0:T(8,128)(2,1)S(1)}, u32[]{:S(2)}, u32[]{:S(2)}) collective-permute-start(f16[64,256]{1,0:T(8,128)(2,1)S(1)} %multiply_convert_fusion.3), channel_id=1, source_target_pairs={{0,24},{2,26},{4,28},{6,30},{8,16},{10,18},{12,20},{14,22},{16,8},... | collective-permute-start | bytes 98312 | tf_op jit(solution)/shard_map/ppermute | solution.py:275
  57.6 4.8 %collective-permute-start.11 = (f16[64,256]{1,0:T(8,128)(2,1)S(1)}, f16[64,256]{1,0:T(8,128)(2,1)S(1)}, u32[]{:S(2)}, u32[]{:S(2)}) collective-permute-start(f16[64,256]{1,0:T(8,128)(2,1)S(1)} %multiply_convert_fusion.3), channel_id=1, source_target_pairs={{0,16},{2,18},{4,20},{6,22},{8,24},{10,26},{12,28},{14,30},{16,0},... | collective-permute-start | bytes 98312 | tf_op jit(solution)/shard_map/ppermute | solution.py:275
  57.6 4.8 %collective-permute-start.10 = (f16[64,256]{1,0:T(8,128)(2,1)S(1)}, f16[64,256]{1,0:T(8,128)(2,1)S(1)}, u32[]{:S(2)}, u32[]{:S(2)}) collective-permute-start(f16[64,256]{1,0:T(8,128)(2,1)S(1)} %multiply_convert_fusion.3), channel_id=1, source_target_pairs={{0,8},{2,10},{4,12},{6,14},{8,0},{10,2},{12,4},{14,6},{16,24},{18,... | collective-permute-start | bytes 98312 | tf_op jit(solution)/shard_map/ppermute | solution.py:275
  60.6 14.6 %copy-start = (f32[512,256]{1,0:T(8,128)S(1)}, f32[512,256]{1,0:T(8,128)}, u32[]{:S(2)}) copy-start(f32[512,256]{1,0:T(8,128)} %table.2) | copy-start | bytes 1572868
  60.6 14.6 %copy-start.2 = (f32[512]{0:T(512)S(1)}, f32[512]{0:T(512)}, u32[]{:S(2)}) copy-start(f32[512]{0:T(512)} %param.10) | copy-start | bytes 6148
  60.6 16.0 %copy-start.3 = (f32[400]{0:T(512)S(1)}, f32[400]{0:T(512)}, u32[]{:S(2)}) copy-start(f32[400]{0:T(512)} %param.12) | copy-start | bytes 4804
  62.6 12.5 %collective-permute-start.14 = (f16[512,256]{1,0:T(8,128)(2,1)S(1)}, f16[512,256]{1,0:T(8,128)(2,1)S(1)}, u32[]{:S(2)}, u32[]{:S(2)}) collective-permute-start(f16[512,256]{1,0:T(8,128)(2,1)S(1)} %multiply_convert_fusion.1), channel_id=1, source_target_pairs={{0,16},{2,18},{4,20},{6,22},{8,24},{10,26},{12,28},{14,30},{16,0},... | collective-permute-start | bytes 786440 | tf_op jit(solution)/shard_map/ppermute | solution.py:275
  64.7 10.4 %collective-permute-start.18 = (f16[512,256]{1,0:T(8,128)(2,1)S(1)}, f16[512,256]{1,0:T(8,128)(2,1)S(1)}, u32[]{:S(2)}, u32[]{:S(2)}) collective-permute-start(f16[512,256]{1,0:T(8,128)(2,1)S(1)} %multiply_convert_fusion), channel_id=1, source_target_pairs={{0,1},{1,0},{2,3},{3,2},{4,5},{5,4},{6,7},{7,6},{8,9},{9,8},{10,11... | collective-permute-start | bytes 786440 | tf_op jit(solution)/shard_map/ppermute | solution.py:275
  65.0 5.8 %collective-permute-start.17 = (f32[64,256]{1,0:T(8,128)S(1)}, f32[64,256]{1,0:T(8,128)S(1)}, u32[]{:S(2)}, u32[]{:S(2)}) collective-permute-start(f32[64,256]{1,0:T(8,128)S(1)} %add_multiply_fusion.1), channel_id=1, source_target_pairs={{0,5},{1,4},{2,7},{3,6},{4,1},{5,0},{6,3},{7,2},{8,13},{9,12},{10,... | collective-permute-start | bytes 196616 | tf_op jit(solution)/shard_map/ppermute | solution.py:343
  66.2 4.9 %collective-permute-start.16 = (f32[64,256]{1,0:T(8,128)S(1)}, f32[64,256]{1,0:T(8,128)S(1)}, u32[]{:S(2)}, u32[]{:S(2)}) collective-permute-start(f32[64,256]{1,0:T(8,128)S(1)} %add_multiply_fusion.1), channel_id=1, source_target_pairs={{0,4},{1,5},{2,6},{3,7},{4,0},{5,1},{6,2},{7,3},{8,12},{9,13},{10,... | collective-permute-start | bytes 196616 | tf_op jit(solution)/shard_map/ppermute | solution.py:343
  68.1 4.7 %collective-permute-start.15 = (f32[64,256]{1,0:T(8,128)S(1)}, f32[64,256]{1,0:T(8,128)S(1)}, u32[]{:S(2)}, u32[]{:S(2)}) collective-permute-start(f32[64,256]{1,0:T(8,128)S(1)} %add_multiply_fusion.1), channel_id=1, source_target_pairs={{0,1},{1,0},{2,3},{3,2},{4,5},{5,4},{6,7},{7,6},{8,9},{9,8},{10,11... | collective-permute-start | bytes 196616 | tf_op jit(solution)/shard_map/ppermute | solution.py:343
  75.1 1.5 %collective-permute-start.19 = (f32[256,256]{1,0:T(8,128)S(1)}, f32[256,256]{1,0:T(8,128)S(1)}, u32[]{:S(2)}, u32[]{:S(2)}) collective-permute-start(f32[256,256]{1,0:T(8,128)S(1)} %pad_maximum_fusion.mine), channel_id=1, source_target_pairs={{0,2},{2,0},{4,6},{6,4},{8,10},{10,8},{12,14},{14,12},{16,18},{18,... | collective-permute-start | bytes 786440 | tf_op jit(solution)/shard_map/ppermute | solution.py:275
